TPU v7x, 32 devices: a whole 2x2x4 slice. The times are simulated.
32 devices in a mesh: line: 4 (over y, x), patch: 8 (over z, core).
Axes of the slice: x: 2, y: 2, z: 4, core: 2. Of those that a mesh axis runs over, the one named last changes fastest.
Arguments:
- newton_residual: float32 [8, 48, 8, 128], P('line', None, 'patch'), may hold values from -24 to 24
- diag_block: bfloat16 [8, 48, 48, 8, 128], P('line', None, None, 'patch'), may hold values from -0.6 to 5
- lower: bfloat16 [8, 48, 48, 8, 128], P('line', None, None, 'patch'), may hold values from -1.296875 to 1.296875
- upper: bfloat16 [8, 48, 48, 8, 128], P('line', None, None, 'patch'), may hold values from -1.296875 to 1.296875
- west: bfloat16 [8, 48, 48, 8, 128], P('line', None, None, 'patch'), may hold values from -0.5390625 to 0.5390625
- east: bfloat16 [8, 48, 48, 8, 128], P('line', None, None, 'patch'), may hold values from -0.5390625 to 0.5390625
- pivot_inverse: bfloat16 [8, 48, 48, 8, 128], P('line', None, None, 'patch'), may hold values from -0.05 to 0.34
Outputs:
- newton_step: float32 [8, 48, 8, 128], P('line', None, 'patch')
All inputs are finite; a program needn't handle non-finite values.
Results may differ from a plain program's by a relative error of at most 0.0003.
Values sent between devices are 32-bit elements; how exact they have to be, the bound alone decides.
No kernel may reach another device: no remote copies, remote signals or barrier semaphores. Data moves between devices by JAX's collectives and lax.ppermute only.
A program may use at most 64 MiB of HBM per device.

v0:
```python
import jax
import jax.numpy as jnp
from jax import lax
from jax.sharding import PartitionSpec as P

ITERS = 4


def with_halo(block, sides, width):
    for axis, dim in sides:
        count = lax.axis_size(axis)
        forward = [(i, i + 1) for i in range(count - 1)]
        backward = [(target, source) for source, target in forward]
        low = lax.ppermute(
            lax.slice_in_dim(block, block.shape[dim] - width, None, axis=dim), axis, forward
        )
        high = lax.ppermute(lax.slice_in_dim(block, 0, width, axis=dim), axis, backward)
        block = jnp.concatenate([low, block, high], axis=dim)
    return block


def passed_along(block, axis, distance):
    devices = range(lax.axis_size(axis))
    route = [(i - distance, i) for i in devices if i - distance in devices]
    return lax.ppermute(block, axis, route)


def block_apply(block_mat, vector):
    return jnp.sum(block_mat.astype(jnp.float32) * vector[:, None], axis=2)


def single_apply(block_mat, vector):
    return jnp.sum(block_mat.astype(jnp.float32) * vector[None], axis=1)


def operator_apply(field, diag_block, lower, upper, west, east):
    padded = with_halo(field, (("line", 0), ("patch", 2)), 1)
    total = block_apply(diag_block, field) + block_apply(lower, padded[:-2, :, 1:-1])
    total = total + block_apply(upper, padded[2:, :, 1:-1])
    return total + block_apply(west, padded[1:-1, :, :-2]) + block_apply(east, padded[1:-1, :, 2:])


def sweep_down(vector, lower, pivot, incoming):
    previous = incoming
    forward = []
    for k in range(vector.shape[0]):
        previous = single_apply(pivot[k], vector[k] - single_apply(lower[k], previous))
        forward.append(previous)
    return jnp.stack(forward)


def sweep_up(forward, upper, pivot, incoming):
    count = forward.shape[0]
    following = incoming
    result = [None] * count
    for k in reversed(range(count)):
        following = forward[k] - single_apply(pivot[k], single_apply(upper[k], following))
        result[k] = following
    return jnp.stack(result)


def precondition(vector, lower, upper, pivot):
    zero_carry = jnp.zeros_like(vector[0])
    count = lax.axis_size("line")
    incoming = zero_carry
    for turn in range(count - 1):
        outgoing_down = sweep_down(vector, lower, pivot, incoming)[-1]
        incoming = passed_along(outgoing_down, "line", 1)
    forward = sweep_down(vector, lower, pivot, incoming)
    outgoing = zero_carry
    for turn in range(count - 1):
        first_up = sweep_up(forward, upper, pivot, outgoing)[0]
        outgoing = passed_along(first_up, "line", -1)
    return sweep_up(forward, upper, pivot, outgoing)


def norm_squared(vector):
    return lax.psum(jnp.sum(vector * vector), ("line", "patch"))


def least_squares(hess, beta):
    width = hess.shape[1]
    hess_rows = [hess[i] for i in range(width + 1)]
    target = [beta] + [jnp.zeros((), jnp.float32) for i in range(width)]
    for j in range(width):
        first = hess_rows[j][j]
        second = hess_rows[j + 1][j]
        radius = jnp.sqrt(first * first + second * second)
        cosine = first / radius
        sine_part = second / radius
        upper_row = cosine * hess_rows[j] + sine_part * hess_rows[j + 1]
        lower_row = cosine * hess_rows[j + 1] - sine_part * hess_rows[j]
        hess_rows[j] = upper_row
        hess_rows[j + 1] = lower_row
        top_value = cosine * target[j] + sine_part * target[j + 1]
        low_value = cosine * target[j + 1] - sine_part * target[j]
        target[j] = top_value
        target[j + 1] = low_value
    solution = [None] * width
    for i in reversed(range(width)):
        accum_value = target[i]
        for k in range(i + 1, width):
            accum_value = accum_value - hess_rows[i][k] * solution[k]
        solution[i] = accum_value / hess_rows[i][i]
    return solution


def per_device(newton_residual, diag_block, lower, upper, west, east, pivot_inverse):
    beta = jnp.sqrt(norm_squared(newton_residual))
    basis = [newton_residual / beta]
    directions = []
    columns = []
    for j in range(ITERS):
        direction = precondition(basis[j], lower, upper, pivot_inverse)
        directions.append(direction)
        image = operator_apply(direction, diag_block, lower, upper, west, east)
        projections = lax.psum(
            jnp.stack([jnp.sum(member * image) for member in basis]), ("line", "patch")
        )
        for i in range(j + 1):
            image = image - projections[i] * basis[i]
        new_norm = jnp.sqrt(norm_squared(image))
        basis.append(image / new_norm)
        columns.append(
            jnp.concatenate([projections, new_norm[None], jnp.zeros((ITERS - 1 - j,), jnp.float32)])
        )
    hess = jnp.stack(columns, axis=1)
    coeffs = least_squares(hess, beta)
    newton_step = coeffs[0] * directions[0]
    for j in range(1, ITERS):
        newton_step = newton_step + coeffs[j] * directions[j]
    return newton_step


def solution(mesh):
    in_specs = (
        P("line", None, "patch", None),
        P("line", None, None, "patch", None),
        P("line", None, None, "patch", None),
        P("line", None, None, "patch", None),
        P("line", None, None, "patch", None),
        P("line", None, None, "patch", None),
        P("line", None, None, "patch", None),
    )
    out_specs = P("line", None, "patch", None)
    return jax.shard_map(
        per_device, mesh=mesh, in_specs=in_specs, out_specs=out_specs, check_vma=False
    )
```

profile of v0, /device:TPU:0, one launch (start us, length us, event | category | flops | bytes accessed | tf_op | source)
XLA Modules:
  0.0 675.5 jit_solution(16361462118647501193)
XLA Ops:
  0.0 1.6 multiply_reduce_fusion.14
  2.8 42.3 %psum.63 = f32[]{:T(128)} all-reduce(f32[]{:T(128)} %multiply_reduce_fusion.14), channel_id=1, replica_groups=mesh['line'=4,'patch'=8] {'line','patch'}, use_global_device_ids=true, to_apply=%region_1.0 | all-reduce | flops 1 | bytes 8 | tf_op jit(solution)/shard_map/psum | solution.py:78
  49.3 4.3 collective-permute-start
  57.2 4.2 collective-permute-start.1
  61.5 1.5 collective-permute-done.1
  63.7 4.5 collective-permute-start.2
  68.1 1.5 collective-permute-done.2
  72.1 5.6 collective-permute-done.3
  79.7 5.7 collective-permute-done.4
  87.4 5.3 collective-permute-done.5
  94.7 5.7 collective-permute-start.6
  100.4 1.5 collective-permute-done.6
  103.2 3.0 collective-permute-start.8
  110.2 43.0 %psum.64 = f32[1]{0:T(128)} all-reduce(f32[1]{0:T(128)} %bitcast.49), channel_id=1, replica_groups=mesh['line'=4,'patch'=8] {'line','patch'}, use_global_device_ids=true, to_apply=%region_40.0 | all-reduce | flops 1 | bytes 8 | tf_op jit(solution)/shard_map/psum | solution.py:117
  153.2 2.1 multiply_reduce_fusion.12
  155.3 40.7 %psum.65 = f32[]{:T(128)} all-reduce(f32[]{:T(128)} %multiply_reduce_fusion.12), channel_id=1, replica_groups=mesh['line'=4,'patch'=8] {'line','patch'}, use_global_device_ids=true, to_apply=%region_42.0 | all-reduce | flops 1 | bytes 8 | tf_op jit(solution)/shard_map/psum | solution.py:78
  196.7 1.4 broadcast_divide_fusion.2
  199.5 4.2 collective-permute-start.10
  203.7 1.5 collective-permute-done.10
  205.9 4.2 collective-permute-start.11
  210.1 1.5 collective-permute-done.11
  212.3 4.5 collective-permute-start.12
  216.8 1.5 collective-permute-done.12
  220.9 5.6 collective-permute-done.13
  228.5 5.9 collective-permute-done.14
  236.3 5.3 collective-permute-done.15
  242.4 1.4 collective-permute-start.17
  243.8 5.6 collective-permute-start.16
  249.4 1.5 collective-permute-done.16
  252.2 3.0 collective-permute-start.18
  260.3 43.2 %psum.66 = f32[2]{0:T(128)S(1)} all-reduce(f32[2]{0:T(128)S(1)} %pad_maximum_fusion.11), channel_id=1, replica_groups=mesh['line'=4,'patch'=8] {'line','patch'}, use_global_device_ids=true, to_apply=%region_79.0 | all-reduce | flops 2 | bytes 16 | tf_op jit(solution)/shard_map/psum | solution.py:117
  304.0 3.4 multiply_reduce_fusion.9
  307.4 40.1 %psum.67 = f32[]{:T(128)} all-reduce(f32[]{:T(128)} %get-tuple-element.18), channel_id=1, replica_groups=mesh['line'=4,'patch'=8] {'line','patch'}, use_global_device_ids=true, to_apply=%region_81.0 | all-reduce | flops 1 | bytes 8 | tf_op jit(solution)/shard_map/psum | solution.py:78
  350.4 4.4 collective-permute-start.20
  356.8 4.2 collective-permute-start.21
  361.0 1.5 collective-permute-done.21
  363.2 4.5 collective-permute-start.22
  367.7 1.5 collective-permute-done.22
  371.8 5.6 collective-permute-done.23
  379.4 5.8 collective-permute-done.24
  387.2 5.3 collective-permute-done.25
  393.2 1.4 collective-permute-start.27
  394.7 5.7 collective-permute-start.26
  400.3 1.5 collective-permute-done.26
  403.1 3.0 collective-permute-start.28
  409.8 2.0 pad_maximum_fusion.12
  411.8 43.2 %psum.68 = f32[3]{0:T(128)S(1)} all-reduce(f32[3]{0:T(128)S(1)} %pad_maximum_fusion.12), channel_id=1, replica_groups=mesh['line'=4,'patch'=8] {'line','patch'}, use_global_device_ids=true, to_apply=%region_119.0 | all-reduce | flops 3 | bytes 24 | tf_op jit(solution)/shard_map/psum | solution.py:117
  455.7 4.3 multiply_reduce_fusion.5
  459.9 40.1 %psum.69 = f32[]{:T(128)} all-reduce(f32[]{:T(128)} %get-tuple-element.16), channel_id=1, replica_groups=mesh['line'=4,'patch'=8] {'line','patch'}, use_global_device_ids=true, to_apply=%region_121.0 | all-reduce | flops 1 | bytes 8 | tf_op jit(solution)/shard_map/psum | solution.py:78
  502.9 4.2 collective-permute-start.30
  507.1 1.5 collective-permute-done.30
  509.3 4.2 collective-permute-start.31
  513.5 1.5 collective-permute-done.31
  515.8 4.8 collective-permute-start.32
  524.4 5.6 collective-permute-done.33
  532.0 5.9 collective-permute-done.34
  542.9 3.3 collective-permute-done.35
  550.9 6.1 collective-permute-start.36
  560.2 3.0 collective-permute-start.38
  567.9 2.5 pad_maximum_fusion.13
  570.5 42.6 %psum.70 = f32[4]{0:T(128)S(1)} all-reduce(f32[4]{0:T(128)S(1)} %pad_maximum_fusion.13), channel_id=1, replica_groups=mesh['line'=4,'patch'=8] {'line','patch'}, use_global_device_ids=true, to_apply=%region_160.0 | all-reduce | flops 4 | bytes 32 | tf_op jit(solution)/shard_map/psum | solution.py:117
  613.8 3.3 multiply_reduce_fusion
  617.1 39.9 %psum.71 = f32[]{:T(128)} all-reduce(f32[]{:T(128)} %multiply_reduce_fusion), channel_id=1, replica_groups=mesh['line'=4,'patch'=8] {'line','patch'}, use_global_device_ids=true, to_apply=%region_162.0 | all-reduce | flops 1 | bytes 8 | tf_op jit(solution)/shard_map/psum | solution.py:78
  673.6 1.4 multiply_add_fusion
  (383 shorter events, 85.4 us)
Async XLA Ops:
  0.0 49.1 %copy-start = (bf16[2,48,48,1,128]{4,2,3,1,0:T(8,128)(2,1)S(1)}, bf16[2,48,48,1,128]{4,2,3,1,0:T(8,128)(2,1)}, u32[]{:S(2)}) copy-start(bf16[2,48,48,1,128]{4,2,3,1,0:T(8,128)(2,1)} %param.13) | copy-start | bytes 3538948
  2.8 46.5 %copy-start.32 = (f32[48,128]{1,0:T(8,128)}, f32[48,128]{1,0:T(8,128)S(1)}, u32[]{:S(2)}) copy-start(f32[48,128]{1,0:T(8,128)S(1)} %fusion.20) | copy-start | bytes 73732
  2.8 50.8 %copy-start.1 = (bf16[2,48,48,1,128]{4,2,3,1,0:T(8,128)(2,1)S(1)}, bf16[2,48,48,1,128]{4,2,3,1,0:T(8,128)(2,1)}, u32[]{:S(2)}) copy-start(bf16[2,48,48,1,128]{4,2,3,1,0:T(8,128)(2,1)} %param.10) | copy-start | bytes 3538948
  49.3 7.5 %copy-start.2 = (bf16[2,48,48,1,128]{4,2,3,1,0:T(8,128)(2,1)S(1)}, bf16[2,48,48,1,128]{4,2,3,1,0:T(8,128)(2,1)}, u32[]{:S(2)}) copy-start(bf16[2,48,48,1,128]{4,2,3,1,0:T(8,128)(2,1)} %param.9) | copy-start | bytes 3538948
  49.3 5.8 collective-permute-start
  56.8 13.5 %copy-start.37 = (f32[48,128]{1,0:T(8,128)}, f32[48,128]{1,0:T(8,128)S(1)}, u32[]{:S(2)}) copy-start(f32[48,128]{1,0:T(8,128)S(1)} %get-tuple-element.5) | copy-start | bytes 73732
  57.2 5.7 collective-permute-start.1
  63.7 6.0 collective-permute-start.2
  70.8 6.9 %collective-permute-start.3 = (f32[48,1,128]{2,0,1:T(8,128)S(1)}, f32[48,1,128]{2,0,1:T(8,128)S(1)}, u32[]{:S(2)}, u32[]{:S(2)}) collective-permute-start(f32[48,1,128]{2,0,1:T(8,128)S(1)} %subtract_bitcast_fusion.14), channel_id=1, source_target_pairs={{8,0},{16,8},{24,16},{9,1},{17,9},{25,17},{10,2},{18,10},{26,18},{... | collective-permute-start | bytes 73736 | tf_op jit(solution)/shard_map/ppermute | solution.py:25
  78.4 7.0 %collective-permute-start.4 = (f32[48,1,128]{2,0,1:T(8,128)S(1)}, f32[48,1,128]{2,0,1:T(8,128)S(1)}, u32[]{:S(2)}, u32[]{:S(2)}) collective-permute-start(f32[48,1,128]{2,0,1:T(8,128)S(1)} %subtract_bitcast_fusion.13), channel_id=1, source_target_pairs={{8,0},{16,8},{24,16},{9,1},{17,9},{25,17},{10,2},{18,10},{26,18},{... | collective-permute-start | bytes 73736 | tf_op jit(solution)/shard_map/ppermute | solution.py:25
  86.1 6.6 collective-permute-start.5
  92.9 13.4 %copy-start.3 = (bf16[2,48,48,1,128]{4,2,3,1,0:T(8,128)(2,1)S(1)}, bf16[2,48,48,1,128]{4,2,3,1,0:T(8,128)(2,1)}, u32[]{:S(2)}) copy-start(bf16[2,48,48,1,128]{4,2,3,1,0:T(8,128)(2,1)} %param.8) | copy-start | bytes 3538948
  93.1 13.2 %copy-start.28 = (f32[48,128]{1,0:T(8,128)}, f32[48,128]{1,0:T(8,128)S(1)}, u32[]{:S(2)}) copy-start(f32[48,128]{1,0:T(8,128)S(1)} %sub.791) | copy-start | bytes 73732
  93.4 12.9 %copy-start.43 = (f32[1,48,1,128]{3,1,2,0:T(8,128)}, f32[1,48,1,128]{3,1,2,0:T(8,128)S(1)}, u32[]{:S(2)}) copy-start(f32[1,48,1,128]{3,1,2,0:T(8,128)S(1)} %subtract_bitcast_fusion.11) | copy-start | bytes 73732
  93.4 7.0 %collective-permute-start.7 = (f32[1,48,1,128]{3,1,2,0:T(8,128)S(1)}, f32[1,48,1,128]{3,1,2,0:T(8,128)S(1)}, u32[]{:S(2)}, u32[]{:S(2)}) collective-permute-start(f32[1,48,1,128]{3,1,2,0:T(8,128)S(1)} %subtract_bitcast_fusion.11), channel_id=1, source_target_pairs={{8,0},{16,8},{24,16},{9,1},{17,9},{25,17},{10,2},{18,10},{26,18},{... | collective-permute-start | bytes 73736 | tf_op jit(solution)/shard_map/ppermute | solution.py:17
  94.7 7.2 %collective-permute-start.6 = (f32[1,48,1,128]{3,1,2,0:T(8,128)S(1)}, f32[1,48,1,128]{3,1,2,0:T(8,128)S(1)}, u32[]{:S(2)}, u32[]{:S(2)}) collective-permute-start(f32[1,48,1,128]{3,1,2,0:T(8,128)S(1)} %bitcast.430), channel_id=1, source_target_pairs={{0,8},{8,16},{16,24},{1,9},{9,17},{17,25},{2,10},{10,18},{18,26},{... | collective-permute-start | bytes 73736 | tf_op jit(solution)/shard_map/ppermute | solution.py:14
  101.9 5.8 collective-permute-start.9
  103.2 5.8 collective-permute-start.8
  198.1 59.9 %copy-start.19 = (f32[2,6,8,128]{3,2,1,0:T(8,128)}, f32[2,6,8,128]{3,2,1,0:T(8,128)S(1)}, u32[]{:S(2)}) copy-start(f32[2,6,8,128]{3,2,1,0:T(8,128)S(1)} %broadcast_divide_fusion.2) | copy-start | bytes 147460
  199.5 5.7 collective-permute-start.10
  205.9 5.7 collective-permute-start.11
  212.3 6.0 collective-permute-start.12
  219.6 6.9 %collective-permute-start.13 = (f32[48,1,128]{2,0,1:T(8,128)S(1)}, f32[48,1,128]{2,0,1:T(8,128)S(1)}, u32[]{:S(2)}, u32[]{:S(2)}) collective-permute-start(f32[48,1,128]{2,0,1:T(8,128)S(1)} %subtract_bitcast_fusion.10), channel_id=1, source_target_pairs={{8,0},{16,8},{24,16},{9,1},{17,9},{25,17},{10,2},{18,10},{26,18},{... | collective-permute-start | bytes 73736 | tf_op jit(solution)/shard_map/ppermute | solution.py:25
  227.2 7.2 %collective-permute-start.14 = (f32[48,1,128]{2,0,1:T(8,128)S(1)}, f32[48,1,128]{2,0,1:T(8,128)S(1)}, u32[]{:S(2)}, u32[]{:S(2)}) collective-permute-start(f32[48,1,128]{2,0,1:T(8,128)S(1)} %subtract_bitcast_fusion.9), channel_id=1, source_target_pairs={{8,0},{16,8},{24,16},{9,1},{17,9},{25,17},{10,2},{18,10},{26,18},{... | collective-permute-start | bytes 73736 | tf_op jit(solution)/shard_map/ppermute | solution.py:25
  235.0 6.6 collective-permute-start.15
  242.0 13.3 %copy-start.30 = (f32[48,128]{1,0:T(8,128)}, f32[48,128]{1,0:T(8,128)S(1)}, u32[]{:S(2)}) copy-start(f32[48,128]{1,0:T(8,128)S(1)} %sub.813) | copy-start | bytes 73732
  242.2 13.6 %copy-start.4 = (bf16[2,48,48,1,128]{4,2,3,1,0:T(8,128)(2,1)S(1)}, bf16[2,48,48,1,128]{4,2,3,1,0:T(8,128)(2,1)}, u32[]{:S(2)}) copy-start(bf16[2,48,48,1,128]{4,2,3,1,0:T(8,128)(2,1)} %param.8) | copy-start | bytes 3538948
  242.4 12.9 %copy-start.45 = (f32[1,48,1,128]{3,1,2,0:T(8,128)}, f32[1,48,1,128]{3,1,2,0:T(8,128)S(1)}, u32[]{:S(2)}) copy-start(f32[1,48,1,128]{3,1,2,0:T(8,128)S(1)} %subtract_bitcast_fusion.7) | copy-start | bytes 73732
  242.4 7.1 %collective-permute-start.17 = (f32[1,48,1,128]{3,1,2,0:T(8,128)S(1)}, f32[1,48,1,128]{3,1,2,0:T(8,128)S(1)}, u32[]{:S(2)}, u32[]{:S(2)}) collective-permute-start(f32[1,48,1,128]{3,1,2,0:T(8,128)S(1)} %subtract_bitcast_fusion.7), channel_id=1, source_target_pairs={{8,0},{16,8},{24,16},{9,1},{17,9},{25,17},{10,2},{18,10},{26,18},{... | collective-permute-start | bytes 73736 | tf_op jit(solution)/shard_map/ppermute | solution.py:17
  243.8 7.1 %collective-permute-start.16 = (f32[1,48,1,128]{3,1,2,0:T(8,128)S(1)}, f32[1,48,1,128]{3,1,2,0:T(8,128)S(1)}, u32[]{:S(2)}, u32[]{:S(2)}) collective-permute-start(f32[1,48,1,128]{3,1,2,0:T(8,128)S(1)} %bitcast.434), channel_id=1, source_target_pairs={{0,8},{8,16},{16,24},{1,9},{9,17},{17,25},{2,10},{10,18},{18,26},{... | collective-permute-start | bytes 73736 | tf_op jit(solution)/shard_map/ppermute | solution.py:14
  251.0 5.7 collective-permute-start.19
  252.2 5.2 collective-permute-start.18
  350.4 5.7 collective-permute-start.20
  356.8 5.7 collective-permute-start.21
  363.2 6.0 collective-permute-start.22
  370.5 6.9 %collective-permute-start.23 = (f32[48,1,128]{2,0,1:T(8,128)S(1)}, f32[48,1,128]{2,0,1:T(8,128)S(1)}, u32[]{:S(2)}, u32[]{:S(2)}) collective-permute-start(f32[48,1,128]{2,0,1:T(8,128)S(1)} %subtract_bitcast_fusion.6), channel_id=1, source_target_pairs={{8,0},{16,8},{24,16},{9,1},{17,9},{25,17},{10,2},{18,10},{26,18},{... | collective-permute-start | bytes 73736 | tf_op jit(solution)/shard_map/ppermute | solution.py:25
  378.1 7.1 %collective-permute-start.24 = (f32[48,1,128]{2,0,1:T(8,128)S(1)}, f32[48,1,128]{2,0,1:T(8,128)S(1)}, u32[]{:S(2)}, u32[]{:S(2)}) collective-permute-start(f32[48,1,128]{2,0,1:T(8,128)S(1)} %subtract_bitcast_fusion.5), channel_id=1, source_target_pairs={{8,0},{16,8},{24,16},{9,1},{17,9},{25,17},{10,2},{18,10},{26,18},{... | collective-permute-start | bytes 73736 | tf_op jit(solution)/shard_map/ppermute | solution.py:25
  385.9 6.6 collective-permute-start.25
  392.9 13.3 %copy-start.33 = (f32[48,128]{1,0:T(8,128)}, f32[48,128]{1,0:T(8,128)S(1)}, u32[]{:S(2)}) copy-start(f32[48,128]{1,0:T(8,128)S(1)} %sub.836) | copy-start | bytes 73732
  393.0 13.6 %copy-start.5 = (bf16[2,48,48,1,128]{4,2,3,1,0:T(8,128)(2,1)S(1)}, bf16[2,48,48,1,128]{4,2,3,1,0:T(8,128)(2,1)}, u32[]{:S(2)}) copy-start(bf16[2,48,48,1,128]{4,2,3,1,0:T(8,128)(2,1)} %param.8) | copy-start | bytes 3538948
  393.2 13.0 %copy-start.47 = (f32[1,48,1,128]{3,1,2,0:T(8,128)}, f32[1,48,1,128]{3,1,2,0:T(8,128)S(1)}, u32[]{:S(2)}) copy-start(f32[1,48,1,128]{3,1,2,0:T(8,128)S(1)} %subtract_bitcast_fusion.3) | copy-start | bytes 73732
  393.2 7.1 %collective-permute-start.27 = (f32[1,48,1,128]{3,1,2,0:T(8,128)S(1)}, f32[1,48,1,128]{3,1,2,0:T(8,128)S(1)}, u32[]{:S(2)}, u32[]{:S(2)}) collective-permute-start(f32[1,48,1,128]{3,1,2,0:T(8,128)S(1)} %subtract_bitcast_fusion.3), channel_id=1, source_target_pairs={{8,0},{16,8},{24,16},{9,1},{17,9},{25,17},{10,2},{18,10},{26,18},{... | collective-permute-start | bytes 73736 | tf_op jit(solution)/shard_map/ppermute | solution.py:17
  394.7 7.2 %collective-permute-start.26 = (f32[1,48,1,128]{3,1,2,0:T(8,128)S(1)}, f32[1,48,1,128]{3,1,2,0:T(8,128)S(1)}, u32[]{:S(2)}, u32[]{:S(2)}) collective-permute-start(f32[1,48,1,128]{3,1,2,0:T(8,128)S(1)} %bitcast.442), channel_id=1, source_target_pairs={{0,8},{8,16},{16,24},{1,9},{9,17},{17,25},{2,10},{10,18},{18,26},{... | collective-permute-start | bytes 73736 | tf_op jit(solution)/shard_map/ppermute | solution.py:14
  401.8 5.7 collective-permute-start.29
  403.1 5.2 collective-permute-start.28
  502.9 5.7 collective-permute-start.30
  509.3 5.7 collective-permute-start.31
  515.8 6.0 collective-permute-start.32
  522.2 16.4 %copy-start.24 = (f32[48,128]{1,0:T(8,128)}, f32[48,128]{1,0:T(8,128)S(1)}, u32[]{:S(2)}) copy-start(f32[48,128]{1,0:T(8,128)S(1)} %fusion.134) | copy-start | bytes 73732
  522.7 15.5 %copy-start.35 = (f32[48,128]{1,0:T(8,128)}, f32[48,128]{1,0:T(8,128)S(1)}, u32[]{:S(2)}) copy-start(f32[48,128]{1,0:T(8,128)S(1)} %fusion.103) | copy-start | bytes 73732
  523.1 6.9 %collective-permute-start.33 = (f32[48,1,128]{2,0,1:T(8,128)S(1)}, f32[48,1,128]{2,0,1:T(8,128)S(1)}, u32[]{:S(2)}, u32[]{:S(2)}) collective-permute-start(f32[48,1,128]{2,0,1:T(8,128)S(1)} %subtract_bitcast_fusion.2), channel_id=1, source_target_pairs={{8,0},{16,8},{24,16},{9,1},{17,9},{25,17},{10,2},{18,10},{26,18},{... | collective-permute-start | bytes 73736 | tf_op jit(solution)/shard_map/ppermute | solution.py:25
  530.7 7.2 %collective-permute-start.34 = (f32[48,1,128]{2,0,1:T(8,128)S(1)}, f32[48,1,128]{2,0,1:T(8,128)S(1)}, u32[]{:S(2)}, u32[]{:S(2)}) collective-permute-start(f32[48,1,128]{2,0,1:T(8,128)S(1)} %subtract_bitcast_fusion.1), channel_id=1, source_target_pairs={{8,0},{16,8},{24,16},{9,1},{17,9},{25,17},{10,2},{18,10},{26,18},{... | collective-permute-start | bytes 73736 | tf_op jit(solution)/shard_map/ppermute | solution.py:25
  539.2 7.0 %collective-permute-start.35 = (f32[48,1,128]{2,0,1:T(8,128)}, f32[48,1,128]{2,0,1:T(8,128)}, u32[]{:S(2)}, u32[]{:S(2)}) collective-permute-start(f32[48,1,128]{2,0,1:T(8,128)} %subtract_bitcast_fusion), channel_id=1, source_target_pairs={{8,0},{16,8},{24,16},{9,1},{17,9},{25,17},{10,2},{18,10},{26,18},{... | collective-permute-start | bytes 73736 | tf_op jit(solution)/shard_map/ppermute | solution.py:25
  549.0 15.7 %copy-start.6 = (bf16[2,48,48,1,128]{4,2,3,1,0:T(8,128)(2,1)S(1)}, bf16[2,48,48,1,128]{4,2,3,1,0:T(8,128)(2,1)}, u32[]{:S(2)}) copy-start(bf16[2,48,48,1,128]{4,2,3,1,0:T(8,128)(2,1)} %param.8) | copy-start | bytes 3538948
  549.6 7.4 %collective-permute-start.37 = (f32[1,48,1,128]{3,2,1,0:T(1,128)}, f32[1,48,1,128]{3,2,1,0:T(1,128)}, u32[]{:S(2)}, u32[]{:S(2)}) collective-permute-start(f32[1,48,1,128]{3,2,1,0:T(1,128)} %bitcast.164), channel_id=1, source_target_pairs={{8,0},{16,8},{24,16},{9,1},{17,9},{25,17},{10,2},{18,10},{26,18},{... | collective-permute-start | bytes 73736 | tf_op jit(solution)/shard_map/ppermute | solution.py:17
  550.9 7.2 %collective-permute-start.36 = (f32[1,48,1,128]{3,2,1,0:T(1,128)}, f32[1,48,1,128]{3,2,1,0:T(1,128)}, u32[]{:S(2)}, u32[]{:S(2)}) collective-permute-start(f32[1,48,1,128]{3,2,1,0:T(1,128)} %bitcast.165), channel_id=1, source_target_pairs={{0,8},{8,16},{16,24},{1,9},{9,17},{17,25},{2,10},{10,18},{18,26},{... | collective-permute-start | bytes 73736 | tf_op jit(solution)/shard_map/ppermute | solution.py:14
  558.9 6.6 collective-permute-start.39
  560.2 6.2 collective-permute-start.38
  566.4 107.2 %copy-start.29 = (f32[48,128]{1,0:T(8,128)S(1)}, f32[48,128]{1,0:T(8,128)}, u32[]{:S(2)}) copy-start(f32[48,128]{1,0:T(8,128)} %copy-done.28) | copy-start | bytes 73732
  566.4 107.2 %copy-start.31 = (f32[48,128]{1,0:T(8,128)S(1)}, f32[48,128]{1,0:T(8,128)}, u32[]{:S(2)}) copy-start(f32[48,128]{1,0:T(8,128)} %copy-done.30) | copy-start | bytes 73732
  566.4 107.2 %copy-start.34 = (f32[48,128]{1,0:T(8,128)S(1)}, f32[48,128]{1,0:T(8,128)}, u32[]{:S(2)}) copy-start(f32[48,128]{1,0:T(8,128)} %copy-done.33) | copy-start | bytes 73732
  566.4 107.2 %copy-start.44 = (f32[1,48,1,128]{3,1,2,0:T(8,128)S(1)}, f32[1,48,1,128]{3,1,2,0:T(8,128)}, u32[]{:S(2)}) copy-start(f32[1,48,1,128]{3,1,2,0:T(8,128)} %copy-done.43) | copy-start | bytes 73732
  566.5 107.2 %copy-start.46 = (f32[1,48,1,128]{3,1,2,0:T(8,128)S(1)}, f32[1,48,1,128]{3,1,2,0:T(8,128)}, u32[]{:S(2)}) copy-start(f32[1,48,1,128]{3,1,2,0:T(8,128)} %copy-done.45) | copy-start | bytes 73732
  566.5 107.2 %copy-start.48 = (f32[1,48,1,128]{3,1,2,0:T(8,128)S(1)}, f32[1,48,1,128]{3,1,2,0:T(8,128)}, u32[]{:S(2)}) copy-start(f32[1,48,1,128]{3,1,2,0:T(8,128)} %copy-done.47) | copy-start | bytes 73732
  (25 other events, 31.7 us)
where the time goes:
time: 687 us; the launch traced here: 676 us
  blocking collectives  375 us (55%)
  starting transfers between devices  113 us (16%)
  waiting for transfers between devices  87.9 us (13%)
  other arithmetic  70.9 us (10%)
  between operations  19.7 us (3%)
  local copies, waits for them, and re-layouts  8.52 us (1%)
    psum x5, blocking collectives, norm_squared(): return lax.psum(jnp.sum(vector * vector), ('line', 'patch'))  203 us
    psum x4, blocking collectives, per_device(): lax.psum(jnp.stack([jnp.sum(member * image) for member in basis]), ('line...  172 us
    ppermute x24, waiting for transfers between devices, passed_along(): return lax.ppermute(block, axis, route)  82.4 us
    ppermute x24, starting transfers between devices, passed_along(): return lax.ppermute(block, axis, route)  67.6 us
    ppermute x8, starting transfers between devices, with_halo(): lax.ppermute(lax.slice_in_dim(block, block.shape[dim] - width, None, axis...  35.2 us
    reduce_sum x118, other arithmetic, single_apply(): return jnp.sum(block_mat.astype(jnp.float32) * vector[None], axis=1)  24.7 us
    reduce_sum x5, other arithmetic, norm_squared(): return lax.psum(jnp.sum(vector * vector), ('line', 'patch'))  14.7 us
  transfers between devices with their start and end apart: 40, of which 28 were waited for; matrix products, arithmetic and copies ran while one was open for 1% of the time, Pallas kernels for 0%

commit v1 on v0

v1 whole, which is shorter than its diff:
```python
import jax
import jax.numpy as jnp
from jax import lax
from jax.experimental import pallas as pl
from jax.experimental.pallas import tpu as pltpu
from jax.sharding import PartitionSpec as P

ITERS = 4


def single_apply(block_mat, vector):
    return jnp.sum(block_mat.astype(jnp.float32) * vector[None], axis=1)


def block_apply(block_mat, vector):
    return jnp.sum(block_mat.astype(jnp.float32) * vector[:, None], axis=2)


def sweep_down(vector, lower, pivot, incoming):
    previous = incoming
    forward = []
    for k in range(vector.shape[0]):
        previous = single_apply(pivot[k], vector[k] - single_apply(lower[k], previous))
        forward.append(previous)
    return forward


def sweep_up(forward, upper, pivot, incoming):
    count = len(forward)
    following = incoming
    result = [None] * count
    coupled = [None] * count
    for k in reversed(range(count)):
        coupled[k] = single_apply(upper[k], following)
        following = forward[k] - single_apply(pivot[k], coupled[k])
        result[k] = following
    return result, coupled


def precondition(vector, lower, upper, pivot):
    count = lax.axis_size("line")
    incoming = jnp.zeros_like(vector[0])
    for turn in range(count - 1):
        outgoing = sweep_down(vector, lower, pivot, incoming)[-1]
        incoming = incoming + lax.ppermute(outgoing, "line", [(turn, turn + 1)])
    forward = sweep_down(vector, lower, pivot, incoming)
    incoming = jnp.zeros_like(vector[0])
    for turn in reversed(range(count - 1)):
        outgoing = sweep_up(forward, upper, pivot, incoming)[0][0]
        incoming = incoming + lax.ppermute(outgoing, "line", [(turn + 1, turn)])
    result, coupled = sweep_up(forward, upper, pivot, incoming)
    return jnp.stack(result), jnp.stack(coupled)


def rows_beside(field, across):
    count = lax.axis_size("patch")
    even = [(i, i + 1) for i in range(0, count - 1, 2)]
    odd = [(i, i + 1) for i in range(1, count - 1, 2)]
    is_even = lax.axis_index("patch") % 2 == 0
    first, last = field[..., :across], field[..., -across:]
    several = field.shape[-1] > across
    to_far = jnp.where(is_even, first, last) if several else field
    to_near = jnp.where(is_even, last, first) if several else field
    far = lax.ppermute(to_far, "patch", odd + [(b, a) for a, b in odd])
    near = lax.ppermute(to_near, "patch", even + [(b, a) for a, b in even])
    before, after = jnp.where(is_even, far, near), jnp.where(is_even, near, far)
    if several:
        before = jnp.concatenate([before, field[..., :-across]], axis=-1)
        after = jnp.concatenate([field[..., across:], after], axis=-1)
    return before, after


def pairs_of(count):
    return [(i, j) for i in range(count) for j in range(i, count)]


def gram_kernel(*refs):
    ins, out = refs[:-1], refs[-1]
    lane = lax.broadcasted_iota(jnp.int32, (1, 128), 1)
    total = jnp.zeros((1, 128), jnp.float32)
    vectors = [ref[...] for ref in ins]
    for place, (i, j) in enumerate(pairs_of(len(vectors))):
        part = jnp.sum(vectors[i] * vectors[j], axis=0, keepdims=True)
        total = jnp.where(lane == place, jnp.sum(part, axis=1, keepdims=True), total)
    out[...] = jnp.broadcast_to(total, out.shape)


def finish_kernel(parts_ref, *refs):
    directions, out = refs[:-1], refs[-1]
    width = len(directions)
    total = jnp.sum(parts_ref[...], axis=0, keepdims=True)
    lane = lax.broadcasted_iota(jnp.int32, total.shape, 1)
    gram = {}
    for place, pair in enumerate(pairs_of(width + 1)):
        value = jnp.sum(jnp.where(lane == place, total, 0.0), axis=1, keepdims=True)
        gram[pair] = gram[pair[::-1]] = value
    half = [[gram[j + 1, i] + gram[j, i] for i in range(width + 1)] for j in range(width)]
    normal = [[half[j][i + 1] + half[j][i] for i in range(width)] for j in range(width)]
    right = [half[j][0] for j in range(width)]
    for i in range(width):
        inverse = 1.0 / normal[i][i]
        for j in range(i + 1, width):
            factor = normal[j][i] * inverse
            for k in range(i, width):
                normal[j][k] = normal[j][k] - factor * normal[i][k]
            right[j] = right[j] - factor * right[i]
    coeffs = [None] * width
    for i in reversed(range(width)):
        value = right[i]
        for k in range(i + 1, width):
            value = value - normal[i][k] * coeffs[k]
        coeffs[i] = value / normal[i][i]
    step = coeffs[0] * directions[0][...]
    for j in range(1, width):
        step = step + coeffs[j] * directions[j][...]
    out[...] = step


def per_device(newton_residual, diag_block, lower, upper, west, east, pivot_inverse):
    shape = newton_residual.shape
    count, block, rows, across = shape
    wide = rows * across

    def flat(matrix):
        return matrix.reshape(count, block, block, wide)

    diag_block, lower, upper, west, east, pivot = map(
        flat, (diag_block, lower, upper, west, east, pivot_inverse)
    )
    line = lax.axis_size("line")
    devices = line * lax.axis_size("patch")
    basis = [newton_residual.reshape(count, block, wide)]
    directions = []
    for j in range(ITERS):
        direction, coupled = precondition(basis[j], lower, upper, pivot)
        directions.append(direction)
        before, after = rows_beside(direction, across)
        below = lax.ppermute(direction[-1], "line", [(i, i + 1) for i in range(line - 1)])
        image = coupled - basis[j] + block_apply(diag_block, direction)
        image = image + block_apply(lower, jnp.concatenate([below[None], direction[:-1]]))
        image = image + block_apply(west, before) + block_apply(east, after)
        basis.append(image)
    sums = pl.pallas_call(
        gram_kernel,
        out_shape=jax.ShapeDtypeStruct((devices, 128), jnp.float32),
    )(*[member.reshape(count * block, wide) for member in basis])
    sums = lax.all_to_all(sums, ("line", "patch"), 0, 0, tiled=True)
    step = pl.pallas_call(
        finish_kernel,
        out_shape=jax.ShapeDtypeStruct((count * block, wide), jnp.float32),
    )(sums, *[direction.reshape(count * block, wide) for direction in directions])
    return step.reshape(shape)


def solution(mesh):
    blocks = P("line", None, None, "patch", None)
    field = P("line", None, "patch", None)
    return jax.shard_map(
        per_device, mesh=mesh, in_specs=(field,) + (blocks,) * 6, out_specs=field, check_vma=False
    )
```

time: 687 us -> 201 us (0.29); the launches traced: 676 us -> 199 us
  blocking collectives: 375 us -> 23.2 us
  starting transfers between devices: 113 us -> 48.1 us
  other arithmetic: 70.9 us -> 34 us
  between operations: 19.7 us -> 2.18 us
    psum x9 -> x0, blocking collectives: 375 us -> none  [the longest x5 203 us: norm_squared(): return lax.psum(jnp.sum(vector * vector), ('line', 'patch'))]
    ppermute x40 -> x36, starting transfers between devices: 113 us -> 48.1 us  [the longest x12 22.5 us: precondition(): incoming = incoming + lax.ppermute(outgoing, 'line', [(turn, turn + 1)])]
    all_to_all x0 -> x1, blocking collectives: none -> 23.2 us  [per_device(): sums = lax.all_to_all(sums, ('line', 'patch'), 0, 0, tiled=True)]
    reduce_sum x9 -> x0, other arithmetic: 18 us -> none  [the longest x5 14.7 us: norm_squared(): return lax.psum(jnp.sum(vector * vector), ('line', 'patch'))]
    ppermute x40 -> x36, waiting for transfers between devices: 87.9 us -> 86.2 us  [the longest x12 76 us: precondition(): incoming = incoming + lax.ppermute(outgoing, 'line', [(turn + 1, turn)])]
  transfers between devices with their start and end apart: 40 -> 36, of which waited for: 28 -> 13; matrix products, arithmetic and copies ran while one was open for 1% -> 2% of each run, Pallas kernels for 0% -> 0%
where the time goes in v1:
time: 201 us; the launch traced here: 199 us
  waiting for transfers between devices  86.2 us (43%)
  starting transfers between devices  48.1 us (24%)
  other arithmetic  34 us (17%)
  blocking collectives  23.2 us (12%)
  Pallas kernels  3.29 us (2%)
  local copies, waits for them, and re-layouts  2.35 us (1%)
  between operations  2.18 us (1%)
    ppermute x12, waiting for transfers between devices, precondition(): incoming = incoming + lax.ppermute(outgoing, 'line', [(turn + 1, turn)])  76 us
    reduce_sum x118, other arithmetic, single_apply(): return jnp.sum(block_mat.astype(jnp.float32) * vector[None], axis=1)  23.4 us
    all_to_all x1, blocking collectives, per_device(): sums = lax.all_to_all(sums, ('line', 'patch'), 0, 0, tiled=True)  23.2 us
    ppermute x12, starting transfers between devices, precondition(): incoming = incoming + lax.ppermute(outgoing, 'line', [(turn, turn + 1)])  22.5 us
    ppermute x12, starting transfers between devices, precondition(): incoming = incoming + lax.ppermute(outgoing, 'line', [(turn + 1, turn)])  10.6 us
    reduce_sum x14, other arithmetic, block_apply(): return jnp.sum(block_mat.astype(jnp.float32) * vector[:, None], axis=2)  7.12 us
    ppermute x4, starting transfers between devices, per_device(): lax.ppermute(direction[-1], 'line', [(i, i + 1) for i in range(line - 1)])  6.39 us
    ppermute x4, starting transfers between devices, rows_beside(): near = lax.ppermute(to_near, 'patch', even + [(b, a) for a, b in even])  5.71 us
  transfers between devices with their start and end apart: 36, of which 13 were waited for; matrix products, arithmetic and copies ran while one was open for 2% of the time, Pallas kernels for 0%

profile of v1, /device:TPU:0, one launch (start us, length us, event | category | flops | bytes accessed | tf_op | source)
XLA Modules:
  0.0 199.3 jit_solution(3526725174633267057)
XLA Ops:
  0.0 1.3 fusion.16
  1.3 0.7 slice.38
  2.1 0.7 fusion.162
  2.8 1.3 fusion.103
  4.2 1.2 fusion.42
  5.6 4.8 %collective-permute-start = (f32[48,128]{1,0:T(8,128)S(1)}, f32[48,128]{1,0:T(8,128)S(1)}, u32[]{:S(2)}, u32[]{:S(2)}) collective-permute-start(f32[48,128]{1,0:T(8,128)S(1)} %fusion.74), channel_id=1, source_target_pairs={{0,8},{1,9},{2,10},{3,11},{4,12},{5,13},{6,14},{7,15}} | collective-permute-start | bytes 73736 | tf_op jit(solution)/shard_map/ppermute | solution.py:45
  10.4 1.2 fusion.29
  12.9 0.7 collective-permute-start.1
  14.3 0.7 collective-permute-start.2
  15.7 0.7 copy-done.2
  16.8 0.7 collective-permute-start.3
  18.2 0.7 collective-permute-start.4
  19.6 0.6 sub.421
  20.2 1.3 collective-permute-start.5
  21.5 19.2 %collective-permute-done.5 = f32[48,128]{1,0:T(8,128)} collective-permute-done((f32[48,128]{1,0:T(8,128)}, f32[48,128]{1,0:T(8,128)}, u32[]{:S(2)}, u32[]{:S(2)}) %collective-permute-start.5) | collective-permute-done | bytes 24608 | tf_op jit(solution)/shard_map/ppermute | solution.py:50
  40.7 0.8 add.170
  42.0 1.5 collective-permute-start.6
  43.7 1.3 collective-permute-done.6
  45.1 0.7 collective-permute-start.7
  45.8 0.9 fusion
  47.4 1.0 fusion.8
  49.0 4.2 %collective-permute-start.9 = (f32[48,128]{1,0:T(8,128)S(1)}, f32[48,128]{1,0:T(8,128)S(1)}, u32[]{:S(2)}, u32[]{:S(2)}) collective-permute-start(f32[48,128]{1,0:T(8,128)S(1)} %fusion.82), channel_id=1, source_target_pairs={{0,8},{1,9},{2,10},{3,11},{4,12},{5,13},{6,14},{7,15}} | collective-permute-start | bytes 73736 | tf_op jit(solution)/shard_map/ppermute | solution.py:45
  53.2 1.5 collective-permute-done.9
  55.4 0.7 collective-permute-start.10
  56.8 0.7 collective-permute-start.11
  58.7 0.8 collective-permute-start.12
  60.3 0.7 collective-permute-start.13
  61.7 1.3 collective-permute-start.14
  63.0 18.9 %collective-permute-done.14 = f32[48,128]{1,0:T(8,128)S(1)} collective-permute-done((f32[48,128]{1,0:T(8,128)S(1)}, f32[48,128]{1,0:T(8,128)S(1)}, u32[]{:S(2)}, u32[]{:S(2)}) %collective-permute-start.14) | collective-permute-done | bytes 24608 | tf_op jit(solution)/shard_map/ppermute | solution.py:50
  82.4 1.6 collective-permute-start.15
  84.2 1.3 collective-permute-done.15
  85.5 0.4 fusion.1
  86.1 0.7 collective-permute-start.16
  87.7 0.4 fusion.13
  88.7 4.2 %collective-permute-start.18 = (f32[48,128]{1,0:T(8,128)S(1)}, f32[48,128]{1,0:T(8,128)S(1)}, u32[]{:S(2)}, u32[]{:S(2)}) collective-permute-start(f32[48,128]{1,0:T(8,128)S(1)} %fusion.89), channel_id=1, source_target_pairs={{0,8},{1,9},{2,10},{3,11},{4,12},{5,13},{6,14},{7,15}} | collective-permute-start | bytes 73736 | tf_op jit(solution)/shard_map/ppermute | solution.py:45
  93.0 1.5 collective-permute-done.18
  95.2 0.7 collective-permute-start.19
  96.5 0.7 collective-permute-start.20
  98.3 0.7 collective-permute-start.21
  99.7 0.7 collective-permute-start.22
  101.0 1.3 collective-permute-start.23
  102.3 18.9 %collective-permute-done.23 = f32[48,128]{1,0:T(8,128)S(1)} collective-permute-done((f32[48,128]{1,0:T(8,128)S(1)}, f32[48,128]{1,0:T(8,128)S(1)}, u32[]{:S(2)}, u32[]{:S(2)}) %collective-permute-start.23) | collective-permute-done | bytes 24608 | tf_op jit(solution)/shard_map/ppermute | solution.py:50
  121.8 1.6 collective-permute-start.24
  123.6 1.3 collective-permute-done.24
  124.9 0.4 fusion.2
  125.4 1.3 collective-permute-start.26
  126.7 0.9 collective-permute-start.25
  128.5 0.4 fusion.14
  129.5 3.9 %collective-permute-start.27 = (f32[48,128]{1,0:T(8,128)S(1)}, f32[48,128]{1,0:T(8,128)S(1)}, u32[]{:S(2)}, u32[]{:S(2)}) collective-permute-start(f32[48,128]{1,0:T(8,128)S(1)} %fusion.96), channel_id=1, source_target_pairs={{0,8},{1,9},{2,10},{3,11},{4,12},{5,13},{6,14},{7,15}} | collective-permute-start | bytes 73736 | tf_op jit(solution)/shard_map/ppermute | solution.py:45
  133.4 1.5 collective-permute-done.27
  135.6 0.7 collective-permute-start.28
  137.0 0.7 collective-permute-start.29
  138.7 0.7 collective-permute-start.30
  140.1 0.7 collective-permute-start.31
  141.5 1.3 collective-permute-start.32
  142.8 18.9 %collective-permute-done.32 = f32[48,128]{1,0:T(8,128)S(1)} collective-permute-done((f32[48,128]{1,0:T(8,128)S(1)}, f32[48,128]{1,0:T(8,128)S(1)}, u32[]{:S(2)}, u32[]{:S(2)}) %collective-permute-start.32) | collective-permute-done | bytes 24608 | tf_op jit(solution)/shard_map/ppermute | solution.py:50
  162.2 1.6 collective-permute-start.33
  164.1 1.3 collective-permute-done.33
  165.8 4.3 %collective-permute-start.35 = (f32[2,48,128]{2,1,0:T(8,128)S(1)}, f32[2,48,128]{2,1,0:T(8,128)S(1)}, u32[]{:S(2)}, u32[]{:S(2)}) collective-permute-start(f32[2,48,128]{2,1,0:T(8,128)S(1)} %get-tuple-element.26), channel_id=1, source_target_pairs={{0,1},{2,3},{4,5},{6,7},{1,0},{3,2},{5,4},{7,6},{8,9},{10,11},{12,... | collective-permute-start | bytes 147464 | tf_op jit(solution)/shard_map/ppermute | solution.py:65
  170.1 0.7 collective-permute-start.34
  172.1 0.7 bitcast_add_fusion
  172.8 1.6 shard_map.73
  174.5 23.2 %all_to_all.11 = f32[32,1,128]{2,1,0:T(1,128)} all-to-all(f32[32,1,128]{2,1,0:T(1,128)} %bitcast.489), channel_id=1, replica_groups=mesh['line'=4,'patch'=8] {'line','patch'}, dimensions={0} | all-to-all | bytes 32768 | tf_op jit(solution)/shard_map/all_to_all | solution.py:147
  197.7 1.7 shard_map.74
  (279 shorter events, 23.9 us)
Async XLA Ops:
  0.0 5.4 %copy-start = (bf16[2,48,48,1,128]{4,2,3,1,0:T(8,128)(2,1)S(1)}, bf16[2,48,48,1,128]{4,2,3,1,0:T(8,128)(2,1)}, u32[]{:S(2)}) copy-start(bf16[2,48,48,1,128]{4,2,3,1,0:T(8,128)(2,1)} %param.13) | copy-start | bytes 3538948
  1.3 10.3 %copy-start.10 = (f32[48,128]{1,0:T(8,128)}, f32[48,128]{1,0:T(8,128)S(1)}, u32[]{:S(2)}) copy-start(f32[48,128]{1,0:T(8,128)S(1)} %fusion.16) | copy-start | bytes 73732
  2.8 9.1 %copy-start.1 = (bf16[2,48,48,1,128]{4,2,3,1,0:T(8,128)(2,1)S(1)}, bf16[2,48,48,1,128]{4,2,3,1,0:T(8,128)(2,1)}, u32[]{:S(2)}) copy-start(bf16[2,48,48,1,128]{4,2,3,1,0:T(8,128)(2,1)} %param.9) | copy-start | bytes 3538948
  4.1 8.0 %copy-start.6 = (f32[2,48,1,128]{3,2,1,0:T(1,128)S(1)}, f32[2,48,1,128]{3,2,1,0:T(1,128)}, u32[]{:S(2)}) copy-start(f32[2,48,1,128]{3,2,1,0:T(1,128)} %param.7) | copy-start | bytes 147460
  5.6 6.4 %collective-permute-start = (f32[48,128]{1,0:T(8,128)S(1)}, f32[48,128]{1,0:T(8,128)S(1)}, u32[]{:S(2)}, u32[]{:S(2)}) collective-permute-start(f32[48,128]{1,0:T(8,128)S(1)} %fusion.74), channel_id=1, source_target_pairs={{0,8},{1,9},{2,10},{3,11},{4,12},{5,13},{6,14},{7,15}} | collective-permute-start | bytes 73736 | tf_op jit(solution)/shard_map/ppermute | solution.py:45
  12.6 3.2 %copy-start.14 = (f32[48,128]{1,0:T(8,128)}, f32[48,128]{1,0:T(8,128)S(1)}, u32[]{:S(2)}) copy-start(f32[48,128]{1,0:T(8,128)S(1)} %get-tuple-element.5) | copy-start | bytes 73732
  12.9 0.7 collective-permute-start.1
  14.3 0.7 collective-permute-start.2
  15.2 1.3 copy-start.2
  15.3 4.2 %copy-start.8 = (f32[48,128]{1,0:T(8,128)}, f32[48,128]{1,0:T(8,128)S(1)}, u32[]{:S(2)}) copy-start(f32[48,128]{1,0:T(8,128)S(1)} %fusion.106) | copy-start | bytes 73732
  15.7 3.5 %copy-start.12 = (f32[48,128]{1,0:T(8,128)}, f32[48,128]{1,0:T(8,128)S(1)}, u32[]{:S(2)}) copy-start(f32[48,128]{1,0:T(8,128)S(1)} %fusion.77) | copy-start | bytes 73732
  16.8 0.7 collective-permute-start.3
  18.2 0.7 collective-permute-start.4
  18.8 1.3 copy-start.20
  20.2 20.5 %collective-permute-start.5 = (f32[48,128]{1,0:T(8,128)}, f32[48,128]{1,0:T(8,128)}, u32[]{:S(2)}, u32[]{:S(2)}) collective-permute-start(f32[48,128]{1,0:T(8,128)} %sub.421), channel_id=1, source_target_pairs={{8,0},{9,1},{10,2},{11,3},{12,4},{13,5},{14,6},{15,7}} | collective-permute-start | bytes 73736 | tf_op jit(solution)/shard_map/ppermute | solution.py:50
  21.5 20.3 %copy-start.13 = (f32[48,128]{1,0:T(8,128)S(1)}, f32[48,128]{1,0:T(8,128)}, u32[]{:S(2)}) copy-start(f32[48,128]{1,0:T(8,128)} %copy-done.12) | copy-start | bytes 73732
  41.5 2.2 %copy-start.9 = (f32[48,128]{1,0:T(8,128)S(1)}, f32[48,128]{1,0:T(8,128)}, u32[]{:S(2)}) copy-start(f32[48,128]{1,0:T(8,128)} %copy-done.8) | copy-start | bytes 73732
  41.6 4.2 %copy-start.3 = (bf16[2,48,48,1,128]{4,2,3,1,0:T(8,128)(2,1)S(1)}, bf16[2,48,48,1,128]{4,2,3,1,0:T(8,128)(2,1)}, u32[]{:S(2)}) copy-start(bf16[2,48,48,1,128]{4,2,3,1,0:T(8,128)(2,1)} %param.8) | copy-start | bytes 3538948
  42.0 3.0 %collective-permute-start.6 = (f32[48,128]{1,0:T(8,128)S(1)}, f32[48,128]{1,0:T(8,128)S(1)}, u32[]{:S(2)}, u32[]{:S(2)}) collective-permute-start(f32[48,128]{1,0:T(8,128)S(1)} %sub.422), channel_id=1, source_target_pairs={{0,8},{8,16},{16,24},{1,9},{9,17},{17,25},{2,10},{10,18},{18,26},{... | collective-permute-start | bytes 73736 | tf_op jit(solution)/shard_map/ppermute | solution.py:138
  45.0 1.7 copy-start.19
  45.0 1.7 collective-permute-start.8
  45.1 1.7 collective-permute-start.7
  45.8 1.3 copy-start.4
  45.8 1.6 copy-start.5
  47.4 1.0 copy-start.7
  47.4 1.0 copy-start.11
  49.0 5.7 %collective-permute-start.9 = (f32[48,128]{1,0:T(8,128)S(1)}, f32[48,128]{1,0:T(8,128)S(1)}, u32[]{:S(2)}, u32[]{:S(2)}) collective-permute-start(f32[48,128]{1,0:T(8,128)S(1)} %fusion.82), channel_id=1, source_target_pairs={{0,8},{1,9},{2,10},{3,11},{4,12},{5,13},{6,14},{7,15}} | collective-permute-start | bytes 73736 | tf_op jit(solution)/shard_map/ppermute | solution.py:45
  55.4 0.7 collective-permute-start.10
  56.8 0.7 collective-permute-start.11
  57.6 0.7 copy-start.15
  58.7 0.9 collective-permute-start.12
  60.3 0.7 collective-permute-start.13
  61.7 20.2 %collective-permute-start.14 = (f32[48,128]{1,0:T(8,128)S(1)}, f32[48,128]{1,0:T(8,128)S(1)}, u32[]{:S(2)}, u32[]{:S(2)}) collective-permute-start(f32[48,128]{1,0:T(8,128)S(1)} %sub.441), channel_id=1, source_target_pairs={{8,0},{9,1},{10,2},{11,3},{12,4},{13,5},{14,6},{15,7}} | collective-permute-start | bytes 73736 | tf_op jit(solution)/shard_map/ppermute | solution.py:50
  82.4 3.1 %collective-permute-start.15 = (f32[48,128]{1,0:T(8,128)S(1)}, f32[48,128]{1,0:T(8,128)S(1)}, u32[]{:S(2)}, u32[]{:S(2)}) collective-permute-start(f32[48,128]{1,0:T(8,128)S(1)} %sub.442), channel_id=1, source_target_pairs={{0,8},{8,16},{16,24},{1,9},{9,17},{17,25},{2,10},{10,18},{18,26},{... | collective-permute-start | bytes 73736 | tf_op jit(solution)/shard_map/ppermute | solution.py:138
  85.5 1.6 copy-start.16
  86.0 1.3 collective-permute-start.17
  86.1 1.2 collective-permute-start.16
  88.7 5.7 %collective-permute-start.18 = (f32[48,128]{1,0:T(8,128)S(1)}, f32[48,128]{1,0:T(8,128)S(1)}, u32[]{:S(2)}, u32[]{:S(2)}) collective-permute-start(f32[48,128]{1,0:T(8,128)S(1)} %fusion.89), channel_id=1, source_target_pairs={{0,8},{1,9},{2,10},{3,11},{4,12},{5,13},{6,14},{7,15}} | collective-permute-start | bytes 73736 | tf_op jit(solution)/shard_map/ppermute | solution.py:45
  95.2 0.7 collective-permute-start.19
  96.5 0.7 collective-permute-start.20
  98.3 0.7 collective-permute-start.21
  99.7 0.7 collective-permute-start.22
  101.0 20.2 %collective-permute-start.23 = (f32[48,128]{1,0:T(8,128)S(1)}, f32[48,128]{1,0:T(8,128)S(1)}, u32[]{:S(2)}, u32[]{:S(2)}) collective-permute-start(f32[48,128]{1,0:T(8,128)S(1)} %sub.461), channel_id=1, source_target_pairs={{8,0},{9,1},{10,2},{11,3},{12,4},{13,5},{14,6},{15,7}} | collective-permute-start | bytes 73736 | tf_op jit(solution)/shard_map/ppermute | solution.py:50
  121.8 3.1 %collective-permute-start.24 = (f32[48,128]{1,0:T(8,128)S(1)}, f32[48,128]{1,0:T(8,128)S(1)}, u32[]{:S(2)}, u32[]{:S(2)}) collective-permute-start(f32[48,128]{1,0:T(8,128)S(1)} %sub.462), channel_id=1, source_target_pairs={{0,8},{8,16},{16,24},{1,9},{9,17},{17,25},{2,10},{10,18},{18,26},{... | collective-permute-start | bytes 73736 | tf_op jit(solution)/shard_map/ppermute | solution.py:138
  124.9 3.1 %copy-start.17 = (f32[2,48,128]{2,1,0:T(8,128)}, f32[2,48,128]{2,1,0:T(8,128)S(1)}, u32[]{:S(2)}) copy-start(f32[2,48,128]{2,1,0:T(8,128)S(1)} %get-tuple-element.28) | copy-start | bytes 147460
  125.4 2.6 %collective-permute-start.26 = (f32[2,48,128]{2,1,0:T(8,128)S(1)}, f32[2,48,128]{2,1,0:T(8,128)S(1)}, u32[]{:S(2)}, u32[]{:S(2)}) collective-permute-start(f32[2,48,128]{2,1,0:T(8,128)S(1)} %get-tuple-element.28), channel_id=1, source_target_pairs={{0,1},{2,3},{4,5},{6,7},{1,0},{3,2},{5,4},{7,6},{8,9},{10,11},{12,... | collective-permute-start | bytes 147464 | tf_op jit(solution)/shard_map/ppermute | solution.py:65
  126.7 1.3 collective-permute-start.25
  129.5 5.4 %collective-permute-start.27 = (f32[48,128]{1,0:T(8,128)S(1)}, f32[48,128]{1,0:T(8,128)S(1)}, u32[]{:S(2)}, u32[]{:S(2)}) collective-permute-start(f32[48,128]{1,0:T(8,128)S(1)} %fusion.96), channel_id=1, source_target_pairs={{0,8},{1,9},{2,10},{3,11},{4,12},{5,13},{6,14},{7,15}} | collective-permute-start | bytes 73736 | tf_op jit(solution)/shard_map/ppermute | solution.py:45
  135.6 0.7 collective-permute-start.28
  137.0 0.7 collective-permute-start.29
  138.7 0.7 collective-permute-start.30
  140.1 0.7 collective-permute-start.31
  141.5 20.2 %collective-permute-start.32 = (f32[48,128]{1,0:T(8,128)S(1)}, f32[48,128]{1,0:T(8,128)S(1)}, u32[]{:S(2)}, u32[]{:S(2)}) collective-permute-start(f32[48,128]{1,0:T(8,128)S(1)} %sub.481), channel_id=1, source_target_pairs={{8,0},{9,1},{10,2},{11,3},{12,4},{13,5},{14,6},{15,7}} | collective-permute-start | bytes 73736 | tf_op jit(solution)/shard_map/ppermute | solution.py:50
  162.2 3.1 %collective-permute-start.33 = (f32[48,128]{1,0:T(8,128)S(1)}, f32[48,128]{1,0:T(8,128)S(1)}, u32[]{:S(2)}, u32[]{:S(2)}) collective-permute-start(f32[48,128]{1,0:T(8,128)S(1)} %sub.482), channel_id=1, source_target_pairs={{0,8},{8,16},{16,24},{1,9},{9,17},{17,25},{2,10},{10,18},{18,26},{... | collective-permute-start | bytes 73736 | tf_op jit(solution)/shard_map/ppermute | solution.py:138
  165.4 5.8 %copy-start.18 = (f32[2,48,128]{2,1,0:T(8,128)}, f32[2,48,128]{2,1,0:T(8,128)S(1)}, u32[]{:S(2)}) copy-start(f32[2,48,128]{2,1,0:T(8,128)S(1)} %get-tuple-element.26) | copy-start | bytes 147460
  165.8 5.4 %collective-permute-start.35 = (f32[2,48,128]{2,1,0:T(8,128)S(1)}, f32[2,48,128]{2,1,0:T(8,128)S(1)}, u32[]{:S(2)}, u32[]{:S(2)}) collective-permute-start(f32[2,48,128]{2,1,0:T(8,128)S(1)} %get-tuple-element.26), channel_id=1, source_target_pairs={{0,1},{2,3},{4,5},{6,7},{1,0},{3,2},{5,4},{7,6},{8,9},{10,11},{12,... | collective-permute-start | bytes 147464 | tf_op jit(solution)/shard_map/ppermute | solution.py:65
  170.1 1.1 collective-permute-start.34

commit v2 on v1

--- a/solution.py
+++ b/solution.py
@@ -16,12 +16,10 @@
     return jnp.sum(block_mat.astype(jnp.float32) * vector[:, None], axis=2)
 
 
-def sweep_down(vector, lower, pivot, incoming):
-    previous = incoming
-    forward = []
-    for k in range(vector.shape[0]):
-        previous = single_apply(pivot[k], vector[k] - single_apply(lower[k], previous))
-        forward.append(previous)
+def sweep_down(vector, lower, pivot, entry):
+    forward = [single_apply(pivot[0], vector[0] + single_apply(lower[0], entry))]
+    for k in range(1, vector.shape[0]):
+        forward.append(single_apply(pivot[k], vector[k] - single_apply(lower[k], forward[-1])))
     return forward
 
 
@@ -37,19 +35,25 @@
     return result, coupled
 
 
-def precondition(vector, lower, upper, pivot):
+def precondition(vector, last, lower, upper, pivot):
     count = lax.axis_size("line")
-    incoming = jnp.zeros_like(vector[0])
+    incoming = jnp.zeros((1 if last is None else 2,) + vector.shape[1:], vector.dtype)
+
+    def entry():
+        return -incoming[0] if last is None else incoming[1] - incoming[0]
+
     for turn in range(count - 1):
-        outgoing = sweep_down(vector, lower, pivot, incoming)[-1]
-        incoming = incoming + lax.ppermute(outgoing, "line", [(turn, turn + 1)])
-    forward = sweep_down(vector, lower, pivot, incoming)
+        outgoing = sweep_down(vector, lower, pivot, entry())[-1]
+        message = outgoing[None] if last is None else jnp.stack([outgoing, last])
+        incoming = incoming + lax.ppermute(message, "line", [(turn, turn + 1)])
+    forward = sweep_down(vector, lower, pivot, entry())
+    below = None if last is None else incoming[1]
     incoming = jnp.zeros_like(vector[0])
     for turn in reversed(range(count - 1)):
         outgoing = sweep_up(forward, upper, pivot, incoming)[0][0]
         incoming = incoming + lax.ppermute(outgoing, "line", [(turn + 1, turn)])
     result, coupled = sweep_up(forward, upper, pivot, incoming)
-    return jnp.stack(result), jnp.stack(coupled)
+    return jnp.stack(result), jnp.stack(coupled), below
 
 
 def rows_beside(field, across):
@@ -131,13 +135,22 @@
     devices = line * lax.axis_size("patch")
     basis = [newton_residual.reshape(count, block, wide)]
     directions = []
+    last = None
     for j in range(ITERS):
-        direction, coupled = precondition(basis[j], lower, upper, pivot)
+        direction, coupled, below = precondition(basis[j], last, lower, upper, pivot)
+        if below is not None:
+            basis[j] = basis[j].at[0].add(single_apply(lower[0], below))
         directions.append(direction)
         before, after = rows_beside(direction, across)
-        below = lax.ppermute(direction[-1], "line", [(i, i + 1) for i in range(line - 1)])
+        last = direction[-1]
         image = coupled - basis[j] + block_apply(diag_block, direction)
-        image = image + block_apply(lower, jnp.concatenate([below[None], direction[:-1]]))
+        inner = [single_apply(lower[k], direction[k - 1]) for k in range(1, count)]
+        if j == ITERS - 1:
+            below = lax.ppermute(last, "line", [(i, i + 1) for i in range(line - 1)])
+            inner = [single_apply(lower[0], below)] + inner
+        else:
+            inner = [jnp.zeros_like(last)] + inner
+        image = image + jnp.stack(inner)
         image = image + block_apply(west, before) + block_apply(east, after)
         basis.append(image)
     sums = pl.pallas_call(

time: 201 us -> 182 us (0.905)
  blocking collectives: 23.2 us -> 11.8 us
  starting transfers between devices: 48.1 us -> 43.6 us
    ppermute x16 -> x13, starting transfers between devices: 28.9 us -> 16.8 us  [the longest x12 15.1 us: precondition(): incoming = incoming + lax.ppermute(message, 'line', [(turn, turn + 1)])]
    all_to_all x1, blocking collectives: 23.2 us -> 11.8 us  [per_device(): sums = lax.all_to_all(sums, ('line', 'patch'), 0, 0, tiled=True)]
    ppermute x4, starting transfers between devices: 5.71 us -> 13.4 us  [rows_beside(): near = lax.ppermute(to_near, 'patch', even + [(b, a) for a, b in even])]
    ppermute x16 -> x13, waiting for transfers between devices: 10.1 us -> 6.02 us  [the longest x12 6.01 us: precondition(): incoming = incoming + lax.ppermute(message, 'line', [(turn, turn + 1)])]
    reduce_sum x118 -> x123, other arithmetic: 23.4 us -> 25.6 us  [single_apply(): return jnp.sum(block_mat.astype(jnp.float32) * vector[None], axis=1)]
    reduce_sum x14 -> x11, other arithmetic: 7.12 us -> 5.33 us  [block_apply(): return jnp.sum(block_mat.astype(jnp.float32) * vector[:, None], axis=2)]
  transfers between devices with their start and end apart: 36 -> 33, of which waited for: 13 -> 11; matrix products, arithmetic and copies ran while one was open for 2% -> 2% of each run, Pallas kernels for 0% -> 0%
where the time goes in v2:
time: 182 us; the launch traced here: 181 us
  waiting for transfers between devices  84.7 us (47%)
  starting transfers between devices  43.6 us (24%)
  other arithmetic  33.7 us (19%)
  blocking collectives  11.8 us (6%)
  Pallas kernels  3.29 us (2%)
  between operations  2.28 us (1%)
  local copies, waits for them, and re-layouts  1.89 us (1%)
    ppermute x12, waiting for transfers between devices, precondition(): incoming = incoming + lax.ppermute(outgoing, 'line', [(turn + 1, turn)])  77.8 us
    reduce_sum x123, other arithmetic, single_apply(): return jnp.sum(block_mat.astype(jnp.float32) * vector[None], axis=1)  25.6 us
    ppermute x12, starting transfers between devices, precondition(): incoming = incoming + lax.ppermute(message, 'line', [(turn, turn + 1)])  15.1 us
    ppermute x4, starting transfers between devices, rows_beside(): near = lax.ppermute(to_near, 'patch', even + [(b, a) for a, b in even])  13.4 us
    all_to_all x1, blocking collectives, per_device(): sums = lax.all_to_all(sums, ('line', 'patch'), 0, 0, tiled=True)  11.8 us
    ppermute x12, starting transfers between devices, precondition(): incoming = incoming + lax.ppermute(outgoing, 'line', [(turn + 1, turn)])  10.6 us
    ppermute x12, waiting for transfers between devices, precondition(): incoming = incoming + lax.ppermute(message, 'line', [(turn, turn + 1)])  6.01 us
    reduce_sum x11, other arithmetic, block_apply(): return jnp.sum(block_mat.astype(jnp.float32) * vector[:, None], axis=2)  5.33 us
  transfers between devices with their start and end apart: 33, of which 11 were waited for; matrix products, arithmetic and copies ran while one was open for 2% of the time, Pallas kernels for 0%

profile of v2, /device:TPU:0, one launch (start us, length us, event | category | flops | bytes accessed | tf_op | source)
XLA Modules:
  0.0 181.1 jit_solution(17342802059554371493)
XLA Ops:
  0.0 0.9 fusion.192
  0.9 1.2 fusion.41
  2.1 1.3 fusion.108
  3.4 1.2 fusion.59
  4.8 4.8 %collective-permute-start = (f32[1,48,128]{2,1,0:T(8,128)S(1)}, f32[1,48,128]{2,1,0:T(8,128)S(1)}, u32[]{:S(2)}, u32[]{:S(2)}) collective-permute-start(f32[1,48,128]{2,1,0:T(8,128)S(1)} %bitcast.487), channel_id=1, source_target_pairs={{0,8},{1,9},{2,10},{3,11},{4,12},{5,13},{6,14},{7,15}} | collective-permute-start | bytes 73736 | tf_op jit(solution)/shard_map/ppermute | solution.py:48
  9.7 1.2 fusion.12
  12.2 0.7 collective-permute-start.1
  13.6 0.7 collective-permute-start.2
  14.3 0.9 fusion.45
  15.7 0.7 copy-done.2
  16.8 0.7 collective-permute-start.3
  18.2 0.7 collective-permute-start.4
  19.6 0.6 sub.365
  20.2 1.3 collective-permute-start.5
  21.5 19.2 %collective-permute-done.5 = f32[48,128]{1,0:T(8,128)} collective-permute-done((f32[48,128]{1,0:T(8,128)}, f32[48,128]{1,0:T(8,128)}, u32[]{:S(2)}, u32[]{:S(2)}) %collective-permute-start.5) | collective-permute-done | bytes 24608 | tf_op jit(solution)/shard_map/ppermute | solution.py:54
  40.7 0.8 add.213
  42.3 0.8 collective-permute-start.6
  43.1 3.0 %collective-permute-start.7 = (f32[2,48,128]{2,1,0:T(8,128)S(1)}, f32[2,48,128]{2,1,0:T(8,128)S(1)}, u32[]{:S(2)}, u32[]{:S(2)}) collective-permute-start(f32[2,48,128]{2,1,0:T(8,128)S(1)} %pad_maximum_fusion.3), channel_id=1, source_target_pairs={{0,1},{2,3},{4,5},{6,7},{1,0},{3,2},{5,4},{7,6},{8,9},{10,11},{12,... | collective-permute-start | bytes 147464 | tf_op jit(solution)/shard_map/ppermute | solution.py:69
  46.1 0.4 fusion
  47.0 1.0 fusion.4
  48.5 1.5 collective-permute-start.8
  50.1 2.0 %collective-permute-done.8 = f32[2,48,128]{2,1,0:T(8,128)S(1)} collective-permute-done((f32[2,48,128]{2,1,0:T(8,128)S(1)}, f32[2,48,128]{2,1,0:T(8,128)S(1)}, u32[]{:S(2)}, u32[]{:S(2)}) %collective-permute-start.8) | collective-permute-done | bytes 49184 | tf_op jit(solution)/shard_map/ppermute | solution.py:48
  52.8 0.7 collective-permute-start.9
  54.2 0.7 collective-permute-start.10
  56.4 0.8 collective-permute-start.11
  57.9 0.7 collective-permute-start.12
  59.3 1.3 collective-permute-start.13
  60.6 19.4 %collective-permute-done.13 = f32[48,128]{1,0:T(8,128)S(1)} collective-permute-done((f32[48,128]{1,0:T(8,128)S(1)}, f32[48,128]{1,0:T(8,128)S(1)}, u32[]{:S(2)}, u32[]{:S(2)}) %collective-permute-start.13) | collective-permute-done | bytes 24608 | tf_op jit(solution)/shard_map/ppermute | solution.py:54
  80.8 0.7 collective-permute-start.14
  81.4 3.4 %collective-permute-start.15 = (f32[2,48,128]{2,1,0:T(8,128)S(1)}, f32[2,48,128]{2,1,0:T(8,128)S(1)}, u32[]{:S(2)}, u32[]{:S(2)}) collective-permute-start(f32[2,48,128]{2,1,0:T(8,128)S(1)} %pad_maximum_fusion.7), channel_id=1, source_target_pairs={{0,1},{2,3},{4,5},{6,7},{1,0},{3,2},{5,4},{7,6},{8,9},{10,11},{12,... | collective-permute-start | bytes 147464 | tf_op jit(solution)/shard_map/ppermute | solution.py:69
  84.9 0.4 fusion.1
  85.8 0.4 fusion.9
  86.2 0.4 fusion.5
  87.2 1.6 collective-permute-start.16
  88.9 2.0 %collective-permute-done.16 = f32[2,48,128]{2,1,0:T(8,128)S(1)} collective-permute-done((f32[2,48,128]{2,1,0:T(8,128)S(1)}, f32[2,48,128]{2,1,0:T(8,128)S(1)}, u32[]{:S(2)}, u32[]{:S(2)}) %collective-permute-start.16) | collective-permute-done | bytes 49184 | tf_op jit(solution)/shard_map/ppermute | solution.py:48
  91.5 0.7 collective-permute-start.17
  93.0 0.7 collective-permute-start.18
  95.0 0.7 collective-permute-start.19
  96.3 0.7 collective-permute-start.20
  97.7 1.3 collective-permute-start.21
  99.0 19.6 %collective-permute-done.21 = f32[48,128]{1,0:T(8,128)S(1)} collective-permute-done((f32[48,128]{1,0:T(8,128)S(1)}, f32[48,128]{1,0:T(8,128)S(1)}, u32[]{:S(2)}, u32[]{:S(2)}) %collective-permute-start.21) | collective-permute-done | bytes 24608 | tf_op jit(solution)/shard_map/ppermute | solution.py:54
  119.3 0.7 collective-permute-start.22
  120.0 3.5 %collective-permute-start.23 = (f32[2,48,128]{2,1,0:T(8,128)S(1)}, f32[2,48,128]{2,1,0:T(8,128)S(1)}, u32[]{:S(2)}, u32[]{:S(2)}) collective-permute-start(f32[2,48,128]{2,1,0:T(8,128)S(1)} %pad_maximum_fusion.11), channel_id=1, source_target_pairs={{0,1},{2,3},{4,5},{6,7},{1,0},{3,2},{5,4},{7,6},{8,9},{10,11},{12,... | collective-permute-start | bytes 147464 | tf_op jit(solution)/shard_map/ppermute | solution.py:69
  123.5 0.4 fusion.2
  124.4 0.4 fusion.10
  124.8 0.4 fusion.6
  125.8 1.8 %collective-permute-start.24 = (f32[2,48,128]{2,1,0:T(8,128)S(1)}, f32[2,48,128]{2,1,0:T(8,128)S(1)}, u32[]{:S(2)}, u32[]{:S(2)}) collective-permute-start(f32[2,48,128]{2,1,0:T(8,128)S(1)} %pad_maximum_fusion.10), channel_id=1, source_target_pairs={{0,8},{1,9},{2,10},{3,11},{4,12},{5,13},{6,14},{7,15}} | collective-permute-start | bytes 147464 | tf_op jit(solution)/shard_map/ppermute | solution.py:48
  127.7 1.7 collective-permute-done.24
  130.1 0.7 collective-permute-start.25
  131.6 0.7 collective-permute-start.26
  133.3 0.7 collective-permute-start.27
  134.7 0.7 collective-permute-start.28
  136.1 1.3 collective-permute-start.29
  137.4 19.6 %collective-permute-done.29 = f32[48,128]{1,0:T(8,128)S(1)} collective-permute-done((f32[48,128]{1,0:T(8,128)S(1)}, f32[48,128]{1,0:T(8,128)S(1)}, u32[]{:S(2)}, u32[]{:S(2)}) %collective-permute-start.29) | collective-permute-done | bytes 24608 | tf_op jit(solution)/shard_map/ppermute | solution.py:54
  157.3 1.6 collective-permute-start.30
  159.3 0.7 collective-permute-start.31
  160.0 3.5 %collective-permute-start.32 = (f32[2,48,128]{2,1,0:T(8,128)S(1)}, f32[2,48,128]{2,1,0:T(8,128)S(1)}, u32[]{:S(2)}, u32[]{:S(2)}) collective-permute-start(f32[2,48,128]{2,1,0:T(8,128)S(1)} %pad_maximum_fusion.12), channel_id=1, source_target_pairs={{0,1},{2,3},{4,5},{6,7},{1,0},{3,2},{5,4},{7,6},{8,9},{10,11},{12,... | collective-permute-start | bytes 147464 | tf_op jit(solution)/shard_map/ppermute | solution.py:69
  163.5 0.4 fusion.3
  164.6 0.4 fusion.11
  165.0 0.4 fusion.7
  165.4 0.6 fusion.155
  166.1 1.6 shard_map.73
  167.7 11.8 %all_to_all.11 = f32[32,1,128]{2,1,0:T(1,128)} all-to-all(f32[32,1,128]{2,1,0:T(1,128)} %bitcast.486), channel_id=1, replica_groups=mesh['line'=4,'patch'=8] {'line','patch'}, dimensions={0} | all-to-all | bytes 32768 | tf_op jit(solution)/shard_map/all_to_all | solution.py:160
  179.5 1.7 shard_map.74
  (296 shorter events, 21.8 us)
Async XLA Ops:
  0.0 4.7 %copy-start = (bf16[2,48,48,1,128]{4,2,3,1,0:T(8,128)(2,1)S(1)}, bf16[2,48,48,1,128]{4,2,3,1,0:T(8,128)(2,1)}, u32[]{:S(2)}) copy-start(bf16[2,48,48,1,128]{4,2,3,1,0:T(8,128)(2,1)} %param.19) | copy-start | bytes 3538948
  2.1 9.1 %copy-start.1 = (bf16[2,48,48,1,128]{4,2,3,1,0:T(8,128)(2,1)S(1)}, bf16[2,48,48,1,128]{4,2,3,1,0:T(8,128)(2,1)}, u32[]{:S(2)}) copy-start(bf16[2,48,48,1,128]{4,2,3,1,0:T(8,128)(2,1)} %param.15) | copy-start | bytes 3538948
  4.8 6.4 %collective-permute-start = (f32[1,48,128]{2,1,0:T(8,128)S(1)}, f32[1,48,128]{2,1,0:T(8,128)S(1)}, u32[]{:S(2)}, u32[]{:S(2)}) collective-permute-start(f32[1,48,128]{2,1,0:T(8,128)S(1)} %bitcast.487), channel_id=1, source_target_pairs={{0,8},{1,9},{2,10},{3,11},{4,12},{5,13},{6,14},{7,15}} | collective-permute-start | bytes 73736 | tf_op jit(solution)/shard_map/ppermute | solution.py:48
  11.8 3.9 %copy-start.13 = (f32[48,128]{1,0:T(8,128)}, f32[48,128]{1,0:T(8,128)S(1)}, u32[]{:S(2)}) copy-start(f32[48,128]{1,0:T(8,128)S(1)} %get-tuple-element.49) | copy-start | bytes 73732
  12.2 0.7 collective-permute-start.1
  13.6 0.7 collective-permute-start.2
  15.2 1.3 copy-start.2
  15.3 4.2 %copy-start.9 = (f32[48,128]{1,0:T(8,128)}, f32[48,128]{1,0:T(8,128)S(1)}, u32[]{:S(2)}) copy-start(f32[48,128]{1,0:T(8,128)S(1)} %fusion.111) | copy-start | bytes 73732
  15.7 3.5 %copy-start.11 = (f32[48,128]{1,0:T(8,128)}, f32[48,128]{1,0:T(8,128)S(1)}, u32[]{:S(2)}) copy-start(f32[48,128]{1,0:T(8,128)S(1)} %fusion.82) | copy-start | bytes 73732
  16.8 0.7 collective-permute-start.3
  18.2 0.7 collective-permute-start.4
  18.9 0.7 copy-start.21
  20.2 20.5 %collective-permute-start.5 = (f32[48,128]{1,0:T(8,128)}, f32[48,128]{1,0:T(8,128)}, u32[]{:S(2)}, u32[]{:S(2)}) collective-permute-start(f32[48,128]{1,0:T(8,128)} %sub.365), channel_id=1, source_target_pairs={{8,0},{9,1},{10,2},{11,3},{12,4},{13,5},{14,6},{15,7}} | collective-permute-start | bytes 73736 | tf_op jit(solution)/shard_map/ppermute | solution.py:54
  21.5 20.3 %copy-start.12 = (f32[48,128]{1,0:T(8,128)S(1)}, f32[48,128]{1,0:T(8,128)}, u32[]{:S(2)}) copy-start(f32[48,128]{1,0:T(8,128)} %copy-done.11) | copy-start | bytes 73732
  41.5 0.7 copy-start.10
  41.7 4.4 %copy-start.5 = (bf16[2,48,48,1,128]{4,2,3,1,0:T(8,128)(2,1)S(1)}, bf16[2,48,48,1,128]{4,2,3,1,0:T(8,128)(2,1)}, u32[]{:S(2)}) copy-start(bf16[2,48,48,1,128]{4,2,3,1,0:T(8,128)(2,1)} %param.14) | copy-start | bytes 3538948
  42.0 4.9 %copy-start.4 = (bf16[2,48,48,1,128]{4,2,3,1,0:T(8,128)(2,1)S(1)}, bf16[2,48,48,1,128]{4,2,3,1,0:T(8,128)(2,1)}, u32[]{:S(2)}) copy-start(bf16[2,48,48,1,128]{4,2,3,1,0:T(8,128)(2,1)} %param.17) | copy-start | bytes 3538948
  42.2 4.7 %copy-start.3 = (bf16[2,48,48,1,128]{4,2,3,1,0:T(8,128)(2,1)S(1)}, bf16[2,48,48,1,128]{4,2,3,1,0:T(8,128)(2,1)}, u32[]{:S(2)}) copy-start(bf16[2,48,48,1,128]{4,2,3,1,0:T(8,128)(2,1)} %param.18) | copy-start | bytes 3538948
  42.2 3.8 %copy-start.15 = (f32[2,48,128]{2,1,0:T(8,128)}, f32[2,48,128]{2,1,0:T(8,128)S(1)}, u32[]{:S(2)}) copy-start(f32[2,48,128]{2,1,0:T(8,128)S(1)} %pad_maximum_fusion.3) | copy-start | bytes 147460
  42.3 4.4 %collective-permute-start.6 = (f32[2,48,128]{2,1,0:T(8,128)S(1)}, f32[2,48,128]{2,1,0:T(8,128)S(1)}, u32[]{:S(2)}, u32[]{:S(2)}) collective-permute-start(f32[2,48,128]{2,1,0:T(8,128)S(1)} %pad_maximum_fusion.3), channel_id=1, source_target_pairs={{1,2},{3,4},{5,6},{2,1},{4,3},{6,5},{9,10},{11,12},{13,14},{10,9},... | collective-permute-start | bytes 147464 | tf_op jit(solution)/shard_map/ppermute | solution.py:68
  43.1 3.9 %collective-permute-start.7 = (f32[2,48,128]{2,1,0:T(8,128)S(1)}, f32[2,48,128]{2,1,0:T(8,128)S(1)}, u32[]{:S(2)}, u32[]{:S(2)}) collective-permute-start(f32[2,48,128]{2,1,0:T(8,128)S(1)} %pad_maximum_fusion.3), channel_id=1, source_target_pairs={{0,1},{2,3},{4,5},{6,7},{1,0},{3,2},{5,4},{7,6},{8,9},{10,11},{12,... | collective-permute-start | bytes 147464 | tf_op jit(solution)/shard_map/ppermute | solution.py:69
  47.0 1.0 copy-start.19
  47.0 1.0 copy-start.20
  48.5 3.5 %collective-permute-start.8 = (f32[2,48,128]{2,1,0:T(8,128)S(1)}, f32[2,48,128]{2,1,0:T(8,128)S(1)}, u32[]{:S(2)}, u32[]{:S(2)}) collective-permute-start(f32[2,48,128]{2,1,0:T(8,128)S(1)} %pad_maximum_fusion.2), channel_id=1, source_target_pairs={{0,8},{1,9},{2,10},{3,11},{4,12},{5,13},{6,14},{7,15}} | collective-permute-start | bytes 147464 | tf_op jit(solution)/shard_map/ppermute | solution.py:48
  52.8 0.7 collective-permute-start.9
  54.2 0.7 collective-permute-start.10
  55.3 0.7 copy-start.14
  55.7 31.0 %copy-start.6 = (f32[2,48,128]{2,1,0:T(8,128)}, f32[2,48,128]{2,1,0:T(8,128)S(1)}, u32[]{:S(2)}) copy-start(f32[2,48,128]{2,1,0:T(8,128)S(1)} %get-tuple-element.68) | copy-start | bytes 147460
  56.4 0.9 collective-permute-start.11
  57.9 0.7 collective-permute-start.12
  59.3 20.7 %collective-permute-start.13 = (f32[48,128]{1,0:T(8,128)S(1)}, f32[48,128]{1,0:T(8,128)S(1)}, u32[]{:S(2)}, u32[]{:S(2)}) collective-permute-start(f32[48,128]{1,0:T(8,128)S(1)} %sub.383), channel_id=1, source_target_pairs={{8,0},{9,1},{10,2},{11,3},{12,4},{13,5},{14,6},{15,7}} | collective-permute-start | bytes 73736 | tf_op jit(solution)/shard_map/ppermute | solution.py:54
  80.8 5.5 %copy-start.16 = (f32[2,48,128]{2,1,0:T(8,128)}, f32[2,48,128]{2,1,0:T(8,128)S(1)}, u32[]{:S(2)}) copy-start(f32[2,48,128]{2,1,0:T(8,128)S(1)} %pad_maximum_fusion.7) | copy-start | bytes 147460
  80.8 4.7 %collective-permute-start.14 = (f32[2,48,128]{2,1,0:T(8,128)S(1)}, f32[2,48,128]{2,1,0:T(8,128)S(1)}, u32[]{:S(2)}, u32[]{:S(2)}) collective-permute-start(f32[2,48,128]{2,1,0:T(8,128)S(1)} %pad_maximum_fusion.7), channel_id=1, source_target_pairs={{1,2},{3,4},{5,6},{2,1},{4,3},{6,5},{9,10},{11,12},{13,14},{10,9},... | collective-permute-start | bytes 147464 | tf_op jit(solution)/shard_map/ppermute | solution.py:68
  81.4 4.3 %collective-permute-start.15 = (f32[2,48,128]{2,1,0:T(8,128)S(1)}, f32[2,48,128]{2,1,0:T(8,128)S(1)}, u32[]{:S(2)}, u32[]{:S(2)}) collective-permute-start(f32[2,48,128]{2,1,0:T(8,128)S(1)} %pad_maximum_fusion.7), channel_id=1, source_target_pairs={{0,1},{2,3},{4,5},{6,7},{1,0},{3,2},{5,4},{7,6},{8,9},{10,11},{12,... | collective-permute-start | bytes 147464 | tf_op jit(solution)/shard_map/ppermute | solution.py:69
  87.2 3.6 %collective-permute-start.16 = (f32[2,48,128]{2,1,0:T(8,128)S(1)}, f32[2,48,128]{2,1,0:T(8,128)S(1)}, u32[]{:S(2)}, u32[]{:S(2)}) collective-permute-start(f32[2,48,128]{2,1,0:T(8,128)S(1)} %pad_maximum_fusion.6), channel_id=1, source_target_pairs={{0,8},{1,9},{2,10},{3,11},{4,12},{5,13},{6,14},{7,15}} | collective-permute-start | bytes 147464 | tf_op jit(solution)/shard_map/ppermute | solution.py:48
  91.5 0.7 collective-permute-start.17
  93.0 0.7 collective-permute-start.18
  94.4 30.9 %copy-start.7 = (f32[2,48,128]{2,1,0:T(8,128)}, f32[2,48,128]{2,1,0:T(8,128)S(1)}, u32[]{:S(2)}) copy-start(f32[2,48,128]{2,1,0:T(8,128)S(1)} %get-tuple-element.64) | copy-start | bytes 147460
  95.0 0.7 collective-permute-start.19
  96.3 0.7 collective-permute-start.20
  97.7 20.9 %collective-permute-start.21 = (f32[48,128]{1,0:T(8,128)S(1)}, f32[48,128]{1,0:T(8,128)S(1)}, u32[]{:S(2)}, u32[]{:S(2)}) collective-permute-start(f32[48,128]{1,0:T(8,128)S(1)} %sub.401), channel_id=1, source_target_pairs={{8,0},{9,1},{10,2},{11,3},{12,4},{13,5},{14,6},{15,7}} | collective-permute-start | bytes 73736 | tf_op jit(solution)/shard_map/ppermute | solution.py:54
  119.3 5.5 %copy-start.17 = (f32[2,48,128]{2,1,0:T(8,128)}, f32[2,48,128]{2,1,0:T(8,128)S(1)}, u32[]{:S(2)}) copy-start(f32[2,48,128]{2,1,0:T(8,128)S(1)} %pad_maximum_fusion.11) | copy-start | bytes 147460
  119.3 4.8 %collective-permute-start.22 = (f32[2,48,128]{2,1,0:T(8,128)S(1)}, f32[2,48,128]{2,1,0:T(8,128)S(1)}, u32[]{:S(2)}, u32[]{:S(2)}) collective-permute-start(f32[2,48,128]{2,1,0:T(8,128)S(1)} %pad_maximum_fusion.11), channel_id=1, source_target_pairs={{1,2},{3,4},{5,6},{2,1},{4,3},{6,5},{9,10},{11,12},{13,14},{10,9},... | collective-permute-start | bytes 147464 | tf_op jit(solution)/shard_map/ppermute | solution.py:68
  120.0 4.4 %collective-permute-start.23 = (f32[2,48,128]{2,1,0:T(8,128)S(1)}, f32[2,48,128]{2,1,0:T(8,128)S(1)}, u32[]{:S(2)}, u32[]{:S(2)}) collective-permute-start(f32[2,48,128]{2,1,0:T(8,128)S(1)} %pad_maximum_fusion.11), channel_id=1, source_target_pairs={{0,1},{2,3},{4,5},{6,7},{1,0},{3,2},{5,4},{7,6},{8,9},{10,11},{12,... | collective-permute-start | bytes 147464 | tf_op jit(solution)/shard_map/ppermute | solution.py:69
  125.8 3.6 %collective-permute-start.24 = (f32[2,48,128]{2,1,0:T(8,128)S(1)}, f32[2,48,128]{2,1,0:T(8,128)S(1)}, u32[]{:S(2)}, u32[]{:S(2)}) collective-permute-start(f32[2,48,128]{2,1,0:T(8,128)S(1)} %pad_maximum_fusion.10), channel_id=1, source_target_pairs={{0,8},{1,9},{2,10},{3,11},{4,12},{5,13},{6,14},{7,15}} | collective-permute-start | bytes 147464 | tf_op jit(solution)/shard_map/ppermute | solution.py:48
  130.1 0.7 collective-permute-start.25
  131.6 0.7 collective-permute-start.26
  133.3 0.7 collective-permute-start.27
  134.7 0.7 collective-permute-start.28
  136.1 20.9 %collective-permute-start.29 = (f32[48,128]{1,0:T(8,128)S(1)}, f32[48,128]{1,0:T(8,128)S(1)}, u32[]{:S(2)}, u32[]{:S(2)}) collective-permute-start(f32[48,128]{1,0:T(8,128)S(1)} %sub.419), channel_id=1, source_target_pairs={{8,0},{9,1},{10,2},{11,3},{12,4},{13,5},{14,6},{15,7}} | collective-permute-start | bytes 73736 | tf_op jit(solution)/shard_map/ppermute | solution.py:54
  157.3 6.8 %collective-permute-start.30 = (f32[48,128]{1,0:T(8,128)S(1)}, f32[48,128]{1,0:T(8,128)S(1)}, u32[]{:S(2)}, u32[]{:S(2)}) collective-permute-start(f32[48,128]{1,0:T(8,128)S(1)} %sub.420), channel_id=1, source_target_pairs={{0,8},{8,16},{16,24},{1,9},{9,17},{17,25},{2,10},{10,18},{18,26},{... | collective-permute-start | bytes 73736 | tf_op jit(solution)/shard_map/ppermute | solution.py:149
  159.3 5.2 %copy-start.18 = (f32[2,48,128]{2,1,0:T(8,128)}, f32[2,48,128]{2,1,0:T(8,128)S(1)}, u32[]{:S(2)}) copy-start(f32[2,48,128]{2,1,0:T(8,128)S(1)} %pad_maximum_fusion.12) | copy-start | bytes 147460
  159.3 5.2 %collective-permute-start.31 = (f32[2,48,128]{2,1,0:T(8,128)S(1)}, f32[2,48,128]{2,1,0:T(8,128)S(1)}, u32[]{:S(2)}, u32[]{:S(2)}) collective-permute-start(f32[2,48,128]{2,1,0:T(8,128)S(1)} %pad_maximum_fusion.12), channel_id=1, source_target_pairs={{1,2},{3,4},{5,6},{2,1},{4,3},{6,5},{9,10},{11,12},{13,14},{10,9},... | collective-permute-start | bytes 147464 | tf_op jit(solution)/shard_map/ppermute | solution.py:68
  160.0 4.5 %collective-permute-start.32 = (f32[2,48,128]{2,1,0:T(8,128)S(1)}, f32[2,48,128]{2,1,0:T(8,128)S(1)}, u32[]{:S(2)}, u32[]{:S(2)}) collective-permute-start(f32[2,48,128]{2,1,0:T(8,128)S(1)} %pad_maximum_fusion.12), channel_id=1, source_target_pairs={{0,1},{2,3},{4,5},{6,7},{1,0},{3,2},{5,4},{7,6},{8,9},{10,11},{12,... | collective-permute-start | bytes 147464 | tf_op jit(solution)/shard_map/ppermute | solution.py:69
  164.5 0.9 copy-start.8

commit v3 on v2

--- a/solution.py
+++ b/solution.py
@@ -35,25 +35,186 @@
     return result, coupled
 
 
-def precondition(vector, last, lower, upper, pivot):
+def down_entry(message):
+    return -message[0] if message.shape[0] == 1 else message[1] - message[0]
+
+
+def precondition(vector, last, lower, upper, pivot, products=None):
     count = lax.axis_size("line")
     incoming = jnp.zeros((1 if last is None else 2,) + vector.shape[1:], vector.dtype)
-
-    def entry():
-        return -incoming[0] if last is None else incoming[1] - incoming[0]
-
     for turn in range(count - 1):
-        outgoing = sweep_down(vector, lower, pivot, entry())[-1]
+        outgoing = sweep_down(vector, lower, pivot, down_entry(incoming))[-1]
+        if products is not None:
+            products.down(turn, outgoing)
         message = outgoing[None] if last is None else jnp.stack([outgoing, last])
         incoming = incoming + lax.ppermute(message, "line", [(turn, turn + 1)])
-    forward = sweep_down(vector, lower, pivot, entry())
+    forward = sweep_down(vector, lower, pivot, down_entry(incoming))
     below = None if last is None else incoming[1]
     incoming = jnp.zeros_like(vector[0])
-    for turn in reversed(range(count - 1)):
+    for turn in range(count - 1):
         outgoing = sweep_up(forward, upper, pivot, incoming)[0][0]
-        incoming = incoming + lax.ppermute(outgoing, "line", [(turn + 1, turn)])
+        if products is not None:
+            outgoing = products.up(turn, outgoing)
+        pair = (count - 1 - turn, count - 2 - turn)
+        incoming = incoming + lax.ppermute(outgoing, "line", [pair])
     result, coupled = sweep_up(forward, upper, pivot, incoming)
     return jnp.stack(result), jnp.stack(coupled), below
+
+
+def short_precondition(vector, last, lower, upper, pivot, near, far):
+    nothing = jnp.zeros_like(last)
+    outgoing = sweep_down(vector, lower, pivot, nothing)[-1]
+    first = lax.ppermute(jnp.stack([outgoing, last]), "line", [(0, 1), (2, 3)])
+    entry = down_entry(first)
+    message = jnp.stack([sweep_down(vector, lower, pivot, entry)[-1], last])
+    to_last = lax.ppermute(message, "line", [(1, 3)])
+    to_next = lax.ppermute(message, "line", [(1, 2)])
+    entry = entry + down_entry(to_next) + single_apply(near, down_entry(to_last))
+    below = first[1] + to_next[1]
+    forward = sweep_down(vector, lower, pivot, entry)
+    outgoing = sweep_up(forward, upper, pivot, nothing)[0][0]
+    third = lax.ppermute(outgoing, "line", [(3, 0)])
+    second = lax.ppermute(outgoing, "line", [(2, 0)])
+    beside = lax.ppermute(outgoing, "line", [(3, 2), (1, 0)])
+    incoming = beside + single_apply(near, second + single_apply(far, third))
+    outgoing = sweep_up(forward, upper, pivot, incoming)[0][0]
+    incoming = incoming + lax.ppermute(outgoing, "line", [(2, 1)])
+    result, coupled = sweep_up(forward, upper, pivot, incoming)
+    return jnp.stack(result), jnp.stack(coupled), below
+
+
+def multiply_lines(left, right, out):
+    block = right.shape[0]
+    group = max(g for g in (1, 2, 3, 4) if block % g == 0)
+    unroll = max(u for u in (1, 2, 4, 8) if block % u == 0)
+
+    def rows(step, carry):
+        start = step * group
+
+        def add(j, totals):
+            row = right[j]
+            return tuple(
+                total + left[start + q, pl.ds(j, 1), :] * row for q, total in enumerate(totals)
+            )
+
+        zero = jnp.zeros(right.shape[1:], jnp.float32)
+        totals = lax.fori_loop(0, block, add, (zero,) * group, unroll=unroll)
+        for q, total in enumerate(totals):
+            out[start + q] = total
+        return carry
+
+    lax.fori_loop(0, block // group, rows, 0)
+
+
+def factors_kernel(up_on, down_on, lower, upper, pivot, after, out, held, left, right, made, sem):
+    me = lax.axis_index("line")
+    up = me == up_on
+
+    def widen(source, target):
+        def row(i, carry):
+            target[i] = source[i].astype(jnp.float32)
+            return carry
+
+        lax.fori_loop(0, target.shape[0], row, 0, unroll=4)
+
+    def run(coupling, order):
+        for place, k in enumerate(order):
+            copies = [
+                pltpu.make_async_copy(pivot.at[k], held.at[0], sem.at[0]),
+                pltpu.make_async_copy(coupling.at[k], held.at[1], sem.at[1]),
+            ]
+            for copy in copies:
+                copy.start()
+            for copy in copies:
+                copy.wait()
+            widen(held.at[0], left)
+            widen(held.at[1], right)
+            multiply_lines(left, right, made)
+            copy = pltpu.make_async_copy(made, out.at[place], sem.at[0])
+            copy.start()
+            copy.wait()
+
+    if up_on is not None:
+        pl.when(up)(lambda: run(upper, (0, 1)))
+    if down_on is not None:
+        pl.when(me == down_on)(lambda: run(lower, (1, 0)))
+
+
+def factors(up_on, down_on, lower, upper, pivot, after):
+    shape = lower.shape[1:]
+    anywhere = pl.BlockSpec(memory_space=pl.ANY)
+    return pl.pallas_call(
+        lambda *refs: factors_kernel(up_on, down_on, *refs),
+        out_shape=jax.ShapeDtypeStruct((2,) + shape, jnp.float32),
+        in_specs=[anywhere] * 4,
+        out_specs=anywhere,
+        scratch_shapes=[
+            pltpu.VMEM((2,) + shape, lower.dtype),
+            pltpu.VMEM(shape, jnp.float32),
+            pltpu.VMEM(shape, jnp.float32),
+            pltpu.VMEM(shape, jnp.float32),
+            pltpu.SemaphoreType.DMA((2,)),
+        ],
+        compiler_params=pltpu.CompilerParams(vmem_limit_bytes=12 << 20),
+    )(lower, upper, pivot, after)
+
+
+def product_kernel(on, pair, after, out, left, right, made, sem):
+    me = lax.axis_index("line")
+    here = me == on[0]
+    for other in on[1:]:
+        here = here | (me == other)
+
+    @pl.when(here)
+    def _():
+        copies = [
+            pltpu.make_async_copy(pair.at[0], left, sem.at[0]),
+            pltpu.make_async_copy(pair.at[1], right, sem.at[1]),
+        ]
+        for copy in copies:
+            copy.start()
+        for copy in copies:
+            copy.wait()
+        multiply_lines(left, right, made)
+        copy = pltpu.make_async_copy(made, out, sem.at[0])
+        copy.start()
+        copy.wait()
+
+
+def product(on, pair, after):
+    shape = pair.shape[1:]
+    anywhere = pl.BlockSpec(memory_space=pl.ANY)
+    return pl.pallas_call(
+        lambda *refs: product_kernel(on, *refs),
+        out_shape=jax.ShapeDtypeStruct(shape, jnp.float32),
+        in_specs=[anywhere] * 2,
+        out_specs=anywhere,
+        scratch_shapes=[pltpu.VMEM(shape, jnp.float32)] * 3 + [pltpu.SemaphoreType.DMA((2,))],
+        compiler_params=pltpu.CompilerParams(vmem_limit_bytes=12 << 20),
+    )(pair, after)
+
+
+class Products:
+    def __init__(self, vector, lower, upper, pivot):
+        self.blocks = lower, upper, pivot
+        self.early = product((2,), factors(2, None, *self.blocks, vector), vector)
+
+    def down(self, turn, outgoing):
+        if turn == 1:
+            early, _ = lax.optimization_barrier((self.early, outgoing))
+            self.far = lax.ppermute(early, "line", [(2, 0)])
+        if turn == 2:
+            self.pair = factors(1, 2, *self.blocks, outgoing)
+
+    def up(self, turn, outgoing):
+        if turn == 0:
+            outgoing, self.pair = lax.optimization_barrier((outgoing, self.pair))
+        if turn == 1:
+            self.made = product((1, 2), self.pair, outgoing)
+        if turn == 2:
+            outgoing, made = lax.optimization_barrier((outgoing, self.made))
+            self.near = lax.ppermute(made, "line", [(1, 0), (2, 3)])
+        return outgoing
 
 
 def rows_beside(field, across):
@@ -136,8 +297,16 @@
     basis = [newton_residual.reshape(count, block, wide)]
     directions = []
     last = None
+    short = line == 4 and count == 2
     for j in range(ITERS):
-        direction, coupled, below = precondition(basis[j], last, lower, upper, pivot)
+        blocks = lower, upper, pivot
+        if j == 0 or not short:
+            products = Products(basis[0], *blocks) if short else None
+            direction, coupled, below = precondition(basis[j], last, *blocks, products)
+        else:
+            direction, coupled, below = short_precondition(
+                basis[j], last, *blocks, products.near, products.far
+            )
         if below is not None:
             basis[j] = basis[j].at[0].add(single_apply(lower[0], below))
         directions.append(direction)

time: 182 us -> 205 us (1.13)
  starting transfers between devices: 43.6 us -> 71.1 us
  other arithmetic: 33.7 us -> 30.9 us
    ppermute x12 -> x26, starting transfers between devices: 10.6 us -> 39.3 us  [the longest x3 16.4 us: short_precondition(): first = lax.ppermute(jnp.stack([outgoing, last]), 'line', [(0, 1), (2, 3)])]
    ppermute x12 -> x3, starting transfers between devices: 15.1 us -> 6.17 us  [precondition(): incoming = incoming + lax.ppermute(message, 'line', [(turn, turn + 1)])]
    ppermute x1, starting transfers between devices: 1.62 us -> 9.54 us  [per_device(): below = lax.ppermute(last, 'line', [(i, i + 1) for i in range(line - 1)])]
    ppermute x12 -> x3, waiting for transfers between devices: 6.01 us -> 0.28 us  [precondition(): incoming = incoming + lax.ppermute(message, 'line', [(turn, turn + 1)])]
    ppermute x12 -> x26, waiting for transfers between devices: 77.8 us -> 81.4 us  [the longest x3 27.5 us: precondition(): incoming = incoming + lax.ppermute(outgoing, 'line', [pair])]
    reduce_sum x123 -> x108, other arithmetic: 25.6 us -> 22.9 us  [single_apply(): return jnp.sum(block_mat.astype(jnp.float32) * vector[None], axis=1)]
  transfers between devices with their start and end apart: 33 -> 38, of which waited for: 11 -> 16; matrix products, arithmetic and copies ran while one was open for 2% -> 3% of each run, Pallas kernels for 0% -> 0%
where the time goes in v3:
time: 205 us; the launch traced here: 204 us
  waiting for transfers between devices  83.8 us (41%)
  starting transfers between devices  71.1 us (35%)
  other arithmetic  30.9 us (15%)
  blocking collectives  10.8 us (5%)
  Pallas kernels  3.41 us (2%)
  between operations  2.14 us (1%)
    ppermute x3, waiting for transfers between devices, precondition(): incoming = incoming + lax.ppermute(outgoing, 'line', [pair])  27.5 us
    ppermute x1, waiting for transfers between devices, up(): self.near = lax.ppermute(made, 'line', [(1, 0), (2, 3)])  25 us
    reduce_sum x108, other arithmetic, single_apply(): return jnp.sum(block_mat.astype(jnp.float32) * vector[None], axis=1)  22.9 us
    ppermute x3, starting transfers between devices, short_precondition(): first = lax.ppermute(jnp.stack([outgoing, last]), 'line', [(0, 1), (2, 3)])  16.4 us
    ppermute x4, starting transfers between devices, rows_beside(): near = lax.ppermute(to_near, 'patch', even + [(b, a) for a, b in even])  13 us
    all_to_all x1, blocking collectives, per_device(): sums = lax.all_to_all(sums, ('line', 'patch'), 0, 0, tiled=True)  10.8 us
    ppermute x1, waiting for transfers between devices, down(): self.far = lax.ppermute(early, 'line', [(2, 0)])  10.7 us
    ppermute x3, waiting for transfers between devices, short_precondition(): third = lax.ppermute(outgoing, 'line', [(3, 0)])  10.2 us
  transfers between devices with their start and end apart: 38, of which 16 were waited for; matrix products, arithmetic and copies ran while one was open for 3% of the time, Pallas kernels for 0%

profile of v3, /device:TPU:0, one launch (start us, length us, event | category | flops | bytes accessed | tf_op | source)
XLA Modules:
  0.0 203.6 jit_solution(6781779238746458027)
XLA Ops:
  0.0 1.3 fusion.35
  1.3 0.8 fusion.168
  2.1 1.3 fusion.90
  3.4 1.2 fusion.50
  4.8 4.8 %collective-permute-start = (f32[1,48,128]{2,1,0:T(8,128)S(1)}, f32[1,48,128]{2,1,0:T(8,128)S(1)}, u32[]{:S(2)}, u32[]{:S(2)}) collective-permute-start(f32[1,48,128]{2,1,0:T(8,128)S(1)} %bitcast.430), channel_id=1, source_target_pairs={{0,8},{1,9},{2,10},{3,11},{4,12},{5,13},{6,14},{7,15}} | collective-permute-start | bytes 73736 | tf_op jit(solution)/shard_map/ppermute | solution.py:50
  9.7 1.2 fusion.12
  12.2 0.7 collective-permute-start.1
  13.6 0.7 collective-permute-start.2
  14.4 0.9 fusion.39
  16.2 0.7 collective-permute-start.3
  17.6 0.7 collective-permute-start.4
  19.3 0.6 sub.326
  19.9 1.3 collective-permute-start.5
  21.2 27.5 %collective-permute-done.5 = f32[48,128]{1,0:T(8,128)} collective-permute-done((f32[48,128]{1,0:T(8,128)}, f32[48,128]{1,0:T(8,128)}, u32[]{:S(2)}, u32[]{:S(2)}) %collective-permute-start.5) | collective-permute-done | bytes 24608 | tf_op jit(solution)/shard_map/ppermute | solution.py:59
  48.7 0.8 add.228
  50.2 0.8 collective-permute-start.6
  51.0 3.0 %collective-permute-start.7 = (f32[2,48,128]{2,1,0:T(8,128)S(1)}, f32[2,48,128]{2,1,0:T(8,128)S(1)}, u32[]{:S(2)}, u32[]{:S(2)}) collective-permute-start(f32[2,48,128]{2,1,0:T(8,128)S(1)} %pad_maximum_fusion.2), channel_id=1, source_target_pairs={{0,1},{2,3},{4,5},{6,7},{1,0},{3,2},{5,4},{7,6},{8,9},{10,11},{12,... | collective-permute-start | bytes 147464 | tf_op jit(solution)/shard_map/ppermute | solution.py:230
  55.0 1.0 fusion.4
  56.5 1.5 collective-permute-start.8
  58.1 1.3 collective-permute-start.10
  59.4 0.7 collective-permute-done.8
  60.8 0.7 collective-permute-start.11
  61.5 1.3 collective-permute-start.14
  62.8 0.8 collective-permute-start.9
  63.7 25.0 %collective-permute-done.10 = f32[48,48,128]{2,1,0:T(8,128)S(1)} collective-permute-done((f32[48,48,128]{2,1,0:T(8,128)S(1)}, f32[48,48,128]{2,1,0:T(8,128)S(1)}, u32[]{:S(2)}, u32[]{:S(2)}) %collective-permute-start.10) | collective-permute-done | bytes 1179680 | tf_op jit(solution)/shard_map/ppermute | solution.py:216
  90.3 1.3 collective-permute-start.15
  91.6 1.3 collective-permute-start.13
  92.9 1.3 collective-permute-start.12
  94.2 10.7 %collective-permute-done.14 = f32[48,48,128]{2,1,0:T(8,128)S(1)} collective-permute-done((f32[48,48,128]{2,1,0:T(8,128)S(1)}, f32[48,48,128]{2,1,0:T(8,128)S(1)}, u32[]{:S(2)}, u32[]{:S(2)}) %collective-permute-start.14) | collective-permute-done | bytes 1179680 | tf_op jit(solution)/shard_map/ppermute | solution.py:205
  106.1 0.7 collective-permute-start.16
  107.5 0.7 collective-permute-start.17
  108.2 3.1 %collective-permute-start.18 = (f32[2,48,128]{2,1,0:T(8,128)S(1)}, f32[2,48,128]{2,1,0:T(8,128)S(1)}, u32[]{:S(2)}, u32[]{:S(2)}) collective-permute-start(f32[2,48,128]{2,1,0:T(8,128)S(1)} %pad_maximum_fusion.5), channel_id=1, source_target_pairs={{0,1},{2,3},{4,5},{6,7},{1,0},{3,2},{5,4},{7,6},{8,9},{10,11},{12,... | collective-permute-start | bytes 147464 | tf_op jit(solution)/shard_map/ppermute | solution.py:230
  112.6 0.4 fusion.9
  113.6 5.3 %collective-permute-start.19 = (f32[2,48,128]{2,1,0:T(8,128)S(1)}, f32[2,48,128]{2,1,0:T(8,128)S(1)}, u32[]{:S(2)}, u32[]{:S(2)}) collective-permute-start(f32[2,48,128]{2,1,0:T(8,128)S(1)} %pad_maximum_fusion.4), channel_id=1, source_target_pairs={{0,8},{16,24},{1,9},{17,25},{2,10},{18,26},{3,11},{19,27},{4,12},{... | collective-permute-start | bytes 147464 | tf_op jit(solution)/shard_map/ppermute | solution.py:67
  118.9 2.0 collective-permute-done.19
  121.6 0.7 collective-permute-start.21
  122.2 0.7 collective-permute-start.20
  124.4 1.3 collective-permute-start.24
  125.7 1.3 collective-permute-start.23
  127.0 1.3 collective-permute-start.22
  128.3 5.1 %collective-permute-done.24 = f32[48,128]{1,0:T(8,128)S(1)} collective-permute-done((f32[48,128]{1,0:T(8,128)S(1)}, f32[48,128]{1,0:T(8,128)S(1)}, u32[]{:S(2)}, u32[]{:S(2)}) %collective-permute-start.24) | collective-permute-done | bytes 24608 | tf_op jit(solution)/shard_map/ppermute | solution.py:76
  133.5 1.7 collective-permute-done.23
  136.0 0.7 collective-permute-start.25
  137.5 0.9 collective-permute-start.26
  138.4 3.5 %collective-permute-start.27 = (f32[2,48,128]{2,1,0:T(8,128)S(1)}, f32[2,48,128]{2,1,0:T(8,128)S(1)}, u32[]{:S(2)}, u32[]{:S(2)}) collective-permute-start(f32[2,48,128]{2,1,0:T(8,128)S(1)} %pad_maximum_fusion.8), channel_id=1, source_target_pairs={{0,1},{2,3},{4,5},{6,7},{1,0},{3,2},{5,4},{7,6},{8,9},{10,11},{12,... | collective-permute-start | bytes 147464 | tf_op jit(solution)/shard_map/ppermute | solution.py:230
  141.8 0.4 fusion.2
  144.2 9.5 %collective-permute-start.28 = (f32[2,48,128]{2,1,0:T(8,128)S(1)}, f32[2,48,128]{2,1,0:T(8,128)S(1)}, u32[]{:S(2)}, u32[]{:S(2)}) collective-permute-start(f32[2,48,128]{2,1,0:T(8,128)S(1)} %pad_maximum_fusion.7), channel_id=1, source_target_pairs={{0,8},{16,24},{1,9},{17,25},{2,10},{18,26},{3,11},{19,27},{4,12},{... | collective-permute-start | bytes 147464 | tf_op jit(solution)/shard_map/ppermute | solution.py:67
  153.7 1.7 collective-permute-done.28
  156.2 0.7 collective-permute-start.30
  156.9 0.7 collective-permute-start.29
  158.8 1.3 collective-permute-start.33
  160.1 1.3 collective-permute-start.32
  161.4 1.3 collective-permute-start.31
  162.7 5.1 %collective-permute-done.33 = f32[48,128]{1,0:T(8,128)S(1)} collective-permute-done((f32[48,128]{1,0:T(8,128)S(1)}, f32[48,128]{1,0:T(8,128)S(1)}, u32[]{:S(2)}, u32[]{:S(2)}) %collective-permute-start.33) | collective-permute-done | bytes 24608 | tf_op jit(solution)/shard_map/ppermute | solution.py:76
  167.9 1.7 collective-permute-done.32
  170.4 0.7 collective-permute-start.34
  171.9 0.7 collective-permute-start.36
  172.5 3.5 %collective-permute-start.37 = (f32[2,48,128]{2,1,0:T(8,128)S(1)}, f32[2,48,128]{2,1,0:T(8,128)S(1)}, u32[]{:S(2)}, u32[]{:S(2)}) collective-permute-start(f32[2,48,128]{2,1,0:T(8,128)S(1)} %pad_maximum_fusion.9), channel_id=1, source_target_pairs={{0,1},{2,3},{4,5},{6,7},{1,0},{3,2},{5,4},{7,6},{8,9},{10,11},{12,... | collective-permute-start | bytes 147464 | tf_op jit(solution)/shard_map/ppermute | solution.py:230
  176.5 9.5 %collective-permute-start.35 = (f32[48,128]{1,0:T(8,128)S(1)}, f32[48,128]{1,0:T(8,128)S(1)}, u32[]{:S(2)}, u32[]{:S(2)}) collective-permute-start(f32[48,128]{1,0:T(8,128)S(1)} %sub.372), channel_id=1, source_target_pairs={{0,8},{8,16},{16,24},{1,9},{9,17},{17,25},{2,10},{10,18},{18,26},{... | collective-permute-start | bytes 73736 | tf_op jit(solution)/shard_map/ppermute | solution.py:318
  186.2 1.3 collective-permute-done.35
  188.9 0.6 fusion.131
  189.5 1.6 shard_map.77
  191.1 10.8 %all_to_all.11 = f32[32,1,128]{2,1,0:T(1,128)} all-to-all(f32[32,1,128]{2,1,0:T(1,128)} %bitcast.429), channel_id=1, replica_groups=mesh['line'=4,'patch'=8] {'line','patch'}, dimensions={0} | all-to-all | bytes 32768 | tf_op jit(solution)/shard_map/all_to_all | solution.py:329
  201.9 1.7 shard_map.78
  (281 shorter events, 23.1 us)
Async XLA Ops:
  0.0 4.7 %copy-start = (bf16[2,48,48,1,128]{4,2,3,1,0:T(8,128)(2,1)S(1)}, bf16[2,48,48,1,128]{4,2,3,1,0:T(8,128)(2,1)}, u32[]{:S(2)}) copy-start(bf16[2,48,48,1,128]{4,2,3,1,0:T(8,128)(2,1)} %param.19) | copy-start | bytes 3538948
  2.1 9.1 %copy-start.1 = (bf16[2,48,48,1,128]{4,2,3,1,0:T(8,128)(2,1)S(1)}, bf16[2,48,48,1,128]{4,2,3,1,0:T(8,128)(2,1)}, u32[]{:S(2)}) copy-start(bf16[2,48,48,1,128]{4,2,3,1,0:T(8,128)(2,1)} %param.15) | copy-start | bytes 3538948
  4.8 6.4 %collective-permute-start = (f32[1,48,128]{2,1,0:T(8,128)S(1)}, f32[1,48,128]{2,1,0:T(8,128)S(1)}, u32[]{:S(2)}, u32[]{:S(2)}) collective-permute-start(f32[1,48,128]{2,1,0:T(8,128)S(1)} %bitcast.430), channel_id=1, source_target_pairs={{0,8},{1,9},{2,10},{3,11},{4,12},{5,13},{6,14},{7,15}} | collective-permute-start | bytes 73736 | tf_op jit(solution)/shard_map/ppermute | solution.py:50
  11.8 4.0 %copy-start.16 = (f32[48,128]{1,0:T(8,128)}, f32[48,128]{1,0:T(8,128)S(1)}, u32[]{:S(2)}) copy-start(f32[48,128]{1,0:T(8,128)S(1)} %get-tuple-element.59) | copy-start | bytes 73732
  12.2 0.7 collective-permute-start.1
  13.0 1.3 copy-start.2
  13.6 0.8 collective-permute-start.2
  15.4 3.6 %copy-start.12 = (f32[48,128]{1,0:T(8,128)}, f32[48,128]{1,0:T(8,128)S(1)}, u32[]{:S(2)}) copy-start(f32[48,128]{1,0:T(8,128)S(1)} %fusion.93) | copy-start | bytes 73732
  15.8 2.8 %copy-start.14 = (f32[48,128]{1,0:T(8,128)}, f32[48,128]{1,0:T(8,128)S(1)}, u32[]{:S(2)}) copy-start(f32[48,128]{1,0:T(8,128)S(1)} %fusion.70) | copy-start | bytes 73732
  16.2 0.7 collective-permute-start.3
  17.6 0.7 collective-permute-start.4
  18.3 1.0 copy-start.4
  18.3 1.6 copy-start.23
  19.9 28.8 %collective-permute-start.5 = (f32[48,128]{1,0:T(8,128)}, f32[48,128]{1,0:T(8,128)}, u32[]{:S(2)}, u32[]{:S(2)}) collective-permute-start(f32[48,128]{1,0:T(8,128)} %sub.326), channel_id=1, source_target_pairs={{8,0},{9,1},{10,2},{11,3},{12,4},{13,5},{14,6},{15,7}} | collective-permute-start | bytes 73736 | tf_op jit(solution)/shard_map/ppermute | solution.py:59
  21.2 28.6 %copy-start.15 = (f32[48,128]{1,0:T(8,128)S(1)}, f32[48,128]{1,0:T(8,128)}, u32[]{:S(2)}) copy-start(f32[48,128]{1,0:T(8,128)} %copy-done.14) | copy-start | bytes 73732
  49.5 0.7 copy-start.13
  49.6 4.4 %copy-start.8 = (bf16[2,48,48,1,128]{4,2,3,1,0:T(8,128)(2,1)S(1)}, bf16[2,48,48,1,128]{4,2,3,1,0:T(8,128)(2,1)}, u32[]{:S(2)}) copy-start(bf16[2,48,48,1,128]{4,2,3,1,0:T(8,128)(2,1)} %param.14) | copy-start | bytes 3538948
  50.0 4.9 %copy-start.7 = (bf16[2,48,48,1,128]{4,2,3,1,0:T(8,128)(2,1)S(1)}, bf16[2,48,48,1,128]{4,2,3,1,0:T(8,128)(2,1)}, u32[]{:S(2)}) copy-start(bf16[2,48,48,1,128]{4,2,3,1,0:T(8,128)(2,1)} %param.17) | copy-start | bytes 3538948
  50.2 4.8 %copy-start.6 = (bf16[2,48,48,1,128]{4,2,3,1,0:T(8,128)(2,1)S(1)}, bf16[2,48,48,1,128]{4,2,3,1,0:T(8,128)(2,1)}, u32[]{:S(2)}) copy-start(bf16[2,48,48,1,128]{4,2,3,1,0:T(8,128)(2,1)} %param.18) | copy-start | bytes 3538948
  50.2 4.7 %copy-start.18 = (f32[2,48,128]{2,1,0:T(8,128)}, f32[2,48,128]{2,1,0:T(8,128)S(1)}, u32[]{:S(2)}) copy-start(f32[2,48,128]{2,1,0:T(8,128)S(1)} %pad_maximum_fusion.2) | copy-start | bytes 147460
  50.2 4.4 %collective-permute-start.6 = (f32[2,48,128]{2,1,0:T(8,128)S(1)}, f32[2,48,128]{2,1,0:T(8,128)S(1)}, u32[]{:S(2)}, u32[]{:S(2)}) collective-permute-start(f32[2,48,128]{2,1,0:T(8,128)S(1)} %pad_maximum_fusion.2), channel_id=1, source_target_pairs={{1,2},{3,4},{5,6},{2,1},{4,3},{6,5},{9,10},{11,12},{13,14},{10,9},... | collective-permute-start | bytes 147464 | tf_op jit(solution)/shard_map/ppermute | solution.py:229
  51.0 3.9 %collective-permute-start.7 = (f32[2,48,128]{2,1,0:T(8,128)S(1)}, f32[2,48,128]{2,1,0:T(8,128)S(1)}, u32[]{:S(2)}, u32[]{:S(2)}) collective-permute-start(f32[2,48,128]{2,1,0:T(8,128)S(1)} %pad_maximum_fusion.2), channel_id=1, source_target_pairs={{0,1},{2,3},{4,5},{6,7},{1,0},{3,2},{5,4},{7,6},{8,9},{10,11},{12,... | collective-permute-start | bytes 147464 | tf_op jit(solution)/shard_map/ppermute | solution.py:230
  54.9 1.0 copy-start.3
  55.0 1.0 copy-start.22
  55.9 2.1 %copy-start.5 = (f32[48,48,128]{2,1,0:T(8,128)S(1)}, f32[48,48,128]{2,1,0:T(8,128)}, u32[]{:S(2)}) copy-start(f32[48,48,128]{2,1,0:T(8,128)} %copy-done.4) | copy-start | bytes 3538948
  56.5 3.5 %collective-permute-start.8 = (f32[2,48,128]{2,1,0:T(8,128)S(1)}, f32[2,48,128]{2,1,0:T(8,128)S(1)}, u32[]{:S(2)}, u32[]{:S(2)}) collective-permute-start(f32[2,48,128]{2,1,0:T(8,128)S(1)} %pad_maximum_fusion.1), channel_id=1, source_target_pairs={{0,8},{16,24},{1,9},{17,25},{2,10},{18,26},{3,11},{19,27},{4,12},{... | collective-permute-start | bytes 147464 | tf_op jit(solution)/shard_map/ppermute | solution.py:67
  58.1 30.6 %collective-permute-start.10 = (f32[48,48,128]{2,1,0:T(8,128)S(1)}, f32[48,48,128]{2,1,0:T(8,128)S(1)}, u32[]{:S(2)}, u32[]{:S(2)}) collective-permute-start(f32[48,48,128]{2,1,0:T(8,128)S(1)} %copy-done.5), channel_id=1, source_target_pairs={{8,0},{16,24},{9,1},{17,25},{10,2},{18,26},{11,3},{19,27},{12,4},{... | collective-permute-start | bytes 3538952 | tf_op jit(solution)/shard_map/ppermute | solution.py:216
  60.8 2.9 %collective-permute-start.11 = (f32[2,48,128]{2,1,0:T(8,128)S(1)}, f32[2,48,128]{2,1,0:T(8,128)S(1)}, u32[]{:S(2)}, u32[]{:S(2)}) collective-permute-start(f32[2,48,128]{2,1,0:T(8,128)S(1)} %pad_maximum_fusion), channel_id=1, source_target_pairs={{8,24},{9,25},{10,26},{11,27},{12,28},{13,29},{14,30},{15,31}} | collective-permute-start | bytes 147464 | tf_op jit(solution)/shard_map/ppermute | solution.py:70
  61.5 43.4 %collective-permute-start.14 = (f32[48,48,128]{2,1,0:T(8,128)S(1)}, f32[48,48,128]{2,1,0:T(8,128)S(1)}, u32[]{:S(2)}, u32[]{:S(2)}) collective-permute-start(f32[48,48,128]{2,1,0:T(8,128)S(1)} %shard_map.76), channel_id=1, source_target_pairs={{16,0},{17,1},{18,2},{19,3},{20,4},{21,5},{22,6},{23,7}} | collective-permute-start | bytes 3538952 | tf_op jit(solution)/shard_map/ppermute | solution.py:205
  62.8 26.0 %collective-permute-start.9 = (f32[2,48,128]{2,1,0:T(8,128)S(1)}, f32[2,48,128]{2,1,0:T(8,128)S(1)}, u32[]{:S(2)}, u32[]{:S(2)}) collective-permute-start(f32[2,48,128]{2,1,0:T(8,128)S(1)} %pad_maximum_fusion), channel_id=1, source_target_pairs={{8,16},{9,17},{10,18},{11,19},{12,20},{13,21},{14,22},{15,23}} | collective-permute-start | bytes 147464 | tf_op jit(solution)/shard_map/ppermute | solution.py:71
  89.3 0.7 copy-start.17
  89.6 23.4 %copy-start.9 = (f32[2,48,128]{2,1,0:T(8,128)}, f32[2,48,128]{2,1,0:T(8,128)S(1)}, u32[]{:S(2)}) copy-start(f32[2,48,128]{2,1,0:T(8,128)S(1)} %get-tuple-element.80) | copy-start | bytes 147460
  90.3 14.6 %collective-permute-start.15 = (f32[48,128]{1,0:T(8,128)S(1)}, f32[48,128]{1,0:T(8,128)S(1)}, u32[]{:S(2)}, u32[]{:S(2)}) collective-permute-start(f32[48,128]{1,0:T(8,128)S(1)} %sub.339), channel_id=1, source_target_pairs={{24,0},{25,1},{26,2},{27,3},{28,4},{29,5},{30,6},{31,7}} | collective-permute-start | bytes 73736 | tf_op jit(solution)/shard_map/ppermute | solution.py:76
  91.6 13.6 %collective-permute-start.13 = (f32[48,128]{1,0:T(8,128)S(1)}, f32[48,128]{1,0:T(8,128)S(1)}, u32[]{:S(2)}, u32[]{:S(2)}) collective-permute-start(f32[48,128]{1,0:T(8,128)S(1)} %sub.339), channel_id=1, source_target_pairs={{16,0},{17,1},{18,2},{19,3},{20,4},{21,5},{22,6},{23,7}} | collective-permute-start | bytes 73736 | tf_op jit(solution)/shard_map/ppermute | solution.py:77
  92.9 12.4 %collective-permute-start.12 = (f32[48,128]{1,0:T(8,128)S(1)}, f32[48,128]{1,0:T(8,128)S(1)}, u32[]{:S(2)}, u32[]{:S(2)}) collective-permute-start(f32[48,128]{1,0:T(8,128)S(1)} %sub.339), channel_id=1, source_target_pairs={{24,16},{8,0},{25,17},{9,1},{26,18},{10,2},{27,19},{11,3},{28,20},... | collective-permute-start | bytes 73736 | tf_op jit(solution)/shard_map/ppermute | solution.py:78
  106.1 0.7 collective-permute-start.16
  107.5 5.1 %copy-start.19 = (f32[2,48,128]{2,1,0:T(8,128)}, f32[2,48,128]{2,1,0:T(8,128)S(1)}, u32[]{:S(2)}) copy-start(f32[2,48,128]{2,1,0:T(8,128)S(1)} %pad_maximum_fusion.5) | copy-start | bytes 147460
  107.5 4.3 %collective-permute-start.17 = (f32[2,48,128]{2,1,0:T(8,128)S(1)}, f32[2,48,128]{2,1,0:T(8,128)S(1)}, u32[]{:S(2)}, u32[]{:S(2)}) collective-permute-start(f32[2,48,128]{2,1,0:T(8,128)S(1)} %pad_maximum_fusion.5), channel_id=1, source_target_pairs={{1,2},{3,4},{5,6},{2,1},{4,3},{6,5},{9,10},{11,12},{13,14},{10,9},... | collective-permute-start | bytes 147464 | tf_op jit(solution)/shard_map/ppermute | solution.py:229
  108.2 3.9 %collective-permute-start.18 = (f32[2,48,128]{2,1,0:T(8,128)S(1)}, f32[2,48,128]{2,1,0:T(8,128)S(1)}, u32[]{:S(2)}, u32[]{:S(2)}) collective-permute-start(f32[2,48,128]{2,1,0:T(8,128)S(1)} %pad_maximum_fusion.5), channel_id=1, source_target_pairs={{0,1},{2,3},{4,5},{6,7},{1,0},{3,2},{5,4},{7,6},{8,9},{10,11},{12,... | collective-permute-start | bytes 147464 | tf_op jit(solution)/shard_map/ppermute | solution.py:230
  113.6 7.3 %collective-permute-start.19 = (f32[2,48,128]{2,1,0:T(8,128)S(1)}, f32[2,48,128]{2,1,0:T(8,128)S(1)}, u32[]{:S(2)}, u32[]{:S(2)}) collective-permute-start(f32[2,48,128]{2,1,0:T(8,128)S(1)} %pad_maximum_fusion.4), channel_id=1, source_target_pairs={{0,8},{16,24},{1,9},{17,25},{2,10},{18,26},{3,11},{19,27},{4,12},{... | collective-permute-start | bytes 147464 | tf_op jit(solution)/shard_map/ppermute | solution.py:67
  121.6 1.3 collective-permute-start.21
  122.2 0.8 collective-permute-start.20
  123.8 19.8 %copy-start.10 = (f32[2,48,128]{2,1,0:T(8,128)}, f32[2,48,128]{2,1,0:T(8,128)S(1)}, u32[]{:S(2)}) copy-start(f32[2,48,128]{2,1,0:T(8,128)S(1)} %get-tuple-element.78) | copy-start | bytes 147460
  124.4 9.0 %collective-permute-start.24 = (f32[48,128]{1,0:T(8,128)S(1)}, f32[48,128]{1,0:T(8,128)S(1)}, u32[]{:S(2)}, u32[]{:S(2)}) collective-permute-start(f32[48,128]{1,0:T(8,128)S(1)} %sub.354), channel_id=1, source_target_pairs={{24,0},{25,1},{26,2},{27,3},{28,4},{29,5},{30,6},{31,7}} | collective-permute-start | bytes 73736 | tf_op jit(solution)/shard_map/ppermute | solution.py:76
  125.7 9.5 %collective-permute-start.23 = (f32[48,128]{1,0:T(8,128)S(1)}, f32[48,128]{1,0:T(8,128)S(1)}, u32[]{:S(2)}, u32[]{:S(2)}) collective-permute-start(f32[48,128]{1,0:T(8,128)S(1)} %sub.354), channel_id=1, source_target_pairs={{16,0},{17,1},{18,2},{19,3},{20,4},{21,5},{22,6},{23,7}} | collective-permute-start | bytes 73736 | tf_op jit(solution)/shard_map/ppermute | solution.py:77
  127.0 8.4 %collective-permute-start.22 = (f32[48,128]{1,0:T(8,128)S(1)}, f32[48,128]{1,0:T(8,128)S(1)}, u32[]{:S(2)}, u32[]{:S(2)}) collective-permute-start(f32[48,128]{1,0:T(8,128)S(1)} %sub.354), channel_id=1, source_target_pairs={{24,16},{8,0},{25,17},{9,1},{26,18},{10,2},{27,19},{11,3},{28,20},... | collective-permute-start | bytes 73736 | tf_op jit(solution)/shard_map/ppermute | solution.py:78
  136.0 0.7 collective-permute-start.25
  137.4 5.7 %copy-start.20 = (f32[2,48,128]{2,1,0:T(8,128)}, f32[2,48,128]{2,1,0:T(8,128)S(1)}, u32[]{:S(2)}) copy-start(f32[2,48,128]{2,1,0:T(8,128)S(1)} %pad_maximum_fusion.8) | copy-start | bytes 147460
  137.5 5.0 %collective-permute-start.26 = (f32[2,48,128]{2,1,0:T(8,128)S(1)}, f32[2,48,128]{2,1,0:T(8,128)S(1)}, u32[]{:S(2)}, u32[]{:S(2)}) collective-permute-start(f32[2,48,128]{2,1,0:T(8,128)S(1)} %pad_maximum_fusion.8), channel_id=1, source_target_pairs={{1,2},{3,4},{5,6},{2,1},{4,3},{6,5},{9,10},{11,12},{13,14},{10,9},... | collective-permute-start | bytes 147464 | tf_op jit(solution)/shard_map/ppermute | solution.py:229
  138.4 4.4 %collective-permute-start.27 = (f32[2,48,128]{2,1,0:T(8,128)S(1)}, f32[2,48,128]{2,1,0:T(8,128)S(1)}, u32[]{:S(2)}, u32[]{:S(2)}) collective-permute-start(f32[2,48,128]{2,1,0:T(8,128)S(1)} %pad_maximum_fusion.8), channel_id=1, source_target_pairs={{0,1},{2,3},{4,5},{6,7},{1,0},{3,2},{5,4},{7,6},{8,9},{10,11},{12,... | collective-permute-start | bytes 147464 | tf_op jit(solution)/shard_map/ppermute | solution.py:230
  144.2 11.3 %collective-permute-start.28 = (f32[2,48,128]{2,1,0:T(8,128)S(1)}, f32[2,48,128]{2,1,0:T(8,128)S(1)}, u32[]{:S(2)}, u32[]{:S(2)}) collective-permute-start(f32[2,48,128]{2,1,0:T(8,128)S(1)} %pad_maximum_fusion.7), channel_id=1, source_target_pairs={{0,8},{16,24},{1,9},{17,25},{2,10},{18,26},{3,11},{19,27},{4,12},{... | collective-permute-start | bytes 147464 | tf_op jit(solution)/shard_map/ppermute | solution.py:67
  156.2 1.3 collective-permute-start.30
  156.9 0.8 collective-permute-start.29
  158.8 9.0 %collective-permute-start.33 = (f32[48,128]{1,0:T(8,128)S(1)}, f32[48,128]{1,0:T(8,128)S(1)}, u32[]{:S(2)}, u32[]{:S(2)}) collective-permute-start(f32[48,128]{1,0:T(8,128)S(1)} %sub.369), channel_id=1, source_target_pairs={{24,0},{25,1},{26,2},{27,3},{28,4},{29,5},{30,6},{31,7}} | collective-permute-start | bytes 73736 | tf_op jit(solution)/shard_map/ppermute | solution.py:76
  160.1 9.5 %collective-permute-start.32 = (f32[48,128]{1,0:T(8,128)S(1)}, f32[48,128]{1,0:T(8,128)S(1)}, u32[]{:S(2)}, u32[]{:S(2)}) collective-permute-start(f32[48,128]{1,0:T(8,128)S(1)} %sub.369), channel_id=1, source_target_pairs={{16,0},{17,1},{18,2},{19,3},{20,4},{21,5},{22,6},{23,7}} | collective-permute-start | bytes 73736 | tf_op jit(solution)/shard_map/ppermute | solution.py:77
  161.4 8.4 %collective-permute-start.31 = (f32[48,128]{1,0:T(8,128)S(1)}, f32[48,128]{1,0:T(8,128)S(1)}, u32[]{:S(2)}, u32[]{:S(2)}) collective-permute-start(f32[48,128]{1,0:T(8,128)S(1)} %sub.369), channel_id=1, source_target_pairs={{24,16},{8,0},{25,17},{9,1},{26,18},{10,2},{27,19},{11,3},{28,20},... | collective-permute-start | bytes 73736 | tf_op jit(solution)/shard_map/ppermute | solution.py:78
  170.4 0.7 collective-permute-start.34
  171.8 16.0 %copy-start.21 = (f32[2,48,128]{2,1,0:T(8,128)}, f32[2,48,128]{2,1,0:T(8,128)S(1)}, u32[]{:S(2)}) copy-start(f32[2,48,128]{2,1,0:T(8,128)S(1)} %pad_maximum_fusion.9) | copy-start | bytes 147460
  171.9 16.1 %collective-permute-start.36 = (f32[2,48,128]{2,1,0:T(8,128)S(1)}, f32[2,48,128]{2,1,0:T(8,128)S(1)}, u32[]{:S(2)}, u32[]{:S(2)}) collective-permute-start(f32[2,48,128]{2,1,0:T(8,128)S(1)} %pad_maximum_fusion.9), channel_id=1, source_target_pairs={{1,2},{3,4},{5,6},{2,1},{4,3},{6,5},{9,10},{11,12},{13,14},{10,9},... | collective-permute-start | bytes 147464 | tf_op jit(solution)/shard_map/ppermute | solution.py:229
  172.5 15.4 %collective-permute-start.37 = (f32[2,48,128]{2,1,0:T(8,128)S(1)}, f32[2,48,128]{2,1,0:T(8,128)S(1)}, u32[]{:S(2)}, u32[]{:S(2)}) collective-permute-start(f32[2,48,128]{2,1,0:T(8,128)S(1)} %pad_maximum_fusion.9), channel_id=1, source_target_pairs={{0,1},{2,3},{4,5},{6,7},{1,0},{3,2},{5,4},{7,6},{8,9},{10,11},{12,... | collective-permute-start | bytes 147464 | tf_op jit(solution)/shard_map/ppermute | solution.py:230
  176.5 11.0 %collective-permute-start.35 = (f32[48,128]{1,0:T(8,128)S(1)}, f32[48,128]{1,0:T(8,128)S(1)}, u32[]{:S(2)}, u32[]{:S(2)}) collective-permute-start(f32[48,128]{1,0:T(8,128)S(1)} %sub.372), channel_id=1, source_target_pairs={{0,8},{8,16},{16,24},{1,9},{9,17},{17,25},{2,10},{10,18},{18,26},{... | collective-permute-start | bytes 73736 | tf_op jit(solution)/shard_map/ppermute | solution.py:318
  187.9 0.9 copy-start.11

commit v4 on v2

--- a/solution.py
+++ b/solution.py
@@ -1,3 +1,5 @@
+import functools
+
 import jax
 import jax.numpy as jnp
 from jax import lax
@@ -35,25 +37,195 @@
     return result, coupled
 
 
-def precondition(vector, last, lower, upper, pivot):
+def down_entry(message):
+    return -message[0] if message.shape[0] == 1 else message[1] - message[0]
+
+
+def precondition(vector, last, lower, upper, pivot, products, step):
     count = lax.axis_size("line")
     incoming = jnp.zeros((1 if last is None else 2,) + vector.shape[1:], vector.dtype)
-
-    def entry():
-        return -incoming[0] if last is None else incoming[1] - incoming[0]
-
     for turn in range(count - 1):
-        outgoing = sweep_down(vector, lower, pivot, entry())[-1]
+        outgoing = sweep_down(vector, lower, pivot, down_entry(incoming))[-1]
+        if products is not None and step == 0:
+            outgoing = products.down(turn, outgoing)
+        if products is not None and step == 1:
+            outgoing = products.send(turn + count - 1, outgoing)
         message = outgoing[None] if last is None else jnp.stack([outgoing, last])
         incoming = incoming + lax.ppermute(message, "line", [(turn, turn + 1)])
-    forward = sweep_down(vector, lower, pivot, entry())
+    forward = sweep_down(vector, lower, pivot, down_entry(incoming))
     below = None if last is None else incoming[1]
     incoming = jnp.zeros_like(vector[0])
-    for turn in reversed(range(count - 1)):
+    if products is not None and step > 0:
+        near, far = products.received()
         outgoing = sweep_up(forward, upper, pivot, incoming)[0][0]
-        incoming = incoming + lax.ppermute(outgoing, "line", [(turn + 1, turn)])
+        two = lax.ppermute(outgoing, "line", [(3, 0), (2, 1)])
+        side = lax.ppermute(outgoing, "line", [(2, 0), (3, 1)])
+        one = lax.ppermute(outgoing, "line", [(3, 2), (1, 0)])
+        passed = single_apply(near, side + single_apply(far, two))
+        incoming = one + jnp.where(lax.axis_index("line") == 1, two, 0.0) + passed
+    else:
+        for turn in range(count - 1):
+            outgoing = sweep_up(forward, upper, pivot, incoming)[0][0]
+            if products is not None:
+                outgoing = products.up(turn, outgoing)
+            pair = (count - 1 - turn, count - 2 - turn)
+            incoming = incoming + lax.ppermute(outgoing, "line", [pair])
     result, coupled = sweep_up(forward, upper, pivot, incoming)
     return jnp.stack(result), jnp.stack(coupled), below
+
+
+def multiply_lines(left, right, out):
+    block = right.shape[0]
+    group = max(g for g in (1, 2, 3, 4) if block % g == 0)
+    unroll = max(u for u in (1, 2, 4, 8) if block % u == 0)
+
+    def rows(step, carry):
+        start = step * group
+
+        def add(j, totals):
+            row = right[j]
+            return tuple(
+                total + left[start + q, pl.ds(j, 1), :] * row for q, total in enumerate(totals)
+            )
+
+        zero = jnp.zeros(right.shape[1:], jnp.float32)
+        totals = lax.fori_loop(0, block, add, (zero,) * group, unroll=unroll)
+        for q, total in enumerate(totals):
+            out[start + q] = total
+        return carry
+
+    lax.fori_loop(0, block // group, rows, 0)
+
+
+def among(devices):
+    me = lax.axis_index("line")
+    here = me == devices[0]
+    for other in devices[1:]:
+        here = here | (me == other)
+    return here
+
+
+def fetch(sources, targets, sem):
+    copies = [
+        pltpu.make_async_copy(source, target, sem.at[place])
+        for place, (source, target) in enumerate(zip(sources, targets))
+    ]
+    for copy in copies:
+        copy.start()
+    for copy in copies:
+        copy.wait()
+
+
+def widen(source, target):
+    def row(i, carry):
+        target[i] = source[i].astype(jnp.float32)
+        return carry
+
+    lax.fori_loop(0, target.shape[0], row, 0, unroll=4)
+
+
+def factor(k, upper, pivot, held, left, right, made, sem):
+    fetch((pivot.at[k], upper.at[k]), (held.at[0], held.at[1]), sem)
+    widen(held.at[0], left)
+    widen(held.at[1], right)
+    multiply_lines(left, right, made)
+
+
+def factor_kernel(k, devices, upper, pivot, after, out, held, left, right, made, sem):
+    @pl.when(among(devices))
+    def _():
+        factor(k, upper, pivot, held, left, right, made, sem)
+        fetch((made,), (out,), sem)
+
+
+def product_kernel(made_here, given, upper, pivot, first, second, after, *rest):
+    *pieces, held, left, right, made, sem = rest
+
+    def deliver(source):
+        start = 0
+        copies = []
+        for piece in pieces:
+            rows = pl.ds(start, piece.shape[0])
+            copies.append(pltpu.make_async_copy(source.at[rows], piece, sem.at[0]))
+            start += piece.shape[0]
+        for copy in copies:
+            copy.start()
+            copy.wait()
+
+    @pl.when(among((made_here,)))
+    def _():
+        factor(0, upper, pivot, held, left, right, made, sem)
+        fetch((second,), (right,), sem)
+        multiply_lines(made, right, left)
+        deliver(left)
+
+    @pl.when(among((given,)))
+    def _():
+        fetch((first, second), (left, right), sem)
+        multiply_lines(left, right, made)
+        deliver(made)
+
+
+def lines_call(kernel, pieces, upper, *operands):
+    shape = upper.shape[1:]
+    bounds = [shape[0] * piece // pieces for piece in range(pieces + 1)]
+    anywhere = pl.BlockSpec(memory_space=pl.ANY)
+    return pl.pallas_call(
+        kernel,
+        out_shape=[
+            jax.ShapeDtypeStruct((end - start,) + shape[1:], jnp.float32)
+            for start, end in zip(bounds, bounds[1:])
+        ],
+        in_specs=[anywhere] * (1 + len(operands)),
+        out_specs=[anywhere] * pieces,
+        scratch_shapes=[pltpu.VMEM((2,) + shape, upper.dtype)]
+        + [pltpu.VMEM(shape, jnp.float32)] * 3
+        + [pltpu.SemaphoreType.DMA((2,))],
+        compiler_params=pltpu.CompilerParams(vmem_limit_bytes=12 << 20),
+    )(upper, *operands)
+
+
+class Products:
+    pieces = 6
+
+    def __init__(self, upper, pivot):
+        self.blocks = upper, pivot
+        self.sent = []
+
+    def down(self, turn, outgoing):
+        def call(kernel, pieces, *operands):
+            return lines_call(kernel, pieces, *self.blocks, *operands, outgoing)
+
+        if turn == 0:
+            (self.second,) = call(functools.partial(factor_kernel, 1, (1, 2)), 1)
+            outgoing, self.second = lax.optimization_barrier((outgoing, self.second))
+        if turn == 1:
+            (self.first,) = call(functools.partial(factor_kernel, 0, (2,)), 1)
+        if turn == 2:
+            outgoing, self.first = lax.optimization_barrier((outgoing, self.first))
+            kernel = functools.partial(product_kernel, 1, 2)
+            self.made = call(kernel, self.pieces, self.first, self.second)
+        return outgoing
+
+    def up(self, turn, outgoing):
+        if turn == 0:
+            outgoing, *self.made = lax.optimization_barrier((outgoing, *self.made))
+            return outgoing
+        return self.send(turn - 1, outgoing)
+
+    def send(self, place, value):
+        if place >= self.pieces:
+            return value
+        value, piece = lax.optimization_barrier((value, self.made[place]))
+        if place >= 2:
+            value, *self.sent[place - 2] = lax.optimization_barrier((value, *self.sent[place - 2]))
+        near = lax.ppermute(piece, "line", [(1, 0), (2, 1)])
+        far = lax.ppermute(piece, "line", [(2, 0)])
+        self.sent.append([near, far])
+        return value
+
+    def received(self):
+        return [jnp.concatenate(pieces) for pieces in zip(*self.sent)]
 
 
 def rows_beside(field, across):
@@ -136,8 +308,13 @@
     basis = [newton_residual.reshape(count, block, wide)]
     directions = []
     last = None
+    products = Products(upper, pivot) if line == 4 and count == 2 else None
     for j in range(ITERS):
-        direction, coupled, below = precondition(basis[j], last, lower, upper, pivot)
+        direction, coupled, below = precondition(
+            basis[j], last, lower, upper, pivot, products, j
+        )
+        if products is not None and j == 0:
+            direction = products.send(2, direction)
         if below is not None:
             basis[j] = basis[j].at[0].add(single_apply(lower[0], below))
         directions.append(direction)

time: 182 us -> 194 us (1.066)
  starting transfers between devices: 43.6 us -> 76.5 us
  waiting for transfers between devices: 84.7 us -> 65.4 us
  other arithmetic: 33.7 us -> 29.5 us
  blocking collectives: 11.8 us -> 14.6 us
    ppermute x12 -> x24, waiting for transfers between devices: 77.8 us -> 56.8 us  [the longest x3 27.9 us: precondition(): two = lax.ppermute(outgoing, 'line', [(3, 0), (2, 1)])]
    ppermute x12 -> x24, starting transfers between devices: 10.6 us -> 30 us  [the longest x6 7.88 us: send(): far = lax.ppermute(piece, 'line', [(2, 0)])]
    ppermute x12, starting transfers between devices: 15.1 us -> 26.6 us  [precondition(): incoming = incoming + lax.ppermute(message, 'line', [(turn, turn + 1)])]
    reduce_sum x123 -> x105, other arithmetic: 25.6 us -> 21.4 us  [single_apply(): return jnp.sum(block_mat.astype(jnp.float32) * vector[None], axis=1)]
    all_to_all x1, blocking collectives: 11.8 us -> 14.6 us  [per_device(): sums = lax.all_to_all(sums, ('line', 'patch'), 0, 0, tiled=True)]
    ppermute x1, starting transfers between devices: 1.62 us -> 3.62 us  [per_device(): below = lax.ppermute(last, 'line', [(i, i + 1) for i in range(line - 1)])]
  transfers between devices with their start and end apart: 33 -> 45, of which waited for: 11 -> 14; matrix products, arithmetic and copies ran while one was open for 2% -> 5% of each run, Pallas kernels for 0% -> 0%
where the time goes in v4:
time: 194 us; the launch traced here: 193 us
  starting transfers between devices  76.5 us (39%)
  waiting for transfers between devices  65.4 us (34%)
  other arithmetic  29.5 us (15%)
  blocking collectives  14.6 us (8%)
  Pallas kernels  3.4 us (2%)
  between operations  2.38 us (1%)
    ppermute x3, waiting for transfers between devices, precondition(): two = lax.ppermute(outgoing, 'line', [(3, 0), (2, 1)])  27.9 us
    ppermute x12, starting transfers between devices, precondition(): incoming = incoming + lax.ppermute(message, 'line', [(turn, turn + 1)])  26.6 us
    reduce_sum x105, other arithmetic, single_apply(): return jnp.sum(block_mat.astype(jnp.float32) * vector[None], axis=1)  21.4 us
    ppermute x3, waiting for transfers between devices, precondition(): incoming = incoming + lax.ppermute(outgoing, 'line', [pair])  18.9 us
    all_to_all x1, blocking collectives, per_device(): sums = lax.all_to_all(sums, ('line', 'patch'), 0, 0, tiled=True)  14.6 us
    ppermute x4, starting transfers between devices, rows_beside(): near = lax.ppermute(to_near, 'patch', even + [(b, a) for a, b in even])  13.4 us
    ppermute x6, waiting for transfers between devices, send(): far = lax.ppermute(piece, 'line', [(2, 0)])  8.52 us
    ppermute x6, starting transfers between devices, send(): far = lax.ppermute(piece, 'line', [(2, 0)])  7.88 us
  transfers between devices with their start and end apart: 45, of which 14 were waited for; matrix products, arithmetic and copies ran while one was open for 5% of the time, Pallas kernels for 0%

profile of v4, /device:TPU:0, one launch (start us, length us, event | category | flops | bytes accessed | tf_op | source)
XLA Modules:
  0.0 193.1 jit_solution(15920922466405693656)
XLA Ops:
  0.0 1.3 fusion.29
  1.3 0.9 fusion.169
  2.2 1.2 fusion.90
  3.4 1.2 fusion.47
  4.9 9.9 %collective-permute-start = (f32[1,48,128]{2,1,0:T(8,128)S(1)}, f32[1,48,128]{2,1,0:T(8,128)S(1)}, u32[]{:S(2)}, u32[]{:S(2)}) collective-permute-start(f32[1,48,128]{2,1,0:T(8,128)S(1)} %bitcast.402), channel_id=1, source_target_pairs={{0,8},{1,9},{2,10},{3,11},{4,12},{5,13},{6,14},{7,15}} | collective-permute-start | bytes 73736 | tf_op jit(solution)/shard_map/ppermute | solution.py:54
  15.0 1.3 collective-permute-done
  17.3 0.7 collective-permute-start.1
  19.5 0.9 fusion.33
  22.7 0.7 collective-permute-start.4
  24.7 1.3 collective-permute-start.5
  26.0 1.3 collective-permute-start.6
  27.3 1.3 collective-permute-start.7
  28.6 1.3 collective-permute-start.10
  29.9 1.3 collective-permute-start.11
  31.2 18.9 %collective-permute-done.5 = f32[48,128]{1,0:T(8,128)} collective-permute-done((f32[48,128]{1,0:T(8,128)}, f32[48,128]{1,0:T(8,128)}, u32[]{:S(2)}, u32[]{:S(2)}) %collective-permute-start.5) | collective-permute-done | bytes 24608 | tf_op jit(solution)/shard_map/ppermute | solution.py:72
  50.0 0.8 add.222
  51.6 1.4 collective-permute-start.13
  53.0 1.4 collective-permute-done.6
  54.4 2.5 %collective-permute-done.7 = f32[8,48,128]{2,1,0:T(8,128)S(1)} collective-permute-done((f32[8,48,128]{2,1,0:T(8,128)S(1)}, f32[8,48,128]{2,1,0:T(8,128)S(1)}, u32[]{:S(2)}, u32[]{:S(2)}) %collective-permute-start.7) | collective-permute-done | bytes 196640 | tf_op jit(solution)/shard_map/ppermute | solution.py:223
  57.6 3.0 %collective-permute-start.9 = (f32[2,48,128]{2,1,0:T(8,128)S(1)}, f32[2,48,128]{2,1,0:T(8,128)S(1)}, u32[]{:S(2)}, u32[]{:S(2)}) collective-permute-start(f32[2,48,128]{2,1,0:T(8,128)S(1)} %pad_maximum_fusion.11), channel_id=1, source_target_pairs={{0,1},{2,3},{4,5},{6,7},{1,0},{3,2},{5,4},{7,6},{8,9},{10,11},{12,... | collective-permute-start | bytes 147464 | tf_op jit(solution)/shard_map/ppermute | solution.py:241
  61.3 1.4 collective-permute-start.14
  62.8 1.0 fusion.4
  64.3 1.3 collective-permute-start.16
  65.6 1.3 collective-permute-start.17
  67.0 3.9 %collective-permute-start.12 = (f32[2,48,128]{2,1,0:T(8,128)S(1)}, f32[2,48,128]{2,1,0:T(8,128)S(1)}, u32[]{:S(2)}, u32[]{:S(2)}) collective-permute-start(f32[2,48,128]{2,1,0:T(8,128)S(1)} %pad_maximum_fusion.10), channel_id=1, source_target_pairs={{0,8},{1,9},{2,10},{3,11},{4,12},{5,13},{6,14},{7,15}} | collective-permute-start | bytes 147464 | tf_op jit(solution)/shard_map/ppermute | solution.py:54
  71.0 1.7 collective-permute-done.12
  73.3 1.3 collective-permute-start.24
  74.6 1.3 collective-permute-start.21
  76.0 0.8 collective-permute-start.15
  77.6 1.3 collective-permute-start.25
  78.9 1.3 collective-permute-start.22
  80.2 0.7 collective-permute-start.18
  82.5 1.3 collective-permute-start.20
  83.8 1.3 collective-permute-start.23
  85.1 1.3 collective-permute-start.19
  86.4 6.0 %collective-permute-done.25 = f32[8,48,128]{2,1,0:T(8,128)S(1)} collective-permute-done((f32[8,48,128]{2,1,0:T(8,128)S(1)}, f32[8,48,128]{2,1,0:T(8,128)S(1)}, u32[]{:S(2)}, u32[]{:S(2)}) %collective-permute-start.25) | collective-permute-done | bytes 196640 | tf_op jit(solution)/shard_map/ppermute | solution.py:223
  92.4 8.2 %collective-permute-done.20 = f32[48,128]{1,0:T(8,128)S(1)} collective-permute-done((f32[48,128]{1,0:T(8,128)S(1)}, f32[48,128]{1,0:T(8,128)S(1)}, u32[]{:S(2)}, u32[]{:S(2)}) %collective-permute-start.20) | collective-permute-done | bytes 24608 | tf_op jit(solution)/shard_map/ppermute | solution.py:61
  101.7 0.7 collective-permute-start.26
  102.3 3.5 %collective-permute-start.27 = (f32[2,48,128]{2,1,0:T(8,128)S(1)}, f32[2,48,128]{2,1,0:T(8,128)S(1)}, u32[]{:S(2)}, u32[]{:S(2)}) collective-permute-start(f32[2,48,128]{2,1,0:T(8,128)S(1)} %pad_maximum_fusion.3), channel_id=1, source_target_pairs={{0,1},{2,3},{4,5},{6,7},{1,0},{3,2},{5,4},{7,6},{8,9},{10,11},{12,... | collective-permute-start | bytes 147464 | tf_op jit(solution)/shard_map/ppermute | solution.py:241
  108.2 3.6 %collective-permute-start.28 = (f32[2,48,128]{2,1,0:T(8,128)S(1)}, f32[2,48,128]{2,1,0:T(8,128)S(1)}, u32[]{:S(2)}, u32[]{:S(2)}) collective-permute-start(f32[2,48,128]{2,1,0:T(8,128)S(1)} %pad_maximum_fusion.2), channel_id=1, source_target_pairs={{0,8},{1,9},{2,10},{3,11},{4,12},{5,13},{6,14},{7,15}} | collective-permute-start | bytes 147464 | tf_op jit(solution)/shard_map/ppermute | solution.py:54
  111.8 2.0 %collective-permute-done.28 = f32[2,48,128]{2,1,0:T(8,128)S(1)} collective-permute-done((f32[2,48,128]{2,1,0:T(8,128)S(1)}, f32[2,48,128]{2,1,0:T(8,128)S(1)}, u32[]{:S(2)}, u32[]{:S(2)}) %collective-permute-start.28) | collective-permute-done | bytes 49184 | tf_op jit(solution)/shard_map/ppermute | solution.py:54
  114.5 0.7 collective-permute-start.29
  115.9 0.7 collective-permute-start.30
  117.9 1.3 collective-permute-start.32
  119.2 1.3 collective-permute-start.33
  120.5 1.3 collective-permute-start.31
  121.8 9.9 %collective-permute-done.32 = f32[48,128]{1,0:T(8,128)S(1)} collective-permute-done((f32[48,128]{1,0:T(8,128)S(1)}, f32[48,128]{1,0:T(8,128)S(1)}, u32[]{:S(2)}, u32[]{:S(2)}) %collective-permute-start.32) | collective-permute-done | bytes 24608 | tf_op jit(solution)/shard_map/ppermute | solution.py:61
  132.7 0.9 collective-permute-start.34
  133.6 3.5 %collective-permute-start.35 = (f32[2,48,128]{2,1,0:T(8,128)S(1)}, f32[2,48,128]{2,1,0:T(8,128)S(1)}, u32[]{:S(2)}, u32[]{:S(2)}) collective-permute-start(f32[2,48,128]{2,1,0:T(8,128)S(1)} %pad_maximum_fusion.7), channel_id=1, source_target_pairs={{0,1},{2,3},{4,5},{6,7},{1,0},{3,2},{5,4},{7,6},{8,9},{10,11},{12,... | collective-permute-start | bytes 147464 | tf_op jit(solution)/shard_map/ppermute | solution.py:241
  139.4 3.6 %collective-permute-start.36 = (f32[2,48,128]{2,1,0:T(8,128)S(1)}, f32[2,48,128]{2,1,0:T(8,128)S(1)}, u32[]{:S(2)}, u32[]{:S(2)}) collective-permute-start(f32[2,48,128]{2,1,0:T(8,128)S(1)} %pad_maximum_fusion.6), channel_id=1, source_target_pairs={{0,8},{1,9},{2,10},{3,11},{4,12},{5,13},{6,14},{7,15}} | collective-permute-start | bytes 147464 | tf_op jit(solution)/shard_map/ppermute | solution.py:54
  143.1 1.7 collective-permute-done.36
  145.5 0.7 collective-permute-start.37
  146.9 0.7 collective-permute-start.38
  148.7 1.3 collective-permute-start.40
  150.0 1.3 collective-permute-start.41
  151.3 1.3 collective-permute-start.39
  152.6 9.9 %collective-permute-done.40 = f32[48,128]{1,0:T(8,128)S(1)} collective-permute-done((f32[48,128]{1,0:T(8,128)S(1)}, f32[48,128]{1,0:T(8,128)S(1)}, u32[]{:S(2)}, u32[]{:S(2)}) %collective-permute-start.40) | collective-permute-done | bytes 24608 | tf_op jit(solution)/shard_map/ppermute | solution.py:61
  163.5 0.7 collective-permute-start.43
  164.2 3.5 %collective-permute-start.44 = (f32[2,48,128]{2,1,0:T(8,128)S(1)}, f32[2,48,128]{2,1,0:T(8,128)S(1)}, u32[]{:S(2)}, u32[]{:S(2)}) collective-permute-start(f32[2,48,128]{2,1,0:T(8,128)S(1)} %pad_maximum_fusion.12), channel_id=1, source_target_pairs={{0,1},{2,3},{4,5},{6,7},{1,0},{3,2},{5,4},{7,6},{8,9},{10,11},{12,... | collective-permute-start | bytes 147464 | tf_op jit(solution)/shard_map/ppermute | solution.py:241
  168.1 3.6 %collective-permute-start.42 = (f32[48,128]{1,0:T(8,128)S(1)}, f32[48,128]{1,0:T(8,128)S(1)}, u32[]{:S(2)}, u32[]{:S(2)}) collective-permute-start(f32[48,128]{1,0:T(8,128)S(1)} %sub.347), channel_id=1, source_target_pairs={{0,8},{8,16},{16,24},{1,9},{9,17},{17,25},{2,10},{10,18},{18,26},{... | collective-permute-start | bytes 73736 | tf_op jit(solution)/shard_map/ppermute | solution.py:326
  171.9 1.3 collective-permute-done.42
  175.2 1.6 shard_map.76
  176.9 14.6 %all_to_all.11 = f32[32,1,128]{2,1,0:T(1,128)} all-to-all(f32[32,1,128]{2,1,0:T(1,128)} %bitcast.472), channel_id=1, replica_groups=mesh['line'=4,'patch'=8] {'line','patch'}, dimensions={0} | all-to-all | bytes 32768 | tf_op jit(solution)/shard_map/all_to_all | solution.py:337
  191.4 1.7 shard_map.77
  (307 shorter events, 26.3 us)
Async XLA Ops:
  0.0 4.7 %copy-start = (bf16[2,48,48,1,128]{4,2,3,1,0:T(8,128)(2,1)S(1)}, bf16[2,48,48,1,128]{4,2,3,1,0:T(8,128)(2,1)}, u32[]{:S(2)}) copy-start(bf16[2,48,48,1,128]{4,2,3,1,0:T(8,128)(2,1)} %param.19) | copy-start | bytes 3538948
  1.3 3.5 %copy-start.1 = (bf16[2,48,48,1,128]{4,2,3,1,0:T(8,128)(2,1)S(1)}, bf16[2,48,48,1,128]{4,2,3,1,0:T(8,128)(2,1)}, u32[]{:S(2)}) copy-start(bf16[2,48,48,1,128]{4,2,3,1,0:T(8,128)(2,1)} %param.16) | copy-start | bytes 3538948
  4.9 11.5 %copy-start.2 = (bf16[2,48,48,1,128]{4,2,3,1,0:T(8,128)(2,1)S(1)}, bf16[2,48,48,1,128]{4,2,3,1,0:T(8,128)(2,1)}, u32[]{:S(2)}) copy-start(bf16[2,48,48,1,128]{4,2,3,1,0:T(8,128)(2,1)} %param.15) | copy-start | bytes 3538948
  4.9 11.4 %collective-permute-start = (f32[1,48,128]{2,1,0:T(8,128)S(1)}, f32[1,48,128]{2,1,0:T(8,128)S(1)}, u32[]{:S(2)}, u32[]{:S(2)}) collective-permute-start(f32[1,48,128]{2,1,0:T(8,128)S(1)} %bitcast.402), channel_id=1, source_target_pairs={{0,8},{1,9},{2,10},{3,11},{4,12},{5,13},{6,14},{7,15}} | collective-permute-start | bytes 73736 | tf_op jit(solution)/shard_map/ppermute | solution.py:54
  16.9 4.0 %copy-start.15 = (f32[48,128]{1,0:T(8,128)}, f32[48,128]{1,0:T(8,128)S(1)}, u32[]{:S(2)}) copy-start(f32[48,128]{1,0:T(8,128)S(1)} %get-tuple-element.131) | copy-start | bytes 73732
  17.3 0.7 collective-permute-start.1
  18.7 0.7 collective-permute-start.2
  20.5 3.5 %copy-start.10 = (f32[48,128]{1,0:T(8,128)}, f32[48,128]{1,0:T(8,128)S(1)}, u32[]{:S(2)}) copy-start(f32[48,128]{1,0:T(8,128)S(1)} %fusion.93) | copy-start | bytes 73732
  20.9 2.8 %copy-start.13 = (f32[48,128]{1,0:T(8,128)}, f32[48,128]{1,0:T(8,128)S(1)}, u32[]{:S(2)}) copy-start(f32[48,128]{1,0:T(8,128)S(1)} %fusion.70) | copy-start | bytes 73732
  21.3 0.7 collective-permute-start.3
  22.7 0.7 collective-permute-start.4
  23.3 1.3 copy-start.22
  24.7 25.4 %collective-permute-start.5 = (f32[48,128]{1,0:T(8,128)}, f32[48,128]{1,0:T(8,128)}, u32[]{:S(2)}, u32[]{:S(2)}) collective-permute-start(f32[48,128]{1,0:T(8,128)} %sub.304), channel_id=1, source_target_pairs={{8,0},{9,1},{10,2},{11,3},{12,4},{13,5},{14,6},{15,7}} | collective-permute-start | bytes 73736 | tf_op jit(solution)/shard_map/ppermute | solution.py:72
  26.0 25.2 %copy-start.14 = (f32[48,128]{1,0:T(8,128)S(1)}, f32[48,128]{1,0:T(8,128)}, u32[]{:S(2)}) copy-start(f32[48,128]{1,0:T(8,128)} %copy-done.13) | copy-start | bytes 73732
  26.0 28.4 %collective-permute-start.6 = (f32[8,48,128]{2,1,0:T(8,128)S(1)}, f32[8,48,128]{2,1,0:T(8,128)S(1)}, u32[]{:S(2)}, u32[]{:S(2)}) collective-permute-start(f32[8,48,128]{2,1,0:T(8,128)S(1)} %get-tuple-element.99), channel_id=1, source_target_pairs={{8,0},{16,8},{9,1},{17,9},{10,2},{18,10},{11,3},{19,11},{12,4},{20... | collective-permute-start | bytes 589832 | tf_op jit(solution)/shard_map/ppermute | solution.py:222
  27.3 29.6 %collective-permute-start.7 = (f32[8,48,128]{2,1,0:T(8,128)S(1)}, f32[8,48,128]{2,1,0:T(8,128)S(1)}, u32[]{:S(2)}, u32[]{:S(2)}) collective-permute-start(f32[8,48,128]{2,1,0:T(8,128)S(1)} %get-tuple-element.99), channel_id=1, source_target_pairs={{16,0},{17,1},{18,2},{19,3},{20,4},{21,5},{22,6},{23,7}} | collective-permute-start | bytes 589832 | tf_op jit(solution)/shard_map/ppermute | solution.py:223
  28.6 37.1 %collective-permute-start.10 = (f32[8,48,128]{2,1,0:T(8,128)S(1)}, f32[8,48,128]{2,1,0:T(8,128)S(1)}, u32[]{:S(2)}, u32[]{:S(2)}) collective-permute-start(f32[8,48,128]{2,1,0:T(8,128)S(1)} %get-tuple-element.103), channel_id=1, source_target_pairs={{8,0},{16,8},{9,1},{17,9},{10,2},{18,10},{11,3},{19,11},{12,4},{20... | collective-permute-start | bytes 589832 | tf_op jit(solution)/shard_map/ppermute | solution.py:222
  29.9 37.1 %collective-permute-start.11 = (f32[8,48,128]{2,1,0:T(8,128)S(1)}, f32[8,48,128]{2,1,0:T(8,128)S(1)}, u32[]{:S(2)}, u32[]{:S(2)}) collective-permute-start(f32[8,48,128]{2,1,0:T(8,128)S(1)} %get-tuple-element.103), channel_id=1, source_target_pairs={{16,0},{17,1},{18,2},{19,3},{20,4},{21,5},{22,6},{23,7}} | collective-permute-start | bytes 589832 | tf_op jit(solution)/shard_map/ppermute | solution.py:223
  51.0 9.6 %copy-start.3 = (bf16[2,48,48,1,128]{4,2,3,1,0:T(8,128)(2,1)S(1)}, bf16[2,48,48,1,128]{4,2,3,1,0:T(8,128)(2,1)}, u32[]{:S(2)}) copy-start(bf16[2,48,48,1,128]{4,2,3,1,0:T(8,128)(2,1)} %param.15) | copy-start | bytes 3538948
  51.2 9.6 %copy-start.6 = (bf16[2,48,48,1,128]{4,2,3,1,0:T(8,128)(2,1)S(1)}, bf16[2,48,48,1,128]{4,2,3,1,0:T(8,128)(2,1)}, u32[]{:S(2)}) copy-start(bf16[2,48,48,1,128]{4,2,3,1,0:T(8,128)(2,1)} %param.14) | copy-start | bytes 3538948
  51.6 9.7 %copy-start.12 = (f32[2,48,128]{2,1,0:T(8,128)}, f32[2,48,128]{2,1,0:T(8,128)S(1)}, u32[]{:S(2)}) copy-start(f32[2,48,128]{2,1,0:T(8,128)S(1)} %pad_maximum_fusion.11) | copy-start | bytes 147460
  51.6 23.1 %collective-permute-start.13 = (f32[8,48,128]{2,1,0:T(8,128)S(1)}, f32[8,48,128]{2,1,0:T(8,128)S(1)}, u32[]{:S(2)}, u32[]{:S(2)}) collective-permute-start(f32[8,48,128]{2,1,0:T(8,128)S(1)} %get-tuple-element.107), channel_id=1, source_target_pairs={{8,0},{16,8},{9,1},{17,9},{10,2},{18,10},{11,3},{19,11},{12,4},{20... | collective-permute-start | bytes 589832 | tf_op jit(solution)/shard_map/ppermute | solution.py:222
  56.9 4.4 %collective-permute-start.8 = (f32[2,48,128]{2,1,0:T(8,128)S(1)}, f32[2,48,128]{2,1,0:T(8,128)S(1)}, u32[]{:S(2)}, u32[]{:S(2)}) collective-permute-start(f32[2,48,128]{2,1,0:T(8,128)S(1)} %pad_maximum_fusion.11), channel_id=1, source_target_pairs={{1,2},{3,4},{5,6},{2,1},{4,3},{6,5},{9,10},{11,12},{13,14},{10,9},... | collective-permute-start | bytes 147464 | tf_op jit(solution)/shard_map/ppermute | solution.py:240
  57.6 5.1 %collective-permute-start.9 = (f32[2,48,128]{2,1,0:T(8,128)S(1)}, f32[2,48,128]{2,1,0:T(8,128)S(1)}, u32[]{:S(2)}, u32[]{:S(2)}) collective-permute-start(f32[2,48,128]{2,1,0:T(8,128)S(1)} %pad_maximum_fusion.11), channel_id=1, source_target_pairs={{0,1},{2,3},{4,5},{6,7},{1,0},{3,2},{5,4},{7,6},{8,9},{10,11},{12,... | collective-permute-start | bytes 147464 | tf_op jit(solution)/shard_map/ppermute | solution.py:241
  60.6 2.2 %copy-start.5 = (bf16[2,48,48,1,128]{4,2,3,1,0:T(8,128)(2,1)S(1)}, bf16[2,48,48,1,128]{4,2,3,1,0:T(8,128)(2,1)}, u32[]{:S(2)}) copy-start(bf16[2,48,48,1,128]{4,2,3,1,0:T(8,128)(2,1)} %param.17) | copy-start | bytes 3538948
  60.8 2.0 %copy-start.4 = (bf16[2,48,48,1,128]{4,2,3,1,0:T(8,128)(2,1)S(1)}, bf16[2,48,48,1,128]{4,2,3,1,0:T(8,128)(2,1)}, u32[]{:S(2)}) copy-start(bf16[2,48,48,1,128]{4,2,3,1,0:T(8,128)(2,1)} %param.18) | copy-start | bytes 3538948
  61.3 14.7 %collective-permute-start.14 = (f32[8,48,128]{2,1,0:T(8,128)S(1)}, f32[8,48,128]{2,1,0:T(8,128)S(1)}, u32[]{:S(2)}, u32[]{:S(2)}) collective-permute-start(f32[8,48,128]{2,1,0:T(8,128)S(1)} %get-tuple-element.107), channel_id=1, source_target_pairs={{16,0},{17,1},{18,2},{19,3},{20,4},{21,5},{22,6},{23,7}} | collective-permute-start | bytes 589832 | tf_op jit(solution)/shard_map/ppermute | solution.py:223
  62.8 1.0 copy-start.21
  64.3 14.6 %collective-permute-start.16 = (f32[8,48,128]{2,1,0:T(8,128)S(1)}, f32[8,48,128]{2,1,0:T(8,128)S(1)}, u32[]{:S(2)}, u32[]{:S(2)}) collective-permute-start(f32[8,48,128]{2,1,0:T(8,128)S(1)} %get-tuple-element.111), channel_id=1, source_target_pairs={{8,0},{16,8},{9,1},{17,9},{10,2},{18,10},{11,3},{19,11},{12,4},{20... | collective-permute-start | bytes 589832 | tf_op jit(solution)/shard_map/ppermute | solution.py:222
  65.6 14.6 %collective-permute-start.17 = (f32[8,48,128]{2,1,0:T(8,128)S(1)}, f32[8,48,128]{2,1,0:T(8,128)S(1)}, u32[]{:S(2)}, u32[]{:S(2)}) collective-permute-start(f32[8,48,128]{2,1,0:T(8,128)S(1)} %get-tuple-element.111), channel_id=1, source_target_pairs={{16,0},{17,1},{18,2},{19,3},{20,4},{21,5},{22,6},{23,7}} | collective-permute-start | bytes 589832 | tf_op jit(solution)/shard_map/ppermute | solution.py:223
  67.0 5.7 %collective-permute-start.12 = (f32[2,48,128]{2,1,0:T(8,128)S(1)}, f32[2,48,128]{2,1,0:T(8,128)S(1)}, u32[]{:S(2)}, u32[]{:S(2)}) collective-permute-start(f32[2,48,128]{2,1,0:T(8,128)S(1)} %pad_maximum_fusion.10), channel_id=1, source_target_pairs={{0,8},{1,9},{2,10},{3,11},{4,12},{5,13},{6,14},{7,15}} | collective-permute-start | bytes 147464 | tf_op jit(solution)/shard_map/ppermute | solution.py:54
  73.3 10.4 %collective-permute-start.24 = (f32[8,48,128]{2,1,0:T(8,128)S(1)}, f32[8,48,128]{2,1,0:T(8,128)S(1)}, u32[]{:S(2)}, u32[]{:S(2)}) collective-permute-start(f32[8,48,128]{2,1,0:T(8,128)S(1)} %get-tuple-element.117), channel_id=1, source_target_pairs={{16,0},{17,1},{18,2},{19,3},{20,4},{21,5},{22,6},{23,7}} | collective-permute-start | bytes 589832 | tf_op jit(solution)/shard_map/ppermute | solution.py:223
  74.6 10.5 %collective-permute-start.21 = (f32[8,48,128]{2,1,0:T(8,128)S(1)}, f32[8,48,128]{2,1,0:T(8,128)S(1)}, u32[]{:S(2)}, u32[]{:S(2)}) collective-permute-start(f32[8,48,128]{2,1,0:T(8,128)S(1)} %get-tuple-element.117), channel_id=1, source_target_pairs={{8,0},{16,8},{9,1},{17,9},{10,2},{18,10},{11,3},{19,11},{12,4},{20... | collective-permute-start | bytes 589832 | tf_op jit(solution)/shard_map/ppermute | solution.py:222
  76.0 0.9 collective-permute-start.15
  77.6 14.8 %collective-permute-start.25 = (f32[8,48,128]{2,1,0:T(8,128)S(1)}, f32[8,48,128]{2,1,0:T(8,128)S(1)}, u32[]{:S(2)}, u32[]{:S(2)}) collective-permute-start(f32[8,48,128]{2,1,0:T(8,128)S(1)} %get-tuple-element.118), channel_id=1, source_target_pairs={{16,0},{17,1},{18,2},{19,3},{20,4},{21,5},{22,6},{23,7}} | collective-permute-start | bytes 589832 | tf_op jit(solution)/shard_map/ppermute | solution.py:223
  78.9 21.9 %collective-permute-start.22 = (f32[8,48,128]{2,1,0:T(8,128)S(1)}, f32[8,48,128]{2,1,0:T(8,128)S(1)}, u32[]{:S(2)}, u32[]{:S(2)}) collective-permute-start(f32[8,48,128]{2,1,0:T(8,128)S(1)} %get-tuple-element.118), channel_id=1, source_target_pairs={{8,0},{16,8},{9,1},{17,9},{10,2},{18,10},{11,3},{19,11},{12,4},{20... | collective-permute-start | bytes 589832 | tf_op jit(solution)/shard_map/ppermute | solution.py:222
  80.2 0.7 collective-permute-start.18
  81.8 25.8 %copy-start.7 = (f32[2,48,128]{2,1,0:T(8,128)}, f32[2,48,128]{2,1,0:T(8,128)S(1)}, u32[]{:S(2)}) copy-start(f32[2,48,128]{2,1,0:T(8,128)S(1)} %get-tuple-element.150) | copy-start | bytes 147460
  82.5 18.1 %collective-permute-start.20 = (f32[48,128]{1,0:T(8,128)S(1)}, f32[48,128]{1,0:T(8,128)S(1)}, u32[]{:S(2)}, u32[]{:S(2)}) collective-permute-start(f32[48,128]{1,0:T(8,128)S(1)} %sub.318), channel_id=1, source_target_pairs={{24,0},{16,8},{25,1},{17,9},{26,2},{18,10},{27,3},{19,11},{28,4},{... | collective-permute-start | bytes 73736 | tf_op jit(solution)/shard_map/ppermute | solution.py:61
  83.8 17.0 %collective-permute-start.23 = (f32[48,128]{1,0:T(8,128)S(1)}, f32[48,128]{1,0:T(8,128)S(1)}, u32[]{:S(2)}, u32[]{:S(2)}) collective-permute-start(f32[48,128]{1,0:T(8,128)S(1)} %sub.318), channel_id=1, source_target_pairs={{16,0},{24,8},{17,1},{25,9},{18,2},{26,10},{19,3},{27,11},{20,4},{... | collective-permute-start | bytes 73736 | tf_op jit(solution)/shard_map/ppermute | solution.py:62
  85.1 15.8 %collective-permute-start.19 = (f32[48,128]{1,0:T(8,128)S(1)}, f32[48,128]{1,0:T(8,128)S(1)}, u32[]{:S(2)}, u32[]{:S(2)}) collective-permute-start(f32[48,128]{1,0:T(8,128)S(1)} %sub.318), channel_id=1, source_target_pairs={{24,16},{8,0},{25,17},{9,1},{26,18},{10,2},{27,19},{11,3},{28,20},... | collective-permute-start | bytes 73736 | tf_op jit(solution)/shard_map/ppermute | solution.py:63
  101.7 5.5 %copy-start.17 = (f32[2,48,128]{2,1,0:T(8,128)}, f32[2,48,128]{2,1,0:T(8,128)S(1)}, u32[]{:S(2)}) copy-start(f32[2,48,128]{2,1,0:T(8,128)S(1)} %pad_maximum_fusion.3) | copy-start | bytes 147460
  101.7 4.7 %collective-permute-start.26 = (f32[2,48,128]{2,1,0:T(8,128)S(1)}, f32[2,48,128]{2,1,0:T(8,128)S(1)}, u32[]{:S(2)}, u32[]{:S(2)}) collective-permute-start(f32[2,48,128]{2,1,0:T(8,128)S(1)} %pad_maximum_fusion.3), channel_id=1, source_target_pairs={{1,2},{3,4},{5,6},{2,1},{4,3},{6,5},{9,10},{11,12},{13,14},{10,9},... | collective-permute-start | bytes 147464 | tf_op jit(solution)/shard_map/ppermute | solution.py:240
  102.3 4.3 %collective-permute-start.27 = (f32[2,48,128]{2,1,0:T(8,128)S(1)}, f32[2,48,128]{2,1,0:T(8,128)S(1)}, u32[]{:S(2)}, u32[]{:S(2)}) collective-permute-start(f32[2,48,128]{2,1,0:T(8,128)S(1)} %pad_maximum_fusion.3), channel_id=1, source_target_pairs={{0,1},{2,3},{4,5},{6,7},{1,0},{3,2},{5,4},{7,6},{8,9},{10,11},{12,... | collective-permute-start | bytes 147464 | tf_op jit(solution)/shard_map/ppermute | solution.py:241
  108.2 5.6 %collective-permute-start.28 = (f32[2,48,128]{2,1,0:T(8,128)S(1)}, f32[2,48,128]{2,1,0:T(8,128)S(1)}, u32[]{:S(2)}, u32[]{:S(2)}) collective-permute-start(f32[2,48,128]{2,1,0:T(8,128)S(1)} %pad_maximum_fusion.2), channel_id=1, source_target_pairs={{0,8},{1,9},{2,10},{3,11},{4,12},{5,13},{6,14},{7,15}} | collective-permute-start | bytes 147464 | tf_op jit(solution)/shard_map/ppermute | solution.py:54
  114.5 0.7 collective-permute-start.29
  115.9 0.7 collective-permute-start.30
  117.3 21.5 %copy-start.8 = (f32[2,48,128]{2,1,0:T(8,128)}, f32[2,48,128]{2,1,0:T(8,128)S(1)}, u32[]{:S(2)}) copy-start(f32[2,48,128]{2,1,0:T(8,128)S(1)} %get-tuple-element.146) | copy-start | bytes 147460
  117.9 13.8 %collective-permute-start.32 = (f32[48,128]{1,0:T(8,128)S(1)}, f32[48,128]{1,0:T(8,128)S(1)}, u32[]{:S(2)}, u32[]{:S(2)}) collective-permute-start(f32[48,128]{1,0:T(8,128)S(1)} %sub.332), channel_id=1, source_target_pairs={{24,0},{16,8},{25,1},{17,9},{26,2},{18,10},{27,3},{19,11},{28,4},{... | collective-permute-start | bytes 73736 | tf_op jit(solution)/shard_map/ppermute | solution.py:61
  119.2 12.6 %collective-permute-start.33 = (f32[48,128]{1,0:T(8,128)S(1)}, f32[48,128]{1,0:T(8,128)S(1)}, u32[]{:S(2)}, u32[]{:S(2)}) collective-permute-start(f32[48,128]{1,0:T(8,128)S(1)} %sub.332), channel_id=1, source_target_pairs={{16,0},{24,8},{17,1},{25,9},{18,2},{26,10},{19,3},{27,11},{20,4},{... | collective-permute-start | bytes 73736 | tf_op jit(solution)/shard_map/ppermute | solution.py:62
  120.5 11.5 %collective-permute-start.31 = (f32[48,128]{1,0:T(8,128)S(1)}, f32[48,128]{1,0:T(8,128)S(1)}, u32[]{:S(2)}, u32[]{:S(2)}) collective-permute-start(f32[48,128]{1,0:T(8,128)S(1)} %sub.332), channel_id=1, source_target_pairs={{24,16},{8,0},{25,17},{9,1},{26,18},{10,2},{27,19},{11,3},{28,20},... | collective-permute-start | bytes 73736 | tf_op jit(solution)/shard_map/ppermute | solution.py:63
  132.7 5.7 %copy-start.18 = (f32[2,48,128]{2,1,0:T(8,128)}, f32[2,48,128]{2,1,0:T(8,128)S(1)}, u32[]{:S(2)}) copy-start(f32[2,48,128]{2,1,0:T(8,128)S(1)} %pad_maximum_fusion.7) | copy-start | bytes 147460
  132.7 5.0 %collective-permute-start.34 = (f32[2,48,128]{2,1,0:T(8,128)S(1)}, f32[2,48,128]{2,1,0:T(8,128)S(1)}, u32[]{:S(2)}, u32[]{:S(2)}) collective-permute-start(f32[2,48,128]{2,1,0:T(8,128)S(1)} %pad_maximum_fusion.7), channel_id=1, source_target_pairs={{1,2},{3,4},{5,6},{2,1},{4,3},{6,5},{9,10},{11,12},{13,14},{10,9},... | collective-permute-start | bytes 147464 | tf_op jit(solution)/shard_map/ppermute | solution.py:240
  133.6 4.4 %collective-permute-start.35 = (f32[2,48,128]{2,1,0:T(8,128)S(1)}, f32[2,48,128]{2,1,0:T(8,128)S(1)}, u32[]{:S(2)}, u32[]{:S(2)}) collective-permute-start(f32[2,48,128]{2,1,0:T(8,128)S(1)} %pad_maximum_fusion.7), channel_id=1, source_target_pairs={{0,1},{2,3},{4,5},{6,7},{1,0},{3,2},{5,4},{7,6},{8,9},{10,11},{12,... | collective-permute-start | bytes 147464 | tf_op jit(solution)/shard_map/ppermute | solution.py:241
  139.4 5.4 %collective-permute-start.36 = (f32[2,48,128]{2,1,0:T(8,128)S(1)}, f32[2,48,128]{2,1,0:T(8,128)S(1)}, u32[]{:S(2)}, u32[]{:S(2)}) collective-permute-start(f32[2,48,128]{2,1,0:T(8,128)S(1)} %pad_maximum_fusion.6), channel_id=1, source_target_pairs={{0,8},{1,9},{2,10},{3,11},{4,12},{5,13},{6,14},{7,15}} | collective-permute-start | bytes 147464 | tf_op jit(solution)/shard_map/ppermute | solution.py:54
  145.5 0.7 collective-permute-start.37
  146.9 0.7 collective-permute-start.38
  148.7 13.8 %collective-permute-start.40 = (f32[48,128]{1,0:T(8,128)S(1)}, f32[48,128]{1,0:T(8,128)S(1)}, u32[]{:S(2)}, u32[]{:S(2)}) collective-permute-start(f32[48,128]{1,0:T(8,128)S(1)} %sub.346), channel_id=1, source_target_pairs={{24,0},{16,8},{25,1},{17,9},{26,2},{18,10},{27,3},{19,11},{28,4},{... | collective-permute-start | bytes 73736 | tf_op jit(solution)/shard_map/ppermute | solution.py:61
  150.0 12.6 %collective-permute-start.41 = (f32[48,128]{1,0:T(8,128)S(1)}, f32[48,128]{1,0:T(8,128)S(1)}, u32[]{:S(2)}, u32[]{:S(2)}) collective-permute-start(f32[48,128]{1,0:T(8,128)S(1)} %sub.346), channel_id=1, source_target_pairs={{16,0},{24,8},{17,1},{25,9},{18,2},{26,10},{19,3},{27,11},{20,4},{... | collective-permute-start | bytes 73736 | tf_op jit(solution)/shard_map/ppermute | solution.py:62
  151.3 11.5 %collective-permute-start.39 = (f32[48,128]{1,0:T(8,128)S(1)}, f32[48,128]{1,0:T(8,128)S(1)}, u32[]{:S(2)}, u32[]{:S(2)}) collective-permute-start(f32[48,128]{1,0:T(8,128)S(1)} %sub.346), channel_id=1, source_target_pairs={{24,16},{8,0},{25,17},{9,1},{26,18},{10,2},{27,19},{11,3},{28,20},... | collective-permute-start | bytes 73736 | tf_op jit(solution)/shard_map/ppermute | solution.py:63
  163.5 10.1 %copy-start.19 = (f32[2,48,128]{2,1,0:T(8,128)}, f32[2,48,128]{2,1,0:T(8,128)S(1)}, u32[]{:S(2)}) copy-start(f32[2,48,128]{2,1,0:T(8,128)S(1)} %pad_maximum_fusion.12) | copy-start | bytes 147460
  163.5 10.2 %collective-permute-start.43 = (f32[2,48,128]{2,1,0:T(8,128)S(1)}, f32[2,48,128]{2,1,0:T(8,128)S(1)}, u32[]{:S(2)}, u32[]{:S(2)}) collective-permute-start(f32[2,48,128]{2,1,0:T(8,128)S(1)} %pad_maximum_fusion.12), channel_id=1, source_target_pairs={{1,2},{3,4},{5,6},{2,1},{4,3},{6,5},{9,10},{11,12},{13,14},{10,9},... | collective-permute-start | bytes 147464 | tf_op jit(solution)/shard_map/ppermute | solution.py:240
  164.2 9.5 %collective-permute-start.44 = (f32[2,48,128]{2,1,0:T(8,128)S(1)}, f32[2,48,128]{2,1,0:T(8,128)S(1)}, u32[]{:S(2)}, u32[]{:S(2)}) collective-permute-start(f32[2,48,128]{2,1,0:T(8,128)S(1)} %pad_maximum_fusion.12), channel_id=1, source_target_pairs={{0,1},{2,3},{4,5},{6,7},{1,0},{3,2},{5,4},{7,6},{8,9},{10,11},{12,... | collective-permute-start | bytes 147464 | tf_op jit(solution)/shard_map/ppermute | solution.py:241
  168.1 5.1 %collective-permute-start.42 = (f32[48,128]{1,0:T(8,128)S(1)}, f32[48,128]{1,0:T(8,128)S(1)}, u32[]{:S(2)}, u32[]{:S(2)}) collective-permute-start(f32[48,128]{1,0:T(8,128)S(1)} %sub.347), channel_id=1, source_target_pairs={{0,8},{8,16},{16,24},{1,9},{9,17},{17,25},{2,10},{10,18},{18,26},{... | collective-permute-start | bytes 73736 | tf_op jit(solution)/shard_map/ppermute | solution.py:326
  (4 other events, 3.4 us)

commit v5 on v4

--- a/solution.py
+++ b/solution.py
@@ -41,35 +41,56 @@
     return -message[0] if message.shape[0] == 1 else message[1] - message[0]
 
 
-def precondition(vector, last, lower, upper, pivot, products, step):
+def carry_down(vector, last, lower, pivot, products=None):
     count = lax.axis_size("line")
     incoming = jnp.zeros((1 if last is None else 2,) + vector.shape[1:], vector.dtype)
     for turn in range(count - 1):
         outgoing = sweep_down(vector, lower, pivot, down_entry(incoming))[-1]
-        if products is not None and step == 0:
+        if products is not None:
             outgoing = products.down(turn, outgoing)
-        if products is not None and step == 1:
-            outgoing = products.send(turn + count - 1, outgoing)
         message = outgoing[None] if last is None else jnp.stack([outgoing, last])
         incoming = incoming + lax.ppermute(message, "line", [(turn, turn + 1)])
+    return incoming
+
+
+def carry_up(forward, upper, pivot, products=None):
+    count = lax.axis_size("line")
+    incoming = jnp.zeros_like(forward[0])
+    for turn in range(count - 1):
+        outgoing = sweep_up(forward, upper, pivot, incoming)[0][0]
+        if products is not None:
+            outgoing = products.up(turn, outgoing)
+        pair = (count - 1 - turn, count - 2 - turn)
+        incoming = incoming + lax.ppermute(outgoing, "line", [pair])
+    return incoming
+
+
+def carry_up_at_once(forward, upper, pivot, near, far):
+    outgoing = sweep_up(forward, upper, pivot, jnp.zeros_like(forward[0]))[0][0]
+    two = lax.ppermute(outgoing, "line", [(3, 0), (2, 1)])
+    side = lax.ppermute(outgoing, "line", [(2, 0), (3, 1)])
+    one = lax.ppermute(outgoing, "line", [(3, 2), (1, 0)])
+    passed = single_apply(near, side + single_apply(far, two))
+    return one + jnp.where(lax.axis_index("line") == 1, two, 0.0) + passed
+
+
+def precondition(vector, last, lower, upper, pivot, products, step):
+    if products is not None and step == 1:
+        shape = (2,) + vector.shape[1:]
+        incoming = lax.cond(
+            lax.axis_index("patch") < lax.axis_size("patch"),
+            carry_down,
+            lambda *_: jnp.zeros(shape, vector.dtype),
+            *(vector, last, lower, pivot),
+        )
+    else:
+        incoming = carry_down(vector, last, lower, pivot, products if step == 0 else None)
     forward = sweep_down(vector, lower, pivot, down_entry(incoming))
     below = None if last is None else incoming[1]
-    incoming = jnp.zeros_like(vector[0])
     if products is not None and step > 0:
-        near, far = products.received()
-        outgoing = sweep_up(forward, upper, pivot, incoming)[0][0]
-        two = lax.ppermute(outgoing, "line", [(3, 0), (2, 1)])
-        side = lax.ppermute(outgoing, "line", [(2, 0), (3, 1)])
-        one = lax.ppermute(outgoing, "line", [(3, 2), (1, 0)])
-        passed = single_apply(near, side + single_apply(far, two))
-        incoming = one + jnp.where(lax.axis_index("line") == 1, two, 0.0) + passed
+        incoming = carry_up_at_once(forward, upper, pivot, products.near, products.far)
     else:
-        for turn in range(count - 1):
-            outgoing = sweep_up(forward, upper, pivot, incoming)[0][0]
-            if products is not None:
-                outgoing = products.up(turn, outgoing)
-            pair = (count - 1 - turn, count - 2 - turn)
-            incoming = incoming + lax.ppermute(outgoing, "line", [pair])
+        incoming = carry_up(forward, upper, pivot, products)
     result, coupled = sweep_up(forward, upper, pivot, incoming)
     return jnp.stack(result), jnp.stack(coupled), below
 
@@ -138,94 +159,78 @@
         fetch((made,), (out,), sem)
 
 
-def product_kernel(made_here, given, upper, pivot, first, second, after, *rest):
-    *pieces, held, left, right, made, sem = rest
-
-    def deliver(source):
-        start = 0
-        copies = []
-        for piece in pieces:
-            rows = pl.ds(start, piece.shape[0])
-            copies.append(pltpu.make_async_copy(source.at[rows], piece, sem.at[0]))
-            start += piece.shape[0]
-        for copy in copies:
-            copy.start()
-            copy.wait()
-
-    @pl.when(among((made_here,)))
+def whole_kernel(devices, upper, pivot, after, out, held, left, right, made, sem):
+    @pl.when(among(devices))
     def _():
+        factor(1, upper, pivot, held, left, right, made, sem)
+        fetch((made,), (out,), sem)
         factor(0, upper, pivot, held, left, right, made, sem)
-        fetch((second,), (right,), sem)
+        fetch((out,), (right,), sem)
         multiply_lines(made, right, left)
-        deliver(left)
-
-    @pl.when(among((given,)))
+        fetch((left,), (out,), sem)
+
+
+def product_kernel(devices, upper, first, second, after, other, out, held, left, right, made, sem):
+    @pl.when(among(devices))
     def _():
         fetch((first, second), (left, right), sem)
         multiply_lines(left, right, made)
-        deliver(made)
-
-
-def lines_call(kernel, pieces, upper, *operands):
+        fetch((made,), (out,), sem)
+
+
+def lines_call(kernel, upper, *operands, alias=None):
     shape = upper.shape[1:]
-    bounds = [shape[0] * piece // pieces for piece in range(pieces + 1)]
     anywhere = pl.BlockSpec(memory_space=pl.ANY)
     return pl.pallas_call(
         kernel,
-        out_shape=[
-            jax.ShapeDtypeStruct((end - start,) + shape[1:], jnp.float32)
-            for start, end in zip(bounds, bounds[1:])
-        ],
+        out_shape=jax.ShapeDtypeStruct(shape, jnp.float32),
         in_specs=[anywhere] * (1 + len(operands)),
-        out_specs=[anywhere] * pieces,
+        out_specs=anywhere,
         scratch_shapes=[pltpu.VMEM((2,) + shape, upper.dtype)]
         + [pltpu.VMEM(shape, jnp.float32)] * 3
         + [pltpu.SemaphoreType.DMA((2,))],
+        input_output_aliases={} if alias is None else {alias: 0},
         compiler_params=pltpu.CompilerParams(vmem_limit_bytes=12 << 20),
     )(upper, *operands)
 
 
 class Products:
-    pieces = 6
-
     def __init__(self, upper, pivot):
-        self.blocks = upper, pivot
-        self.sent = []
+        self.upper, self.pivot = upper, pivot
 
     def down(self, turn, outgoing):
-        def call(kernel, pieces, *operands):
-            return lines_call(kernel, pieces, *self.blocks, *operands, outgoing)
+        def call(kernel, *leading):
+            return lines_call(
+                functools.partial(kernel, *leading), self.upper, self.pivot, outgoing
+            )
 
         if turn == 0:
-            (self.second,) = call(functools.partial(factor_kernel, 1, (1, 2)), 1)
+            self.second = call(factor_kernel, 1, (2,))
             outgoing, self.second = lax.optimization_barrier((outgoing, self.second))
         if turn == 1:
-            (self.first,) = call(functools.partial(factor_kernel, 0, (2,)), 1)
+            self.first = call(factor_kernel, 0, (2,))
         if turn == 2:
             outgoing, self.first = lax.optimization_barrier((outgoing, self.first))
-            kernel = functools.partial(product_kernel, 1, 2)
-            self.made = call(kernel, self.pieces, self.first, self.second)
+            self.made = call(whole_kernel, (1,))
         return outgoing
 
     def up(self, turn, outgoing):
         if turn == 0:
-            outgoing, *self.made = lax.optimization_barrier((outgoing, *self.made))
-            return outgoing
-        return self.send(turn - 1, outgoing)
-
-    def send(self, place, value):
-        if place >= self.pieces:
-            return value
-        value, piece = lax.optimization_barrier((value, self.made[place]))
-        if place >= 2:
-            value, *self.sent[place - 2] = lax.optimization_barrier((value, *self.sent[place - 2]))
-        near = lax.ppermute(piece, "line", [(1, 0), (2, 1)])
-        far = lax.ppermute(piece, "line", [(2, 0)])
-        self.sent.append([near, far])
-        return value
-
-    def received(self):
-        return [jnp.concatenate(pieces) for pieces in zip(*self.sent)]
+            outgoing, self.made = lax.optimization_barrier((outgoing, self.made))
+        if turn == 1:
+            kernel = functools.partial(product_kernel, (2,))
+            self.made = lines_call(
+                kernel, self.upper, self.first, self.second, outgoing, self.made, alias=4
+            )
+        if turn == 2:
+            outgoing, self.made = lax.optimization_barrier((outgoing, self.made))
+        return outgoing
+
+    def send(self, direction):
+        direction, made = lax.optimization_barrier((direction, self.made))
+        self.near = lax.ppermute(made, "line", [(1, 0), (2, 1)])
+        self.far = lax.ppermute(made, "line", [(2, 0)])
+        return direction
 
 
 def rows_beside(field, across):
@@ -314,7 +319,7 @@
             basis[j], last, lower, upper, pivot, products, j
         )
         if products is not None and j == 0:
-            direction = products.send(2, direction)
+            direction = products.send(direction)
         if below is not None:
             basis[j] = basis[j].at[0].add(single_apply(lower[0], below))
         directions.append(direction)

time: 194 us -> 203 us (1.046)
  other arithmetic: 29.5 us -> 50.6 us
  starting transfers between devices: 76.5 us -> 56.7 us
  waiting for transfers between devices: 65.4 us -> 71.5 us
  local copies, waits for them, and re-layouts: 1.37 us -> 4.71 us
  blocking collectives: 14.6 us -> 11.9 us
    ppermute x36 -> x26, starting transfers between devices: 56.6 us -> 37.9 us  [the longest x12 20.7 us: carry_down(): incoming = incoming + lax.ppermute(message, 'line', [(turn, turn + 1)])]
    reduce_sum x105 -> x106, other arithmetic: 21.4 us -> 30.2 us  [single_apply(): return jnp.sum(block_mat.astype(jnp.float32) * vector[None], axis=1)]
    mul x36, other arithmetic: 0.25 us -> 7.63 us  [single_apply(): return jnp.sum(block_mat.astype(jnp.float32) * vector[None], axis=1)]
    ppermute x36 -> x26, waiting for transfers between devices: 63.5 us -> 69.6 us  [the longest x3 33.7 us: carry_up_at_once(): two = lax.ppermute(outgoing, 'line', [(3, 0), (2, 1)])]
    another operation x0 -> x1, local copies, waits for them, and re-layouts: none -> 3.11 us
    all_to_all x1, blocking collectives: 14.6 us -> 11.9 us  [per_device(): sums = lax.all_to_all(sums, ('line', 'patch'), 0, 0, tiled=True)]
    convert_element_type x0 -> x1, other arithmetic: none -> 2.43 us  [single_apply(): return jnp.sum(block_mat.astype(jnp.float32) * vector[None], axis=1)]
  transfers between devices with their start and end apart: 45 -> 35, of which waited for: 14 -> 11; matrix products, arithmetic and copies ran while one was open for 5% -> 16% of each run, Pallas kernels for 0% -> 0%
where the time goes in v5:
time: 203 us; the launch traced here: 201 us
  waiting for transfers between devices  71.5 us (35%)
  starting transfers between devices  56.7 us (28%)
  other arithmetic  50.6 us (25%)
  blocking collectives  11.9 us (6%)
  local copies, waits for them, and re-layouts  4.71 us (2%)
  Pallas kernels  3.4 us (2%)
  between operations  2.1 us (1%)
    ppermute x3, waiting for transfers between devices, carry_up_at_once(): two = lax.ppermute(outgoing, 'line', [(3, 0), (2, 1)])  33.7 us
    reduce_sum x106, other arithmetic, single_apply(): return jnp.sum(block_mat.astype(jnp.float32) * vector[None], axis=1)  30.2 us
    ppermute x3, waiting for transfers between devices, carry_up(): incoming = incoming + lax.ppermute(outgoing, 'line', [pair])  29.1 us
    ppermute x12, starting transfers between devices, carry_down(): incoming = incoming + lax.ppermute(message, 'line', [(turn, turn + 1)])  20.7 us
    ppermute x4, starting transfers between devices, rows_beside(): near = lax.ppermute(to_near, 'patch', even + [(b, a) for a, b in even])  13.2 us
    all_to_all x1, blocking collectives, per_device(): sums = lax.all_to_all(sums, ('line', 'patch'), 0, 0, tiled=True)  11.9 us
    mul x36, other arithmetic, single_apply(): return jnp.sum(block_mat.astype(jnp.float32) * vector[None], axis=1)  7.63 us
    ppermute x12, waiting for transfers between devices, carry_down(): incoming = incoming + lax.ppermute(message, 'line', [(turn, turn + 1)])  6.78 us
  transfers between devices with their start and end apart: 35, of which 11 were waited for; matrix products, arithmetic and copies ran while one was open for 16% of the time, Pallas kernels for 0%

profile of v5, /device:TPU:0, one launch (start us, length us, event | category | flops | bytes accessed | tf_op | source)
XLA Modules:
  0.0 201.0 jit_solution(3031675067525139268)
XLA Ops:
  0.0 1.3 fusion.43
  1.3 0.9 fusion.163
  2.2 1.2 fusion.96
  3.4 1.2 fusion.59
  4.9 5.0 %collective-permute-start.3 = (f32[1,48,128]{2,1,0:T(8,128)S(1)}, f32[1,48,128]{2,1,0:T(8,128)S(1)}, u32[]{:S(2)}, u32[]{:S(2)}) collective-permute-start(f32[1,48,128]{2,1,0:T(8,128)S(1)} %bitcast.397), channel_id=1, source_target_pairs={{0,8},{1,9},{2,10},{3,11},{4,12},{5,13},{6,14},{7,15}} | collective-permute-start | bytes 73736 | tf_op jit(solution)/shard_map/ppermute | solution.py:52
  10.1 1.3 collective-permute-done.3
  19.1 1.3 collective-permute-start.8
  20.4 29.1 %collective-permute-done.8 = f32[48,128]{1,0:T(8,128)} collective-permute-done((f32[48,128]{1,0:T(8,128)}, f32[48,128]{1,0:T(8,128)}, u32[]{:S(2)}, u32[]{:S(2)}) %collective-permute-start.8) | collective-permute-done | bytes 24608 | tf_op jit(solution)/shard_map/ppermute | solution.py:64
  49.5 0.8 add.222
  51.1 0.8 collective-permute-start.9
  51.9 1.3 collective-permute-start.15
  53.2 1.5 collective-permute-start.13
  55.4 1.0 fusion.18
  57.0 20.2 %conditional.1 = (f32[2,48,128]{2,1,0:T(8,128)}) conditional(s32[]{:T(128)} %convert_element_type.97, () %tuple.33, (bf16[2,48,48,128]{3,2,1,0:T(8,128)(2,1)S(1)}, f32[2,48,128]{2,1,0:T(8,128)}, bf16[2,48,48,1,128]{4,2,3,1,0:T(8,128)(2,1)}, f32[2,48,128]{2,1,0:T(8,128)}) %tuple.58), branch_computations={%region_36.37_spmd, %region_37.50_spmd} | conditional | flops 9474048 | bytes 19095708 | solution.py:80
  57.0 3.1 %copy.13 = bf16[2,48,48,1,128]{4,3,2,1,0:T(2,128)(2,1)S(1)} copy(bf16[2,48,48,1,128]{4,2,3,1,0:T(8,128)(2,1)} %get-tuple-element.84) | data formatting | bytes 2359296 | tf_op jit(solution)/shard_map
  60.1 2.4 %slice_convert_fusion = (f32[1,48,48,1,128]{4,3,2,1,0:T(1,128)S(1)}, f32[1,48,48,1,128]{4,3,2,1,0:T(1,128)S(1)}) fusion(bf16[2,48,48,1,128]{4,3,2,1,0:T(2,128)(2,1)S(1)} %copy.13), kind=kLoop, calls=%fused_computation.12 | loop fusion | flops 589824 | bytes 3538944 | tf_op jit(solution)/shard_map/cond/branch_1_fun/convert_element_type | solution.py:14
  62.7 0.7 fusion.13
  63.8 0.7 fusion.12
  64.7 4.5 %collective-permute-start = (f32[2,48,128]{2,1,0:T(8,128)S(1)}, f32[2,48,128]{2,1,0:T(8,128)S(1)}, u32[]{:S(2)}, u32[]{:S(2)}) collective-permute-start(f32[2,48,128]{2,1,0:T(8,128)S(1)} %pad_maximum_fusion.2), channel_id=1, source_target_pairs={{0,8},{1,9},{2,10},{3,11},{4,12},{5,13},{6,14},{7,15}} | collective-permute-start | bytes 147464 | tf_op jit(solution)/shard_map/cond/branch_1_fun/ppermute | solution.py:52
  69.3 1.7 collective-permute-done
  71.1 0.7 fusion.11
  72.2 0.7 fusion.10
  73.1 0.7 collective-permute-start.1
  73.9 0.7 fusion.9
  75.0 0.7 fusion.8
  75.9 0.7 collective-permute-start.2
  77.2 0.9 slice_bitcast_fusion.4
  78.1 2.3 %fusion.49 = (f32[48,128]{1,0:T(8,128)}, f32[48,128]{1,0:T(8,128)S(1)}, f32[48,128]{1,0:T(8,128)S(1)}) fusion(bf16[2,48,48,1,128]{4,2,1,3,0:T(8,128)(2,1)} %bitcast.405, f32[48,128]{1,0:T(8,128)S(1)} %get-tuple-element.116, f32[48,128]{1,0:T(8,128)S(1)} %get-tuple-element.115), kind=kLoop, calls=%fused_computation.179 | loop fusion | flops 2045952 | bytes 712704 | tf_op jit(solution)/shard_map/reduce_sum | solution.py:14
  80.4 0.7 fusion.161
  81.5 1.4 fusion.142
  84.0 1.3 collective-permute-start.12
  85.3 1.3 collective-permute-start.14
  86.6 1.3 collective-permute-start.11
  87.9 14.3 %collective-permute-done.12 = f32[48,128]{1,0:T(8,128)} collective-permute-done((f32[48,128]{1,0:T(8,128)}, f32[48,128]{1,0:T(8,128)}, u32[]{:S(2)}, u32[]{:S(2)}) %collective-permute-start.12) | collective-permute-done | bytes 24608 | tf_op jit(solution)/shard_map/ppermute | solution.py:70
  102.2 1.4 multiply_reduce_fusion.11
  103.7 1.4 multiply_reduce_fusion.10
  105.9 1.0 collective-permute-start.16
  106.9 6.4 %collective-permute-start.17 = (f32[2,48,128]{2,1,0:T(8,128)S(1)}, f32[2,48,128]{2,1,0:T(8,128)S(1)}, u32[]{:S(2)}, u32[]{:S(2)}) collective-permute-start(f32[2,48,128]{2,1,0:T(8,128)S(1)} %pad_maximum_fusion.6), channel_id=1, source_target_pairs={{0,1},{2,3},{4,5},{6,7},{1,0},{3,2},{5,4},{7,6},{8,9},{10,11},{12,... | collective-permute-start | bytes 147464 | tf_op jit(solution)/shard_map/ppermute | solution.py:246
  115.4 0.8 fusion.126
  116.8 3.5 %collective-permute-start.18 = (f32[2,48,128]{2,1,0:T(8,128)S(1)}, f32[2,48,128]{2,1,0:T(8,128)S(1)}, u32[]{:S(2)}, u32[]{:S(2)}) collective-permute-start(f32[2,48,128]{2,1,0:T(8,128)S(1)} %pad_maximum_fusion.5), channel_id=1, source_target_pairs={{0,8},{1,9},{2,10},{3,11},{4,12},{5,13},{6,14},{7,15}} | collective-permute-start | bytes 147464 | tf_op jit(solution)/shard_map/ppermute | solution.py:52
  120.3 1.7 collective-permute-done.18
  122.8 0.7 collective-permute-start.19
  124.2 0.7 collective-permute-start.20
  126.4 1.3 collective-permute-start.22
  127.7 1.3 collective-permute-start.23
  129.0 1.3 collective-permute-start.21
  130.3 9.7 %collective-permute-done.22 = f32[48,128]{1,0:T(8,128)S(1)} collective-permute-done((f32[48,128]{1,0:T(8,128)S(1)}, f32[48,128]{1,0:T(8,128)S(1)}, u32[]{:S(2)}, u32[]{:S(2)}) %collective-permute-start.22) | collective-permute-done | bytes 24608 | tf_op jit(solution)/shard_map/ppermute | solution.py:70
  140.0 1.4 multiply_reduce_fusion.9
  141.4 1.4 multiply_reduce_fusion.8
  144.2 3.3 %collective-permute-start.25 = (f32[2,48,128]{2,1,0:T(8,128)S(1)}, f32[2,48,128]{2,1,0:T(8,128)S(1)}, u32[]{:S(2)}, u32[]{:S(2)}) collective-permute-start(f32[2,48,128]{2,1,0:T(8,128)S(1)} %pad_maximum_fusion.10), channel_id=1, source_target_pairs={{0,1},{2,3},{4,5},{6,7},{1,0},{3,2},{5,4},{7,6},{8,9},{10,11},{12,... | collective-permute-start | bytes 147464 | tf_op jit(solution)/shard_map/ppermute | solution.py:246
  149.9 2.4 %collective-permute-start.26 = (f32[2,48,128]{2,1,0:T(8,128)S(1)}, f32[2,48,128]{2,1,0:T(8,128)S(1)}, u32[]{:S(2)}, u32[]{:S(2)}) collective-permute-start(f32[2,48,128]{2,1,0:T(8,128)S(1)} %pad_maximum_fusion.9), channel_id=1, source_target_pairs={{0,8},{1,9},{2,10},{3,11},{4,12},{5,13},{6,14},{7,15}} | collective-permute-start | bytes 147464 | tf_op jit(solution)/shard_map/ppermute | solution.py:52
  152.2 2.0 collective-permute-done.26
  158.1 1.3 collective-permute-start.30
  159.4 1.3 collective-permute-start.31
  160.7 1.6 collective-permute-start.29
  162.2 9.6 %collective-permute-done.30 = f32[48,128]{1,0:T(8,128)S(1)} collective-permute-done((f32[48,128]{1,0:T(8,128)S(1)}, f32[48,128]{1,0:T(8,128)S(1)}, u32[]{:S(2)}, u32[]{:S(2)}) %collective-permute-start.30) | collective-permute-done | bytes 24608 | tf_op jit(solution)/shard_map/ppermute | solution.py:70
  171.9 1.4 multiply_reduce_fusion.7
  173.3 1.4 multiply_reduce_fusion.6
  176.1 3.5 %collective-permute-start.34 = (f32[2,48,128]{2,1,0:T(8,128)S(1)}, f32[2,48,128]{2,1,0:T(8,128)S(1)}, u32[]{:S(2)}, u32[]{:S(2)}) collective-permute-start(f32[2,48,128]{2,1,0:T(8,128)S(1)} %pad_maximum_fusion.12), channel_id=1, source_target_pairs={{0,1},{2,3},{4,5},{6,7},{1,0},{3,2},{5,4},{7,6},{8,9},{10,11},{12,... | collective-permute-start | bytes 147464 | tf_op jit(solution)/shard_map/ppermute | solution.py:246
  180.0 2.3 %collective-permute-start.32 = (f32[48,128]{1,0:T(8,128)S(1)}, f32[48,128]{1,0:T(8,128)S(1)}, u32[]{:S(2)}, u32[]{:S(2)}) collective-permute-start(f32[48,128]{1,0:T(8,128)S(1)} %sub.342), channel_id=1, source_target_pairs={{0,8},{8,16},{16,24},{1,9},{9,17},{17,25},{2,10},{10,18},{18,26},{... | collective-permute-start | bytes 73736 | tf_op jit(solution)/shard_map/ppermute | solution.py:331
  182.5 1.3 collective-permute-done.32
  185.8 1.6 shard_map.77
  187.5 11.9 %all_to_all.11 = f32[32,1,128]{2,1,0:T(1,128)} all-to-all(f32[32,1,128]{2,1,0:T(1,128)} %bitcast.475), channel_id=1, replica_groups=mesh['line'=4,'patch'=8] {'line','patch'}, dimensions={0} | all-to-all | bytes 32768 | tf_op jit(solution)/shard_map/all_to_all | solution.py:342
  199.3 1.6 shard_map.78
  (304 shorter events, 30.5 us)
Async XLA Ops:
  0.0 4.7 %copy-start.1 = (bf16[2,48,48,1,128]{4,2,3,1,0:T(8,128)(2,1)S(1)}, bf16[2,48,48,1,128]{4,2,3,1,0:T(8,128)(2,1)}, u32[]{:S(2)}) copy-start(bf16[2,48,48,1,128]{4,2,3,1,0:T(8,128)(2,1)} %param.21) | copy-start | bytes 3538948
  1.3 3.5 %copy-start = (bf16[2,48,48,1,128]{4,2,3,1,0:T(8,128)(2,1)S(1)}, bf16[2,48,48,1,128]{4,2,3,1,0:T(8,128)(2,1)}, u32[]{:S(2)}) copy-start(bf16[2,48,48,1,128]{4,2,3,1,0:T(8,128)(2,1)} %param.18) | copy-start | bytes 3538948
  4.9 6.5 %copy-start.2 = (bf16[2,48,48,1,128]{4,2,3,1,0:T(8,128)(2,1)S(1)}, bf16[2,48,48,1,128]{4,2,3,1,0:T(8,128)(2,1)}, u32[]{:S(2)}) copy-start(bf16[2,48,48,1,128]{4,2,3,1,0:T(8,128)(2,1)} %param.17) | copy-start | bytes 3538948
  4.9 6.5 %collective-permute-start.3 = (f32[1,48,128]{2,1,0:T(8,128)S(1)}, f32[1,48,128]{2,1,0:T(8,128)S(1)}, u32[]{:S(2)}, u32[]{:S(2)}) collective-permute-start(f32[1,48,128]{2,1,0:T(8,128)S(1)} %bitcast.397), channel_id=1, source_target_pairs={{0,8},{1,9},{2,10},{3,11},{4,12},{5,13},{6,14},{7,15}} | collective-permute-start | bytes 73736 | tf_op jit(solution)/shard_map/ppermute | solution.py:52
  12.0 3.2 %copy-start.21 = (f32[48,128]{1,0:T(8,128)}, f32[48,128]{1,0:T(8,128)S(1)}, u32[]{:S(2)}) copy-start(f32[48,128]{1,0:T(8,128)S(1)} %get-tuple-element.93) | copy-start | bytes 73732
  12.4 0.7 collective-permute-start.4
  13.8 0.7 collective-permute-start.5
  14.9 3.5 %copy-start.14 = (f32[48,128]{1,0:T(8,128)}, f32[48,128]{1,0:T(8,128)S(1)}, u32[]{:S(2)}) copy-start(f32[48,128]{1,0:T(8,128)S(1)} %fusion.99) | copy-start | bytes 73732
  15.2 2.8 %copy-start.19 = (f32[48,128]{1,0:T(8,128)}, f32[48,128]{1,0:T(8,128)S(1)}, u32[]{:S(2)}) copy-start(f32[48,128]{1,0:T(8,128)S(1)} %fusion.79) | copy-start | bytes 73732
  15.6 0.7 collective-permute-start.6
  17.0 0.7 collective-permute-start.7
  19.1 30.5 %collective-permute-start.8 = (f32[48,128]{1,0:T(8,128)}, f32[48,128]{1,0:T(8,128)}, u32[]{:S(2)}, u32[]{:S(2)}) collective-permute-start(f32[48,128]{1,0:T(8,128)} %sub.304), channel_id=1, source_target_pairs={{8,0},{9,1},{10,2},{11,3},{12,4},{13,5},{14,6},{15,7}} | collective-permute-start | bytes 73736 | tf_op jit(solution)/shard_map/ppermute | solution.py:64
  20.4 30.3 %copy-start.20 = (f32[48,128]{1,0:T(8,128)S(1)}, f32[48,128]{1,0:T(8,128)}, u32[]{:S(2)}) copy-start(f32[48,128]{1,0:T(8,128)} %copy-done.19) | copy-start | bytes 73732
  50.3 4.5 %copy-start.10 = (bf16[2,48,48,1,128]{4,2,3,1,0:T(8,128)(2,1)S(1)}, bf16[2,48,48,1,128]{4,2,3,1,0:T(8,128)(2,1)}, u32[]{:S(2)}) copy-start(bf16[2,48,48,1,128]{4,2,3,1,0:T(8,128)(2,1)} %param.16) | copy-start | bytes 3538948
  50.6 4.8 %copy-start.8 = (bf16[2,48,48,1,128]{4,2,3,1,0:T(8,128)(2,1)S(1)}, bf16[2,48,48,1,128]{4,2,3,1,0:T(8,128)(2,1)}, u32[]{:S(2)}) copy-start(bf16[2,48,48,1,128]{4,2,3,1,0:T(8,128)(2,1)} %param.20) | copy-start | bytes 3538948
  50.8 4.4 %copy-start.3 = (bf16[2,48,48,1,128]{4,2,3,1,0:T(8,128)(2,1)S(1)}, bf16[2,48,48,1,128]{4,2,3,1,0:T(8,128)(2,1)}, u32[]{:S(2)}) copy-start(bf16[2,48,48,1,128]{4,2,3,1,0:T(8,128)(2,1)} %param.17) | copy-start | bytes 3538948
  51.0 4.4 %copy-start.6 = (bf16[2,48,48,1,128]{4,2,3,1,0:T(8,128)(2,1)S(1)}, bf16[2,48,48,1,128]{4,2,3,1,0:T(8,128)(2,1)}, u32[]{:S(2)}) copy-start(bf16[2,48,48,1,128]{4,2,3,1,0:T(8,128)(2,1)} %param.19) | copy-start | bytes 3538948
  51.0 4.3 %copy-start.16 = (f32[2,48,128]{2,1,0:T(8,128)}, f32[2,48,128]{2,1,0:T(8,128)S(1)}, u32[]{:S(2)}) copy-start(f32[2,48,128]{2,1,0:T(8,128)S(1)} %pad_maximum_fusion.11) | copy-start | bytes 147460
  51.0 4.3 %collective-permute-start.10 = (f32[2,48,128]{2,1,0:T(8,128)S(1)}, f32[2,48,128]{2,1,0:T(8,128)S(1)}, u32[]{:S(2)}, u32[]{:S(2)}) collective-permute-start(f32[2,48,128]{2,1,0:T(8,128)S(1)} %pad_maximum_fusion.11), channel_id=1, source_target_pairs={{0,1},{2,3},{4,5},{6,7},{1,0},{3,2},{5,4},{7,6},{8,9},{10,11},{12,... | collective-permute-start | bytes 147464 | tf_op jit(solution)/shard_map/ppermute | solution.py:246
  51.1 4.2 %collective-permute-start.9 = (f32[2,48,128]{2,1,0:T(8,128)S(1)}, f32[2,48,128]{2,1,0:T(8,128)S(1)}, u32[]{:S(2)}, u32[]{:S(2)}) collective-permute-start(f32[2,48,128]{2,1,0:T(8,128)S(1)} %pad_maximum_fusion.11), channel_id=1, source_target_pairs={{1,2},{3,4},{5,6},{2,1},{4,3},{6,5},{9,10},{11,12},{13,14},{10,9},... | collective-permute-start | bytes 147464 | tf_op jit(solution)/shard_map/ppermute | solution.py:245
  51.9 50.3 %collective-permute-start.15 = (f32[48,48,128]{2,1,0:T(8,128)S(1)}, f32[48,48,128]{2,1,0:T(8,128)}, u32[]{:S(2)}, u32[]{:S(2)}) collective-permute-start(f32[48,48,128]{2,1,0:T(8,128)S(1)} %shard_map.76), channel_id=1, source_target_pairs={{16,0},{17,1},{18,2},{19,3},{20,4},{21,5},{22,6},{23,7}} | collective-permute-start | bytes 3538952 | tf_op jit(solution)/shard_map/ppermute | solution.py:232
  53.2 50.4 %collective-permute-start.13 = (f32[48,48,128]{2,1,0:T(8,128)S(1)}, f32[48,48,128]{2,1,0:T(8,128)}, u32[]{:S(2)}, u32[]{:S(2)}) collective-permute-start(f32[48,48,128]{2,1,0:T(8,128)S(1)} %shard_map.76), channel_id=1, source_target_pairs={{8,0},{16,8},{9,1},{17,9},{10,2},{18,10},{11,3},{19,11},{12,4},{20... | collective-permute-start | bytes 3538952 | tf_op jit(solution)/shard_map/ppermute | solution.py:231
  55.4 1.0 copy-start.27
  63.5 1.2 copy-start.18
  64.7 6.3 %collective-permute-start = (f32[2,48,128]{2,1,0:T(8,128)S(1)}, f32[2,48,128]{2,1,0:T(8,128)S(1)}, u32[]{:S(2)}, u32[]{:S(2)}) collective-permute-start(f32[2,48,128]{2,1,0:T(8,128)S(1)} %pad_maximum_fusion.2), channel_id=1, source_target_pairs={{0,8},{1,9},{2,10},{3,11},{4,12},{5,13},{6,14},{7,15}} | collective-permute-start | bytes 147464 | tf_op jit(solution)/shard_map/cond/branch_1_fun/ppermute | solution.py:52
  73.1 0.7 collective-permute-start.1
  75.9 0.7 collective-permute-start.2
  77.2 4.1 %copy-start.4 = (bf16[2,48,48,1,128]{4,2,3,1,0:T(8,128)(2,1)S(1)}, bf16[2,48,48,1,128]{4,2,3,1,0:T(8,128)(2,1)}, u32[]{:S(2)}) copy-start(bf16[2,48,48,1,128]{4,2,3,1,0:T(8,128)(2,1)} %param.17) | copy-start | bytes 3538948
  80.4 2.6 %copy-start.22 = (f32[48,128]{1,0:T(8,128)S(1)}, f32[48,128]{1,0:T(8,128)}, u32[]{:S(2)}) copy-start(f32[48,128]{1,0:T(8,128)} %copy-done.21) | copy-start | bytes 73732
  81.3 2.1 %copy-start.28 = (f32[48,128]{1,0:T(8,128)}, f32[48,128]{1,0:T(8,128)S(1)}, u32[]{:S(2)}) copy-start(f32[48,128]{1,0:T(8,128)S(1)} %fusion.104) | copy-start | bytes 73732
  83.0 1.0 copy-start.31
  84.0 18.2 %collective-permute-start.12 = (f32[48,128]{1,0:T(8,128)}, f32[48,128]{1,0:T(8,128)}, u32[]{:S(2)}, u32[]{:S(2)}) collective-permute-start(f32[48,128]{1,0:T(8,128)} %sub.313), channel_id=1, source_target_pairs={{24,0},{16,8},{25,1},{17,9},{26,2},{18,10},{27,3},{19,11},{28,4},{... | collective-permute-start | bytes 73736 | tf_op jit(solution)/shard_map/ppermute | solution.py:70
  85.3 18.3 %collective-permute-start.14 = (f32[48,128]{1,0:T(8,128)}, f32[48,128]{1,0:T(8,128)S(1)}, u32[]{:S(2)}, u32[]{:S(2)}) collective-permute-start(f32[48,128]{1,0:T(8,128)} %sub.313), channel_id=1, source_target_pairs={{16,0},{24,8},{17,1},{25,9},{18,2},{26,10},{19,3},{27,11},{20,4},{... | collective-permute-start | bytes 73736 | tf_op jit(solution)/shard_map/ppermute | solution.py:71
  86.6 18.5 %collective-permute-start.11 = (f32[48,128]{1,0:T(8,128)}, f32[48,128]{1,0:T(8,128)S(1)}, u32[]{:S(2)}, u32[]{:S(2)}) collective-permute-start(f32[48,128]{1,0:T(8,128)} %sub.313), channel_id=1, source_target_pairs={{24,16},{8,0},{25,17},{9,1},{26,18},{10,2},{27,19},{11,3},{28,20},... | collective-permute-start | bytes 73736 | tf_op jit(solution)/shard_map/ppermute | solution.py:72
  103.6 1.8 copy-start.32
  105.3 8.0 %copy-start.11 = (bf16[2,48,48,1,128]{4,2,3,1,0:T(8,128)(2,1)S(1)}, bf16[2,48,48,1,128]{4,2,3,1,0:T(8,128)(2,1)}, u32[]{:S(2)}) copy-start(bf16[2,48,48,1,128]{4,2,3,1,0:T(8,128)(2,1)} %param.16) | copy-start | bytes 3538948
  105.6 8.1 %copy-start.5 = (bf16[2,48,48,1,128]{4,2,3,1,0:T(8,128)(2,1)S(1)}, bf16[2,48,48,1,128]{4,2,3,1,0:T(8,128)(2,1)}, u32[]{:S(2)}) copy-start(bf16[2,48,48,1,128]{4,2,3,1,0:T(8,128)(2,1)} %param.17) | copy-start | bytes 3538948
  105.8 8.3 %copy-start.7 = (bf16[2,48,48,1,128]{4,2,3,1,0:T(8,128)(2,1)S(1)}, bf16[2,48,48,1,128]{4,2,3,1,0:T(8,128)(2,1)}, u32[]{:S(2)}) copy-start(bf16[2,48,48,1,128]{4,2,3,1,0:T(8,128)(2,1)} %param.19) | copy-start | bytes 3538948
  105.9 8.7 %copy-start.24 = (f32[2,48,128]{2,1,0:T(8,128)}, f32[2,48,128]{2,1,0:T(8,128)S(1)}, u32[]{:S(2)}) copy-start(f32[2,48,128]{2,1,0:T(8,128)S(1)} %pad_maximum_fusion.6) | copy-start | bytes 147460
  105.9 8.0 %collective-permute-start.16 = (f32[2,48,128]{2,1,0:T(8,128)S(1)}, f32[2,48,128]{2,1,0:T(8,128)S(1)}, u32[]{:S(2)}, u32[]{:S(2)}) collective-permute-start(f32[2,48,128]{2,1,0:T(8,128)S(1)} %pad_maximum_fusion.6), channel_id=1, source_target_pairs={{1,2},{3,4},{5,6},{2,1},{4,3},{6,5},{9,10},{11,12},{13,14},{10,9},... | collective-permute-start | bytes 147464 | tf_op jit(solution)/shard_map/ppermute | solution.py:245
  106.9 7.3 %collective-permute-start.17 = (f32[2,48,128]{2,1,0:T(8,128)S(1)}, f32[2,48,128]{2,1,0:T(8,128)S(1)}, u32[]{:S(2)}, u32[]{:S(2)}) collective-permute-start(f32[2,48,128]{2,1,0:T(8,128)S(1)} %pad_maximum_fusion.6), channel_id=1, source_target_pairs={{0,1},{2,3},{4,5},{6,7},{1,0},{3,2},{5,4},{7,6},{8,9},{10,11},{12,... | collective-permute-start | bytes 147464 | tf_op jit(solution)/shard_map/ppermute | solution.py:246
  113.7 1.3 copy-start.9
  114.2 2.1 %copy-start.30 = (f32[48,128]{1,0:T(8,128)S(1)}, f32[48,128]{1,0:T(8,128)}, u32[]{:S(2)}) copy-start(f32[48,128]{1,0:T(8,128)} %get-tuple-element.90) | copy-start | bytes 73732
  116.8 5.3 %collective-permute-start.18 = (f32[2,48,128]{2,1,0:T(8,128)S(1)}, f32[2,48,128]{2,1,0:T(8,128)S(1)}, u32[]{:S(2)}, u32[]{:S(2)}) collective-permute-start(f32[2,48,128]{2,1,0:T(8,128)S(1)} %pad_maximum_fusion.5), channel_id=1, source_target_pairs={{0,8},{1,9},{2,10},{3,11},{4,12},{5,13},{6,14},{7,15}} | collective-permute-start | bytes 147464 | tf_op jit(solution)/shard_map/ppermute | solution.py:52
  122.8 0.7 collective-permute-start.19
  124.2 0.7 collective-permute-start.20
  125.6 23.6 %copy-start.12 = (f32[2,48,128]{2,1,0:T(8,128)}, f32[2,48,128]{2,1,0:T(8,128)S(1)}, u32[]{:S(2)}) copy-start(f32[2,48,128]{2,1,0:T(8,128)S(1)} %get-tuple-element.110) | copy-start | bytes 147460
  126.4 13.6 %collective-permute-start.22 = (f32[48,128]{1,0:T(8,128)S(1)}, f32[48,128]{1,0:T(8,128)S(1)}, u32[]{:S(2)}, u32[]{:S(2)}) collective-permute-start(f32[48,128]{1,0:T(8,128)S(1)} %sub.327), channel_id=1, source_target_pairs={{24,0},{16,8},{25,1},{17,9},{26,2},{18,10},{27,3},{19,11},{28,4},{... | collective-permute-start | bytes 73736 | tf_op jit(solution)/shard_map/ppermute | solution.py:70
  127.7 13.7 %collective-permute-start.23 = (f32[48,128]{1,0:T(8,128)S(1)}, f32[48,128]{1,0:T(8,128)S(1)}, u32[]{:S(2)}, u32[]{:S(2)}) collective-permute-start(f32[48,128]{1,0:T(8,128)S(1)} %sub.327), channel_id=1, source_target_pairs={{16,0},{24,8},{17,1},{25,9},{18,2},{26,10},{19,3},{27,11},{20,4},{... | collective-permute-start | bytes 73736 | tf_op jit(solution)/shard_map/ppermute | solution.py:71
  129.0 13.9 %collective-permute-start.21 = (f32[48,128]{1,0:T(8,128)S(1)}, f32[48,128]{1,0:T(8,128)S(1)}, u32[]{:S(2)}, u32[]{:S(2)}) collective-permute-start(f32[48,128]{1,0:T(8,128)S(1)} %sub.327), channel_id=1, source_target_pairs={{24,16},{8,0},{25,17},{9,1},{26,18},{10,2},{27,19},{11,3},{28,20},... | collective-permute-start | bytes 73736 | tf_op jit(solution)/shard_map/ppermute | solution.py:72
  143.6 5.3 %copy-start.25 = (f32[2,48,128]{2,1,0:T(8,128)}, f32[2,48,128]{2,1,0:T(8,128)S(1)}, u32[]{:S(2)}) copy-start(f32[2,48,128]{2,1,0:T(8,128)S(1)} %pad_maximum_fusion.10) | copy-start | bytes 147460
  143.6 4.6 %collective-permute-start.24 = (f32[2,48,128]{2,1,0:T(8,128)S(1)}, f32[2,48,128]{2,1,0:T(8,128)S(1)}, u32[]{:S(2)}, u32[]{:S(2)}) collective-permute-start(f32[2,48,128]{2,1,0:T(8,128)S(1)} %pad_maximum_fusion.10), channel_id=1, source_target_pairs={{1,2},{3,4},{5,6},{2,1},{4,3},{6,5},{9,10},{11,12},{13,14},{10,9},... | collective-permute-start | bytes 147464 | tf_op jit(solution)/shard_map/ppermute | solution.py:245
  144.2 4.2 %collective-permute-start.25 = (f32[2,48,128]{2,1,0:T(8,128)S(1)}, f32[2,48,128]{2,1,0:T(8,128)S(1)}, u32[]{:S(2)}, u32[]{:S(2)}) collective-permute-start(f32[2,48,128]{2,1,0:T(8,128)S(1)} %pad_maximum_fusion.10), channel_id=1, source_target_pairs={{0,1},{2,3},{4,5},{6,7},{1,0},{3,2},{5,4},{7,6},{8,9},{10,11},{12,... | collective-permute-start | bytes 147464 | tf_op jit(solution)/shard_map/ppermute | solution.py:246
  149.9 4.3 %collective-permute-start.26 = (f32[2,48,128]{2,1,0:T(8,128)S(1)}, f32[2,48,128]{2,1,0:T(8,128)S(1)}, u32[]{:S(2)}, u32[]{:S(2)}) collective-permute-start(f32[2,48,128]{2,1,0:T(8,128)S(1)} %pad_maximum_fusion.9), channel_id=1, source_target_pairs={{0,8},{1,9},{2,10},{3,11},{4,12},{5,13},{6,14},{7,15}} | collective-permute-start | bytes 147464 | tf_op jit(solution)/shard_map/ppermute | solution.py:52
  154.9 0.7 collective-permute-start.27
  156.3 0.7 collective-permute-start.28
  158.1 13.8 %collective-permute-start.30 = (f32[48,128]{1,0:T(8,128)S(1)}, f32[48,128]{1,0:T(8,128)S(1)}, u32[]{:S(2)}, u32[]{:S(2)}) collective-permute-start(f32[48,128]{1,0:T(8,128)S(1)} %sub.341), channel_id=1, source_target_pairs={{24,0},{16,8},{25,1},{17,9},{26,2},{18,10},{27,3},{19,11},{28,4},{... | collective-permute-start | bytes 73736 | tf_op jit(solution)/shard_map/ppermute | solution.py:70
  159.4 13.9 %collective-permute-start.31 = (f32[48,128]{1,0:T(8,128)S(1)}, f32[48,128]{1,0:T(8,128)S(1)}, u32[]{:S(2)}, u32[]{:S(2)}) collective-permute-start(f32[48,128]{1,0:T(8,128)S(1)} %sub.341), channel_id=1, source_target_pairs={{16,0},{24,8},{17,1},{25,9},{18,2},{26,10},{19,3},{27,11},{20,4},{... | collective-permute-start | bytes 73736 | tf_op jit(solution)/shard_map/ppermute | solution.py:71
  160.7 14.0 %collective-permute-start.29 = (f32[48,128]{1,0:T(8,128)S(1)}, f32[48,128]{1,0:T(8,128)S(1)}, u32[]{:S(2)}, u32[]{:S(2)}) collective-permute-start(f32[48,128]{1,0:T(8,128)S(1)} %sub.341), channel_id=1, source_target_pairs={{24,16},{8,0},{25,17},{9,1},{26,18},{10,2},{27,19},{11,3},{28,20},... | collective-permute-start | bytes 73736 | tf_op jit(solution)/shard_map/ppermute | solution.py:72
  175.4 8.8 %copy-start.26 = (f32[2,48,128]{2,1,0:T(8,128)}, f32[2,48,128]{2,1,0:T(8,128)S(1)}, u32[]{:S(2)}) copy-start(f32[2,48,128]{2,1,0:T(8,128)S(1)} %pad_maximum_fusion.12) | copy-start | bytes 147460
  175.4 8.9 %collective-permute-start.33 = (f32[2,48,128]{2,1,0:T(8,128)S(1)}, f32[2,48,128]{2,1,0:T(8,128)S(1)}, u32[]{:S(2)}, u32[]{:S(2)}) collective-permute-start(f32[2,48,128]{2,1,0:T(8,128)S(1)} %pad_maximum_fusion.12), channel_id=1, source_target_pairs={{1,2},{3,4},{5,6},{2,1},{4,3},{6,5},{9,10},{11,12},{13,14},{10,9},... | collective-permute-start | bytes 147464 | tf_op jit(solution)/shard_map/ppermute | solution.py:245
  176.1 8.2 %collective-permute-start.34 = (f32[2,48,128]{2,1,0:T(8,128)S(1)}, f32[2,48,128]{2,1,0:T(8,128)S(1)}, u32[]{:S(2)}, u32[]{:S(2)}) collective-permute-start(f32[2,48,128]{2,1,0:T(8,128)S(1)} %pad_maximum_fusion.12), channel_id=1, source_target_pairs={{0,1},{2,3},{4,5},{6,7},{1,0},{3,2},{5,4},{7,6},{8,9},{10,11},{12,... | collective-permute-start | bytes 147464 | tf_op jit(solution)/shard_map/ppermute | solution.py:246
  180.0 3.9 %collective-permute-start.32 = (f32[48,128]{1,0:T(8,128)S(1)}, f32[48,128]{1,0:T(8,128)S(1)}, u32[]{:S(2)}, u32[]{:S(2)}) collective-permute-start(f32[48,128]{1,0:T(8,128)S(1)} %sub.342), channel_id=1, source_target_pairs={{0,8},{8,16},{16,24},{1,9},{9,17},{17,25},{2,10},{10,18},{18,26},{... | collective-permute-start | bytes 73736 | tf_op jit(solution)/shard_map/ppermute | solution.py:331
  184.7 14.6 %copy-start.17 = (f32[2,48,128]{2,1,0:T(8,128)S(1)}, f32[2,48,128]{2,1,0:T(8,128)}, u32[]{:S(2)}) copy-start(f32[2,48,128]{2,1,0:T(8,128)} %copy-done.16) | copy-start | bytes 147460
  (5 other events, 3.8 us)

commit v6 on v2

--- a/solution.py
+++ b/solution.py
@@ -1,3 +1,5 @@
+import functools
+
 import jax
 import jax.numpy as jnp
 from jax import lax
@@ -35,25 +37,205 @@
     return result, coupled
 
 
-def precondition(vector, last, lower, upper, pivot):
+def down_entry(message):
+    return -message[0] if message.shape[0] == 1 else message[1] - message[0]
+
+
+def precondition(vector, last, lower, upper, pivot, turning):
     count = lax.axis_size("line")
     incoming = jnp.zeros((1 if last is None else 2,) + vector.shape[1:], vector.dtype)
-
-    def entry():
-        return -incoming[0] if last is None else incoming[1] - incoming[0]
-
     for turn in range(count - 1):
-        outgoing = sweep_down(vector, lower, pivot, entry())[-1]
+        outgoing = sweep_down(vector, lower, pivot, down_entry(incoming))[-1]
+        if turning is not None:
+            outgoing = turning.down(turn, outgoing)
         message = outgoing[None] if last is None else jnp.stack([outgoing, last])
         incoming = incoming + lax.ppermute(message, "line", [(turn, turn + 1)])
-    forward = sweep_down(vector, lower, pivot, entry())
+    forward = sweep_down(vector, lower, pivot, down_entry(incoming))
     below = None if last is None else incoming[1]
     incoming = jnp.zeros_like(vector[0])
-    for turn in reversed(range(count - 1)):
+    for turn in range(count - 1):
         outgoing = sweep_up(forward, upper, pivot, incoming)[0][0]
-        incoming = incoming + lax.ppermute(outgoing, "line", [(turn + 1, turn)])
+        if turning is not None:
+            outgoing = turning.up(turn, outgoing)
+        pair = (count - 1 - turn, count - 2 - turn)
+        incoming = incoming + lax.ppermute(outgoing, "line", [pair])
     result, coupled = sweep_up(forward, upper, pivot, incoming)
     return jnp.stack(result), jnp.stack(coupled), below
+
+
+def short_precondition(vector, last, lower, upper, pivot, turning):
+    count = lax.axis_size("line")
+    nothing = jnp.zeros_like(last)
+    incoming = jnp.zeros((2,) + vector.shape[1:], vector.dtype)
+    turned = nothing
+    for turn in range(count - 2):
+        forward = sweep_down(vector, lower, pivot, down_entry(incoming))
+        outgoing = forward[-1]
+        if turn == 0:
+            outgoing = turning.settle(outgoing)
+        message = jnp.stack([outgoing, last])
+        incoming = incoming + lax.ppermute(message, "line", [(turn, turn + 1)])
+        if turn == 0:
+            alone = sweep_up(forward, upper, pivot, nothing)[0][0]
+            turned = lax.ppermute(alone, "line", [(count - 1, count - 2)])
+    forward = sweep_down(vector, lower, pivot, down_entry(incoming))
+    message = jnp.stack([forward[-1], last])
+    turned = turned + single_apply(turning.held, down_entry(message))
+    upward = turned
+    for turn in range(1, count - 1):
+        outgoing = sweep_up(forward, upper, pivot, upward)[0][0]
+        if turn == 1:
+            outgoing, message = lax.optimization_barrier((outgoing, message))
+        pair = (count - 1 - turn, count - 2 - turn)
+        upward = upward + lax.ppermute(outgoing, "line", [pair])
+        if turn == 1:
+            incoming = incoming + lax.ppermute(message, "line", [(count - 2, count - 1)])
+    forward = sweep_down(vector, lower, pivot, down_entry(incoming))
+    result, coupled = sweep_up(forward, upper, pivot, upward)
+    return jnp.stack(result), jnp.stack(coupled), incoming[1]
+
+
+def multiply_lines(left, right, out):
+    block = right.shape[0]
+    group = max(g for g in (1, 2, 3, 4) if block % g == 0)
+    unroll = max(u for u in (1, 2, 4, 8) if block % u == 0)
+
+    def rows(step, carry):
+        start = step * group
+
+        def add(j, totals):
+            row = right[j]
+            return tuple(
+                total + left[start + q, pl.ds(j, 1), :] * row for q, total in enumerate(totals)
+            )
+
+        zero = jnp.zeros(right.shape[1:], jnp.float32)
+        totals = lax.fori_loop(0, block, add, (zero,) * group, unroll=unroll)
+        for q, total in enumerate(totals):
+            out[start + q] = total
+        return carry
+
+    lax.fori_loop(0, block // group, rows, 0)
+
+
+def fetch(sources, targets, sem):
+    copies = [
+        pltpu.make_async_copy(source, target, sem.at[place])
+        for place, (source, target) in enumerate(zip(sources, targets))
+    ]
+    for copy in copies:
+        copy.start()
+    for copy in copies:
+        copy.wait()
+
+
+def widen(source, target):
+    def row(i, carry):
+        target[i] = source[i].astype(jnp.float32)
+        return carry
+
+    lax.fori_loop(0, target.shape[0], row, 0, unroll=4)
+
+
+def on_last(body):
+    pl.when(lax.axis_index("line") == lax.axis_size("line") - 1)(body)
+
+
+def first_kernel(lower, pivot, after, factor, out, held, left, right, made, sem):
+    def body():
+        fetch((pivot.at[0], lower.at[0]), (held.at[0], held.at[1]), sem)
+        widen(held.at[0], left)
+        widen(held.at[1], right)
+        multiply_lines(left, right, made)
+        fetch((made, lower.at[1]), (factor, held.at[0]), sem)
+        widen(held.at[0], left)
+        multiply_lines(left, made, right)
+        fetch((right,), (out,), sem)
+
+    on_last(body)
+
+
+def second_kernel(pivot, given, after, out, held, left, right, made, sem):
+    def body():
+        fetch((pivot.at[1], given), (held.at[0], right), sem)
+        widen(held.at[0], left)
+        multiply_lines(left, right, made)
+        fetch((made,), (out,), sem)
+
+    on_last(body)
+
+
+def third_kernel(upper, pivot, given, factor, after, out, held, left, right, made, sem):
+    def body():
+        fetch((upper.at[0], given), (held.at[0], right), sem)
+        fetch((pivot.at[0],), (held.at[1],), sem)
+        widen(held.at[0], left)
+        multiply_lines(left, right, made)
+        widen(held.at[1], left)
+        multiply_lines(left, made, right)
+        fetch((factor,), (made,), sem)
+
+        def row(i, carry):
+            right[i] = right[i] + made[i]
+            return carry
+
+        lax.fori_loop(0, right.shape[0], row, 0, unroll=4)
+        fetch((right,), (out,), sem)
+
+    on_last(body)
+
+
+def lines_call(kernel, results, block, *operands):
+    shape = block.shape[1:]
+    anywhere = pl.BlockSpec(memory_space=pl.ANY)
+    return pl.pallas_call(
+        kernel,
+        out_shape=[jax.ShapeDtypeStruct(shape, jnp.float32)] * results,
+        in_specs=[anywhere] * (1 + len(operands)),
+        out_specs=[anywhere] * results,
+        scratch_shapes=[pltpu.VMEM((2,) + shape, block.dtype)]
+        + [pltpu.VMEM(shape, jnp.float32)] * 3
+        + [pltpu.SemaphoreType.DMA((2,))],
+        compiler_params=pltpu.CompilerParams(vmem_limit_bytes=12 << 20),
+    )(block, *operands)
+
+
+class Turning:
+    def __init__(self, lower, upper, pivot):
+        self.lower, self.upper, self.pivot = lower, upper, pivot
+
+    def down(self, turn, outgoing):
+        end = lax.axis_size("line") - 2
+        if turn == 0:
+            self.factor, self.made = lines_call(first_kernel, 2, self.lower, self.pivot, outgoing)
+        if turn == min(1, end):
+            outgoing, self.made = lax.optimization_barrier((outgoing, self.made))
+        if turn == end:
+            (self.made,) = lines_call(second_kernel, 1, self.pivot, self.made, outgoing)
+        return outgoing
+
+    def up(self, turn, outgoing):
+        end = lax.axis_size("line") - 2
+        if turn == 0:
+            outgoing, self.made = lax.optimization_barrier((outgoing, self.made))
+            (self.made,) = lines_call(
+                third_kernel, 1, self.upper, self.pivot, self.made, self.factor, outgoing
+            )
+        if turn == end:
+            outgoing, self.made = lax.optimization_barrier((outgoing, self.made))
+        return outgoing
+
+    def send(self, direction):
+        direction, made = lax.optimization_barrier((direction, self.made))
+        end = lax.axis_size("line") - 1
+        self.held = lax.ppermute(made, "line", [(end, end - 1)])
+        return direction
+
+    def settle(self, outgoing):
+        if not hasattr(self, "settled"):
+            outgoing, self.held = lax.optimization_barrier((outgoing, self.held))
+            self.settled = True
+        return outgoing
 
 
 def rows_beside(field, across):
@@ -136,8 +318,15 @@
     basis = [newton_residual.reshape(count, block, wide)]
     directions = []
     last = None
+    turning = Turning(lower, upper, pivot) if line > 2 and count == 2 else None
     for j in range(ITERS):
-        direction, coupled, below = precondition(basis[j], last, lower, upper, pivot)
+        blocks = lower, upper, pivot
+        if j == 0 or turning is None:
+            direction, coupled, below = precondition(basis[j], last, *blocks, turning)
+        else:
+            direction, coupled, below = short_precondition(basis[j], last, *blocks, turning)
+        if turning is not None and j == 0:
+            direction = turning.send(direction)
         if below is not None:
             basis[j] = basis[j].at[0].add(single_apply(lower[0], below))
         directions.append(direction)

time: 182 us -> 189 us (1.038)
  blocking collectives: 11.8 us -> 19 us
  starting transfers between devices: 43.6 us -> 39.6 us
    ppermute x12 -> x22, starting transfers between devices: 10.6 us -> 20.6 us  [the longest x6 7.06 us: short_precondition(): incoming = incoming + lax.ppermute(message, 'line', [(turn, turn + 1)])]
    ppermute x12 -> x3, starting transfers between devices: 15.1 us -> 6.17 us  [precondition(): incoming = incoming + lax.ppermute(message, 'line', [(turn, turn + 1)])]
    ppermute x12 -> x22, waiting for transfers between devices: 77.8 us -> 85.6 us  [the longest x6 58 us: short_precondition(): upward = upward + lax.ppermute(outgoing, 'line', [pair])]
    all_to_all x1, blocking collectives: 11.8 us -> 19 us  [per_device(): sums = lax.all_to_all(sums, ('line', 'patch'), 0, 0, tiled=True)]
    ppermute x12 -> x3, waiting for transfers between devices: 6.01 us -> 0.23 us  [precondition(): incoming = incoming + lax.ppermute(message, 'line', [(turn, turn + 1)])]
    ppermute x4, starting transfers between devices: 13.4 us -> 8.42 us  [rows_beside(): near = lax.ppermute(to_near, 'patch', even + [(b, a) for a, b in even])]
    reduce_sum x123 -> x120, other arithmetic: 25.6 us -> 26.5 us  [single_apply(): return jnp.sum(block_mat.astype(jnp.float32) * vector[None], axis=1)]
  transfers between devices with their start and end apart: 33 -> 34, of which waited for: 11 -> 10; matrix products, arithmetic and copies ran while one was open for 2% -> 4% of each run, Pallas kernels for 0% -> 0%
where the time goes in v6:
time: 189 us; the launch traced here: 188 us
  waiting for transfers between devices  86.3 us (46%)
  starting transfers between devices  39.6 us (21%)
  other arithmetic  34.6 us (18%)
  blocking collectives  19 us (10%)
  Pallas kernels  3.4 us (2%)
  local copies, waits for them, and re-layouts  2.78 us (1%)
  between operations  2.41 us (1%)
    ppermute x6, waiting for transfers between devices, short_precondition(): upward = upward + lax.ppermute(outgoing, 'line', [pair])  58 us
    reduce_sum x120, other arithmetic, single_apply(): return jnp.sum(block_mat.astype(jnp.float32) * vector[None], axis=1)  26.5 us
    ppermute x3, waiting for transfers between devices, precondition(): incoming = incoming + lax.ppermute(outgoing, 'line', [pair])  22.9 us
    all_to_all x1, blocking collectives, per_device(): sums = lax.all_to_all(sums, ('line', 'patch'), 0, 0, tiled=True)  19 us
    ppermute x4, starting transfers between devices, rows_beside(): near = lax.ppermute(to_near, 'patch', even + [(b, a) for a, b in even])  8.42 us
    ppermute x6, starting transfers between devices, short_precondition(): incoming = incoming + lax.ppermute(message, 'line', [(turn, turn + 1)])  7.06 us
    ppermute x3, starting transfers between devices, precondition(): incoming = incoming + lax.ppermute(message, 'line', [(turn, turn + 1)])  6.17 us
    ppermute x6, starting transfers between devices, short_precondition(): upward = upward + lax.ppermute(outgoing, 'line', [pair])  5.86 us
  transfers between devices with their start and end apart: 34, of which 10 were waited for; matrix products, arithmetic and copies ran while one was open for 4% of the time, Pallas kernels for 0%

profile of v6, /device:TPU:0, one launch (start us, length us, event | category | flops | bytes accessed | tf_op | source)
XLA Modules:
  0.0 188.2 jit_solution(3436683011315812544)
XLA Ops:
  0.0 1.3 fusion.41
  1.3 0.8 fusion.193
  2.1 1.3 fusion.108
  3.4 1.2 fusion.59
  4.8 4.8 %collective-permute-start = (f32[1,48,128]{2,1,0:T(8,128)S(1)}, f32[1,48,128]{2,1,0:T(8,128)S(1)}, u32[]{:S(2)}, u32[]{:S(2)}) collective-permute-start(f32[1,48,128]{2,1,0:T(8,128)S(1)} %bitcast.442), channel_id=1, source_target_pairs={{0,8},{1,9},{2,10},{3,11},{4,12},{5,13},{6,14},{7,15}} | collective-permute-start | bytes 73736 | tf_op jit(solution)/shard_map/ppermute | solution.py:52
  9.7 1.2 fusion.12
  12.2 0.7 collective-permute-start.1
  13.6 0.7 collective-permute-start.2
  14.3 0.9 fusion.45
  15.8 0.7 copy-done.2
  16.8 0.7 collective-permute-start.3
  18.2 0.7 collective-permute-start.4
  18.9 1.0 copy-done.3
  20.7 0.6 sub.388
  21.3 1.3 collective-permute-start.5
  22.6 22.9 %collective-permute-done.5 = f32[48,128]{1,0:T(8,128)} collective-permute-done((f32[48,128]{1,0:T(8,128)}, f32[48,128]{1,0:T(8,128)}, u32[]{:S(2)}, u32[]{:S(2)}) %collective-permute-start.5) | collective-permute-done | bytes 24608 | tf_op jit(solution)/shard_map/ppermute | solution.py:61
  45.5 0.8 add.222
  47.1 0.8 collective-permute-start.6
  47.9 0.4 fusion
  48.5 0.7 collective-permute-start.8
  49.3 1.0 fusion.4
  51.1 1.5 collective-permute-start.9
  52.8 1.6 collective-permute-done.9
  55.3 0.7 collective-permute-start.10
  56.0 0.8 collective-permute-start.11
  58.4 0.7 collective-permute-start.13
  59.8 1.3 collective-permute-start.14
  61.1 0.7 collective-permute-start.12
  61.8 36.2 %collective-permute-done.14 = f32[48,128]{1,0:T(8,128)S(1)} collective-permute-done((f32[48,128]{1,0:T(8,128)S(1)}, f32[48,128]{1,0:T(8,128)S(1)}, u32[]{:S(2)}, u32[]{:S(2)}) %collective-permute-start.14) | collective-permute-done | bytes 24608 | tf_op jit(solution)/shard_map/ppermute | solution.py:90
  99.8 0.4 fusion.1
  100.3 0.7 collective-permute-start.15
  101.5 0.4 fusion.5
  102.0 0.4 fusion.9
  103.0 1.6 collective-permute-start.17
  104.8 1.6 collective-permute-done.17
  107.3 0.7 collective-permute-start.18
  108.0 0.7 collective-permute-start.19
  110.2 0.7 collective-permute-start.21
  111.6 1.3 collective-permute-start.22
  112.9 0.9 collective-permute-start.20
  113.8 10.8 %collective-permute-done.22 = f32[48,128]{1,0:T(8,128)S(1)} collective-permute-done((f32[48,128]{1,0:T(8,128)S(1)}, f32[48,128]{1,0:T(8,128)S(1)}, u32[]{:S(2)}, u32[]{:S(2)}) %collective-permute-start.22) | collective-permute-done | bytes 24608 | tf_op jit(solution)/shard_map/ppermute | solution.py:90
  126.4 0.4 fusion.2
  126.9 3.9 %collective-permute-start.24 = (f32[2,48,128]{2,1,0:T(8,128)S(1)}, f32[2,48,128]{2,1,0:T(8,128)S(1)}, u32[]{:S(2)}, u32[]{:S(2)}) collective-permute-start(f32[2,48,128]{2,1,0:T(8,128)S(1)} %pad_maximum_fusion.7), channel_id=1, source_target_pairs={{0,1},{2,3},{4,5},{6,7},{1,0},{3,2},{5,4},{7,6},{8,9},{10,11},{12,... | collective-permute-start | bytes 147464 | tf_op jit(solution)/shard_map/ppermute | solution.py:251
  130.8 0.7 collective-permute-start.23
  131.7 0.4 fusion.6
  132.1 0.4 fusion.10
  133.2 1.9 %collective-permute-start.25 = (f32[2,48,128]{2,1,0:T(8,128)S(1)}, f32[2,48,128]{2,1,0:T(8,128)S(1)}, u32[]{:S(2)}, u32[]{:S(2)}) collective-permute-start(f32[2,48,128]{2,1,0:T(8,128)S(1)} %pad_maximum_fusion.6), channel_id=1, source_target_pairs={{0,8},{1,9},{2,10},{3,11},{4,12},{5,13},{6,14},{7,15}} | collective-permute-start | bytes 147464 | tf_op jit(solution)/shard_map/ppermute | solution.py:77
  135.2 1.6 collective-permute-done.25
  137.7 0.7 collective-permute-start.26
  138.4 0.7 collective-permute-start.27
  140.7 0.7 collective-permute-start.29
  142.1 1.3 collective-permute-start.30
  143.4 0.7 collective-permute-start.28
  144.1 11.0 %collective-permute-done.30 = f32[48,128]{1,0:T(8,128)S(1)} collective-permute-done((f32[48,128]{1,0:T(8,128)S(1)}, f32[48,128]{1,0:T(8,128)S(1)}, u32[]{:S(2)}, u32[]{:S(2)}) %collective-permute-start.30) | collective-permute-done | bytes 24608 | tf_op jit(solution)/shard_map/ppermute | solution.py:90
  156.4 1.6 collective-permute-start.31
  158.3 0.4 fusion.3
  158.9 4.4 %collective-permute-start.33 = (f32[2,48,128]{2,1,0:T(8,128)S(1)}, f32[2,48,128]{2,1,0:T(8,128)S(1)}, u32[]{:S(2)}, u32[]{:S(2)}) collective-permute-start(f32[2,48,128]{2,1,0:T(8,128)S(1)} %pad_maximum_fusion.12), channel_id=1, source_target_pairs={{0,1},{2,3},{4,5},{6,7},{1,0},{3,2},{5,4},{7,6},{8,9},{10,11},{12,... | collective-permute-start | bytes 147464 | tf_op jit(solution)/shard_map/ppermute | solution.py:251
  163.2 0.7 collective-permute-start.32
  164.4 0.4 fusion.7
  164.8 0.4 fusion.11
  165.3 0.6 fusion.155
  165.9 1.6 shard_map.76
  167.5 19.0 %all_to_all.11 = f32[32,1,128]{2,1,0:T(1,128)} all-to-all(f32[32,1,128]{2,1,0:T(1,128)} %bitcast.498), channel_id=1, replica_groups=mesh['line'=4,'patch'=8] {'line','patch'}, dimensions={0} | all-to-all | bytes 32768 | tf_op jit(solution)/shard_map/all_to_all | solution.py:349
  186.5 1.7 shard_map.77
  (309 shorter events, 22.6 us)
Async XLA Ops:
  0.0 4.7 %copy-start = (bf16[2,48,48,1,128]{4,2,3,1,0:T(8,128)(2,1)S(1)}, bf16[2,48,48,1,128]{4,2,3,1,0:T(8,128)(2,1)}, u32[]{:S(2)}) copy-start(bf16[2,48,48,1,128]{4,2,3,1,0:T(8,128)(2,1)} %param.19) | copy-start | bytes 3538948
  2.1 8.8 %copy-start.1 = (bf16[2,48,48,1,128]{4,2,3,1,0:T(8,128)(2,1)S(1)}, bf16[2,48,48,1,128]{4,2,3,1,0:T(8,128)(2,1)}, u32[]{:S(2)}) copy-start(bf16[2,48,48,1,128]{4,2,3,1,0:T(8,128)(2,1)} %param.15) | copy-start | bytes 3538948
  4.8 6.4 %collective-permute-start = (f32[1,48,128]{2,1,0:T(8,128)S(1)}, f32[1,48,128]{2,1,0:T(8,128)S(1)}, u32[]{:S(2)}, u32[]{:S(2)}) collective-permute-start(f32[1,48,128]{2,1,0:T(8,128)S(1)} %bitcast.442), channel_id=1, source_target_pairs={{0,8},{1,9},{2,10},{3,11},{4,12},{5,13},{6,14},{7,15}} | collective-permute-start | bytes 73736 | tf_op jit(solution)/shard_map/ppermute | solution.py:52
  11.8 3.9 %copy-start.16 = (f32[48,128]{1,0:T(8,128)}, f32[48,128]{1,0:T(8,128)S(1)}, u32[]{:S(2)}) copy-start(f32[48,128]{1,0:T(8,128)S(1)} %get-tuple-element.97) | copy-start | bytes 73732
  12.2 0.7 collective-permute-start.1
  13.6 0.7 collective-permute-start.2
  15.2 1.3 copy-start.2
  15.4 5.3 %copy-start.12 = (f32[48,128]{1,0:T(8,128)}, f32[48,128]{1,0:T(8,128)S(1)}, u32[]{:S(2)}) copy-start(f32[48,128]{1,0:T(8,128)S(1)} %fusion.111) | copy-start | bytes 73732
  15.7 4.5 %copy-start.14 = (f32[48,128]{1,0:T(8,128)}, f32[48,128]{1,0:T(8,128)S(1)}, u32[]{:S(2)}) copy-start(f32[48,128]{1,0:T(8,128)S(1)} %fusion.82) | copy-start | bytes 73732
  16.8 0.7 collective-permute-start.3
  18.2 1.7 collective-permute-start.4
  18.9 1.0 copy-start.3
  19.9 1.3 copy-start.23
  21.3 24.2 %collective-permute-start.5 = (f32[48,128]{1,0:T(8,128)}, f32[48,128]{1,0:T(8,128)}, u32[]{:S(2)}, u32[]{:S(2)}) collective-permute-start(f32[48,128]{1,0:T(8,128)} %sub.388), channel_id=1, source_target_pairs={{8,0},{9,1},{10,2},{11,3},{12,4},{13,5},{14,6},{15,7}} | collective-permute-start | bytes 73736 | tf_op jit(solution)/shard_map/ppermute | solution.py:61
  22.6 24.0 %copy-start.15 = (f32[48,128]{1,0:T(8,128)S(1)}, f32[48,128]{1,0:T(8,128)}, u32[]{:S(2)}) copy-start(f32[48,128]{1,0:T(8,128)} %copy-done.14) | copy-start | bytes 73732
  46.2 0.7 copy-start.13
  46.2 1.7 copy-start.7
  46.6 2.7 %copy-start.6 = (bf16[2,48,48,1,128]{4,2,3,1,0:T(8,128)(2,1)S(1)}, bf16[2,48,48,1,128]{4,2,3,1,0:T(8,128)(2,1)}, u32[]{:S(2)}) copy-start(bf16[2,48,48,1,128]{4,2,3,1,0:T(8,128)(2,1)} %param.18) | copy-start | bytes 3538948
  47.0 1.6 copy-start.4
  47.0 2.4 %copy-start.5 = (bf16[2,48,48,1,128]{4,2,3,1,0:T(8,128)(2,1)S(1)}, bf16[2,48,48,1,128]{4,2,3,1,0:T(8,128)(2,1)}, u32[]{:S(2)}) copy-start(bf16[2,48,48,1,128]{4,2,3,1,0:T(8,128)(2,1)} %param.17) | copy-start | bytes 3538948
  47.0 10.6 %copy-start.11 = (f32[2,48,128]{2,1,0:T(8,128)}, f32[2,48,128]{2,1,0:T(8,128)S(1)}, u32[]{:S(2)}) copy-start(f32[2,48,128]{2,1,0:T(8,128)S(1)} %pad_maximum_fusion.11) | copy-start | bytes 147460
  47.0 2.3 %collective-permute-start.7 = (f32[2,48,128]{2,1,0:T(8,128)S(1)}, f32[2,48,128]{2,1,0:T(8,128)S(1)}, u32[]{:S(2)}, u32[]{:S(2)}) collective-permute-start(f32[2,48,128]{2,1,0:T(8,128)S(1)} %pad_maximum_fusion.11), channel_id=1, source_target_pairs={{0,1},{2,3},{4,5},{6,7},{1,0},{3,2},{5,4},{7,6},{8,9},{10,11},{12,... | collective-permute-start | bytes 147464 | tf_op jit(solution)/shard_map/ppermute | solution.py:251
  47.1 2.2 %collective-permute-start.6 = (f32[2,48,128]{2,1,0:T(8,128)S(1)}, f32[2,48,128]{2,1,0:T(8,128)S(1)}, u32[]{:S(2)}, u32[]{:S(2)}) collective-permute-start(f32[2,48,128]{2,1,0:T(8,128)S(1)} %pad_maximum_fusion.11), channel_id=1, source_target_pairs={{1,2},{3,4},{5,6},{2,1},{4,3},{6,5},{9,10},{11,12},{13,14},{10,9},... | collective-permute-start | bytes 147464 | tf_op jit(solution)/shard_map/ppermute | solution.py:250
  48.5 2.5 %collective-permute-start.8 = (f32[48,48,128]{2,1,0:T(8,128)S(1)}, f32[48,48,128]{2,1,0:T(8,128)S(1)}, u32[]{:S(2)}, u32[]{:S(2)}) collective-permute-start(f32[48,48,128]{2,1,0:T(8,128)S(1)} %copy-done.4), channel_id=1, source_target_pairs={{24,16},{25,17},{26,18},{27,19},{28,20},{29,21},{30,22},{31,23}} | collective-permute-start | bytes 3538952 | tf_op jit(solution)/shard_map/ppermute | solution.py:231
  49.3 1.0 copy-start.21
  49.3 1.0 copy-start.22
  50.3 0.7 copy-start.17
  51.1 3.3 %collective-permute-start.9 = (f32[2,48,128]{2,1,0:T(8,128)S(1)}, f32[2,48,128]{2,1,0:T(8,128)S(1)}, u32[]{:S(2)}, u32[]{:S(2)}) collective-permute-start(f32[2,48,128]{2,1,0:T(8,128)S(1)} %pad_maximum_fusion.10), channel_id=1, source_target_pairs={{0,8},{1,9},{2,10},{3,11},{4,12},{5,13},{6,14},{7,15}} | collective-permute-start | bytes 147464 | tf_op jit(solution)/shard_map/ppermute | solution.py:77
  55.3 1.5 collective-permute-start.10
  56.0 1.8 collective-permute-start.11
  58.4 0.7 collective-permute-start.13
  59.8 38.2 %collective-permute-start.14 = (f32[48,128]{1,0:T(8,128)S(1)}, f32[48,128]{1,0:T(8,128)S(1)}, u32[]{:S(2)}, u32[]{:S(2)}) collective-permute-start(f32[48,128]{1,0:T(8,128)S(1)} %sub.407), channel_id=1, source_target_pairs={{8,0},{9,1},{10,2},{11,3},{12,4},{13,5},{14,6},{15,7}} | collective-permute-start | bytes 73736 | tf_op jit(solution)/shard_map/ppermute | solution.py:90
  61.1 37.0 %collective-permute-start.12 = (f32[2,48,128]{2,1,0:T(8,128)S(1)}, f32[2,48,128]{2,1,0:T(8,128)S(1)}, u32[]{:S(2)}, u32[]{:S(2)}) collective-permute-start(f32[2,48,128]{2,1,0:T(8,128)S(1)} %pad_maximum_fusion.8), channel_id=1, source_target_pairs={{16,24},{17,25},{18,26},{19,27},{20,28},{21,29},{22,30},{23,31}} | collective-permute-start | bytes 147464 | tf_op jit(solution)/shard_map/ppermute | solution.py:92
  99.2 3.2 %copy-start.8 = (f32[2,48,128]{2,1,0:T(8,128)}, f32[2,48,128]{2,1,0:T(8,128)S(1)}, u32[]{:S(2)}) copy-start(f32[2,48,128]{2,1,0:T(8,128)S(1)} %get-tuple-element.116) | copy-start | bytes 147460
  99.8 2.2 %copy-start.18 = (f32[2,48,128]{2,1,0:T(8,128)}, f32[2,48,128]{2,1,0:T(8,128)S(1)}, u32[]{:S(2)}) copy-start(f32[2,48,128]{2,1,0:T(8,128)S(1)} %pad_maximum_fusion.3) | copy-start | bytes 147460
  100.2 1.3 collective-permute-start.16
  100.3 1.2 collective-permute-start.15
  103.0 3.4 %collective-permute-start.17 = (f32[2,48,128]{2,1,0:T(8,128)S(1)}, f32[2,48,128]{2,1,0:T(8,128)S(1)}, u32[]{:S(2)}, u32[]{:S(2)}) collective-permute-start(f32[2,48,128]{2,1,0:T(8,128)S(1)} %pad_maximum_fusion.2), channel_id=1, source_target_pairs={{0,8},{1,9},{2,10},{3,11},{4,12},{5,13},{6,14},{7,15}} | collective-permute-start | bytes 147464 | tf_op jit(solution)/shard_map/ppermute | solution.py:77
  107.3 1.4 collective-permute-start.18
  108.0 1.6 collective-permute-start.19
  110.2 0.7 collective-permute-start.21
  111.6 13.0 %collective-permute-start.22 = (f32[48,128]{1,0:T(8,128)S(1)}, f32[48,128]{1,0:T(8,128)S(1)}, u32[]{:S(2)}, u32[]{:S(2)}) collective-permute-start(f32[48,128]{1,0:T(8,128)S(1)} %sub.426), channel_id=1, source_target_pairs={{8,0},{9,1},{10,2},{11,3},{12,4},{13,5},{14,6},{15,7}} | collective-permute-start | bytes 73736 | tf_op jit(solution)/shard_map/ppermute | solution.py:90
  112.9 11.9 %collective-permute-start.20 = (f32[2,48,128]{2,1,0:T(8,128)S(1)}, f32[2,48,128]{2,1,0:T(8,128)S(1)}, u32[]{:S(2)}, u32[]{:S(2)}) collective-permute-start(f32[2,48,128]{2,1,0:T(8,128)S(1)} %pad_maximum_fusion), channel_id=1, source_target_pairs={{16,24},{17,25},{18,26},{19,27},{20,28},{21,29},{22,30},{23,31}} | collective-permute-start | bytes 147464 | tf_op jit(solution)/shard_map/ppermute | solution.py:92
  125.9 6.7 %copy-start.9 = (f32[2,48,128]{2,1,0:T(8,128)}, f32[2,48,128]{2,1,0:T(8,128)S(1)}, u32[]{:S(2)}) copy-start(f32[2,48,128]{2,1,0:T(8,128)S(1)} %get-tuple-element.112) | copy-start | bytes 147460
  126.4 5.7 %copy-start.19 = (f32[2,48,128]{2,1,0:T(8,128)}, f32[2,48,128]{2,1,0:T(8,128)S(1)}, u32[]{:S(2)}) copy-start(f32[2,48,128]{2,1,0:T(8,128)S(1)} %pad_maximum_fusion.7) | copy-start | bytes 147460
  126.9 4.8 %collective-permute-start.24 = (f32[2,48,128]{2,1,0:T(8,128)S(1)}, f32[2,48,128]{2,1,0:T(8,128)S(1)}, u32[]{:S(2)}, u32[]{:S(2)}) collective-permute-start(f32[2,48,128]{2,1,0:T(8,128)S(1)} %pad_maximum_fusion.7), channel_id=1, source_target_pairs={{0,1},{2,3},{4,5},{6,7},{1,0},{3,2},{5,4},{7,6},{8,9},{10,11},{12,... | collective-permute-start | bytes 147464 | tf_op jit(solution)/shard_map/ppermute | solution.py:251
  130.8 0.9 collective-permute-start.23
  133.2 3.7 %collective-permute-start.25 = (f32[2,48,128]{2,1,0:T(8,128)S(1)}, f32[2,48,128]{2,1,0:T(8,128)S(1)}, u32[]{:S(2)}, u32[]{:S(2)}) collective-permute-start(f32[2,48,128]{2,1,0:T(8,128)S(1)} %pad_maximum_fusion.6), channel_id=1, source_target_pairs={{0,8},{1,9},{2,10},{3,11},{4,12},{5,13},{6,14},{7,15}} | collective-permute-start | bytes 147464 | tf_op jit(solution)/shard_map/ppermute | solution.py:77
  137.7 1.4 collective-permute-start.26
  138.4 1.6 collective-permute-start.27
  140.7 0.7 collective-permute-start.29
  142.1 13.0 %collective-permute-start.30 = (f32[48,128]{1,0:T(8,128)S(1)}, f32[48,128]{1,0:T(8,128)S(1)}, u32[]{:S(2)}, u32[]{:S(2)}) collective-permute-start(f32[48,128]{1,0:T(8,128)S(1)} %sub.445), channel_id=1, source_target_pairs={{8,0},{9,1},{10,2},{11,3},{12,4},{13,5},{14,6},{15,7}} | collective-permute-start | bytes 73736 | tf_op jit(solution)/shard_map/ppermute | solution.py:90
  143.4 11.9 %collective-permute-start.28 = (f32[2,48,128]{2,1,0:T(8,128)S(1)}, f32[2,48,128]{2,1,0:T(8,128)S(1)}, u32[]{:S(2)}, u32[]{:S(2)}) collective-permute-start(f32[2,48,128]{2,1,0:T(8,128)S(1)} %pad_maximum_fusion.4), channel_id=1, source_target_pairs={{16,24},{17,25},{18,26},{19,27},{20,28},{21,29},{22,30},{23,31}} | collective-permute-start | bytes 147464 | tf_op jit(solution)/shard_map/ppermute | solution.py:92
  156.4 7.5 %collective-permute-start.31 = (f32[48,128]{1,0:T(8,128)S(1)}, f32[48,128]{1,0:T(8,128)S(1)}, u32[]{:S(2)}, u32[]{:S(2)}) collective-permute-start(f32[48,128]{1,0:T(8,128)S(1)} %sub.446), channel_id=1, source_target_pairs={{0,8},{8,16},{16,24},{1,9},{9,17},{17,25},{2,10},{10,18},{18,26},{... | collective-permute-start | bytes 73736 | tf_op jit(solution)/shard_map/ppermute | solution.py:338
  158.3 6.0 %copy-start.20 = (f32[2,48,128]{2,1,0:T(8,128)}, f32[2,48,128]{2,1,0:T(8,128)S(1)}, u32[]{:S(2)}) copy-start(f32[2,48,128]{2,1,0:T(8,128)S(1)} %pad_maximum_fusion.12) | copy-start | bytes 147460
  158.9 5.4 %collective-permute-start.33 = (f32[2,48,128]{2,1,0:T(8,128)S(1)}, f32[2,48,128]{2,1,0:T(8,128)S(1)}, u32[]{:S(2)}, u32[]{:S(2)}) collective-permute-start(f32[2,48,128]{2,1,0:T(8,128)S(1)} %pad_maximum_fusion.12), channel_id=1, source_target_pairs={{0,1},{2,3},{4,5},{6,7},{1,0},{3,2},{5,4},{7,6},{8,9},{10,11},{12,... | collective-permute-start | bytes 147464 | tf_op jit(solution)/shard_map/ppermute | solution.py:251
  163.2 1.1 collective-permute-start.32
  164.3 0.9 copy-start.10

commit v7 on v6

--- a/solution.py
+++ b/solution.py
@@ -41,13 +41,13 @@
     return -message[0] if message.shape[0] == 1 else message[1] - message[0]
 
 
-def precondition(vector, last, lower, upper, pivot, turning):
+def precondition(vector, last, lower, upper, pivot, turning, step):
     count = lax.axis_size("line")
     incoming = jnp.zeros((1 if last is None else 2,) + vector.shape[1:], vector.dtype)
     for turn in range(count - 1):
         outgoing = sweep_down(vector, lower, pivot, down_entry(incoming))[-1]
         if turning is not None:
-            outgoing = turning.down(turn, outgoing)
+            outgoing = turning.down(step, turn, outgoing)
         message = outgoing[None] if last is None else jnp.stack([outgoing, last])
         incoming = incoming + lax.ppermute(message, "line", [(turn, turn + 1)])
     forward = sweep_down(vector, lower, pivot, down_entry(incoming))
@@ -56,7 +56,7 @@
     for turn in range(count - 1):
         outgoing = sweep_up(forward, upper, pivot, incoming)[0][0]
         if turning is not None:
-            outgoing = turning.up(turn, outgoing)
+            outgoing = turning.up(step, turn, outgoing)
         pair = (count - 1 - turn, count - 2 - turn)
         incoming = incoming + lax.ppermute(outgoing, "line", [pair])
     result, coupled = sweep_up(forward, upper, pivot, incoming)
@@ -71,8 +71,6 @@
     for turn in range(count - 2):
         forward = sweep_down(vector, lower, pivot, down_entry(incoming))
         outgoing = forward[-1]
-        if turn == 0:
-            outgoing = turning.settle(outgoing)
         message = jnp.stack([outgoing, last])
         incoming = incoming + lax.ppermute(message, "line", [(turn, turn + 1)])
         if turn == 0:
@@ -141,58 +139,58 @@
     pl.when(lax.axis_index("line") == lax.axis_size("line") - 1)(body)
 
 
-def first_kernel(lower, pivot, after, factor, out, held, left, right, made, sem):
+def factor_kernel(lower, pivot, after, out, held, left, right, made, sem):
     def body():
         fetch((pivot.at[0], lower.at[0]), (held.at[0], held.at[1]), sem)
         widen(held.at[0], left)
         widen(held.at[1], right)
         multiply_lines(left, right, made)
-        fetch((made, lower.at[1]), (factor, held.at[0]), sem)
-        widen(held.at[0], left)
-        multiply_lines(left, made, right)
-        fetch((right,), (out,), sem)
+        fetch((made,), (out,), sem)
 
     on_last(body)
 
 
-def second_kernel(pivot, given, after, out, held, left, right, made, sem):
+def product_kernel(places, *refs):
+    *blocks, given, after, out, held, left, right, made, sem = refs
+
     def body():
-        fetch((pivot.at[1], given), (held.at[0], right), sem)
+        fetch((given,), (right,), sem)
+        source, target = right, made
+        for block, place in zip(blocks, places):
+            fetch((block.at[place],), (held.at[0],), sem)
+            widen(held.at[0], left)
+            multiply_lines(left, source, target)
+            source, target = target, source
+        fetch((source,), (out,), sem)
+
+    on_last(body)
+
+
+def sum_kernel(place, block, given, added, after, out, held, left, right, made, sem):
+    def body():
+        fetch((block.at[place], given), (held.at[0], right), sem)
         widen(held.at[0], left)
         multiply_lines(left, right, made)
+        fetch((added,), (right,), sem)
+
+        def row(i, carry):
+            made[i] = made[i] + right[i]
+            return carry
+
+        lax.fori_loop(0, made.shape[0], row, 0, unroll=4)
         fetch((made,), (out,), sem)
 
     on_last(body)
 
 
-def third_kernel(upper, pivot, given, factor, after, out, held, left, right, made, sem):
-    def body():
-        fetch((upper.at[0], given), (held.at[0], right), sem)
-        fetch((pivot.at[0],), (held.at[1],), sem)
-        widen(held.at[0], left)
-        multiply_lines(left, right, made)
-        widen(held.at[1], left)
-        multiply_lines(left, made, right)
-        fetch((factor,), (made,), sem)
-
-        def row(i, carry):
-            right[i] = right[i] + made[i]
-            return carry
-
-        lax.fori_loop(0, right.shape[0], row, 0, unroll=4)
-        fetch((right,), (out,), sem)
-
-    on_last(body)
-
-
-def lines_call(kernel, results, block, *operands):
+def lines_call(kernel, block, *operands):
     shape = block.shape[1:]
     anywhere = pl.BlockSpec(memory_space=pl.ANY)
     return pl.pallas_call(
         kernel,
-        out_shape=[jax.ShapeDtypeStruct(shape, jnp.float32)] * results,
+        out_shape=jax.ShapeDtypeStruct(shape, jnp.float32),
         in_specs=[anywhere] * (1 + len(operands)),
-        out_specs=[anywhere] * results,
+        out_specs=anywhere,
         scratch_shapes=[pltpu.VMEM((2,) + shape, block.dtype)]
         + [pltpu.VMEM(shape, jnp.float32)] * 3
         + [pltpu.SemaphoreType.DMA((2,))],
@@ -200,42 +198,44 @@
     )(block, *operands)
 
 
+def in_order(first, second):
+    return lax.optimization_barrier((first, second))
+
+
 class Turning:
     def __init__(self, lower, upper, pivot):
         self.lower, self.upper, self.pivot = lower, upper, pivot
 
-    def down(self, turn, outgoing):
+    def down(self, step, turn, outgoing):
         end = lax.axis_size("line") - 2
-        if turn == 0:
-            self.factor, self.made = lines_call(first_kernel, 2, self.lower, self.pivot, outgoing)
-        if turn == min(1, end):
-            outgoing, self.made = lax.optimization_barrier((outgoing, self.made))
-        if turn == end:
-            (self.made,) = lines_call(second_kernel, 1, self.pivot, self.made, outgoing)
+        if step == 0 and turn == 0:
+            self.factor = lines_call(factor_kernel, self.lower, self.pivot, outgoing)
+        if step == 0 and turn == end:
+            outgoing, self.factor = in_order(outgoing, self.factor)
+            kernel = functools.partial(product_kernel, (1,))
+            self.made = lines_call(kernel, self.lower, self.factor, outgoing)
+        if step == 1 and turn == 0:
+            outgoing, self.made = in_order(outgoing, self.made)
+            kernel = functools.partial(sum_kernel, 0)
+            self.made = lines_call(kernel, self.pivot, self.made, self.factor, outgoing)
+        if step == 1 and turn == end:
+            outgoing, self.made = in_order(outgoing, self.made)
         return outgoing
 
-    def up(self, turn, outgoing):
-        end = lax.axis_size("line") - 2
-        if turn == 0:
-            outgoing, self.made = lax.optimization_barrier((outgoing, self.made))
-            (self.made,) = lines_call(
-                third_kernel, 1, self.upper, self.pivot, self.made, self.factor, outgoing
-            )
-        if turn == end:
-            outgoing, self.made = lax.optimization_barrier((outgoing, self.made))
+    def up(self, step, turn, outgoing):
+        if step == 0 and turn == 0:
+            outgoing, self.made = in_order(outgoing, self.made)
+            kernel = functools.partial(product_kernel, (1, 0))
+            self.made = lines_call(kernel, self.pivot, self.upper, self.made, outgoing)
+        if step == 1 and turn == 1:
+            outgoing, made = in_order(outgoing, self.made)
+            end = lax.axis_size("line") - 1
+            self.held = lax.ppermute(made, "line", [(end, end - 1)])
         return outgoing
 
-    def send(self, direction):
-        direction, made = lax.optimization_barrier((direction, self.made))
-        end = lax.axis_size("line") - 1
-        self.held = lax.ppermute(made, "line", [(end, end - 1)])
-        return direction
-
-    def settle(self, outgoing):
-        if not hasattr(self, "settled"):
-            outgoing, self.held = lax.optimization_barrier((outgoing, self.held))
-            self.settled = True
-        return outgoing
+    def settle(self, value):
+        value, self.held = in_order(value, self.held)
+        return value
 
 
 def rows_beside(field, across):
@@ -321,16 +321,16 @@
     turning = Turning(lower, upper, pivot) if line > 2 and count == 2 else None
     for j in range(ITERS):
         blocks = lower, upper, pivot
-        if j == 0 or turning is None:
-            direction, coupled, below = precondition(basis[j], last, *blocks, turning)
+        if j < 2 or turning is None:
+            direction, coupled, below = precondition(basis[j], last, *blocks, turning, j)
         else:
             direction, coupled, below = short_precondition(basis[j], last, *blocks, turning)
-        if turning is not None and j == 0:
-            direction = turning.send(direction)
         if below is not None:
             basis[j] = basis[j].at[0].add(single_apply(lower[0], below))
         directions.append(direction)
         before, after = rows_beside(direction, across)
+        if turning is not None and j == 1:
+            before = turning.settle(before)
         last = direction[-1]
         image = coupled - basis[j] + block_apply(diag_block, direction)
         inner = [single_apply(lower[k], direction[k - 1]) for k in range(1, count)]

time: 189 us -> 184 us (0.974)
  starting transfers between devices: 39.6 us -> 35.9 us
  waiting for transfers between devices: 86.3 us -> 82.7 us
    ppermute x6 -> x4, waiting for transfers between devices: 58 us -> 41.3 us  [short_precondition(): upward = upward + lax.ppermute(outgoing, 'line', [pair])]
    ppermute x3 -> x6, waiting for transfers between devices: 22.9 us -> 35.8 us  [precondition(): incoming = incoming + lax.ppermute(outgoing, 'line', [pair])]
    ppermute x4, starting transfers between devices: 8.42 us -> 3.04 us  [rows_beside(): near = lax.ppermute(to_near, 'patch', even + [(b, a) for a, b in even])]
    ppermute x3 -> x6, starting transfers between devices: 6.17 us -> 10.8 us  [precondition(): incoming = incoming + lax.ppermute(message, 'line', [(turn, turn + 1)])]
    ppermute x3 -> x6, starting transfers between devices: 2.61 us -> 5.22 us  [precondition(): incoming = incoming + lax.ppermute(outgoing, 'line', [pair])]
    ppermute x6 -> x4, starting transfers between devices: 7.06 us -> 4.87 us  [short_precondition(): incoming = incoming + lax.ppermute(message, 'line', [(turn, turn + 1)])]
    ppermute x6 -> x4, starting transfers between devices: 5.86 us -> 3.91 us  [short_precondition(): upward = upward + lax.ppermute(outgoing, 'line', [pair])]
    ppermute x6 -> x4, waiting for transfers between devices: 4.71 us -> 3.14 us  [short_precondition(): incoming = incoming + lax.ppermute(message, 'line', [(turn, turn + 1)])]
  transfers between devices with their start and end apart: 34 -> 34, of which waited for: 10 -> 9; matrix products, arithmetic and copies ran while one was open for 4% -> 4% of each run, Pallas kernels for 0% -> 0%
where the time goes in v7:
time: 184 us; the launch traced here: 182 us
  waiting for transfers between devices  82.7 us (45%)
  starting transfers between devices  35.9 us (20%)
  other arithmetic  34.4 us (19%)
  blocking collectives  19 us (10%)
  local copies, waits for them, and re-layouts  4.45 us (2%)
  Pallas kernels  3.4 us (2%)
  between operations  2.44 us (1%)
    ppermute x4, waiting for transfers between devices, short_precondition(): upward = upward + lax.ppermute(outgoing, 'line', [pair])  41.3 us
    ppermute x6, waiting for transfers between devices, precondition(): incoming = incoming + lax.ppermute(outgoing, 'line', [pair])  35.8 us
    reduce_sum x121, other arithmetic, single_apply(): return jnp.sum(block_mat.astype(jnp.float32) * vector[None], axis=1)  26.2 us
    all_to_all x1, blocking collectives, per_device(): sums = lax.all_to_all(sums, ('line', 'patch'), 0, 0, tiled=True)  19 us
    ppermute x6, starting transfers between devices, precondition(): incoming = incoming + lax.ppermute(message, 'line', [(turn, turn + 1)])  10.8 us
    reduce_sum x11, other arithmetic, block_apply(): return jnp.sum(block_mat.astype(jnp.float32) * vector[:, None], axis=2)  5.34 us
    ppermute x6, starting transfers between devices, precondition(): incoming = incoming + lax.ppermute(outgoing, 'line', [pair])  5.22 us
    ppermute x4, starting transfers between devices, short_precondition(): incoming = incoming + lax.ppermute(message, 'line', [(turn, turn + 1)])  4.87 us
  transfers between devices with their start and end apart: 34, of which 9 were waited for; matrix products, arithmetic and copies ran while one was open for 4% of the time, Pallas kernels for 0%

profile of v7, /device:TPU:0, one launch (start us, length us, event | category | flops | bytes accessed | tf_op | source)
XLA Modules:
  0.0 182.3 jit_solution(9319126536267843679)
XLA Ops:
  0.0 1.3 fusion.41
  1.3 0.8 fusion.192
  2.1 1.3 fusion.108
  3.4 1.2 fusion.59
  4.8 4.8 %collective-permute-start = (f32[1,48,128]{2,1,0:T(8,128)S(1)}, f32[1,48,128]{2,1,0:T(8,128)S(1)}, u32[]{:S(2)}, u32[]{:S(2)}) collective-permute-start(f32[1,48,128]{2,1,0:T(8,128)S(1)} %bitcast.438), channel_id=1, source_target_pairs={{0,8},{1,9},{2,10},{3,11},{4,12},{5,13},{6,14},{7,15}} | collective-permute-start | bytes 73736 | tf_op jit(solution)/shard_map/ppermute | solution.py:52
  9.7 1.2 fusion.12
  12.2 0.7 collective-permute-start.1
  13.6 0.7 collective-permute-start.2
  14.4 1.0 fusion.45
  15.9 0.7 copy-done.2
  16.9 0.7 collective-permute-start.3
  17.6 0.6 copy-done.7
  18.9 0.7 collective-permute-start.4
  20.3 0.6 sub.385
  20.9 1.3 collective-permute-start.5
  22.2 1.3 copy-done.6
  23.5 0.7 copy-done.8
  24.3 16.4 %collective-permute-done.5 = f32[48,128]{1,0:T(8,128)} collective-permute-done((f32[48,128]{1,0:T(8,128)}, f32[48,128]{1,0:T(8,128)}, u32[]{:S(2)}, u32[]{:S(2)}) %collective-permute-start.5) | collective-permute-done | bytes 24608 | tf_op jit(solution)/shard_map/ppermute | solution.py:61
  40.7 0.7 add.219
  42.3 0.8 collective-permute-start.6
  43.1 0.4 fusion
  43.8 1.0 fusion.4
  45.4 3.1 %collective-permute-start.8 = (f32[2,48,128]{2,1,0:T(8,128)S(1)}, f32[2,48,128]{2,1,0:T(8,128)S(1)}, u32[]{:S(2)}, u32[]{:S(2)}) collective-permute-start(f32[2,48,128]{2,1,0:T(8,128)S(1)} %pad_maximum_fusion.2), channel_id=1, source_target_pairs={{0,8},{1,9},{2,10},{3,11},{4,12},{5,13},{6,14},{7,15}} | collective-permute-start | bytes 147464 | tf_op jit(solution)/shard_map/ppermute | solution.py:52
  48.5 1.7 collective-permute-done.8
  51.0 0.7 collective-permute-start.9
  52.5 0.8 collective-permute-start.10
  54.8 0.7 collective-permute-start.11
  56.2 0.7 collective-permute-start.12
  57.6 1.3 collective-permute-start.13
  58.9 0.7 collective-permute-start.16
  59.6 19.4 %collective-permute-done.13 = f32[48,128]{1,0:T(8,128)S(1)} collective-permute-done((f32[48,128]{1,0:T(8,128)S(1)}, f32[48,128]{1,0:T(8,128)S(1)}, u32[]{:S(2)}, u32[]{:S(2)}) %collective-permute-start.13) | collective-permute-done | bytes 24608 | tf_op jit(solution)/shard_map/ppermute | solution.py:61
  79.7 0.8 collective-permute-start.15
  80.5 0.7 collective-permute-start.14
  81.1 0.4 fusion.1
  81.8 0.4 fusion.9
  82.3 0.4 fusion.5
  83.3 1.9 %collective-permute-start.17 = (f32[2,48,128]{2,1,0:T(8,128)S(1)}, f32[2,48,128]{2,1,0:T(8,128)S(1)}, u32[]{:S(2)}, u32[]{:S(2)}) collective-permute-start(f32[2,48,128]{2,1,0:T(8,128)S(1)} %pad_maximum_fusion.6), channel_id=1, source_target_pairs={{0,8},{1,9},{2,10},{3,11},{4,12},{5,13},{6,14},{7,15}} | collective-permute-start | bytes 147464 | tf_op jit(solution)/shard_map/ppermute | solution.py:75
  85.4 1.6 collective-permute-done.17
  87.9 0.7 collective-permute-start.18
  88.6 0.7 collective-permute-start.19
  90.8 0.7 collective-permute-start.21
  92.2 1.3 collective-permute-start.22
  93.5 0.9 collective-permute-start.20
  94.4 30.3 %collective-permute-done.22 = f32[48,128]{1,0:T(8,128)S(1)} collective-permute-done((f32[48,128]{1,0:T(8,128)S(1)}, f32[48,128]{1,0:T(8,128)S(1)}, u32[]{:S(2)}, u32[]{:S(2)}) %collective-permute-start.22) | collective-permute-done | bytes 24608 | tf_op jit(solution)/shard_map/ppermute | solution.py:88
  126.5 0.4 fusion.2
  127.0 0.7 collective-permute-start.23
  129.7 1.6 collective-permute-start.25
  131.5 1.6 collective-permute-done.25
  134.0 0.7 collective-permute-start.26
  134.7 0.7 collective-permute-start.27
  137.0 0.7 collective-permute-start.29
  138.4 1.3 collective-permute-start.30
  139.7 0.7 collective-permute-start.28
  140.3 11.0 %collective-permute-done.30 = f32[48,128]{1,0:T(8,128)S(1)} collective-permute-done((f32[48,128]{1,0:T(8,128)S(1)}, f32[48,128]{1,0:T(8,128)S(1)}, u32[]{:S(2)}, u32[]{:S(2)}) %collective-permute-start.30) | collective-permute-done | bytes 24608 | tf_op jit(solution)/shard_map/ppermute | solution.py:88
  152.7 1.6 collective-permute-start.31
  154.6 0.4 fusion.3
  155.2 2.1 %collective-permute-start.33 = (f32[2,48,128]{2,1,0:T(8,128)S(1)}, f32[2,48,128]{2,1,0:T(8,128)S(1)}, u32[]{:S(2)}, u32[]{:S(2)}) collective-permute-start(f32[2,48,128]{2,1,0:T(8,128)S(1)} %pad_maximum_fusion.12), channel_id=1, source_target_pairs={{0,1},{2,3},{4,5},{6,7},{1,0},{3,2},{5,4},{7,6},{8,9},{10,11},{12,... | collective-permute-start | bytes 147464 | tf_op jit(solution)/shard_map/ppermute | solution.py:251
  157.3 0.7 collective-permute-start.32
  158.4 0.4 fusion.7
  158.9 0.4 fusion.11
  159.3 0.6 fusion.155
  160.0 1.6 shard_map.77
  161.6 19.0 %all_to_all.11 = f32[32,1,128]{2,1,0:T(1,128)} all-to-all(f32[32,1,128]{2,1,0:T(1,128)} %bitcast.497), channel_id=1, replica_groups=mesh['line'=4,'patch'=8] {'line','patch'}, dimensions={0} | all-to-all | bytes 32768 | tf_op jit(solution)/shard_map/all_to_all | solution.py:349
  180.6 1.7 shard_map.78
  (318 shorter events, 23.2 us)
Async XLA Ops:
  0.0 4.7 %copy-start = (bf16[2,48,48,1,128]{4,2,3,1,0:T(8,128)(2,1)S(1)}, bf16[2,48,48,1,128]{4,2,3,1,0:T(8,128)(2,1)}, u32[]{:S(2)}) copy-start(bf16[2,48,48,1,128]{4,2,3,1,0:T(8,128)(2,1)} %param.19) | copy-start | bytes 3538948
  2.1 9.1 %copy-start.1 = (bf16[2,48,48,1,128]{4,2,3,1,0:T(8,128)(2,1)S(1)}, bf16[2,48,48,1,128]{4,2,3,1,0:T(8,128)(2,1)}, u32[]{:S(2)}) copy-start(bf16[2,48,48,1,128]{4,2,3,1,0:T(8,128)(2,1)} %param.15) | copy-start | bytes 3538948
  4.8 6.4 %collective-permute-start = (f32[1,48,128]{2,1,0:T(8,128)S(1)}, f32[1,48,128]{2,1,0:T(8,128)S(1)}, u32[]{:S(2)}, u32[]{:S(2)}) collective-permute-start(f32[1,48,128]{2,1,0:T(8,128)S(1)} %bitcast.438), channel_id=1, source_target_pairs={{0,8},{1,9},{2,10},{3,11},{4,12},{5,13},{6,14},{7,15}} | collective-permute-start | bytes 73736 | tf_op jit(solution)/shard_map/ppermute | solution.py:52
  11.8 4.1 %copy-start.19 = (f32[48,128]{1,0:T(8,128)}, f32[48,128]{1,0:T(8,128)S(1)}, u32[]{:S(2)}) copy-start(f32[48,128]{1,0:T(8,128)S(1)} %get-tuple-element.89) | copy-start | bytes 73732
  12.2 0.7 collective-permute-start.1
  12.9 1.4 copy-start.3
  13.6 0.7 collective-permute-start.2
  14.3 1.5 copy-start.5
  15.3 1.3 copy-start.2
  15.5 4.8 %copy-start.15 = (f32[48,128]{1,0:T(8,128)}, f32[48,128]{1,0:T(8,128)S(1)}, u32[]{:S(2)}) copy-start(f32[48,128]{1,0:T(8,128)S(1)} %fusion.111) | copy-start | bytes 73732
  15.9 4.1 %copy-start.17 = (f32[48,128]{1,0:T(8,128)}, f32[48,128]{1,0:T(8,128)S(1)}, u32[]{:S(2)}) copy-start(f32[48,128]{1,0:T(8,128)S(1)} %fusion.82) | copy-start | bytes 73732
  16.9 1.3 collective-permute-start.3
  17.6 0.6 copy-start.7
  18.9 0.7 collective-permute-start.4
  19.6 0.7 copy-start.27
  20.9 19.8 %collective-permute-start.5 = (f32[48,128]{1,0:T(8,128)}, f32[48,128]{1,0:T(8,128)}, u32[]{:S(2)}, u32[]{:S(2)}) collective-permute-start(f32[48,128]{1,0:T(8,128)} %sub.385), channel_id=1, source_target_pairs={{8,0},{9,1},{10,2},{11,3},{12,4},{13,5},{14,6},{15,7}} | collective-permute-start | bytes 73736 | tf_op jit(solution)/shard_map/ppermute | solution.py:61
  22.2 1.3 copy-start.6
  23.5 0.7 copy-start.8
  24.2 16.5 %copy-start.28 = (f32[48,128]{1,0:T(8,128)S(1)}, f32[48,128]{1,0:T(8,128)}, u32[]{:S(2)}) copy-start(f32[48,128]{1,0:T(8,128)} %copy-done.27) | copy-start | bytes 73732
  24.3 17.5 %copy-start.18 = (f32[48,128]{1,0:T(8,128)S(1)}, f32[48,128]{1,0:T(8,128)}, u32[]{:S(2)}) copy-start(f32[48,128]{1,0:T(8,128)} %copy-done.17) | copy-start | bytes 73732
  41.5 0.7 copy-start.16
  41.6 1.5 copy-start.11
  42.0 1.8 copy-start.10
  42.2 1.6 copy-start.9
  42.2 0.9 copy-start.21
  42.2 1.5 collective-permute-start.7
  42.3 1.4 collective-permute-start.6
  43.8 1.0 copy-start.25
  43.8 1.0 copy-start.26
  45.4 4.9 %collective-permute-start.8 = (f32[2,48,128]{2,1,0:T(8,128)S(1)}, f32[2,48,128]{2,1,0:T(8,128)S(1)}, u32[]{:S(2)}, u32[]{:S(2)}) collective-permute-start(f32[2,48,128]{2,1,0:T(8,128)S(1)} %pad_maximum_fusion.2), channel_id=1, source_target_pairs={{0,8},{1,9},{2,10},{3,11},{4,12},{5,13},{6,14},{7,15}} | collective-permute-start | bytes 147464 | tf_op jit(solution)/shard_map/ppermute | solution.py:52
  50.4 1.3 copy-start.4
  51.0 0.8 collective-permute-start.9
  52.5 0.9 collective-permute-start.10
  53.7 0.7 copy-start.20
  54.1 28.6 %copy-start.13 = (f32[2,48,128]{2,1,0:T(8,128)}, f32[2,48,128]{2,1,0:T(8,128)S(1)}, u32[]{:S(2)}) copy-start(f32[2,48,128]{2,1,0:T(8,128)S(1)} %get-tuple-element.108) | copy-start | bytes 147460
  54.8 0.7 collective-permute-start.11
  56.2 0.7 collective-permute-start.12
  57.6 21.4 %collective-permute-start.13 = (f32[48,128]{1,0:T(8,128)S(1)}, f32[48,128]{1,0:T(8,128)S(1)}, u32[]{:S(2)}, u32[]{:S(2)}) collective-permute-start(f32[48,128]{1,0:T(8,128)S(1)} %sub.403), channel_id=1, source_target_pairs={{8,0},{9,1},{10,2},{11,3},{12,4},{13,5},{14,6},{15,7}} | collective-permute-start | bytes 73736 | tf_op jit(solution)/shard_map/ppermute | solution.py:61
  58.9 23.4 %collective-permute-start.16 = (f32[48,48,128]{2,1,0:T(8,128)S(1)}, f32[48,48,128]{2,1,0:T(8,128)S(1)}, u32[]{:S(2)}, u32[]{:S(2)}) collective-permute-start(f32[48,48,128]{2,1,0:T(8,128)S(1)} %shard_map.76), channel_id=1, source_target_pairs={{24,16},{25,17},{26,18},{27,19},{28,20},{29,21},{30,22},{31,23}} | collective-permute-start | bytes 3538952 | tf_op jit(solution)/shard_map/ppermute | solution.py:233
  79.7 2.5 %copy-start.22 = (f32[2,48,128]{2,1,0:T(8,128)}, f32[2,48,128]{2,1,0:T(8,128)S(1)}, u32[]{:S(2)}) copy-start(f32[2,48,128]{2,1,0:T(8,128)S(1)} %pad_maximum_fusion.7) | copy-start | bytes 147460
  79.7 2.0 %collective-permute-start.15 = (f32[2,48,128]{2,1,0:T(8,128)S(1)}, f32[2,48,128]{2,1,0:T(8,128)S(1)}, u32[]{:S(2)}, u32[]{:S(2)}) collective-permute-start(f32[2,48,128]{2,1,0:T(8,128)S(1)} %pad_maximum_fusion.7), channel_id=1, source_target_pairs={{0,1},{2,3},{4,5},{6,7},{1,0},{3,2},{5,4},{7,6},{8,9},{10,11},{12,... | collective-permute-start | bytes 147464 | tf_op jit(solution)/shard_map/ppermute | solution.py:251
  80.5 1.3 collective-permute-start.14
  83.3 3.7 %collective-permute-start.17 = (f32[2,48,128]{2,1,0:T(8,128)S(1)}, f32[2,48,128]{2,1,0:T(8,128)S(1)}, u32[]{:S(2)}, u32[]{:S(2)}) collective-permute-start(f32[2,48,128]{2,1,0:T(8,128)S(1)} %pad_maximum_fusion.6), channel_id=1, source_target_pairs={{0,8},{1,9},{2,10},{3,11},{4,12},{5,13},{6,14},{7,15}} | collective-permute-start | bytes 147464 | tf_op jit(solution)/shard_map/ppermute | solution.py:75
  87.9 1.4 collective-permute-start.18
  88.6 1.6 collective-permute-start.19
  90.8 0.7 collective-permute-start.21
  92.2 32.5 %collective-permute-start.22 = (f32[48,128]{1,0:T(8,128)S(1)}, f32[48,128]{1,0:T(8,128)S(1)}, u32[]{:S(2)}, u32[]{:S(2)}) collective-permute-start(f32[48,128]{1,0:T(8,128)S(1)} %sub.422), channel_id=1, source_target_pairs={{8,0},{9,1},{10,2},{11,3},{12,4},{13,5},{14,6},{15,7}} | collective-permute-start | bytes 73736 | tf_op jit(solution)/shard_map/ppermute | solution.py:88
  93.5 31.4 %collective-permute-start.20 = (f32[2,48,128]{2,1,0:T(8,128)S(1)}, f32[2,48,128]{2,1,0:T(8,128)S(1)}, u32[]{:S(2)}, u32[]{:S(2)}) collective-permute-start(f32[2,48,128]{2,1,0:T(8,128)S(1)} %pad_maximum_fusion.4), channel_id=1, source_target_pairs={{16,24},{17,25},{18,26},{19,27},{20,28},{21,29},{22,30},{23,31}} | collective-permute-start | bytes 147464 | tf_op jit(solution)/shard_map/ppermute | solution.py:90
  125.9 3.2 %copy-start.12 = (f32[2,48,128]{2,1,0:T(8,128)}, f32[2,48,128]{2,1,0:T(8,128)S(1)}, u32[]{:S(2)}) copy-start(f32[2,48,128]{2,1,0:T(8,128)S(1)} %get-tuple-element.104) | copy-start | bytes 147460
  126.5 2.2 %copy-start.23 = (f32[2,48,128]{2,1,0:T(8,128)}, f32[2,48,128]{2,1,0:T(8,128)S(1)}, u32[]{:S(2)}) copy-start(f32[2,48,128]{2,1,0:T(8,128)S(1)} %pad_maximum_fusion.11) | copy-start | bytes 147460
  126.9 1.3 collective-permute-start.24
  127.0 1.2 collective-permute-start.23
  129.7 3.4 %collective-permute-start.25 = (f32[2,48,128]{2,1,0:T(8,128)S(1)}, f32[2,48,128]{2,1,0:T(8,128)S(1)}, u32[]{:S(2)}, u32[]{:S(2)}) collective-permute-start(f32[2,48,128]{2,1,0:T(8,128)S(1)} %pad_maximum_fusion.10), channel_id=1, source_target_pairs={{0,8},{1,9},{2,10},{3,11},{4,12},{5,13},{6,14},{7,15}} | collective-permute-start | bytes 147464 | tf_op jit(solution)/shard_map/ppermute | solution.py:75
  134.0 1.4 collective-permute-start.26
  134.7 1.6 collective-permute-start.27
  137.0 0.7 collective-permute-start.29
  138.4 13.0 %collective-permute-start.30 = (f32[48,128]{1,0:T(8,128)S(1)}, f32[48,128]{1,0:T(8,128)S(1)}, u32[]{:S(2)}, u32[]{:S(2)}) collective-permute-start(f32[48,128]{1,0:T(8,128)S(1)} %sub.441), channel_id=1, source_target_pairs={{8,0},{9,1},{10,2},{11,3},{12,4},{13,5},{14,6},{15,7}} | collective-permute-start | bytes 73736 | tf_op jit(solution)/shard_map/ppermute | solution.py:88
  139.7 11.9 %collective-permute-start.28 = (f32[2,48,128]{2,1,0:T(8,128)S(1)}, f32[2,48,128]{2,1,0:T(8,128)S(1)}, u32[]{:S(2)}, u32[]{:S(2)}) collective-permute-start(f32[2,48,128]{2,1,0:T(8,128)S(1)} %pad_maximum_fusion.8), channel_id=1, source_target_pairs={{16,24},{17,25},{18,26},{19,27},{20,28},{21,29},{22,30},{23,31}} | collective-permute-start | bytes 147464 | tf_op jit(solution)/shard_map/ppermute | solution.py:90
  152.7 5.2 %collective-permute-start.31 = (f32[48,128]{1,0:T(8,128)S(1)}, f32[48,128]{1,0:T(8,128)S(1)}, u32[]{:S(2)}, u32[]{:S(2)}) collective-permute-start(f32[48,128]{1,0:T(8,128)S(1)} %sub.442), channel_id=1, source_target_pairs={{0,8},{8,16},{16,24},{1,9},{9,17},{17,25},{2,10},{10,18},{18,26},{... | collective-permute-start | bytes 73736 | tf_op jit(solution)/shard_map/ppermute | solution.py:338
  154.5 3.8 %copy-start.24 = (f32[2,48,128]{2,1,0:T(8,128)}, f32[2,48,128]{2,1,0:T(8,128)S(1)}, u32[]{:S(2)}) copy-start(f32[2,48,128]{2,1,0:T(8,128)S(1)} %pad_maximum_fusion.12) | copy-start | bytes 147460
  155.2 3.2 %collective-permute-start.33 = (f32[2,48,128]{2,1,0:T(8,128)S(1)}, f32[2,48,128]{2,1,0:T(8,128)S(1)}, u32[]{:S(2)}, u32[]{:S(2)}) collective-permute-start(f32[2,48,128]{2,1,0:T(8,128)S(1)} %pad_maximum_fusion.12), channel_id=1, source_target_pairs={{0,1},{2,3},{4,5},{6,7},{1,0},{3,2},{5,4},{7,6},{8,9},{10,11},{12,... | collective-permute-start | bytes 147464 | tf_op jit(solution)/shard_map/ppermute | solution.py:251
  157.3 1.1 collective-permute-start.32
  158.4 0.9 copy-start.14

commit v8 on v2

--- a/solution.py
+++ b/solution.py
@@ -1,3 +1,5 @@
+import functools
+
 import jax
 import jax.numpy as jnp
 from jax import lax
@@ -6,6 +8,7 @@
 from jax.sharding import PartitionSpec as P
 
 ITERS = 4
+SUMS = 16
 
 
 def single_apply(block_mat, vector):
@@ -35,6 +38,55 @@
     return result, coupled
 
 
+def first_kernel(vector, lower, pivot, out, field, held, middle, sems):
+    count, block = vector.shape[:2]
+    blocks = [pivot.at[0]]
+    for k in range(1, count):
+        blocks += [lower.at[k], pivot.at[k]]
+    copies = [pltpu.make_async_copy(vector, field, sems.at[0])]
+    for place, source in enumerate(blocks):
+        copies.append(pltpu.make_async_copy(source, held.at[place], sems.at[1 + place]))
+    for copy in copies:
+        copy.start()
+    rows = 16 if block % 16 == 0 else block
+
+    def apply(place, value, target):
+        for start in range(0, block, rows):
+            part = held[place, start : start + rows].astype(jnp.float32)
+            target[start : start + rows] = jnp.sum(part * value[None], axis=1)
+
+    copies[0].wait()
+    copies[1].wait()
+    apply(0, field[0], middle)
+    for k in range(1, count):
+        copies[2 * k].wait()
+        apply(2 * k - 1, middle[...], out)
+        value = field[k] - out[...]
+        copies[2 * k + 1].wait()
+        apply(2 * k, value, out)
+        if k < count - 1:
+            middle[...] = out[...]
+    if count == 1:
+        out[...] = middle[...]
+
+
+def first_carry(vector, lower, pivot):
+    count, block, wide = vector.shape
+    blocks = 2 * count - 1
+    return pl.pallas_call(
+        first_kernel,
+        out_shape=jax.ShapeDtypeStruct((block, wide), jnp.float32),
+        in_specs=[pl.BlockSpec(memory_space=pl.ANY)] * 3,
+        scratch_shapes=[
+            pltpu.VMEM(vector.shape, jnp.float32),
+            pltpu.VMEM((blocks,) + lower.shape[1:], lower.dtype),
+            pltpu.VMEM((block, wide), jnp.float32),
+            pltpu.SemaphoreType.DMA((1 + blocks,)),
+        ],
+        compiler_params=pltpu.CompilerParams(vmem_limit_bytes=8 << 20),
+    )(vector, lower, pivot)
+
+
 def precondition(vector, last, lower, upper, pivot):
     count = lax.axis_size("line")
     incoming = jnp.zeros((1 if last is None else 2,) + vector.shape[1:], vector.dtype)
@@ -43,7 +95,10 @@
         return -incoming[0] if last is None else incoming[1] - incoming[0]
 
     for turn in range(count - 1):
-        outgoing = sweep_down(vector, lower, pivot, entry())[-1]
+        if last is None and turn == 0:
+            outgoing = first_carry(vector, lower, pivot)
+        else:
+            outgoing = sweep_down(vector, lower, pivot, entry())[-1]
         message = outgoing[None] if last is None else jnp.stack([outgoing, last])
         incoming = incoming + lax.ppermute(message, "line", [(turn, turn + 1)])
     forward = sweep_down(vector, lower, pivot, entry())
@@ -67,37 +122,54 @@
     to_near = jnp.where(is_even, last, first) if several else field
     far = lax.ppermute(to_far, "patch", odd + [(b, a) for a, b in odd])
     near = lax.ppermute(to_near, "patch", even + [(b, a) for a, b in even])
-    before, after = jnp.where(is_even, far, near), jnp.where(is_even, near, far)
     if several:
-        before = jnp.concatenate([before, field[..., :-across]], axis=-1)
-        after = jnp.concatenate([field[..., across:], after], axis=-1)
-    return before, after
-
-
-def pairs_of(count):
-    return [(i, j) for i in range(count) for j in range(i, count)]
-
-
-def gram_kernel(*refs):
-    ins, out = refs[:-1], refs[-1]
-    lane = lax.broadcasted_iota(jnp.int32, (1, 128), 1)
-    total = jnp.zeros((1, 128), jnp.float32)
-    vectors = [ref[...] for ref in ins]
-    for place, (i, j) in enumerate(pairs_of(len(vectors))):
-        part = jnp.sum(vectors[i] * vectors[j], axis=0, keepdims=True)
-        total = jnp.where(lane == place, jnp.sum(part, axis=1, keepdims=True), total)
-    out[...] = jnp.broadcast_to(total, out.shape)
+        up = [jnp.concatenate([field[..., across:], row], axis=-1) for row in (near, far)]
+        down = [jnp.concatenate([row, field[..., :-across]], axis=-1) for row in (near, far)]
+        near = jnp.where(is_even, up[0], down[0])
+        far = jnp.where(is_even, down[1], up[1])
+    return near, far
+
+
+def place_of(pair):
+    low, high = sorted(pair)
+    return high * (high + 1) // 2 + low
+
+
+def gram_kernel(pairs, *refs):
+    *ins, given, out = refs
+    row = lax.broadcasted_iota(jnp.int32, given.shape, 0)
+    sums = given[...]
+    for i, j in pairs:
+        part = jnp.sum(ins[i][...] * ins[j][...], axis=0, keepdims=True)
+        sums = jnp.where(row == place_of((i, j)), part, sums)
+    if out.shape != sums.shape:
+        lane = lax.broadcasted_iota(jnp.int32, sums.shape, 1)
+        whole = jnp.sum(sums, axis=1, keepdims=True)
+        sums = jnp.sum(jnp.where(lane == row, whole, 0.0), axis=0, keepdims=True)
+    out[...] = jnp.broadcast_to(sums, out.shape)
+
+
+def gram_sums(basis, pairs, given, rows):
+    return pl.pallas_call(
+        functools.partial(gram_kernel, pairs),
+        out_shape=jax.ShapeDtypeStruct((rows, given.shape[1]), jnp.float32),
+    )(*basis, given)
 
 
 def finish_kernel(parts_ref, *refs):
     directions, out = refs[:-1], refs[-1]
     width = len(directions)
     total = jnp.sum(parts_ref[...], axis=0, keepdims=True)
-    lane = lax.broadcasted_iota(jnp.int32, total.shape, 1)
+    shape = (SUMS, total.shape[1])
+    row = lax.broadcasted_iota(jnp.int32, shape, 0)
+    lane = lax.broadcasted_iota(jnp.int32, shape, 1)
+    sums = jnp.sum(jnp.where(lane == row, total, 0.0), axis=1, keepdims=True)
+    sums = jnp.broadcast_to(sums, shape)
     gram = {}
-    for place, pair in enumerate(pairs_of(width + 1)):
-        value = jnp.sum(jnp.where(lane == place, total, 0.0), axis=1, keepdims=True)
-        gram[pair] = gram[pair[::-1]] = value
+    for i in range(width + 1):
+        for j in range(width + 1):
+            place = place_of((i, j))
+            gram[i, j] = sums[place : place + 1]
     half = [[gram[j + 1, i] + gram[j, i] for i in range(width + 1)] for j in range(width)]
     normal = [[half[j][i + 1] + half[j][i] for i in range(width)] for j in range(width)]
     right = [half[j][0] for j in range(width)]
@@ -134,6 +206,9 @@
     line = lax.axis_size("line")
     devices = line * lax.axis_size("patch")
     basis = [newton_residual.reshape(count, block, wide)]
+    is_even = lax.axis_index("patch") % 2 == 0
+    near_block = jnp.where(is_even, east, west)
+    far_block = jnp.where(is_even, west, east)
     directions = []
     last = None
     for j in range(ITERS):
@@ -141,7 +216,7 @@
         if below is not None:
             basis[j] = basis[j].at[0].add(single_apply(lower[0], below))
         directions.append(direction)
-        before, after = rows_beside(direction, across)
+        near, far = rows_beside(direction, across)
         last = direction[-1]
         image = coupled - basis[j] + block_apply(diag_block, direction)
         inner = [single_apply(lower[k], direction[k - 1]) for k in range(1, count)]
@@ -151,12 +226,12 @@
         else:
             inner = [jnp.zeros_like(last)] + inner
         image = image + jnp.stack(inner)
-        image = image + block_apply(west, before) + block_apply(east, after)
+        image = (image + block_apply(near_block, near)) + block_apply(far_block, far)
         basis.append(image)
-    sums = pl.pallas_call(
-        gram_kernel,
-        out_shape=jax.ShapeDtypeStruct((devices, 128), jnp.float32),
-    )(*[member.reshape(count * block, wide) for member in basis])
+    flat_basis = [member.reshape(count * block, wide) for member in basis]
+    pairs = [(i, j) for i in range(ITERS) for j in range(i, ITERS)]
+    sums = gram_sums(flat_basis[:-1], pairs, jnp.zeros((SUMS, wide), jnp.float32), SUMS)
+    sums = gram_sums(flat_basis, [(i, ITERS) for i in range(ITERS + 1)], sums, devices)
     sums = lax.all_to_all(sums, ("line", "patch"), 0, 0, tiled=True)
     step = pl.pallas_call(
         finish_kernel,

time: 182 us -> 193 us (1.060)
  other arithmetic: 33.7 us -> 41.4 us
  starting transfers between devices: 43.6 us -> 36.9 us
  blocking collectives: 11.8 us -> 17.5 us
  Pallas kernels: 3.29 us -> 5.78 us
  local copies, waits for them, and re-layouts: 1.89 us -> 4.1 us
    ppermute x4, starting transfers between devices: 13.4 us -> 5.7 us  [rows_beside(): near = lax.ppermute(to_near, 'patch', even + [(b, a) for a, b in even])]
    mul x36, other arithmetic: 0.25 us -> 6.14 us  [single_apply(): return jnp.sum(block_mat.astype(jnp.float32) * vector[None], axis=1)]
    all_to_all x1, blocking collectives: 11.8 us -> 17.5 us  [per_device(): sums = lax.all_to_all(sums, ('line', 'patch'), 0, 0, tiled=True)]
    reduce_sum x123 -> x119, other arithmetic: 25.6 us -> 22.2 us  [single_apply(): return jnp.sum(block_mat.astype(jnp.float32) * vector[None], axis=1)]
    reduce_sum x11, other arithmetic: 5.33 us -> 8.52 us  [block_apply(): return jnp.sum(block_mat.astype(jnp.float32) * vector[:, None], axis=2)]
    pallas_call x1 -> x3, Pallas kernels: 1.63 us -> 4.11 us  [the longest x2 3.13 us: gram_sums(): pl.pallas_call(functools.partial(gram_kernel, pairs), out_shape=jax.Shape...]
    unnamed x44 -> x54, local copies, waits for them, and re-layouts: 1.03 us -> 3.5 us
  transfers between devices with their start and end apart: 33 -> 33, of which waited for: 11 -> 8; matrix products, arithmetic and copies ran while one was open for 2% -> 5% of each run, Pallas kernels for 0% -> 1%
where the time goes in v8:
time: 193 us; the launch traced here: 192 us
  waiting for transfers between devices  83.9 us (43%)
  other arithmetic  41.4 us (21%)
  starting transfers between devices  36.9 us (19%)
  blocking collectives  17.5 us (9%)
  Pallas kernels  5.78 us (3%)
  local copies, waits for them, and re-layouts  4.1 us (2%)
  between operations  2.23 us (1%)
    ppermute x12, waiting for transfers between devices, precondition(): incoming = incoming + lax.ppermute(outgoing, 'line', [(turn + 1, turn)])  77.1 us
    reduce_sum x119, other arithmetic, single_apply(): return jnp.sum(block_mat.astype(jnp.float32) * vector[None], axis=1)  22.2 us
    all_to_all x1, blocking collectives, per_device(): sums = lax.all_to_all(sums, ('line', 'patch'), 0, 0, tiled=True)  17.5 us
    ppermute x12, starting transfers between devices, precondition(): incoming = incoming + lax.ppermute(message, 'line', [(turn, turn + 1)])  15.5 us
    ppermute x12, starting transfers between devices, precondition(): incoming = incoming + lax.ppermute(outgoing, 'line', [(turn + 1, turn)])  10.5 us
    reduce_sum x11, other arithmetic, block_apply(): return jnp.sum(block_mat.astype(jnp.float32) * vector[:, None], axis=2)  8.52 us
    ppermute x12, waiting for transfers between devices, precondition(): incoming = incoming + lax.ppermute(message, 'line', [(turn, turn + 1)])  6.69 us
    mul x36, other arithmetic, single_apply(): return jnp.sum(block_mat.astype(jnp.float32) * vector[None], axis=1)  6.14 us
  transfers between devices with their start and end apart: 33, of which 8 were waited for; matrix products, arithmetic and copies ran while one was open for 5% of the time, Pallas kernels for 1%

profile of v8, /device:TPU:0, one launch (start us, length us, event | category | flops | bytes accessed | tf_op | source)
XLA Modules:
  0.0 191.8 jit_solution(4593955466067112829)
XLA Ops:
  0.0 1.3 copy-done
  1.3 1.3 copy-done.2
  2.5 0.8 copy-done.4
  3.3 1.0 shard_map.73
  4.3 4.8 %collective-permute-start = (f32[1,48,128]{2,1,0:T(8,128)S(1)}, f32[1,48,128]{2,1,0:T(8,128)S(1)}, u32[]{:S(2)}, u32[]{:S(2)}) collective-permute-start(f32[1,48,128]{2,1,0:T(8,128)S(1)} %bitcast.430), channel_id=1, source_target_pairs={{0,8},{1,9},{2,10},{3,11},{4,12},{5,13},{6,14},{7,15}} | collective-permute-start | bytes 73736 | tf_op jit(solution)/shard_map/ppermute | solution.py:103
  9.2 1.5 collective-permute-done
  11.4 0.7 collective-permute-start.1
  13.3 0.7 collective-permute-start.2
  15.2 0.7 collective-permute-start.3
  16.6 0.7 collective-permute-start.4
  18.0 1.3 collective-permute-start.5
  19.3 18.7 %collective-permute-done.5 = f32[48,128]{1,0:T(8,128)S(1)} collective-permute-done((f32[48,128]{1,0:T(8,128)S(1)}, f32[48,128]{1,0:T(8,128)S(1)}, u32[]{:S(2)}, u32[]{:S(2)}) %collective-permute-start.5) | collective-permute-done | bytes 24608 | tf_op jit(solution)/shard_map/ppermute | solution.py:109
  38.0 1.2 fusion.15
  39.9 0.8 collective-permute-start.7
  41.4 1.2 fusion.4
  43.1 1.6 collective-permute-start.8
  44.8 1.7 collective-permute-done.8
  47.2 0.7 collective-permute-start.9
  48.6 0.8 collective-permute-start.10
  50.8 0.7 collective-permute-start.11
  52.2 0.7 collective-permute-start.12
  53.5 1.3 collective-permute-start.13
  54.8 19.5 %collective-permute-done.13 = f32[48,128]{1,0:T(8,128)S(1)} collective-permute-done((f32[48,128]{1,0:T(8,128)S(1)}, f32[48,128]{1,0:T(8,128)S(1)}, u32[]{:S(2)}, u32[]{:S(2)}) %collective-permute-start.13) | collective-permute-done | bytes 24608 | tf_op jit(solution)/shard_map/ppermute | solution.py:109
  75.2 0.7 collective-permute-start.15
  77.9 1.6 collective-permute-start.16
  79.6 1.7 collective-permute-done.16
  82.0 0.7 collective-permute-start.17
  83.4 0.7 collective-permute-start.18
  85.4 0.7 collective-permute-start.19
  86.8 0.7 collective-permute-start.20
  88.2 1.3 collective-permute-start.21
  89.5 19.5 %collective-permute-done.21 = f32[48,128]{1,0:T(8,128)S(1)} collective-permute-done((f32[48,128]{1,0:T(8,128)S(1)}, f32[48,128]{1,0:T(8,128)S(1)}, u32[]{:S(2)}, u32[]{:S(2)}) %collective-permute-start.21) | collective-permute-done | bytes 24608 | tf_op jit(solution)/shard_map/ppermute | solution.py:109
  109.6 2.0 %collective-permute-start.22 = (f32[2,48,128]{2,1,0:T(8,128)S(1)}, f32[2,48,128]{2,1,0:T(8,128)S(1)}, u32[]{:S(2)}, u32[]{:S(2)}) collective-permute-start(f32[2,48,128]{2,1,0:T(8,128)S(1)} %pad_maximum_fusion.11), channel_id=1, source_target_pairs={{0,1},{2,3},{4,5},{6,7},{1,0},{3,2},{5,4},{7,6},{8,9},{10,11},{12,... | collective-permute-start | bytes 147464 | tf_op jit(solution)/shard_map/ppermute | solution.py:124
  111.7 0.9 collective-permute-start.23
  114.7 0.7 fusion.187
  115.8 0.7 fusion.168
  116.7 1.9 %collective-permute-start.24 = (f32[2,48,128]{2,1,0:T(8,128)S(1)}, f32[2,48,128]{2,1,0:T(8,128)S(1)}, u32[]{:S(2)}, u32[]{:S(2)}) collective-permute-start(f32[2,48,128]{2,1,0:T(8,128)S(1)} %pad_maximum_fusion.10), channel_id=1, source_target_pairs={{0,8},{1,9},{2,10},{3,11},{4,12},{5,13},{6,14},{7,15}} | collective-permute-start | bytes 147464 | tf_op jit(solution)/shard_map/ppermute | solution.py:103
  118.6 1.7 collective-permute-done.24
  120.5 0.7 fusion.167
  121.6 0.7 fusion.166
  122.5 0.7 collective-permute-start.25
  123.4 0.7 fusion.165
  124.5 0.7 fusion.164
  125.4 0.7 collective-permute-start.26
  126.3 0.7 fusion.162
  127.4 0.7 fusion.161
  128.6 0.7 collective-permute-start.27
  130.0 0.7 collective-permute-start.28
  131.4 1.3 collective-permute-start.29
  132.7 19.5 %collective-permute-done.29 = f32[48,128]{1,0:T(8,128)S(1)} collective-permute-done((f32[48,128]{1,0:T(8,128)S(1)}, f32[48,128]{1,0:T(8,128)S(1)}, u32[]{:S(2)}, u32[]{:S(2)}) %collective-permute-start.29) | collective-permute-done | bytes 24608 | tf_op jit(solution)/shard_map/ppermute | solution.py:109
  152.5 1.6 collective-permute-start.30
  155.1 3.5 %collective-permute-start.31 = (f32[2,48,128]{2,1,0:T(8,128)}, f32[2,48,128]{2,1,0:T(8,128)}, u32[]{:S(2)}, u32[]{:S(2)}) collective-permute-start(f32[2,48,128]{2,1,0:T(8,128)} %pad_maximum_fusion.12), channel_id=1, source_target_pairs={{0,1},{2,3},{4,5},{6,7},{1,0},{3,2},{5,4},{7,6},{8,9},{10,11},{12,... | collective-permute-start | bytes 147464 | tf_op jit(solution)/shard_map/ppermute | solution.py:124
  158.6 1.3 collective-permute-start.32
  159.9 1.8 fusion.3
  161.7 0.8 fusion.76
  162.5 0.9 fusion.57
  163.4 1.3 fusion.163
  165.4 1.5 shard_map.74.refs_5_
  166.9 1.3 fusion.7
  168.2 1.2 fusion.11
  169.5 1.4 fusion.151
  170.9 1.6 shard_map.75
  172.5 17.5 %all_to_all.11 = f32[32,1,128]{2,1,0:T(1,128)} all-to-all(f32[32,1,128]{2,1,0:T(1,128)} %bitcast.484), channel_id=1, replica_groups=mesh['line'=4,'patch'=8] {'line','patch'}, dimensions={0} | all-to-all | bytes 32768 | tf_op jit(solution)/shard_map/all_to_all | solution.py:235
  190.1 1.7 shard_map.76
  (299 shorter events, 25.2 us)
Async XLA Ops:
  0.0 1.3 copy-start
  1.3 1.3 copy-start.2
  2.5 0.8 copy-start.4
  3.3 5.9 %copy-start.5 = (f32[2,48,1,128]{3,2,1,0:T(1,128)S(1)}, f32[2,48,1,128]{3,2,1,0:T(1,128)}, u32[]{:S(2)}) copy-start(f32[2,48,1,128]{3,2,1,0:T(1,128)} %param.13) | copy-start | bytes 147460
  3.3 7.4 %copy-start.3 = (bf16[2,48,48,1,128]{4,2,3,1,0:T(8,128)(2,1)S(1)}, bf16[2,48,48,1,128]{4,2,3,1,0:T(8,128)(2,1)}, u32[]{:S(2)}) copy-start(bf16[2,48,48,1,128]{4,2,3,1,0:T(8,128)(2,1)} %param.15) | copy-start | bytes 3538948
  3.3 7.5 %copy-start.1 = (bf16[2,48,48,1,128]{4,2,3,1,0:T(8,128)(2,1)S(1)}, bf16[2,48,48,1,128]{4,2,3,1,0:T(8,128)(2,1)}, u32[]{:S(2)}) copy-start(bf16[2,48,48,1,128]{4,2,3,1,0:T(8,128)(2,1)} %param.19) | copy-start | bytes 3538948
  4.3 6.4 %collective-permute-start = (f32[1,48,128]{2,1,0:T(8,128)S(1)}, f32[1,48,128]{2,1,0:T(8,128)S(1)}, u32[]{:S(2)}, u32[]{:S(2)}) collective-permute-start(f32[1,48,128]{2,1,0:T(8,128)S(1)} %bitcast.430), channel_id=1, source_target_pairs={{0,8},{1,9},{2,10},{3,11},{4,12},{5,13},{6,14},{7,15}} | collective-permute-start | bytes 73736 | tf_op jit(solution)/shard_map/ppermute | solution.py:103
  10.9 1.3 copy-start.6
  11.4 0.9 collective-permute-start.1
  13.3 0.7 collective-permute-start.2
  15.2 0.7 collective-permute-start.3
  16.6 0.7 collective-permute-start.4
  18.0 20.0 %collective-permute-start.5 = (f32[48,128]{1,0:T(8,128)S(1)}, f32[48,128]{1,0:T(8,128)S(1)}, u32[]{:S(2)}, u32[]{:S(2)}) collective-permute-start(f32[48,128]{1,0:T(8,128)S(1)} %sub.357), channel_id=1, source_target_pairs={{8,0},{9,1},{10,2},{11,3},{12,4},{13,5},{14,6},{15,7}} | collective-permute-start | bytes 73736 | tf_op jit(solution)/shard_map/ppermute | solution.py:109
  19.3 20.1 %copy-start.7 = (bf16[2,48,48,1,128]{4,2,3,1,0:T(8,128)(2,1)S(1)}, bf16[2,48,48,1,128]{4,2,3,1,0:T(8,128)(2,1)}, u32[]{:S(2)}) copy-start(bf16[2,48,48,1,128]{4,2,3,1,0:T(8,128)(2,1)} %param.16) | copy-start | bytes 3538948
  39.2 1.5 copy-start.12
  39.6 1.7 copy-start.16
  39.8 1.6 copy-start.15
  39.8 2.7 %copy-start.17 = (f32[2,48,128]{2,1,0:T(8,128)}, f32[2,48,128]{2,1,0:T(8,128)S(1)}, u32[]{:S(2)}) copy-start(f32[2,48,128]{2,1,0:T(8,128)S(1)} %pad_maximum_fusion.3) | copy-start | bytes 147460
  39.8 1.5 collective-permute-start.6
  39.9 1.4 collective-permute-start.7
  42.5 70.6 %copy-start.10 = (bf16[2,48,48,1,128]{4,2,3,1,0:T(8,128)(2,1)}, bf16[2,48,48,1,128]{4,2,3,1,0:T(8,128)(2,1)S(1)}, u32[]{:S(2)}) copy-start(bf16[2,48,48,1,128]{4,2,3,1,0:T(8,128)(2,1)S(1)} %get-tuple-element.52) | copy-start | bytes 3538948
  42.5 71.1 %copy-start.8 = (bf16[2,48,48,1,128]{4,2,3,1,0:T(8,128)(2,1)}, bf16[2,48,48,1,128]{4,2,3,1,0:T(8,128)(2,1)S(1)}, u32[]{:S(2)}) copy-start(bf16[2,48,48,1,128]{4,2,3,1,0:T(8,128)(2,1)S(1)} %get-tuple-element.58) | copy-start | bytes 3538948
  43.1 3.4 %collective-permute-start.8 = (f32[2,48,128]{2,1,0:T(8,128)S(1)}, f32[2,48,128]{2,1,0:T(8,128)S(1)}, u32[]{:S(2)}, u32[]{:S(2)}) collective-permute-start(f32[2,48,128]{2,1,0:T(8,128)S(1)} %pad_maximum_fusion.2), channel_id=1, source_target_pairs={{0,8},{1,9},{2,10},{3,11},{4,12},{5,13},{6,14},{7,15}} | collective-permute-start | bytes 147464 | tf_op jit(solution)/shard_map/ppermute | solution.py:103
  47.2 0.7 collective-permute-start.9
  48.6 0.9 collective-permute-start.10
  50.3 27.1 %copy-start.13 = (f32[2,48,128]{2,1,0:T(8,128)}, f32[2,48,128]{2,1,0:T(8,128)S(1)}, u32[]{:S(2)}) copy-start(f32[2,48,128]{2,1,0:T(8,128)S(1)} %get-tuple-element.66) | copy-start | bytes 147460
  50.8 0.7 collective-permute-start.11
  52.2 0.7 collective-permute-start.12
  53.5 20.8 %collective-permute-start.13 = (f32[48,128]{1,0:T(8,128)S(1)}, f32[48,128]{1,0:T(8,128)S(1)}, u32[]{:S(2)}, u32[]{:S(2)}) collective-permute-start(f32[48,128]{1,0:T(8,128)S(1)} %sub.375), channel_id=1, source_target_pairs={{8,0},{9,1},{10,2},{11,3},{12,4},{13,5},{14,6},{15,7}} | collective-permute-start | bytes 73736 | tf_op jit(solution)/shard_map/ppermute | solution.py:109
  75.1 1.8 copy-start.18
  75.1 1.4 collective-permute-start.14
  75.2 1.7 collective-permute-start.15
  77.9 3.4 %collective-permute-start.16 = (f32[2,48,128]{2,1,0:T(8,128)S(1)}, f32[2,48,128]{2,1,0:T(8,128)S(1)}, u32[]{:S(2)}, u32[]{:S(2)}) collective-permute-start(f32[2,48,128]{2,1,0:T(8,128)S(1)} %pad_maximum_fusion.6), channel_id=1, source_target_pairs={{0,8},{1,9},{2,10},{3,11},{4,12},{5,13},{6,14},{7,15}} | collective-permute-start | bytes 147464 | tf_op jit(solution)/shard_map/ppermute | solution.py:103
  82.0 0.7 collective-permute-start.17
  83.4 0.7 collective-permute-start.18
  84.9 29.2 %copy-start.14 = (f32[2,48,128]{2,1,0:T(8,128)}, f32[2,48,128]{2,1,0:T(8,128)S(1)}, u32[]{:S(2)}) copy-start(f32[2,48,128]{2,1,0:T(8,128)S(1)} %get-tuple-element.62) | copy-start | bytes 147460
  85.4 0.7 collective-permute-start.19
  86.8 0.7 collective-permute-start.20
  88.2 20.8 %collective-permute-start.21 = (f32[48,128]{1,0:T(8,128)S(1)}, f32[48,128]{1,0:T(8,128)S(1)}, u32[]{:S(2)}, u32[]{:S(2)}) collective-permute-start(f32[48,128]{1,0:T(8,128)S(1)} %sub.393), channel_id=1, source_target_pairs={{8,0},{9,1},{10,2},{11,3},{12,4},{13,5},{14,6},{15,7}} | collective-permute-start | bytes 73736 | tf_op jit(solution)/shard_map/ppermute | solution.py:109
  109.6 4.0 %copy-start.19 = (f32[2,48,128]{2,1,0:T(8,128)}, f32[2,48,128]{2,1,0:T(8,128)S(1)}, u32[]{:S(2)}) copy-start(f32[2,48,128]{2,1,0:T(8,128)S(1)} %pad_maximum_fusion.11) | copy-start | bytes 147460
  109.6 3.5 %collective-permute-start.22 = (f32[2,48,128]{2,1,0:T(8,128)S(1)}, f32[2,48,128]{2,1,0:T(8,128)S(1)}, u32[]{:S(2)}, u32[]{:S(2)}) collective-permute-start(f32[2,48,128]{2,1,0:T(8,128)S(1)} %pad_maximum_fusion.11), channel_id=1, source_target_pairs={{0,1},{2,3},{4,5},{6,7},{1,0},{3,2},{5,4},{7,6},{8,9},{10,11},{12,... | collective-permute-start | bytes 147464 | tf_op jit(solution)/shard_map/ppermute | solution.py:124
  111.7 2.0 %collective-permute-start.23 = (f32[2,48,128]{2,1,0:T(8,128)S(1)}, f32[2,48,128]{2,1,0:T(8,128)S(1)}, u32[]{:S(2)}, u32[]{:S(2)}) collective-permute-start(f32[2,48,128]{2,1,0:T(8,128)S(1)} %pad_maximum_fusion.11), channel_id=1, source_target_pairs={{1,2},{3,4},{5,6},{2,1},{4,3},{6,5},{9,10},{11,12},{13,14},{10,9},... | collective-permute-start | bytes 147464 | tf_op jit(solution)/shard_map/ppermute | solution.py:123
  116.7 3.7 %collective-permute-start.24 = (f32[2,48,128]{2,1,0:T(8,128)S(1)}, f32[2,48,128]{2,1,0:T(8,128)S(1)}, u32[]{:S(2)}, u32[]{:S(2)}) collective-permute-start(f32[2,48,128]{2,1,0:T(8,128)S(1)} %pad_maximum_fusion.10), channel_id=1, source_target_pairs={{0,8},{1,9},{2,10},{3,11},{4,12},{5,13},{6,14},{7,15}} | collective-permute-start | bytes 147464 | tf_op jit(solution)/shard_map/ppermute | solution.py:103
  122.5 0.7 collective-permute-start.25
  125.4 0.7 collective-permute-start.26
  128.6 0.7 collective-permute-start.27
  130.0 0.7 collective-permute-start.28
  131.4 20.8 %collective-permute-start.29 = (f32[48,128]{1,0:T(8,128)S(1)}, f32[48,128]{1,0:T(8,128)S(1)}, u32[]{:S(2)}, u32[]{:S(2)}) collective-permute-start(f32[48,128]{1,0:T(8,128)S(1)} %sub.411), channel_id=1, source_target_pairs={{8,0},{9,1},{10,2},{11,3},{12,4},{13,5},{14,6},{15,7}} | collective-permute-start | bytes 73736 | tf_op jit(solution)/shard_map/ppermute | solution.py:109
  152.3 9.4 %copy-start.20 = (f32[48,128]{1,0:T(8,128)}, f32[48,128]{1,0:T(8,128)S(1)}, u32[]{:S(2)}) copy-start(f32[48,128]{1,0:T(8,128)S(1)} %fusion.24) | copy-start | bytes 73732
  152.5 10.0 %collective-permute-start.30 = (f32[48,128]{1,0:T(8,128)S(1)}, f32[48,128]{1,0:T(8,128)S(1)}, u32[]{:S(2)}, u32[]{:S(2)}) collective-permute-start(f32[48,128]{1,0:T(8,128)S(1)} %sub.412), channel_id=1, source_target_pairs={{0,8},{8,16},{16,24},{1,9},{9,17},{17,25},{2,10},{10,18},{18,26},{... | collective-permute-start | bytes 73736 | tf_op jit(solution)/shard_map/ppermute | solution.py:224
  154.3 8.2 %copy-start.22 = (f32[48,128]{1,0:T(8,128)}, f32[48,128]{1,0:T(8,128)S(1)}, u32[]{:S(2)}) copy-start(f32[48,128]{1,0:T(8,128)S(1)} %fusion.40) | copy-start | bytes 73732
  155.1 11.8 %copy-start.11 = (bf16[2,48,48,1,128]{4,2,3,1,0:T(8,128)(2,1)S(1)}, bf16[2,48,48,1,128]{4,2,3,1,0:T(8,128)(2,1)}, u32[]{:S(2)}) copy-start(bf16[2,48,48,1,128]{4,2,3,1,0:T(8,128)(2,1)} %copy-done.10) | copy-start | bytes 3538948
  155.1 11.8 %collective-permute-start.31 = (f32[2,48,128]{2,1,0:T(8,128)}, f32[2,48,128]{2,1,0:T(8,128)}, u32[]{:S(2)}, u32[]{:S(2)}) collective-permute-start(f32[2,48,128]{2,1,0:T(8,128)} %pad_maximum_fusion.12), channel_id=1, source_target_pairs={{0,1},{2,3},{4,5},{6,7},{1,0},{3,2},{5,4},{7,6},{8,9},{10,11},{12,... | collective-permute-start | bytes 147464 | tf_op jit(solution)/shard_map/ppermute | solution.py:124
  158.6 9.6 %collective-permute-start.32 = (f32[2,48,128]{2,1,0:T(8,128)}, f32[2,48,128]{2,1,0:T(8,128)}, u32[]{:S(2)}, u32[]{:S(2)}) collective-permute-start(f32[2,48,128]{2,1,0:T(8,128)} %pad_maximum_fusion.12), channel_id=1, source_target_pairs={{1,2},{3,4},{5,6},{2,1},{4,3},{6,5},{9,10},{11,12},{13,14},{10,9},... | collective-permute-start | bytes 147464 | tf_op jit(solution)/shard_map/ppermute | solution.py:123
  162.5 5.7 %copy-start.9 = (bf16[2,48,48,1,128]{4,2,3,1,0:T(8,128)(2,1)S(1)}, bf16[2,48,48,1,128]{4,2,3,1,0:T(8,128)(2,1)}, u32[]{:S(2)}) copy-start(bf16[2,48,48,1,128]{4,2,3,1,0:T(8,128)(2,1)} %copy-done.8) | copy-start | bytes 3538948
  166.9 2.6 %copy-start.21 = (f32[48,128]{1,0:T(8,128)S(1)}, f32[48,128]{1,0:T(8,128)}, u32[]{:S(2)}) copy-start(f32[48,128]{1,0:T(8,128)} %copy-done.20) | copy-start | bytes 73732
  166.9 2.6 %copy-start.23 = (f32[48,128]{1,0:T(8,128)S(1)}, f32[48,128]{1,0:T(8,128)}, u32[]{:S(2)}) copy-start(f32[48,128]{1,0:T(8,128)} %copy-done.22) | copy-start | bytes 73732
  166.9 2.6 %copy-start.24 = (f32[2,48,128]{2,1,0:T(8,128)S(1)}, f32[2,48,128]{2,1,0:T(8,128)}, u32[]{:S(2)}) copy-start(f32[2,48,128]{2,1,0:T(8,128)} %fusion.3) | copy-start | bytes 147460
  166.9 2.6 %copy-start.25 = (f32[48,128]{1,0:T(8,128)S(1)}, f32[48,128]{1,0:T(8,128)}, u32[]{:S(2)}) copy-start(f32[48,128]{1,0:T(8,128)} %fusion.76) | copy-start | bytes 73732
  166.9 2.6 %copy-start.26 = (f32[48,128]{1,0:T(8,128)S(1)}, f32[48,128]{1,0:T(8,128)}, u32[]{:S(2)}) copy-start(f32[48,128]{1,0:T(8,128)} %get-tuple-element.41) | copy-start | bytes 73732

commit v9 on v8

--- a/solution.py
+++ b/solution.py
@@ -38,56 +38,90 @@
     return result, coupled
 
 
-def first_kernel(vector, lower, pivot, out, field, held, middle, sems):
-    count, block = vector.shape[:2]
-    blocks = [pivot.at[0]]
-    for k in range(1, count):
-        blocks += [lower.at[k], pivot.at[k]]
-    copies = [pltpu.make_async_copy(vector, field, sems.at[0])]
-    for place, source in enumerate(blocks):
-        copies.append(pltpu.make_async_copy(source, held.at[place], sems.at[1 + place]))
+ROOM = 56 << 20
+
+
+def start_all(pairs, sems):
+    copies = [
+        pltpu.make_async_copy(source, target, sems.at[place])
+        for place, (source, target) in enumerate(pairs)
+    ]
     for copy in copies:
         copy.start()
+    return copies
+
+
+def apply_into(block_mat, value, target):
+    block = target.shape[0]
     rows = 16 if block % 16 == 0 else block
-
-    def apply(place, value, target):
-        for start in range(0, block, rows):
-            part = held[place, start : start + rows].astype(jnp.float32)
-            target[start : start + rows] = jnp.sum(part * value[None], axis=1)
-
+    for start in range(0, block, rows):
+        part = block_mat[start : start + rows].astype(jnp.float32)
+        target[start : start + rows] = jnp.sum(part * value[None], axis=1)
+
+
+def first_kernel(vector, lower, pivot, lower_held, pivot_held, out, field, middle, sems):
+    count = vector.shape[0]
+    pairs = [(vector, field), (pivot.at[0], pivot_held.at[0])]
+    for k in range(1, count):
+        pairs += [(lower.at[k], lower_held.at[k]), (pivot.at[k], pivot_held.at[k])]
+    pairs.append((lower.at[0], lower_held.at[0]))
+    copies = start_all(pairs, sems)
     copies[0].wait()
     copies[1].wait()
-    apply(0, field[0], middle)
+    apply_into(pivot_held.at[0], field[0], out)
     for k in range(1, count):
         copies[2 * k].wait()
-        apply(2 * k - 1, middle[...], out)
-        value = field[k] - out[...]
+        apply_into(lower_held.at[k], out[...], middle)
         copies[2 * k + 1].wait()
-        apply(2 * k, value, out)
-        if k < count - 1:
-            middle[...] = out[...]
-    if count == 1:
-        out[...] = middle[...]
+        apply_into(pivot_held.at[k], field[k] - middle[...], out)
+    copies[-1].wait()
 
 
 def first_carry(vector, lower, pivot):
     count, block, wide = vector.shape
-    blocks = 2 * count - 1
+    vmem = pl.BlockSpec(memory_space=pltpu.VMEM)
     return pl.pallas_call(
         first_kernel,
-        out_shape=jax.ShapeDtypeStruct((block, wide), jnp.float32),
-        in_specs=[pl.BlockSpec(memory_space=pl.ANY)] * 3,
+        out_shape=[
+            pltpu.VMEM(lower.shape, lower.dtype),
+            pltpu.VMEM(pivot.shape, pivot.dtype),
+            pltpu.VMEM((block, wide), jnp.float32),
+        ],
+        in_specs=[pl.BlockSpec(memory_space=pltpu.HBM)] * 3,
+        out_specs=[vmem] * 3,
         scratch_shapes=[
             pltpu.VMEM(vector.shape, jnp.float32),
-            pltpu.VMEM((blocks,) + lower.shape[1:], lower.dtype),
             pltpu.VMEM((block, wide), jnp.float32),
-            pltpu.SemaphoreType.DMA((1 + blocks,)),
+            pltpu.SemaphoreType.DMA((1 + 2 * count,)),
         ],
-        compiler_params=pltpu.CompilerParams(vmem_limit_bytes=8 << 20),
+        compiler_params=pltpu.CompilerParams(vmem_limit_bytes=ROOM),
     )(vector, lower, pivot)
 
 
-def precondition(vector, last, lower, upper, pivot):
+def hold_kernel(upper, diag_block, west, east, after, upper_held, diag_held, near, far, sems):
+    even = lax.axis_index("patch") % 2 == 0
+
+    def run(first, second):
+        pairs = [(upper, upper_held), (diag_block, diag_held), (first, near), (second, far)]
+        for copy in start_all(pairs, sems):
+            copy.wait()
+
+    pl.when(even)(lambda: run(east, west))
+    pl.when(jnp.logical_not(even))(lambda: run(west, east))
+
+
+def hold(upper, diag_block, west, east, after):
+    return pl.pallas_call(
+        hold_kernel,
+        out_shape=[pltpu.VMEM(upper.shape, upper.dtype)] * 4,
+        in_specs=[pl.BlockSpec(memory_space=pltpu.HBM)] * 4 + [pl.BlockSpec(memory_space=pl.ANY)],
+        out_specs=[pl.BlockSpec(memory_space=pltpu.VMEM)] * 4,
+        scratch_shapes=[pltpu.SemaphoreType.DMA((4,))],
+        compiler_params=pltpu.CompilerParams(vmem_limit_bytes=ROOM),
+    )(upper, diag_block, west, east, after)
+
+
+def precondition(vector, last, lower, upper, pivot, carry=None):
     count = lax.axis_size("line")
     incoming = jnp.zeros((1 if last is None else 2,) + vector.shape[1:], vector.dtype)
 
@@ -95,8 +129,8 @@
         return -incoming[0] if last is None else incoming[1] - incoming[0]
 
     for turn in range(count - 1):
-        if last is None and turn == 0:
-            outgoing = first_carry(vector, lower, pivot)
+        if carry is not None and turn == 0:
+            outgoing = carry
         else:
             outgoing = sweep_down(vector, lower, pivot, entry())[-1]
         message = outgoing[None] if last is None else jnp.stack([outgoing, last])
@@ -206,13 +240,14 @@
     line = lax.axis_size("line")
     devices = line * lax.axis_size("patch")
     basis = [newton_residual.reshape(count, block, wide)]
-    is_even = lax.axis_index("patch") % 2 == 0
-    near_block = jnp.where(is_even, east, west)
-    far_block = jnp.where(is_even, west, east)
+    lower, pivot, carry = first_carry(basis[0], lower, pivot)
+    upper, diag_block, near_block, far_block = hold(upper, diag_block, west, east, carry)
     directions = []
     last = None
     for j in range(ITERS):
-        direction, coupled, below = precondition(basis[j], last, lower, upper, pivot)
+        direction, coupled, below = precondition(
+            basis[j], last, lower, upper, pivot, carry if j == 0 else None
+        )
         if below is not None:
             basis[j] = basis[j].at[0].add(single_apply(lower[0], below))
         directions.append(direction)

time: 193 us -> 177 us (0.917)
  other arithmetic: 41.4 us -> 28 us
  blocking collectives: 17.5 us -> 10.2 us
  starting transfers between devices: 36.9 us -> 43.9 us
  local copies, waits for them, and re-layouts: 4.1 us -> 0.68 us
  Pallas kernels: 5.78 us -> 8.84 us
    ppermute x4, starting transfers between devices: 5.7 us -> 13.7 us  [rows_beside(): near = lax.ppermute(to_near, 'patch', even + [(b, a) for a, b in even])]
    all_to_all x1, blocking collectives: 17.5 us -> 10.2 us  [per_device(): sums = lax.all_to_all(sums, ('line', 'patch'), 0, 0, tiled=True)]
    mul x36, other arithmetic: 6.14 us -> 0.22 us  [single_apply(): return jnp.sum(block_mat.astype(jnp.float32) * vector[None], axis=1)]
    unnamed x54 -> x30, local copies, waits for them, and re-layouts: 3.5 us -> 0.07 us
    pallas_call x1 -> x2, Pallas kernels: 0.99 us -> 4.06 us  [the longest x1 2.39 us: hold(): pl.pallas_call(hold_kernel, out_shape=[pltpu.VMEM(upper.shape, upper.dtyp...]
    reduce_sum x11 -> x12, other arithmetic: 8.52 us -> 6.4 us  [block_apply(): return jnp.sum(block_mat.astype(jnp.float32) * vector[:, None], axis=2)]
    reduce_sum x119 -> x118, other arithmetic: 22.2 us -> 20.3 us  [single_apply(): return jnp.sum(block_mat.astype(jnp.float32) * vector[None], axis=1)]
  transfers between devices with their start and end apart: 33 -> 33, of which waited for: 8 -> 7; matrix products, arithmetic and copies ran while one was open for 5% -> 4% of each run, Pallas kernels for 1% -> 2%
where the time goes in v9:
time: 177 us; the launch traced here: 176 us
  waiting for transfers between devices  82.1 us (46%)
  starting transfers between devices  43.9 us (25%)
  other arithmetic  28 us (16%)
  blocking collectives  10.2 us (6%)
  Pallas kernels  8.84 us (5%)
  between operations  2.29 us (1%)
    ppermute x12, waiting for transfers between devices, precondition(): incoming = incoming + lax.ppermute(outgoing, 'line', [(turn + 1, turn)])  76.4 us
    reduce_sum x118, other arithmetic, single_apply(): return jnp.sum(block_mat.astype(jnp.float32) * vector[None], axis=1)  20.3 us
    ppermute x12, starting transfers between devices, precondition(): incoming = incoming + lax.ppermute(message, 'line', [(turn, turn + 1)])  15 us
    ppermute x4, starting transfers between devices, rows_beside(): near = lax.ppermute(to_near, 'patch', even + [(b, a) for a, b in even])  13.7 us
    ppermute x12, starting transfers between devices, precondition(): incoming = incoming + lax.ppermute(outgoing, 'line', [(turn + 1, turn)])  10.7 us
    all_to_all x1, blocking collectives, per_device(): sums = lax.all_to_all(sums, ('line', 'patch'), 0, 0, tiled=True)  10.2 us
    reduce_sum x12, other arithmetic, block_apply(): return jnp.sum(block_mat.astype(jnp.float32) * vector[:, None], axis=2)  6.4 us
    ppermute x12, waiting for transfers between devices, precondition(): incoming = incoming + lax.ppermute(message, 'line', [(turn, turn + 1)])  5.68 us
  transfers between devices with their start and end apart: 33, of which 7 were waited for; matrix products, arithmetic and copies ran while one was open for 4% of the time, Pallas kernels for 2%

profile of v9, /device:TPU:0, one launch (start us, length us, event | category | flops | bytes accessed | tf_op | source)
XLA Modules:
  0.0 176.1 jit_solution(7236718272186888020)
XLA Ops:
  0.0 1.7 shard_map.73
  1.7 4.8 %collective-permute-start = (f32[1,48,128]{2,1,0:T(8,128)S(1)}, f32[1,48,128]{2,1,0:T(8,128)S(1)}, u32[]{:S(2)}, u32[]{:S(2)}) collective-permute-start(f32[1,48,128]{2,1,0:T(8,128)S(1)} %bitcast.378), channel_id=1, source_target_pairs={{0,8},{1,9},{2,10},{3,11},{4,12},{5,13},{6,14},{7,15}} | collective-permute-start | bytes 73736 | tf_op jit(solution)/shard_map/ppermute | solution.py:137
  6.6 2.4 %shard_map.74 = (bf16[2,48,48,128]{3,2,1,0:T(8,128)(2,1)S(1)}, bf16[2,48,48,128]{3,2,1,0:T(8,128)(2,1)S(1)}, bf16[2,48,48,128]{3,2,1,0:T(8,128)(2,1)S(1)}, bf16[2,48,48,128]{3,2,1,0:T(8,128)(2,1)S(1)}) custom-call(bf16[2,48,48,128]{3,2,1,0:T(8,128)(2,1)} %bitcast.391, bf16[2,48,48,128]{3,2,1,0:T(8,128)(2,1)} %bitcast.392, ...), custom_call_target="tpu_custom_call" | custom-call | tf_op jit(solution)/shard_map/pallas_call | solution.py:114
  9.7 0.7 collective-permute-start.1
  10.7 0.4 fusion.80
  11.8 0.7 collective-permute-start.2
  13.5 0.7 collective-permute-start.3
  14.9 0.7 collective-permute-start.4
  16.3 1.3 collective-permute-start.5
  17.6 17.8 %collective-permute-done.5 = f32[48,128]{1,0:T(8,128)S(1)} collective-permute-done((f32[48,128]{1,0:T(8,128)S(1)}, f32[48,128]{1,0:T(8,128)S(1)}, u32[]{:S(2)}, u32[]{:S(2)}) %collective-permute-start.5) | collective-permute-done | bytes 24608 | tf_op jit(solution)/shard_map/ppermute | solution.py:143
  36.1 0.7 collective-permute-start.7
  36.8 3.0 %collective-permute-start.6 = (f32[2,48,128]{2,1,0:T(8,128)S(1)}, f32[2,48,128]{2,1,0:T(8,128)S(1)}, u32[]{:S(2)}, u32[]{:S(2)}) collective-permute-start(f32[2,48,128]{2,1,0:T(8,128)S(1)} %pad_maximum_fusion.3), channel_id=1, source_target_pairs={{0,1},{2,3},{4,5},{6,7},{1,0},{3,2},{5,4},{7,6},{8,9},{10,11},{12,... | collective-permute-start | bytes 147464 | tf_op jit(solution)/shard_map/ppermute | solution.py:158
  39.8 0.4 fusion
  40.4 0.4 fusion.8
  40.8 0.4 fusion.4
  41.8 1.6 collective-permute-start.8
  43.5 2.0 %collective-permute-done.8 = f32[2,48,128]{2,1,0:T(8,128)S(1)} collective-permute-done((f32[2,48,128]{2,1,0:T(8,128)S(1)}, f32[2,48,128]{2,1,0:T(8,128)S(1)}, u32[]{:S(2)}, u32[]{:S(2)}) %collective-permute-start.8) | collective-permute-done | bytes 49184 | tf_op jit(solution)/shard_map/ppermute | solution.py:137
  46.2 0.7 collective-permute-start.9
  47.6 0.7 collective-permute-start.10
  49.3 0.8 collective-permute-start.11
  50.9 0.7 collective-permute-start.12
  52.3 1.3 collective-permute-start.13
  53.6 19.4 %collective-permute-done.13 = f32[48,128]{1,0:T(8,128)S(1)} collective-permute-done((f32[48,128]{1,0:T(8,128)S(1)}, f32[48,128]{1,0:T(8,128)S(1)}, u32[]{:S(2)}, u32[]{:S(2)}) %collective-permute-start.13) | collective-permute-done | bytes 24608 | tf_op jit(solution)/shard_map/ppermute | solution.py:143
  73.7 0.7 collective-permute-start.15
  74.4 3.7 %collective-permute-start.14 = (f32[2,48,128]{2,1,0:T(8,128)S(1)}, f32[2,48,128]{2,1,0:T(8,128)S(1)}, u32[]{:S(2)}, u32[]{:S(2)}) collective-permute-start(f32[2,48,128]{2,1,0:T(8,128)S(1)} %pad_maximum_fusion.7), channel_id=1, source_target_pairs={{0,1},{2,3},{4,5},{6,7},{1,0},{3,2},{5,4},{7,6},{8,9},{10,11},{12,... | collective-permute-start | bytes 147464 | tf_op jit(solution)/shard_map/ppermute | solution.py:158
  78.1 0.4 fusion.66
  78.6 0.4 fusion.1
  79.0 0.4 fusion.9
  79.5 0.4 fusion.5
  80.5 1.6 collective-permute-start.16
  82.1 1.9 %collective-permute-done.16 = f32[2,48,128]{2,1,0:T(8,128)S(1)} collective-permute-done((f32[2,48,128]{2,1,0:T(8,128)S(1)}, f32[2,48,128]{2,1,0:T(8,128)S(1)}, u32[]{:S(2)}, u32[]{:S(2)}) %collective-permute-start.16) | collective-permute-done | bytes 49184 | tf_op jit(solution)/shard_map/ppermute | solution.py:137
  84.7 0.7 collective-permute-start.17
  86.1 0.7 collective-permute-start.18
  87.9 0.7 collective-permute-start.19
  89.3 0.7 collective-permute-start.20
  90.7 1.3 collective-permute-start.21
  92.0 19.6 %collective-permute-done.21 = f32[48,128]{1,0:T(8,128)S(1)} collective-permute-done((f32[48,128]{1,0:T(8,128)S(1)}, f32[48,128]{1,0:T(8,128)S(1)}, u32[]{:S(2)}, u32[]{:S(2)}) %collective-permute-start.21) | collective-permute-done | bytes 24608 | tf_op jit(solution)/shard_map/ppermute | solution.py:143
  112.3 0.9 collective-permute-start.23
  113.2 3.5 %collective-permute-start.22 = (f32[2,48,128]{2,1,0:T(8,128)S(1)}, f32[2,48,128]{2,1,0:T(8,128)S(1)}, u32[]{:S(2)}, u32[]{:S(2)}) collective-permute-start(f32[2,48,128]{2,1,0:T(8,128)S(1)} %pad_maximum_fusion.11), channel_id=1, source_target_pairs={{0,1},{2,3},{4,5},{6,7},{1,0},{3,2},{5,4},{7,6},{8,9},{10,11},{12,... | collective-permute-start | bytes 147464 | tf_op jit(solution)/shard_map/ppermute | solution.py:158
  116.7 0.4 fusion.71
  117.1 0.4 fusion.2
  117.6 0.4 fusion.10
  118.0 0.4 fusion.6
  119.0 1.6 collective-permute-start.24
  120.6 1.7 collective-permute-done.24
  123.1 0.7 collective-permute-start.25
  124.5 0.7 collective-permute-start.26
  126.3 0.7 collective-permute-start.27
  127.6 0.7 collective-permute-start.28
  129.0 1.3 collective-permute-start.29
  130.3 19.6 %collective-permute-done.29 = f32[48,128]{1,0:T(8,128)S(1)} collective-permute-done((f32[48,128]{1,0:T(8,128)S(1)}, f32[48,128]{1,0:T(8,128)S(1)}, u32[]{:S(2)}, u32[]{:S(2)}) %collective-permute-start.29) | collective-permute-done | bytes 24608 | tf_op jit(solution)/shard_map/ppermute | solution.py:143
  150.3 1.6 collective-permute-start.30
  152.3 0.7 collective-permute-start.32
  152.9 3.5 %collective-permute-start.31 = (f32[2,48,128]{2,1,0:T(8,128)S(1)}, f32[2,48,128]{2,1,0:T(8,128)S(1)}, u32[]{:S(2)}, u32[]{:S(2)}) collective-permute-start(f32[2,48,128]{2,1,0:T(8,128)S(1)} %pad_maximum_fusion.12), channel_id=1, source_target_pairs={{0,1},{2,3},{4,5},{6,7},{1,0},{3,2},{5,4},{7,6},{8,9},{10,11},{12,... | collective-permute-start | bytes 147464 | tf_op jit(solution)/shard_map/ppermute | solution.py:158
  156.4 0.4 fusion.3
  156.9 0.7 fusion.57
  157.6 0.6 broadcast_in_dim.23.refs_4_
  158.2 1.5 shard_map.75.refs_5_
  159.7 1.7 fusion.11
  161.5 0.4 fusion.7
  161.9 0.6 fusion.151
  162.6 1.6 shard_map.76
  164.2 10.2 %all_to_all.11 = f32[32,1,128]{2,1,0:T(1,128)} all-to-all(f32[32,1,128]{2,1,0:T(1,128)} %bitcast.445), channel_id=1, replica_groups=mesh['line'=4,'patch'=8] {'line','patch'}, dimensions={0} | all-to-all | bytes 32768 | tf_op jit(solution)/shard_map/all_to_all | solution.py:270
  174.4 1.7 shard_map.77
  (278 shorter events, 19.2 us)
Async XLA Ops:
  0.0 6.5 %copy-start.6 = (f32[2,48,1,128]{3,2,1,0:T(1,128)S(1)}, f32[2,48,1,128]{3,2,1,0:T(1,128)}, u32[]{:S(2)}) copy-start(f32[2,48,1,128]{3,2,1,0:T(1,128)} %param.13) | copy-start | bytes 147460
  1.7 4.9 %copy-start.1 = (f32[48,128]{1,0:T(8,128)}, f32[48,128]{1,0:T(8,128)S(1)}, u32[]{:S(2)}) copy-start(f32[48,128]{1,0:T(8,128)S(1)} %get-tuple-element.48.after) | copy-start | bytes 73732
  1.7 7.3 %collective-permute-start = (f32[1,48,128]{2,1,0:T(8,128)S(1)}, f32[1,48,128]{2,1,0:T(8,128)S(1)}, u32[]{:S(2)}, u32[]{:S(2)}) collective-permute-start(f32[1,48,128]{2,1,0:T(8,128)S(1)} %bitcast.378), channel_id=1, source_target_pairs={{0,8},{1,9},{2,10},{3,11},{4,12},{5,13},{6,14},{7,15}} | collective-permute-start | bytes 73736 | tf_op jit(solution)/shard_map/ppermute | solution.py:137
  9.0 108.6 %copy-start = (bf16[2,48,48,128]{3,2,1,0:T(8,128)(2,1)}, bf16[2,48,48,128]{3,2,1,0:T(8,128)(2,1)S(1)}, u32[]{:S(2)}) copy-start(bf16[2,48,48,128]{3,2,1,0:T(8,128)(2,1)S(1)} %get-tuple-element.54) | copy-start | bytes 3538948
  9.7 0.8 collective-permute-start.1
  11.8 0.7 collective-permute-start.2
  13.5 0.7 collective-permute-start.3
  14.9 0.7 collective-permute-start.4
  16.3 19.1 %collective-permute-start.5 = (f32[48,128]{1,0:T(8,128)S(1)}, f32[48,128]{1,0:T(8,128)S(1)}, u32[]{:S(2)}, u32[]{:S(2)}) collective-permute-start(f32[48,128]{1,0:T(8,128)S(1)} %sub.357), channel_id=1, source_target_pairs={{8,0},{9,1},{10,2},{11,3},{12,4},{13,5},{14,6},{15,7}} | collective-permute-start | bytes 73736 | tf_op jit(solution)/shard_map/ppermute | solution.py:143
  36.1 4.7 %copy-start.7 = (f32[2,48,128]{2,1,0:T(8,128)}, f32[2,48,128]{2,1,0:T(8,128)S(1)}, u32[]{:S(2)}) copy-start(f32[2,48,128]{2,1,0:T(8,128)S(1)} %pad_maximum_fusion.3) | copy-start | bytes 147460
  36.1 4.3 %collective-permute-start.7 = (f32[2,48,128]{2,1,0:T(8,128)S(1)}, f32[2,48,128]{2,1,0:T(8,128)S(1)}, u32[]{:S(2)}, u32[]{:S(2)}) collective-permute-start(f32[2,48,128]{2,1,0:T(8,128)S(1)} %pad_maximum_fusion.3), channel_id=1, source_target_pairs={{1,2},{3,4},{5,6},{2,1},{4,3},{6,5},{9,10},{11,12},{13,14},{10,9},... | collective-permute-start | bytes 147464 | tf_op jit(solution)/shard_map/ppermute | solution.py:157
  36.8 4.0 %collective-permute-start.6 = (f32[2,48,128]{2,1,0:T(8,128)S(1)}, f32[2,48,128]{2,1,0:T(8,128)S(1)}, u32[]{:S(2)}, u32[]{:S(2)}) collective-permute-start(f32[2,48,128]{2,1,0:T(8,128)S(1)} %pad_maximum_fusion.3), channel_id=1, source_target_pairs={{0,1},{2,3},{4,5},{6,7},{1,0},{3,2},{5,4},{7,6},{8,9},{10,11},{12,... | collective-permute-start | bytes 147464 | tf_op jit(solution)/shard_map/ppermute | solution.py:158
  41.8 3.6 %collective-permute-start.8 = (f32[2,48,128]{2,1,0:T(8,128)S(1)}, f32[2,48,128]{2,1,0:T(8,128)S(1)}, u32[]{:S(2)}, u32[]{:S(2)}) collective-permute-start(f32[2,48,128]{2,1,0:T(8,128)S(1)} %pad_maximum_fusion.2), channel_id=1, source_target_pairs={{0,8},{1,9},{2,10},{3,11},{4,12},{5,13},{6,14},{7,15}} | collective-permute-start | bytes 147464 | tf_op jit(solution)/shard_map/ppermute | solution.py:137
  46.2 0.7 collective-permute-start.9
  47.6 0.7 collective-permute-start.10
  49.3 0.9 collective-permute-start.11
  50.9 0.7 collective-permute-start.12
  52.3 20.7 %collective-permute-start.13 = (f32[48,128]{1,0:T(8,128)S(1)}, f32[48,128]{1,0:T(8,128)S(1)}, u32[]{:S(2)}, u32[]{:S(2)}) collective-permute-start(f32[48,128]{1,0:T(8,128)S(1)} %sub.375), channel_id=1, source_target_pairs={{8,0},{9,1},{10,2},{11,3},{12,4},{13,5},{14,6},{15,7}} | collective-permute-start | bytes 73736 | tf_op jit(solution)/shard_map/ppermute | solution.py:143
  73.7 5.3 %copy-start.8 = (f32[2,48,128]{2,1,0:T(8,128)}, f32[2,48,128]{2,1,0:T(8,128)S(1)}, u32[]{:S(2)}) copy-start(f32[2,48,128]{2,1,0:T(8,128)S(1)} %pad_maximum_fusion.7) | copy-start | bytes 147460
  73.7 5.3 %collective-permute-start.15 = (f32[2,48,128]{2,1,0:T(8,128)S(1)}, f32[2,48,128]{2,1,0:T(8,128)S(1)}, u32[]{:S(2)}, u32[]{:S(2)}) collective-permute-start(f32[2,48,128]{2,1,0:T(8,128)S(1)} %pad_maximum_fusion.7), channel_id=1, source_target_pairs={{1,2},{3,4},{5,6},{2,1},{4,3},{6,5},{9,10},{11,12},{13,14},{10,9},... | collective-permute-start | bytes 147464 | tf_op jit(solution)/shard_map/ppermute | solution.py:157
  74.4 5.1 %collective-permute-start.14 = (f32[2,48,128]{2,1,0:T(8,128)S(1)}, f32[2,48,128]{2,1,0:T(8,128)S(1)}, u32[]{:S(2)}, u32[]{:S(2)}) collective-permute-start(f32[2,48,128]{2,1,0:T(8,128)S(1)} %pad_maximum_fusion.7), channel_id=1, source_target_pairs={{0,1},{2,3},{4,5},{6,7},{1,0},{3,2},{5,4},{7,6},{8,9},{10,11},{12,... | collective-permute-start | bytes 147464 | tf_op jit(solution)/shard_map/ppermute | solution.py:158
  78.5 1.3 copy-start.2
  80.5 3.6 %collective-permute-start.16 = (f32[2,48,128]{2,1,0:T(8,128)S(1)}, f32[2,48,128]{2,1,0:T(8,128)S(1)}, u32[]{:S(2)}, u32[]{:S(2)}) collective-permute-start(f32[2,48,128]{2,1,0:T(8,128)S(1)} %pad_maximum_fusion.6), channel_id=1, source_target_pairs={{0,8},{1,9},{2,10},{3,11},{4,12},{5,13},{6,14},{7,15}} | collective-permute-start | bytes 147464 | tf_op jit(solution)/shard_map/ppermute | solution.py:137
  84.7 0.7 collective-permute-start.17
  86.1 0.7 collective-permute-start.18
  87.9 0.7 collective-permute-start.19
  89.3 0.7 collective-permute-start.20
  90.7 20.9 %collective-permute-start.21 = (f32[48,128]{1,0:T(8,128)S(1)}, f32[48,128]{1,0:T(8,128)S(1)}, u32[]{:S(2)}, u32[]{:S(2)}) collective-permute-start(f32[48,128]{1,0:T(8,128)S(1)} %sub.393), channel_id=1, source_target_pairs={{8,0},{9,1},{10,2},{11,3},{12,4},{13,5},{14,6},{15,7}} | collective-permute-start | bytes 73736 | tf_op jit(solution)/shard_map/ppermute | solution.py:143
  112.3 5.3 %copy-start.9 = (f32[2,48,128]{2,1,0:T(8,128)}, f32[2,48,128]{2,1,0:T(8,128)S(1)}, u32[]{:S(2)}) copy-start(f32[2,48,128]{2,1,0:T(8,128)S(1)} %pad_maximum_fusion.11) | copy-start | bytes 147460
  112.3 5.3 %collective-permute-start.23 = (f32[2,48,128]{2,1,0:T(8,128)S(1)}, f32[2,48,128]{2,1,0:T(8,128)S(1)}, u32[]{:S(2)}, u32[]{:S(2)}) collective-permute-start(f32[2,48,128]{2,1,0:T(8,128)S(1)} %pad_maximum_fusion.11), channel_id=1, source_target_pairs={{1,2},{3,4},{5,6},{2,1},{4,3},{6,5},{9,10},{11,12},{13,14},{10,9},... | collective-permute-start | bytes 147464 | tf_op jit(solution)/shard_map/ppermute | solution.py:157
  113.2 4.8 %collective-permute-start.22 = (f32[2,48,128]{2,1,0:T(8,128)S(1)}, f32[2,48,128]{2,1,0:T(8,128)S(1)}, u32[]{:S(2)}, u32[]{:S(2)}) collective-permute-start(f32[2,48,128]{2,1,0:T(8,128)S(1)} %pad_maximum_fusion.11), channel_id=1, source_target_pairs={{0,1},{2,3},{4,5},{6,7},{1,0},{3,2},{5,4},{7,6},{8,9},{10,11},{12,... | collective-permute-start | bytes 147464 | tf_op jit(solution)/shard_map/ppermute | solution.py:158
  117.1 1.3 copy-start.3
  119.0 3.4 %collective-permute-start.24 = (f32[2,48,128]{2,1,0:T(8,128)S(1)}, f32[2,48,128]{2,1,0:T(8,128)S(1)}, u32[]{:S(2)}, u32[]{:S(2)}) collective-permute-start(f32[2,48,128]{2,1,0:T(8,128)S(1)} %pad_maximum_fusion.10), channel_id=1, source_target_pairs={{0,8},{1,9},{2,10},{3,11},{4,12},{5,13},{6,14},{7,15}} | collective-permute-start | bytes 147464 | tf_op jit(solution)/shard_map/ppermute | solution.py:137
  123.1 0.7 collective-permute-start.25
  124.5 0.7 collective-permute-start.26
  126.3 0.7 collective-permute-start.27
  127.6 0.7 collective-permute-start.28
  129.0 20.9 %collective-permute-start.29 = (f32[48,128]{1,0:T(8,128)S(1)}, f32[48,128]{1,0:T(8,128)S(1)}, u32[]{:S(2)}, u32[]{:S(2)}) collective-permute-start(f32[48,128]{1,0:T(8,128)S(1)} %sub.411), channel_id=1, source_target_pairs={{8,0},{9,1},{10,2},{11,3},{12,4},{13,5},{14,6},{15,7}} | collective-permute-start | bytes 73736 | tf_op jit(solution)/shard_map/ppermute | solution.py:143
  150.1 6.8 %copy-start.11 = (f32[48,128]{1,0:T(8,128)}, f32[48,128]{1,0:T(8,128)S(1)}, u32[]{:S(2)}) copy-start(f32[48,128]{1,0:T(8,128)S(1)} %fusion.24) | copy-start | bytes 73732
  150.3 6.6 %collective-permute-start.30 = (f32[48,128]{1,0:T(8,128)S(1)}, f32[48,128]{1,0:T(8,128)S(1)}, u32[]{:S(2)}, u32[]{:S(2)}) collective-permute-start(f32[48,128]{1,0:T(8,128)S(1)} %sub.412), channel_id=1, source_target_pairs={{0,8},{8,16},{16,24},{1,9},{9,17},{17,25},{2,10},{10,18},{18,26},{... | collective-permute-start | bytes 73736 | tf_op jit(solution)/shard_map/ppermute | solution.py:259
  152.1 5.5 %copy-start.13 = (f32[48,128]{1,0:T(8,128)}, f32[48,128]{1,0:T(8,128)S(1)}, u32[]{:S(2)}) copy-start(f32[48,128]{1,0:T(8,128)S(1)} %fusion.40) | copy-start | bytes 73732
  152.3 5.3 %copy-start.10 = (f32[2,48,128]{2,1,0:T(8,128)}, f32[2,48,128]{2,1,0:T(8,128)S(1)}, u32[]{:S(2)}) copy-start(f32[2,48,128]{2,1,0:T(8,128)S(1)} %pad_maximum_fusion.12) | copy-start | bytes 147460
  152.3 7.5 %collective-permute-start.32 = (f32[2,48,128]{2,1,0:T(8,128)S(1)}, f32[2,48,128]{2,1,0:T(8,128)S(1)}, u32[]{:S(2)}, u32[]{:S(2)}) collective-permute-start(f32[2,48,128]{2,1,0:T(8,128)S(1)} %pad_maximum_fusion.12), channel_id=1, source_target_pairs={{1,2},{3,4},{5,6},{2,1},{4,3},{6,5},{9,10},{11,12},{13,14},{10,9},... | collective-permute-start | bytes 147464 | tf_op jit(solution)/shard_map/ppermute | solution.py:157
  152.9 8.5 %collective-permute-start.31 = (f32[2,48,128]{2,1,0:T(8,128)S(1)}, f32[2,48,128]{2,1,0:T(8,128)S(1)}, u32[]{:S(2)}, u32[]{:S(2)}) collective-permute-start(f32[2,48,128]{2,1,0:T(8,128)S(1)} %pad_maximum_fusion.12), channel_id=1, source_target_pairs={{0,1},{2,3},{4,5},{6,7},{1,0},{3,2},{5,4},{7,6},{8,9},{10,11},{12,... | collective-permute-start | bytes 147464 | tf_op jit(solution)/shard_map/ppermute | solution.py:158
  157.6 0.6 copy-start.4
  159.7 2.2 %copy-start.5 = (f32[2,48,128]{2,1,0:T(8,128)S(1)}, f32[2,48,128]{2,1,0:T(8,128)}, u32[]{:S(2)}) copy-start(f32[2,48,128]{2,1,0:T(8,128)} %copy-done.4) | copy-start | bytes 147460
  159.7 2.2 %copy-start.12 = (f32[48,128]{1,0:T(8,128)S(1)}, f32[48,128]{1,0:T(8,128)}, u32[]{:S(2)}) copy-start(f32[48,128]{1,0:T(8,128)} %copy-done.11) | copy-start | bytes 73732
  159.7 2.2 %copy-start.14 = (f32[48,128]{1,0:T(8,128)S(1)}, f32[48,128]{1,0:T(8,128)}, u32[]{:S(2)}) copy-start(f32[48,128]{1,0:T(8,128)} %copy-done.13) | copy-start | bytes 73732

commit v10 on v9

v10 whole, which is shorter than its diff:
```python
import functools

import jax
import jax.numpy as jnp
from jax import lax
from jax.experimental import pallas as pl
from jax.experimental.pallas import tpu as pltpu
from jax.sharding import PartitionSpec as P

ITERS = 4
SUMS = 16
FETCH_ROOM = 56 << 20
LOAD_ROOM = 40 << 20
STAGE_ROOM = 16 << 20


def start_all(pairs, sems):
    copies = [
        pltpu.make_async_copy(source, target, sems.at[place])
        for place, (source, target) in enumerate(pairs)
    ]
    for copy in copies:
        copy.start()
    return copies


def turn_over(source, target):
    block = source.shape[0]
    high = 16 if block % 16 == 0 else block
    wide = 8 if block % 8 == 0 else block
    for i in range(0, block, wide):
        for j in range(0, block, high):
            part = source[i : i + wide, j : j + high].astype(jnp.float32)
            target[j : j + high, i : i + wide] = jnp.swapaxes(part, 0, 1)


def apply_plain(block_mat, value, target):
    block = target.shape[0]
    rows = 16 if block % 16 == 0 else block
    for start in range(0, block, rows):
        part = block_mat[start : start + rows].astype(jnp.float32)
        target[start : start + rows] = jnp.sum(part * value[None], axis=1)


def apply_turned(block_mat, vector):
    totals = [None, None]
    for j in range(block_mat.shape[0]):
        term = block_mat[j] * vector[j : j + 1]
        totals[j % 2] = term if totals[j % 2] is None else totals[j % 2] + term
    return totals[0] + totals[1]


def first_kernel(vector, lower, pivot, lower_held, pivot_held, out, field, middle, sems):
    count = vector.shape[0]
    pairs = [(vector, field), (pivot.at[0], pivot_held.at[0])]
    for k in range(1, count):
        pairs += [(lower.at[k], lower_held.at[k]), (pivot.at[k], pivot_held.at[k])]
    pairs.append((lower.at[0], lower_held.at[0]))
    copies = start_all(pairs, sems)
    copies[0].wait()
    copies[1].wait()
    apply_plain(pivot_held.at[0], field[0], out.at[0])
    for k in range(1, count):
        copies[2 * k].wait()
        apply_plain(lower_held.at[k], out[0], middle)
        copies[2 * k + 1].wait()
        apply_plain(pivot_held.at[k], field[k] - middle[...], out.at[0])
    copies[-1].wait()


def first_carry(vector, lower, pivot):
    count, block, wide = vector.shape
    return pl.pallas_call(
        first_kernel,
        out_shape=[
            pltpu.VMEM(lower.shape, lower.dtype),
            pltpu.VMEM(pivot.shape, pivot.dtype),
            jax.ShapeDtypeStruct((1, block, wide), jnp.float32),
        ],
        in_specs=[pl.BlockSpec(memory_space=pl.ANY)] * 3,
        out_specs=[pl.BlockSpec(memory_space=pltpu.VMEM)] * 3,
        scratch_shapes=[
            pltpu.VMEM(vector.shape, jnp.float32),
            pltpu.VMEM((block, wide), jnp.float32),
            pltpu.SemaphoreType.DMA((1 + 2 * count,)),
        ],
        compiler_params=pltpu.CompilerParams(vmem_limit_bytes=FETCH_ROOM),
    )(vector, lower, pivot)


def turn_held_kernel(*refs):
    half = len(refs) // 2
    for source, target in zip(refs[:half], refs[half:]):
        for k in range(source.shape[0]):
            turn_over(source.at[k], target.at[k])


def turn_held(*blocks):
    vmem = pl.BlockSpec(memory_space=pltpu.VMEM)
    return pl.pallas_call(
        turn_held_kernel,
        out_shape=[pltpu.VMEM(block.shape, jnp.float32) for block in blocks],
        in_specs=[vmem] * len(blocks),
        out_specs=[vmem] * len(blocks),
        compiler_params=pltpu.CompilerParams(vmem_limit_bytes=STAGE_ROOM),
    )(*blocks)


def load_kernel(choose, *refs):
    *refs, held, sems = refs
    size = (len(refs) - 1) // 2
    sources, targets = refs[:size], refs[size + 1 :]

    def run(sources):
        copies = start_all([(s, held.at[place]) for place, s in enumerate(sources)], sems)
        for place, target in enumerate(targets):
            copies[place].wait()
            for k in range(target.shape[0]):
                turn_over(held.at[place, k], target.at[k])

    if choose:
        even = lax.axis_index("patch") % 2 == 0
        pl.when(even)(lambda: run(sources))
        pl.when(jnp.logical_not(even))(lambda: run((*sources[:-2], sources[-1], sources[-2])))
    else:
        run(sources)


def load(blocks, after, choose=False):
    shape = blocks[0].shape
    return pl.pallas_call(
        functools.partial(load_kernel, choose),
        out_shape=[pltpu.VMEM(shape, jnp.float32) for block in blocks],
        in_specs=[pl.BlockSpec(memory_space=pl.ANY)] * (len(blocks) + 1),
        out_specs=[pl.BlockSpec(memory_space=pltpu.VMEM)] * len(blocks),
        scratch_shapes=[
            pltpu.VMEM((len(blocks),) + shape, blocks[0].dtype),
            pltpu.SemaphoreType.DMA((len(blocks),)),
        ],
        compiler_params=pltpu.CompilerParams(vmem_limit_bytes=LOAD_ROOM),
    )(*blocks, after)


def stage(kernel, out_shapes, operands, scratch=()):
    vmem = pl.BlockSpec(memory_space=pltpu.VMEM)
    return pl.pallas_call(
        kernel,
        out_shape=[jax.ShapeDtypeStruct(shape, jnp.float32) for shape in out_shapes],
        in_specs=[vmem] * len(operands),
        out_specs=[vmem] * len(out_shapes),
        scratch_shapes=[pltpu.VMEM(shape, jnp.float32) for shape in scratch],
        compiler_params=pltpu.CompilerParams(vmem_limit_bytes=STAGE_ROOM),
    )(*operands)


def run_down(vector, lower, pivot, entry, forward, work):
    for k in range(vector.shape[0]):
        if k > 0:
            work[...] = vector[k] - apply_turned(lower.at[k], forward.at[k - 1])
        elif entry is not None:
            work[...] = vector[k] + apply_turned(lower.at[k], entry)
        else:
            work[...] = vector[k]
        forward[k] = apply_turned(pivot.at[k], work)


def run_up(forward, upper, pivot, incoming, result, coupled):
    count = forward.shape[0]
    for k in reversed(range(count)):
        following = result.at[k + 1] if k < count - 1 else incoming
        if following is None:
            result[k] = forward[k]
        else:
            coupled[k] = apply_turned(upper.at[k], following)
            result[k] = forward[k] - apply_turned(pivot.at[k], coupled.at[k])


def add_up(parts, target):
    total = parts[0][...]
    for part in parts[1:]:
        total = total + part[...]
    target[...] = total


def set_entry(carried, entry):
    both = carried.shape[0] == 2
    entry[...] = carried[1] - carried[0] if both else -carried[0]


def hop_down_kernel(parts, has_last, vector, lower, pivot, *refs):
    carried_in, refs = refs[:parts], refs[parts:]
    if has_last:
        last, *refs = refs
    carried, message, entry, forward, work = refs
    add_up(carried_in, carried)
    set_entry(carried, entry)
    run_down(vector, lower, pivot, entry, forward, work)
    message[0] = forward[forward.shape[0] - 1]
    if has_last:
        message[1] = last[...]


def turn_kernel(parts, vector, lower, pivot, upper, *refs):
    carried_in = refs[:parts]
    carried, forward, outgoing, entry, work, result, coupled = refs[parts:]
    add_up(carried_in, carried)
    set_entry(carried, entry)
    run_down(vector, lower, pivot, entry, forward, work)
    run_up(forward, upper, pivot, None, result, coupled)
    outgoing[...] = result[0]


def hop_up_kernel(parts, forward, upper, pivot, *refs):
    carried_in = refs[:parts]
    carried, outgoing, result, coupled = refs[parts:]
    add_up(carried_in, carried)
    run_up(forward, upper, pivot, carried, result, coupled)
    outgoing[...] = result[0]


def end_kernel(parts, forward, upper, pivot, *refs):
    carried_in = refs[:parts]
    result, coupled, last, carried = refs[parts:]
    add_up(carried_in, carried)
    run_up(forward, upper, pivot, carried, result, coupled)
    last[...] = result[result.shape[0] - 1]


def own_kernel(vector, carried, lower, diag_block, direction, coupled, whole, image):
    for k in range(vector.shape[0]):
        value = vector[k]
        if k == 0 and carried.shape[0] == 2:
            value = value + apply_turned(lower.at[0], carried.at[1])
        whole[k] = value
        value = coupled[k] - value + apply_turned(diag_block.at[k], direction.at[k])
        if k > 0:
            value = value + apply_turned(lower.at[k], direction.at[k - 1])
        image[k] = value


def near_kernel(image, near_block, near, out):
    for k in range(image.shape[0]):
        out[k] = image[k] + apply_turned(near_block.at[k], near.at[k])


def next_kernel(image, far_block, far, lower, pivot, last, out, message, forward, work):
    for k in range(image.shape[0]):
        out[k] = image[k] + apply_turned(far_block.at[k], far.at[k])
    run_down(out, lower, pivot, None, forward, work)
    message[0] = forward[forward.shape[0] - 1]
    message[1] = last[...]


def place_of(pair):
    low, high = sorted(pair)
    return high * (high + 1) // 2 + low


def pair_sum(left, right):
    total = left[0] * right[0]
    for k in range(1, left.shape[0]):
        total = total + left[k] * right[k]
    return jnp.sum(total, axis=0, keepdims=True)


def sums_kernel(*refs):
    *basis, out = refs
    row = lax.broadcasted_iota(jnp.int32, out.shape, 0)
    sums = jnp.zeros(out.shape, jnp.float32)
    for i in range(len(basis)):
        for j in range(i, len(basis)):
            sums = jnp.where(row == place_of((i, j)), pair_sum(basis[i], basis[j]), sums)
    out[...] = sums


def last_kernel(image, far_block, far, lower, below, sums_in, *refs):
    *basis, out, newest = refs
    for k in range(image.shape[0]):
        value = image[k] + apply_turned(far_block.at[k], far.at[k])
        if k == 0:
            value = value + apply_turned(lower.at[0], below)
        newest[k] = value
    sums = sums_in[...]
    row = lax.broadcasted_iota(jnp.int32, sums.shape, 0)
    lane = lax.broadcasted_iota(jnp.int32, sums.shape, 1)
    high = len(basis)
    for i, member in enumerate((*basis, newest)):
        sums = jnp.where(row == place_of((i, high)), pair_sum(member, newest), sums)
    whole = jnp.sum(sums, axis=1, keepdims=True)
    sums = jnp.sum(jnp.where(lane == row, whole, 0.0), axis=0, keepdims=True)
    out[...] = jnp.broadcast_to(sums, out.shape)


def finish_kernel(parts_ref, *refs):
    directions, out = refs[:-1], refs[-1]
    width = len(directions)
    total = jnp.sum(parts_ref[...], axis=0, keepdims=True)
    shape = (SUMS, total.shape[1])
    row = lax.broadcasted_iota(jnp.int32, shape, 0)
    lane = lax.broadcasted_iota(jnp.int32, shape, 1)
    sums = jnp.sum(jnp.where(lane == row, total, 0.0), axis=1, keepdims=True)
    sums = jnp.broadcast_to(sums, shape)
    gram = {}
    for i in range(width + 1):
        for j in range(width + 1):
            place = place_of((i, j))
            gram[i, j] = sums[place : place + 1]
    half = [[gram[j + 1, i] + gram[j, i] for i in range(width + 1)] for j in range(width)]
    normal = [[half[j][i + 1] + half[j][i] for i in range(width)] for j in range(width)]
    right = [half[j][0] for j in range(width)]
    for i in range(width):
        inverse = 1.0 / normal[i][i]
        for j in range(i + 1, width):
            factor = normal[j][i] * inverse
            for k in range(i, width):
                normal[j][k] = normal[j][k] - factor * normal[i][k]
            right[j] = right[j] - factor * right[i]
    coeffs = [None] * width
    for i in reversed(range(width)):
        value = right[i]
        for k in range(i + 1, width):
            value = value - normal[i][k] * coeffs[k]
        coeffs[i] = value / normal[i][i]
    for k in range(out.shape[0]):
        step = coeffs[0] * directions[0][k]
        for j in range(1, width):
            step = step + coeffs[j] * directions[j][k]
        out[k] = step


def rows_beside(field, across):
    count = lax.axis_size("patch")
    even = [(i, i + 1) for i in range(0, count - 1, 2)]
    odd = [(i, i + 1) for i in range(1, count - 1, 2)]
    is_even = lax.axis_index("patch") % 2 == 0
    first, last = field[..., :across], field[..., -across:]
    several = field.shape[-1] > across
    to_far = jnp.where(is_even, first, last) if several else field
    to_near = jnp.where(is_even, last, first) if several else field
    far = lax.ppermute(to_far, "patch", odd + [(b, a) for a, b in odd])
    near = lax.ppermute(to_near, "patch", even + [(b, a) for a, b in even])
    if several:
        up = [jnp.concatenate([field[..., across:], row], axis=-1) for row in (near, far)]
        down = [jnp.concatenate([row, field[..., :-across]], axis=-1) for row in (near, far)]
        near = jnp.where(is_even, up[0], down[0])
        far = jnp.where(is_even, down[1], up[1])
    return near, far


def per_device(newton_residual, diag_block, lower, upper, west, east, pivot_inverse):
    shape = newton_residual.shape
    count, block, rows, across = shape
    wide = rows * across

    def flat(matrix):
        return matrix.reshape(count, block, block, wide)

    diag_block, lower, upper, west, east, pivot = map(
        flat, (diag_block, lower, upper, west, east, pivot_inverse)
    )
    line = lax.axis_size("line")
    devices = line * lax.axis_size("patch")
    one, field = (block, wide), (count, block, wide)
    vector = newton_residual.reshape(field)
    lower, pivot, message = first_carry(vector, lower, pivot)
    lower, pivot = turn_held(lower, pivot)
    basis = []
    directions = []
    last = None
    for j in range(ITERS):
        parts = []
        for turn in range(line - 1):
            parts.append(lax.ppermute(message, "line", [(turn, turn + 1)]))
            if j == 0 and turn == 0:
                (upper,) = load((upper,), message)
            if turn < line - 2:
                lasts = [] if last is None else [last]
                carried, message = stage(
                    functools.partial(hop_down_kernel, len(parts), bool(lasts)),
                    [message.shape, message.shape],
                    [vector, lower, pivot, *parts, *lasts],
                    [one, field, one],
                )
                parts = [carried]
        parts = parts or [jnp.zeros_like(message)]
        carried_down, forward, outgoing = stage(
            functools.partial(turn_kernel, len(parts)),
            [message.shape, field, one],
            [vector, lower, pivot, upper, *parts],
            [one, one, field, field],
        )
        parts = []
        for turn in reversed(range(line - 1)):
            parts.append(lax.ppermute(outgoing, "line", [(turn + 1, turn)]))
            if j == 0 and turn == line - 2:
                diag_block, near_block, far_block = load((diag_block, east, west), outgoing, True)
            if turn > 0:
                carried, outgoing = stage(
                    functools.partial(hop_up_kernel, len(parts)),
                    [one, one],
                    [forward, upper, pivot, *parts],
                    [field, field],
                )
                parts = [carried]
        parts = parts or [jnp.zeros_like(outgoing)]
        direction, coupled, last = stage(
            functools.partial(end_kernel, len(parts)),
            [field, field, one],
            [forward, upper, pivot, *parts],
            [one],
        )
        directions.append(direction)
        near, far = rows_beside(direction, across)
        whole, image = stage(
            own_kernel,
            [field, field],
            [vector, carried_down, lower, diag_block, direction, coupled],
        )
        basis.append(whole)
        (image,) = stage(near_kernel, [field], [image, near_block, near])
        if j < ITERS - 1:
            vector, message = stage(
                next_kernel,
                [field, (2,) + one],
                [image, far_block, far, lower, pivot, last],
                [field, one],
            )
        else:
            below = lax.ppermute(last, "line", [(i, i + 1) for i in range(line - 1)])
            (sums,) = stage(sums_kernel, [(SUMS, wide)], basis)
            (sums,) = stage(
                last_kernel,
                [(devices, wide)],
                [image, far_block, far, lower, below, sums, *basis],
                [field],
            )
    sums = lax.all_to_all(sums, ("line", "patch"), 0, 0, tiled=True)
    (step,) = stage(finish_kernel, [field], [sums, *directions])
    return step.reshape(shape)


def solution(mesh):
    blocks = P("line", None, None, "patch", None)
    field = P("line", None, "patch", None)
    return jax.shard_map(
        per_device, mesh=mesh, in_specs=(field,) + (blocks,) * 6, out_specs=field, check_vma=False
    )
```

time: 177 us -> 162 us (0.915)
  other arithmetic: 28 us -> 0 us
  Pallas kernels: 8.84 us -> 21.9 us
  blocking collectives: 10.2 us -> 19.7 us
  starting transfers between devices: 43.9 us -> 34.5 us
    reduce_sum x130 -> x0, other arithmetic: 26.7 us -> none  [the longest x118 20.3 us: single_apply(): return jnp.sum(block_mat.astype(jnp.float32) * vector[None], axis=1)]
    pallas_call x4 -> x41, Pallas kernels: 7.17 us -> 19.6 us  [the longest x38 15.9 us: stage(): pl.pallas_call(kernel, out_shape=[jax.ShapeDtypeStruct(shape, jnp.float32...]
    ppermute x4, starting transfers between devices: 13.7 us -> 4.11 us  [rows_beside(): near = lax.ppermute(to_near, 'patch', even + [(b, a) for a, b in even])]
    all_to_all x1, blocking collectives: 10.2 us -> 19.7 us  [per_device(): sums = lax.all_to_all(sums, ('line', 'patch'), 0, 0, tiled=True)]
  transfers between devices with their start and end apart: 33 -> 33, of which waited for: 7 -> 9; matrix products, arithmetic and copies ran while one was open for 4% -> 0% of each run, Pallas kernels for 2% -> 4%
where the time goes in v10:
time: 162 us; the launch traced here: 161 us
  waiting for transfers between devices  83.5 us (52%)
  starting transfers between devices  34.5 us (21%)
  Pallas kernels  21.9 us (14%)
  blocking collectives  19.7 us (12%)
    ppermute x12, waiting for transfers between devices, per_device(): parts.append(lax.ppermute(outgoing, 'line', [(turn + 1, turn)]))  76.8 us
    all_to_all x1, blocking collectives, per_device(): sums = lax.all_to_all(sums, ('line', 'patch'), 0, 0, tiled=True)  19.7 us
    pallas_call x38, Pallas kernels, stage(): pl.pallas_call(kernel, out_shape=[jax.ShapeDtypeStruct(shape, jnp.float32...  15.9 us
    ppermute x12, starting transfers between devices, per_device(): parts.append(lax.ppermute(message, 'line', [(turn, turn + 1)]))  15.1 us
    ppermute x12, starting transfers between devices, per_device(): parts.append(lax.ppermute(outgoing, 'line', [(turn + 1, turn)]))  10.5 us
    ppermute x12, waiting for transfers between devices, per_device(): parts.append(lax.ppermute(message, 'line', [(turn, turn + 1)]))  5.99 us
    ppermute x4, starting transfers between devices, rows_beside(): near = lax.ppermute(to_near, 'patch', even + [(b, a) for a, b in even])  4.11 us
  transfers between devices with their start and end apart: 33, of which 9 were waited for; matrix products, arithmetic and copies ran while one was open for 0% of the time, Pallas kernels for 4%

profile of v10, /device:TPU:0, one launch (start us, length us, event | category | flops | bytes accessed | tf_op | source)
XLA Modules:
  0.0 161.1 jit_solution(6808227029822258624)
XLA Ops:
  0.0 2.3 %shard_map.73 = (bf16[2,48,48,128]{3,2,1,0:T(8,128)(2,1)S(1)}, bf16[2,48,48,128]{3,2,1,0:T(8,128)(2,1)S(1)}, f32[1,48,128]{2,1,0:T(8,128)}) custom-call(f32[2,48,128]{2,1,0:T(8,128)} %bitcast.14, bf16[2,48,48,128]{3,2,1,0:T(8,128)(2,1)} %bitcast.25, bf16[2,48,48,128]{3,2,1,0:T(8,128)(2,1)} %bitcast.26), custom_call_target="tpu_custom_call" | custom-call | tf_op jit(solution)/shard_map/pallas_call | solution.py:73
  2.3 4.8 %collective-permute-start = (f32[1,48,128]{2,1,0:T(8,128)}, f32[1,48,128]{2,1,0:T(8,128)S(1)}, u32[]{:S(2)}, u32[]{:S(2)}) collective-permute-start(f32[1,48,128]{2,1,0:T(8,128)} %get-tuple-element.87.refs_1_), channel_id=1, source_target_pairs={{0,8},{1,9},{2,10},{3,11},{4,12},{5,13},{6,14},{7,15}} | collective-permute-start | bytes 73736 | tf_op jit(solution)/shard_map/ppermute | solution.py:373
  7.1 0.9 shard_map.74
  8.1 0.8 collective-permute-done.refs_0_
  9.3 0.7 collective-permute-start.1
  10.0 0.4 shard_map.77
  10.4 0.7 collective-permute-start.2
  11.2 0.7 shard_map.75.upper
  11.9 0.6 shard_map.78
  12.5 0.7 collective-permute-start.3
  13.6 0.7 collective-permute-start.4
  14.3 0.4 shard_map.81
  14.7 1.3 collective-permute-start.5
  16.0 18.1 %collective-permute-done.5.refs_1_ = f32[48,128]{1,0:T(8,128)S(1)} collective-permute-done((f32[48,128]{1,0:T(8,128)S(1)}, f32[48,128]{1,0:T(8,128)S(1)}, u32[]{:S(2)}, u32[]{:S(2)}) %collective-permute-start.5) | collective-permute-done | bytes 24608 | tf_op jit(solution)/shard_map/ppermute | solution.py:394
  34.6 0.8 collective-permute-start.7
  36.1 2.1 %shard_map.79 = (f32[2,48,48,128]{3,2,1,0:T(8,128)S(1)}, f32[2,48,48,128]{3,2,1,0:T(8,128)S(1)}, f32[2,48,48,128]{3,2,1,0:T(8,128)S(1)}) custom-call(bf16[2,48,48,128]{3,2,1,0:T(8,128)(2,1)S(1)} %bitcast.20, bf16[2,48,48,128]{3,2,1,0:T(8,128)(2,1)S(1)} %bitcast.21, bf16[2,48,48,128]{3,2,1,0:T(8,128)(2,1)S(1)} %bitcast.22, ...), custom_call_target="tpu_custom_call" | custom-call | tf_op jit(solution)/shard_map/pallas_call | solution.py:131
  38.2 0.4 shard_map.83
  38.8 0.5 shard_map.85
  39.3 1.6 %collective-permute-start.8 = (f32[2,48,128]{2,1,0:T(8,128)S(1)}, f32[2,48,128]{2,1,0:T(8,128)S(1)}, u32[]{:S(2)}, u32[]{:S(2)}) collective-permute-start(f32[2,48,128]{2,1,0:T(8,128)S(1)} %get-tuple-element.107), channel_id=1, source_target_pairs={{0,8},{1,9},{2,10},{3,11},{4,12},{5,13},{6,14},{7,15}} | collective-permute-start | bytes 147464 | tf_op jit(solution)/shard_map/ppermute | solution.py:373
  40.9 1.7 %collective-permute-done.8.refs_0_ = f32[2,48,128]{2,1,0:T(8,128)S(1)} collective-permute-done((f32[2,48,128]{2,1,0:T(8,128)S(1)}, f32[2,48,128]{2,1,0:T(8,128)S(1)}, u32[]{:S(2)}, u32[]{:S(2)}) %collective-permute-start.8) | collective-permute-done | bytes 49184 | tf_op jit(solution)/shard_map/ppermute | solution.py:373
  43.1 0.7 collective-permute-start.9
  43.8 0.4 shard_map.87
  44.2 0.7 collective-permute-start.10
  44.9 0.6 shard_map.88
  45.5 0.7 collective-permute-start.11
  46.2 0.4 shard_map.89
  46.6 0.7 collective-permute-start.12
  47.7 1.3 collective-permute-start.13
  49.0 19.6 %collective-permute-done.13.refs_1_ = f32[48,128]{1,0:T(8,128)S(1)} collective-permute-done((f32[48,128]{1,0:T(8,128)S(1)}, f32[48,128]{1,0:T(8,128)S(1)}, u32[]{:S(2)}, u32[]{:S(2)}) %collective-permute-start.13) | collective-permute-done | bytes 24608 | tf_op jit(solution)/shard_map/ppermute | solution.py:394
  69.0 0.8 collective-permute-start.15
  69.9 0.5 shard_map.92
  70.6 0.5 shard_map.94
  71.1 1.6 %collective-permute-start.16 = (f32[2,48,128]{2,1,0:T(8,128)S(1)}, f32[2,48,128]{2,1,0:T(8,128)S(1)}, u32[]{:S(2)}, u32[]{:S(2)}) collective-permute-start(f32[2,48,128]{2,1,0:T(8,128)S(1)} %get-tuple-element.124), channel_id=1, source_target_pairs={{0,8},{1,9},{2,10},{3,11},{4,12},{5,13},{6,14},{7,15}} | collective-permute-start | bytes 147464 | tf_op jit(solution)/shard_map/ppermute | solution.py:373
  72.7 1.7 %collective-permute-done.16.refs_0_ = f32[2,48,128]{2,1,0:T(8,128)S(1)} collective-permute-done((f32[2,48,128]{2,1,0:T(8,128)S(1)}, f32[2,48,128]{2,1,0:T(8,128)S(1)}, u32[]{:S(2)}, u32[]{:S(2)}) %collective-permute-start.16) | collective-permute-done | bytes 49184 | tf_op jit(solution)/shard_map/ppermute | solution.py:373
  74.8 0.7 collective-permute-start.17
  75.5 0.4 shard_map.96
  75.9 0.7 collective-permute-start.18
  76.6 0.6 shard_map.97
  77.2 0.7 collective-permute-start.19
  77.9 0.4 shard_map.98
  78.3 0.7 collective-permute-start.20
  79.4 1.3 collective-permute-start.21
  80.7 19.6 %collective-permute-done.21.refs_1_ = f32[48,128]{1,0:T(8,128)S(1)} collective-permute-done((f32[48,128]{1,0:T(8,128)S(1)}, f32[48,128]{1,0:T(8,128)S(1)}, u32[]{:S(2)}, u32[]{:S(2)}) %collective-permute-start.21) | collective-permute-done | bytes 24608 | tf_op jit(solution)/shard_map/ppermute | solution.py:394
  100.9 0.7 collective-permute-start.23
  101.6 0.5 shard_map.101
  102.3 0.5 shard_map.103
  102.8 1.7 %collective-permute-start.24 = (f32[2,48,128]{2,1,0:T(8,128)S(1)}, f32[2,48,128]{2,1,0:T(8,128)S(1)}, u32[]{:S(2)}, u32[]{:S(2)}) collective-permute-start(f32[2,48,128]{2,1,0:T(8,128)S(1)} %get-tuple-element.141), channel_id=1, source_target_pairs={{0,8},{1,9},{2,10},{3,11},{4,12},{5,13},{6,14},{7,15}} | collective-permute-start | bytes 147464 | tf_op jit(solution)/shard_map/ppermute | solution.py:373
  104.5 1.7 %collective-permute-done.24.refs_0_ = f32[2,48,128]{2,1,0:T(8,128)S(1)} collective-permute-done((f32[2,48,128]{2,1,0:T(8,128)S(1)}, f32[2,48,128]{2,1,0:T(8,128)S(1)}, u32[]{:S(2)}, u32[]{:S(2)}) %collective-permute-start.24) | collective-permute-done | bytes 49184 | tf_op jit(solution)/shard_map/ppermute | solution.py:373
  106.6 0.7 collective-permute-start.25
  107.3 0.4 shard_map.105
  107.7 0.7 collective-permute-start.26
  108.4 0.6 shard_map.106
  109.0 0.7 collective-permute-start.27
  109.7 0.4 shard_map.107
  110.1 0.7 collective-permute-start.28
  111.2 1.3 collective-permute-start.29
  112.5 19.5 %collective-permute-done.29.refs_1_ = f32[48,128]{1,0:T(8,128)S(1)} collective-permute-done((f32[48,128]{1,0:T(8,128)S(1)}, f32[48,128]{1,0:T(8,128)S(1)}, u32[]{:S(2)}, u32[]{:S(2)}) %collective-permute-start.29) | collective-permute-done | bytes 24608 | tf_op jit(solution)/shard_map/ppermute | solution.py:394
  132.4 3.8 %collective-permute-start.30 = (f32[2,48,128]{2,1,0:T(8,128)S(1)}, f32[2,48,128]{2,1,0:T(8,128)S(1)}, u32[]{:S(2)}, u32[]{:S(2)}) collective-permute-start(f32[2,48,128]{2,1,0:T(8,128)S(1)} %get-tuple-element.153.direction.refs_3_), channel_id=1, source_target_pairs={{0,1},{2,3},{4,5},{6,7},{1,0},{3,2},{5,4},{7,6},{8,9},{10,11},{12,... | collective-permute-start | bytes 147464 | tf_op jit(solution)/shard_map/ppermute | solution.py:341
  136.2 0.7 collective-permute-start.31
  136.8 1.9 %collective-permute-start.32 = (f32[48,128]{1,0:T(8,128)S(1)}, f32[48,128]{1,0:T(8,128)S(1)}, u32[]{:S(2)}, u32[]{:S(2)}) collective-permute-start(f32[48,128]{1,0:T(8,128)S(1)} %get-tuple-element.156), channel_id=1, source_target_pairs={{0,8},{8,16},{16,24},{1,9},{9,17},{17,25},{2,10},{10,18},{18,26},{... | collective-permute-start | bytes 73736 | tf_op jit(solution)/shard_map/ppermute | solution.py:429
  138.8 0.5 shard_map.110
  139.5 0.7 collective-permute-done.32.below
  140.6 19.7 %all_to_all.11 = f32[32,1,128]{2,1,0:T(1,128)S(1)} all-to-all(f32[32,1,128]{2,1,0:T(1,128)S(1)} %bitcast.23), channel_id=1, replica_groups=mesh['line'=4,'patch'=8] {'line','patch'}, dimensions={0} | all-to-all | bytes 32768 | tf_op jit(solution)/shard_map/all_to_all | solution.py:437
  160.4 0.8 shard_map.114
  (57 shorter events, 7.3 us)
Async XLA Ops:
  2.3 6.6 %collective-permute-start = (f32[1,48,128]{2,1,0:T(8,128)}, f32[1,48,128]{2,1,0:T(8,128)S(1)}, u32[]{:S(2)}, u32[]{:S(2)}) collective-permute-start(f32[1,48,128]{2,1,0:T(8,128)} %get-tuple-element.87.refs_1_), channel_id=1, source_target_pairs={{0,8},{1,9},{2,10},{3,11},{4,12},{5,13},{6,14},{7,15}} | collective-permute-start | bytes 73736 | tf_op jit(solution)/shard_map/ppermute | solution.py:373
  7.1 1.7 %copy-start = (f32[2,48,1,128]{3,2,1,0:T(1,128)S(1)}, f32[2,48,1,128]{3,2,1,0:T(1,128)}, u32[]{:S(2)}) copy-start(f32[2,48,1,128]{3,2,1,0:T(1,128)} %param.7) | copy-start | bytes 147460
  9.3 0.7 collective-permute-start.1
  9.9 1.3 copy-start.1
  10.0 1.3 copy-start.5
  10.4 1.6 collective-permute-start.2
  12.5 0.7 collective-permute-start.3
  13.6 0.7 collective-permute-start.4
  14.7 19.4 %collective-permute-start.5 = (f32[48,128]{1,0:T(8,128)S(1)}, f32[48,128]{1,0:T(8,128)S(1)}, u32[]{:S(2)}, u32[]{:S(2)}) collective-permute-start(f32[48,128]{1,0:T(8,128)S(1)} %get-tuple-element.99), channel_id=1, source_target_pairs={{8,0},{9,1},{10,2},{11,3},{12,4},{13,5},{14,6},{15,7}} | collective-permute-start | bytes 73736 | tf_op jit(solution)/shard_map/ppermute | solution.py:394
  34.1 1.3 copy-start.2
  34.1 1.6 %copy-start.3 = (bf16[2,48,48,1,128]{4,2,3,1,0:T(8,128)(2,1)S(1)}, bf16[2,48,48,1,128]{4,2,3,1,0:T(8,128)(2,1)}, u32[]{:S(2)}) copy-start(bf16[2,48,48,1,128]{4,2,3,1,0:T(8,128)(2,1)} %param.12) | copy-start | bytes 3538948
  34.1 2.0 %copy-start.4 = (bf16[2,48,48,1,128]{4,2,3,1,0:T(8,128)(2,1)S(1)}, bf16[2,48,48,1,128]{4,2,3,1,0:T(8,128)(2,1)}, u32[]{:S(2)}) copy-start(bf16[2,48,48,1,128]{4,2,3,1,0:T(8,128)(2,1)} %param.11) | copy-start | bytes 3538948
  34.5 4.1 %collective-permute-start.6 = (f32[2,48,128]{2,1,0:T(8,128)S(1)}, f32[2,48,128]{2,1,0:T(8,128)S(1)}, u32[]{:S(2)}, u32[]{:S(2)}) collective-permute-start(f32[2,48,128]{2,1,0:T(8,128)S(1)} %get-tuple-element.100.direction.refs_0_), channel_id=1, source_target_pairs={{0,1},{2,3},{4,5},{6,7},{1,0},{3,2},{5,4},{7,6},{8,9},{10,11},{12,... | collective-permute-start | bytes 147464 | tf_op jit(solution)/shard_map/ppermute | solution.py:341
  34.6 4.3 %collective-permute-start.7 = (f32[2,48,128]{2,1,0:T(8,128)S(1)}, f32[2,48,128]{2,1,0:T(8,128)S(1)}, u32[]{:S(2)}, u32[]{:S(2)}) collective-permute-start(f32[2,48,128]{2,1,0:T(8,128)S(1)} %get-tuple-element.100.direction.refs_0_), channel_id=1, source_target_pairs={{1,2},{3,4},{5,6},{2,1},{4,3},{6,5},{9,10},{11,12},{13,14},{10,9},... | collective-permute-start | bytes 147464 | tf_op jit(solution)/shard_map/ppermute | solution.py:340
  39.3 3.4 %collective-permute-start.8 = (f32[2,48,128]{2,1,0:T(8,128)S(1)}, f32[2,48,128]{2,1,0:T(8,128)S(1)}, u32[]{:S(2)}, u32[]{:S(2)}) collective-permute-start(f32[2,48,128]{2,1,0:T(8,128)S(1)} %get-tuple-element.107), channel_id=1, source_target_pairs={{0,8},{1,9},{2,10},{3,11},{4,12},{5,13},{6,14},{7,15}} | collective-permute-start | bytes 147464 | tf_op jit(solution)/shard_map/ppermute | solution.py:373
  43.1 0.7 collective-permute-start.9
  44.2 0.7 collective-permute-start.10
  45.5 0.7 collective-permute-start.11
  46.6 0.7 collective-permute-start.12
  47.7 20.9 %collective-permute-start.13 = (f32[48,128]{1,0:T(8,128)S(1)}, f32[48,128]{1,0:T(8,128)S(1)}, u32[]{:S(2)}, u32[]{:S(2)}) collective-permute-start(f32[48,128]{1,0:T(8,128)S(1)} %get-tuple-element.118), channel_id=1, source_target_pairs={{8,0},{9,1},{10,2},{11,3},{12,4},{13,5},{14,6},{15,7}} | collective-permute-start | bytes 73736 | tf_op jit(solution)/shard_map/ppermute | solution.py:394
  69.0 1.4 collective-permute-start.14
  69.0 1.5 collective-permute-start.15
  71.1 3.4 %collective-permute-start.16 = (f32[2,48,128]{2,1,0:T(8,128)S(1)}, f32[2,48,128]{2,1,0:T(8,128)S(1)}, u32[]{:S(2)}, u32[]{:S(2)}) collective-permute-start(f32[2,48,128]{2,1,0:T(8,128)S(1)} %get-tuple-element.124), channel_id=1, source_target_pairs={{0,8},{1,9},{2,10},{3,11},{4,12},{5,13},{6,14},{7,15}} | collective-permute-start | bytes 147464 | tf_op jit(solution)/shard_map/ppermute | solution.py:373
  74.8 0.7 collective-permute-start.17
  75.9 0.7 collective-permute-start.18
  77.2 0.7 collective-permute-start.19
  78.3 0.7 collective-permute-start.20
  79.4 20.9 %collective-permute-start.21 = (f32[48,128]{1,0:T(8,128)S(1)}, f32[48,128]{1,0:T(8,128)S(1)}, u32[]{:S(2)}, u32[]{:S(2)}) collective-permute-start(f32[48,128]{1,0:T(8,128)S(1)} %get-tuple-element.135), channel_id=1, source_target_pairs={{8,0},{9,1},{10,2},{11,3},{12,4},{13,5},{14,6},{15,7}} | collective-permute-start | bytes 73736 | tf_op jit(solution)/shard_map/ppermute | solution.py:394
  100.7 1.3 collective-permute-start.22
  100.9 1.4 collective-permute-start.23
  102.8 3.4 %collective-permute-start.24 = (f32[2,48,128]{2,1,0:T(8,128)S(1)}, f32[2,48,128]{2,1,0:T(8,128)S(1)}, u32[]{:S(2)}, u32[]{:S(2)}) collective-permute-start(f32[2,48,128]{2,1,0:T(8,128)S(1)} %get-tuple-element.141), channel_id=1, source_target_pairs={{0,8},{1,9},{2,10},{3,11},{4,12},{5,13},{6,14},{7,15}} | collective-permute-start | bytes 147464 | tf_op jit(solution)/shard_map/ppermute | solution.py:373
  106.6 0.7 collective-permute-start.25
  107.7 0.7 collective-permute-start.26
  109.0 0.7 collective-permute-start.27
  110.1 0.7 collective-permute-start.28
  111.2 20.8 %collective-permute-start.29 = (f32[48,128]{1,0:T(8,128)S(1)}, f32[48,128]{1,0:T(8,128)S(1)}, u32[]{:S(2)}, u32[]{:S(2)}) collective-permute-start(f32[48,128]{1,0:T(8,128)S(1)} %get-tuple-element.152), channel_id=1, source_target_pairs={{8,0},{9,1},{10,2},{11,3},{12,4},{13,5},{14,6},{15,7}} | collective-permute-start | bytes 73736 | tf_op jit(solution)/shard_map/ppermute | solution.py:394
  132.4 6.9 %collective-permute-start.30 = (f32[2,48,128]{2,1,0:T(8,128)S(1)}, f32[2,48,128]{2,1,0:T(8,128)S(1)}, u32[]{:S(2)}, u32[]{:S(2)}) collective-permute-start(f32[2,48,128]{2,1,0:T(8,128)S(1)} %get-tuple-element.153.direction.refs_3_), channel_id=1, source_target_pairs={{0,1},{2,3},{4,5},{6,7},{1,0},{3,2},{5,4},{7,6},{8,9},{10,11},{12,... | collective-permute-start | bytes 147464 | tf_op jit(solution)/shard_map/ppermute | solution.py:341
  136.2 4.1 %collective-permute-start.31 = (f32[2,48,128]{2,1,0:T(8,128)S(1)}, f32[2,48,128]{2,1,0:T(8,128)S(1)}, u32[]{:S(2)}, u32[]{:S(2)}) collective-permute-start(f32[2,48,128]{2,1,0:T(8,128)S(1)} %get-tuple-element.153.direction.refs_3_), channel_id=1, source_target_pairs={{1,2},{3,4},{5,6},{2,1},{4,3},{6,5},{9,10},{11,12},{13,14},{10,9},... | collective-permute-start | bytes 147464 | tf_op jit(solution)/shard_map/ppermute | solution.py:340
  136.8 3.4 %collective-permute-start.32 = (f32[48,128]{1,0:T(8,128)S(1)}, f32[48,128]{1,0:T(8,128)S(1)}, u32[]{:S(2)}, u32[]{:S(2)}) collective-permute-start(f32[48,128]{1,0:T(8,128)S(1)} %get-tuple-element.156), channel_id=1, source_target_pairs={{0,8},{8,16},{16,24},{1,9},{9,17},{17,25},{2,10},{10,18},{18,26},{... | collective-permute-start | bytes 73736 | tf_op jit(solution)/shard_map/ppermute | solution.py:429

commit v11 on v10

--- a/solution.py
+++ b/solution.py
@@ -226,6 +226,83 @@
     last[...] = result[result.shape[0] - 1]
 
 
+def multiply_lines(left, right, out):
+    block = right.shape[0]
+    group = max(g for g in (1, 2, 3, 4) if block % g == 0)
+    unroll = max(u for u in (1, 2, 4, 8) if block % u == 0)
+
+    def rows(step, carry):
+        start = step * group
+
+        def add(j, totals):
+            row = right[j]
+            return tuple(
+                total + left[start + q, pl.ds(j, 1), :] * row for q, total in enumerate(totals)
+            )
+
+        zero = jnp.zeros(right.shape[1:], jnp.float32)
+        totals = lax.fori_loop(0, block, add, (zero,) * group, unroll=unroll)
+        for q, total in enumerate(totals):
+            out[start + q] = total
+        return carry
+
+    lax.fori_loop(0, block // group, rows, 0)
+
+
+def on_last(body):
+    pl.when(lax.axis_index("line") == lax.axis_size("line") - 1)(body)
+
+
+def factor_kernel(lower, pivot, after, factor, out):
+    def body():
+        multiply_lines(lower.at[0], pivot.at[0], factor)
+        multiply_lines(factor, lower.at[1], out)
+
+    on_last(body)
+
+
+def response_kernel(factor, given, upper, pivot, after, out, work):
+    def body():
+        multiply_lines(given, pivot.at[1], out)
+        multiply_lines(out, upper.at[0], work)
+        multiply_lines(work, pivot.at[0], out)
+
+        def row(i, carry):
+            out[i] = out[i] + factor[i]
+            return carry
+
+        lax.fori_loop(0, out.shape[0], row, 0, unroll=4)
+
+    on_last(body)
+
+
+def alone_kernel(forward, upper, pivot, outgoing, result, coupled):
+    run_up(forward, upper, pivot, None, result, coupled)
+    outgoing[...] = result[0]
+
+
+def short_turn_kernel(parts, vector, lower, pivot, upper, response, alone, last, *refs):
+    carried_in = refs[:parts]
+    carried, message, upward, outgoing, forward, entry, work, result, coupled = refs[parts:]
+    add_up(carried_in, carried)
+    set_entry(carried, entry)
+    run_down(vector, lower, pivot, entry, forward, work)
+    message[0] = forward[forward.shape[0] - 1]
+    message[1] = last[...]
+    entry[...] = message[1] - message[0]
+    upward[...] = alone[...] + apply_turned(response, entry)
+    run_up(forward, upper, pivot, upward, result, coupled)
+    outgoing[...] = result[0]
+
+
+def forward_kernel(parts, vector, lower, pivot, *refs):
+    carried_in = refs[:parts]
+    carried, forward, entry, work = refs[parts:]
+    add_up(carried_in, carried)
+    set_entry(carried, entry)
+    run_down(vector, lower, pivot, entry, forward, work)
+
+
 def own_kernel(vector, carried, lower, diag_block, direction, coupled, whole, image):
     for k in range(vector.shape[0]):
         value = vector[k]
@@ -238,9 +315,12 @@
         image[k] = value
 
 
-def near_kernel(image, near_block, near, out):
+def near_kernel(image, near_block, near, *refs):
+    *below, out = refs
     for k in range(image.shape[0]):
         out[k] = image[k] + apply_turned(near_block.at[k], near.at[k])
+    if below:
+        out[0] = out[0] + apply_turned(below[0].at[0], below[1])
 
 
 def next_kernel(image, far_block, far, lower, pivot, last, out, message, forward, work):
@@ -273,13 +353,10 @@
     out[...] = sums
 
 
-def last_kernel(image, far_block, far, lower, below, sums_in, *refs):
+def last_kernel(image, far_block, far, sums_in, *refs):
     *basis, out, newest = refs
     for k in range(image.shape[0]):
-        value = image[k] + apply_turned(far_block.at[k], far.at[k])
-        if k == 0:
-            value = value + apply_turned(lower.at[0], below)
-        newest[k] = value
+        newest[k] = image[k] + apply_turned(far_block.at[k], far.at[k])
     sums = sums_in[...]
     row = lax.broadcasted_iota(jnp.int32, sums.shape, 0)
     lane = lax.broadcasted_iota(jnp.int32, sums.shape, 1)
@@ -347,6 +424,55 @@
     return near, far
 
 
+def sweep_short(vector, message, alone_forward, last, lower, pivot, upper, response):
+    line = lax.axis_size("line")
+    field, one = vector.shape, last.shape
+    parts = []
+    for turn in range(line - 2):
+        parts.append(lax.ppermute(message, "line", [(turn, turn + 1)]))
+        if turn == 0:
+            (alone,) = stage(
+                alone_kernel, [one], [alone_forward, upper, pivot], [field, field]
+            )
+            alone = lax.ppermute(alone, "line", [(line - 1, line - 2)])
+        if turn < line - 3:
+            carried, message = stage(
+                functools.partial(hop_down_kernel, len(parts), True),
+                [message.shape, message.shape],
+                [vector, lower, pivot, *parts, last],
+                [one, field, one],
+            )
+            parts = [carried]
+    carried_down, message, upward, outgoing, forward = stage(
+        functools.partial(short_turn_kernel, len(parts)),
+        [message.shape, message.shape, one, one, field],
+        [vector, lower, pivot, upper, response, alone, last, *parts],
+        [one, one, field, field],
+    )
+    parts = [upward]
+    for turn in reversed(range(line - 2)):
+        if turn == 0:
+            outgoing, message = lax.optimization_barrier((outgoing, message))
+        parts.append(lax.ppermute(outgoing, "line", [(turn + 1, turn)]))
+        if turn == 0:
+            onward = lax.ppermute(message, "line", [(line - 2, line - 1)])
+            carried_down, whole_forward = stage(
+                functools.partial(forward_kernel, 2),
+                [message.shape, field],
+                [vector, lower, pivot, carried_down, onward],
+                [one, one],
+            )
+        if turn > 0:
+            carried, outgoing = stage(
+                functools.partial(hop_up_kernel, len(parts)),
+                [one, one],
+                [forward, upper, pivot, *parts],
+                [field, field],
+            )
+            parts = [carried]
+    return carried_down, whole_forward, parts
+
+
 def per_device(newton_residual, diag_block, lower, upper, west, east, pivot_inverse):
     shape = newton_residual.shape
     count, block, rows, across = shape
@@ -367,42 +493,66 @@
     basis = []
     directions = []
     last = None
+    short = line > 2 and count == 2
     for j in range(ITERS):
-        parts = []
-        for turn in range(line - 1):
-            parts.append(lax.ppermute(message, "line", [(turn, turn + 1)]))
-            if j == 0 and turn == 0:
-                (upper,) = load((upper,), message)
-            if turn < line - 2:
-                lasts = [] if last is None else [last]
-                carried, message = stage(
-                    functools.partial(hop_down_kernel, len(parts), bool(lasts)),
-                    [message.shape, message.shape],
-                    [vector, lower, pivot, *parts, *lasts],
-                    [one, field, one],
-                )
-                parts = [carried]
-        parts = parts or [jnp.zeros_like(message)]
-        carried_down, forward, outgoing = stage(
-            functools.partial(turn_kernel, len(parts)),
-            [message.shape, field, one],
-            [vector, lower, pivot, upper, *parts],
-            [one, one, field, field],
-        )
-        parts = []
-        for turn in reversed(range(line - 1)):
-            parts.append(lax.ppermute(outgoing, "line", [(turn + 1, turn)]))
-            if j == 0 and turn == line - 2:
-                diag_block, near_block, far_block = load((diag_block, east, west), outgoing, True)
-            if turn > 0:
-                carried, outgoing = stage(
-                    functools.partial(hop_up_kernel, len(parts)),
-                    [one, one],
-                    [forward, upper, pivot, *parts],
-                    [field, field],
-                )
-                parts = [carried]
-        parts = parts or [jnp.zeros_like(outgoing)]
+        if j >= 2 and short:
+            carried_down, forward, parts = sweep_short(
+                vector, message, alone_forward, last, lower, pivot, upper, response
+            )
+        else:
+            parts = []
+            for turn in range(line - 1):
+                parts.append(lax.ppermute(message, "line", [(turn, turn + 1)]))
+                if j == 0 and turn == 0:
+                    (upper,) = load((upper,), message)
+                if j == 0 and turn == line - 2 and short:
+                    factor, response = stage(
+                        factor_kernel, [(block,) + one] * 2, [lower, pivot, message]
+                    )
+                if turn < line - 2:
+                    lasts = [] if last is None else [last]
+                    carried, message = stage(
+                        functools.partial(hop_down_kernel, len(parts), bool(lasts)),
+                        [message.shape, message.shape],
+                        [vector, lower, pivot, *parts, *lasts],
+                        [one, field, one],
+                    )
+                    parts = [carried]
+            parts = parts or [jnp.zeros_like(message)]
+            carried_down, forward, outgoing = stage(
+                functools.partial(turn_kernel, len(parts)),
+                [message.shape, field, one],
+                [vector, lower, pivot, upper, *parts],
+                [one, one, field, field],
+            )
+            if j == 0 and short:
+                outgoing, response = lax.optimization_barrier((outgoing, response))
+            parts = []
+            for turn in reversed(range(line - 1)):
+                if j == 1 and turn == line - 3 and short:
+                    outgoing, ready = lax.optimization_barrier((outgoing, response))
+                    response = lax.ppermute(ready, "line", [(line - 1, line - 2)])
+                parts.append(lax.ppermute(outgoing, "line", [(turn + 1, turn)]))
+                if j == 0 and turn == line - 2:
+                    diag_block, near_block, far_block = load(
+                        (diag_block, east, west), outgoing, True
+                    )
+                if j == 0 and turn == line - 3 and short:
+                    (response,) = stage(
+                        response_kernel,
+                        [(block,) + one],
+                        [factor, response, upper, pivot, outgoing],
+                        [(block,) + one],
+                    )
+                if turn > 0:
+                    carried, outgoing = stage(
+                        functools.partial(hop_up_kernel, len(parts)),
+                        [one, one],
+                        [forward, upper, pivot, *parts],
+                        [field, field],
+                    )
+                    parts = [carried]
+            parts = parts or [jnp.zeros_like(outgoing)]
         direction, coupled, last = stage(
             functools.partial(end_kernel, len(parts)),
             [field, field, one],
@@ -411,27 +561,34 @@
         )
         directions.append(direction)
         near, far = rows_beside(direction, across)
+        if j == 1 and short:
+            near, response = lax.optimization_barrier((near, response))
         whole, image = stage(
             own_kernel,
             [field, field],
             [vector, carried_down, lower, diag_block, direction, coupled],
         )
         basis.append(whole)
-        (image,) = stage(near_kernel, [field], [image, near_block, near])
+        beneath = []
+        if j == ITERS - 1:
+            (sums,) = stage(sums_kernel, [(SUMS, wide)], basis)
+            below = lax.ppermute(last, "line", [(i, i + 1) for i in range(line - 1)])
+            beneath = [lower, below]
+        (image,) = stage(near_kernel, [field], [image, near_block, near, *beneath])
         if j < ITERS - 1:
-            vector, message = stage(
+            vector, message, alone_forward = stage(
                 next_kernel,
-                [field, (2,) + one],
+                [field, (2,) + one, field],
                 [image, far_block, far, lower, pivot, last],
-                [field, one],
-            )
+                [one],
+            )
+            if j == 0 and short:
+                message, response = lax.optimization_barrier((message, response))
         else:
-            below = lax.ppermute(last, "line", [(i, i + 1) for i in range(line - 1)])
-            (sums,) = stage(sums_kernel, [(SUMS, wide)], basis)
             (sums,) = stage(
                 last_kernel,
                 [(devices, wide)],
-                [image, far_block, far, lower, below, sums, *basis],
+                [image, far_block, far, sums, *basis],
                 [field],
             )
     sums = lax.all_to_all(sums, ("line", "patch"), 0, 0, tiled=True)

time: 162 us -> 157 us (0.969)
  starting transfers between devices: 34.5 us -> 32.1 us
  waiting for transfers between devices: 83.5 us -> 81.8 us
  blocking collectives: 19.7 us -> 18 us
    ppermute x0 -> x13, waiting for transfers between devices: none -> 40.1 us  [the longest x4 36.6 us: sweep_short(): parts.append(lax.ppermute(outgoing, 'line', [(turn + 1, turn)]))]
    ppermute x12 -> x6, waiting for transfers between devices: 76.8 us -> 38 us  [per_device(): parts.append(lax.ppermute(outgoing, 'line', [(turn + 1, turn)]))]
    ppermute x0 -> x13, starting transfers between devices: none -> 11.9 us  [the longest x4 4.58 us: sweep_short(): parts.append(lax.ppermute(message, 'line', [(turn, turn + 1)]))]
    ppermute x12 -> x6, starting transfers between devices: 15.1 us -> 9.11 us  [per_device(): parts.append(lax.ppermute(message, 'line', [(turn, turn + 1)]))]
    ppermute x12 -> x6, starting transfers between devices: 10.5 us -> 5.42 us  [per_device(): parts.append(lax.ppermute(outgoing, 'line', [(turn + 1, turn)]))]
    ppermute x12 -> x6, waiting for transfers between devices: 5.99 us -> 2.52 us  [per_device(): parts.append(lax.ppermute(message, 'line', [(turn, turn + 1)]))]
    ppermute x4, starting transfers between devices: 4.11 us -> 0.98 us  [rows_beside(): near = lax.ppermute(to_near, 'patch', even + [(b, a) for a, b in even])]
    all_to_all x1, blocking collectives: 19.7 us -> 18 us  [per_device(): sums = lax.all_to_all(sums, ('line', 'patch'), 0, 0, tiled=True)]
  transfers between devices with their start and end apart: 33 -> 34, of which waited for: 9 -> 11; matrix products, arithmetic and copies ran while one was open for 0% -> 0% of each run, Pallas kernels for 4% -> 5%
where the time goes in v11:
time: 157 us; the launch traced here: 156 us
  waiting for transfers between devices  81.8 us (52%)
  starting transfers between devices  32.1 us (20%)
  Pallas kernels  22.6 us (14%)
  blocking collectives  18 us (11%)
    ppermute x6, waiting for transfers between devices, per_device(): parts.append(lax.ppermute(outgoing, 'line', [(turn + 1, turn)]))  38 us
    ppermute x4, waiting for transfers between devices, sweep_short(): parts.append(lax.ppermute(outgoing, 'line', [(turn + 1, turn)]))  36.6 us
    all_to_all x1, blocking collectives, per_device(): sums = lax.all_to_all(sums, ('line', 'patch'), 0, 0, tiled=True)  18 us
    pallas_call x40, Pallas kernels, stage(): pl.pallas_call(kernel, out_shape=[jax.ShapeDtypeStruct(shape, jnp.float32...  16.6 us
    ppermute x6, starting transfers between devices, per_device(): parts.append(lax.ppermute(message, 'line', [(turn, turn + 1)]))  9.11 us
    ppermute x6, starting transfers between devices, per_device(): parts.append(lax.ppermute(outgoing, 'line', [(turn + 1, turn)]))  5.42 us
    ppermute x4, starting transfers between devices, sweep_short(): parts.append(lax.ppermute(message, 'line', [(turn, turn + 1)]))  4.58 us
    ppermute x4, starting transfers between devices, sweep_short(): parts.append(lax.ppermute(outgoing, 'line', [(turn + 1, turn)]))  3.91 us
  transfers between devices with their start and end apart: 34, of which 11 were waited for; matrix products, arithmetic and copies ran while one was open for 0% of the time, Pallas kernels for 5%

profile of v11, /device:TPU:0, one launch (start us, length us, event | category | flops | bytes accessed | tf_op | source)
XLA Modules:
  0.0 156.0 jit_solution(10786862979726270858)
XLA Ops:
  0.0 2.3 %shard_map.73 = (bf16[2,48,48,128]{3,2,1,0:T(8,128)(2,1)S(1)}, bf16[2,48,48,128]{3,2,1,0:T(8,128)(2,1)S(1)}, f32[1,48,128]{2,1,0:T(8,128)}) custom-call(f32[2,48,128]{2,1,0:T(8,128)} %bitcast.14, bf16[2,48,48,128]{3,2,1,0:T(8,128)(2,1)} %bitcast.25, bf16[2,48,48,128]{3,2,1,0:T(8,128)(2,1)} %bitcast.26), custom_call_target="tpu_custom_call" | custom-call | tf_op jit(solution)/shard_map/pallas_call | solution.py:73
  2.3 4.8 %collective-permute-start = (f32[1,48,128]{2,1,0:T(8,128)}, f32[1,48,128]{2,1,0:T(8,128)S(1)}, u32[]{:S(2)}, u32[]{:S(2)}) collective-permute-start(f32[1,48,128]{2,1,0:T(8,128)} %get-tuple-element.103.refs_1_), channel_id=1, source_target_pairs={{0,8},{1,9},{2,10},{3,11},{4,12},{5,13},{6,14},{7,15}} | collective-permute-start | bytes 73736 | tf_op jit(solution)/shard_map/ppermute | solution.py:505
  7.1 0.9 shard_map.74
  8.1 0.8 collective-permute-done.refs_0_
  9.3 0.7 collective-permute-start.1
  10.0 0.4 shard_map.77
  10.4 0.7 collective-permute-start.2
  11.2 0.7 shard_map.75.upper
  12.0 0.6 shard_map.78
  12.6 0.7 collective-permute-start.3
  13.6 0.7 collective-permute-start.4
  14.3 0.4 shard_map.82
  14.7 1.3 collective-permute-start.5
  16.0 18.0 %collective-permute-done.5.refs_1_ = f32[48,128]{1,0:T(8,128)S(1)} collective-permute-done((f32[48,128]{1,0:T(8,128)S(1)}, f32[48,128]{1,0:T(8,128)S(1)}, u32[]{:S(2)}, u32[]{:S(2)}) %collective-permute-start.5) | collective-permute-done | bytes 24608 | tf_op jit(solution)/shard_map/ppermute | solution.py:535
  34.6 0.8 collective-permute-start.7
  36.1 2.1 %shard_map.80 = (f32[2,48,48,128]{3,2,1,0:T(8,128)S(1)}, f32[2,48,48,128]{3,2,1,0:T(8,128)S(1)}, f32[2,48,48,128]{3,2,1,0:T(8,128)S(1)}) custom-call(bf16[2,48,48,128]{3,2,1,0:T(8,128)(2,1)S(1)} %bitcast.20, bf16[2,48,48,128]{3,2,1,0:T(8,128)(2,1)S(1)} %bitcast.21, bf16[2,48,48,128]{3,2,1,0:T(8,128)(2,1)S(1)} %bitcast.22, ...), custom_call_target="tpu_custom_call" | custom-call | tf_op jit(solution)/shard_map/pallas_call | solution.py:131
  38.9 1.1 shard_map.86
  40.0 1.6 %collective-permute-start.8 = (f32[2,48,128]{2,1,0:T(8,128)S(1)}, f32[2,48,128]{2,1,0:T(8,128)S(1)}, u32[]{:S(2)}, u32[]{:S(2)}) collective-permute-start(f32[2,48,128]{2,1,0:T(8,128)S(1)} %get-tuple-element.128), channel_id=1, source_target_pairs={{0,8},{1,9},{2,10},{3,11},{4,12},{5,13},{6,14},{7,15}} | collective-permute-start | bytes 147464 | tf_op jit(solution)/shard_map/ppermute | solution.py:505
  41.6 1.7 %collective-permute-done.8.refs_0_ = f32[2,48,128]{2,1,0:T(8,128)S(1)} collective-permute-done((f32[2,48,128]{2,1,0:T(8,128)S(1)}, f32[2,48,128]{2,1,0:T(8,128)S(1)}, u32[]{:S(2)}, u32[]{:S(2)}) %collective-permute-start.8) | collective-permute-done | bytes 49184 | tf_op jit(solution)/shard_map/ppermute | solution.py:505
  43.7 0.7 collective-permute-start.9
  44.4 0.4 shard_map.89
  44.8 0.7 collective-permute-start.10
  45.5 0.6 shard_map.90
  46.1 0.7 collective-permute-start.11
  47.2 0.7 collective-permute-start.15
  48.0 0.7 collective-permute-start.12
  49.0 1.5 collective-permute-start.13
  50.5 20.0 %collective-permute-done.13.refs_1_ = f32[48,128]{1,0:T(8,128)S(1)} collective-permute-done((f32[48,128]{1,0:T(8,128)S(1)}, f32[48,128]{1,0:T(8,128)S(1)}, u32[]{:S(2)}, u32[]{:S(2)}) %collective-permute-start.13) | collective-permute-done | bytes 24608 | tf_op jit(solution)/shard_map/ppermute | solution.py:535
  71.0 0.7 collective-permute-start.16
  71.7 0.5 shard_map.94
  72.4 0.5 shard_map.96
  72.9 1.6 %collective-permute-start.18 = (f32[2,48,128]{2,1,0:T(8,128)S(1)}, f32[2,48,128]{2,1,0:T(8,128)S(1)}, u32[]{:S(2)}, u32[]{:S(2)}) collective-permute-start(f32[2,48,128]{2,1,0:T(8,128)S(1)} %get-tuple-element.151), channel_id=1, source_target_pairs={{0,8},{1,9},{2,10},{3,11},{4,12},{5,13},{6,14},{7,15}} | collective-permute-start | bytes 147464 | tf_op jit(solution)/shard_map/ppermute | solution.py:432
  74.5 1.7 %collective-permute-done.18.refs_0_ = f32[2,48,128]{2,1,0:T(8,128)S(1)} collective-permute-done((f32[2,48,128]{2,1,0:T(8,128)S(1)}, f32[2,48,128]{2,1,0:T(8,128)S(1)}, u32[]{:S(2)}, u32[]{:S(2)}) %collective-permute-start.18) | collective-permute-done | bytes 49184 | tf_op jit(solution)/shard_map/ppermute | solution.py:432
  76.3 0.4 shard_map.98
  76.7 0.7 collective-permute-start.19
  77.6 0.7 collective-permute-start.17
  78.2 0.9 shard_map.99
  79.1 0.7 collective-permute-start.20
  79.8 0.4 shard_map.100
  80.2 0.7 collective-permute-start.21
  80.9 1.3 collective-permute-start.22
  82.2 0.4 shard_map.101
  82.6 25.5 %collective-permute-done.22.refs_1_ = f32[48,128]{1,0:T(8,128)S(1)} collective-permute-done((f32[48,128]{1,0:T(8,128)S(1)}, f32[48,128]{1,0:T(8,128)S(1)}, u32[]{:S(2)}, u32[]{:S(2)}) %collective-permute-start.22) | collective-permute-done | bytes 24608 | tf_op jit(solution)/shard_map/ppermute | solution.py:456
  108.7 0.7 collective-permute-start.24
  109.3 0.5 shard_map.103
  110.1 0.5 shard_map.105
  110.6 1.6 %collective-permute-start.26 = (f32[2,48,128]{2,1,0:T(8,128)S(1)}, f32[2,48,128]{2,1,0:T(8,128)S(1)}, u32[]{:S(2)}, u32[]{:S(2)}) collective-permute-start(f32[2,48,128]{2,1,0:T(8,128)S(1)} %get-tuple-element.171), channel_id=1, source_target_pairs={{0,8},{1,9},{2,10},{3,11},{4,12},{5,13},{6,14},{7,15}} | collective-permute-start | bytes 147464 | tf_op jit(solution)/shard_map/ppermute | solution.py:432
  112.2 1.7 %collective-permute-done.26.refs_0_ = f32[2,48,128]{2,1,0:T(8,128)S(1)} collective-permute-done((f32[2,48,128]{2,1,0:T(8,128)S(1)}, f32[2,48,128]{2,1,0:T(8,128)S(1)}, u32[]{:S(2)}, u32[]{:S(2)}) %collective-permute-start.26) | collective-permute-done | bytes 49184 | tf_op jit(solution)/shard_map/ppermute | solution.py:432
  114.4 0.7 collective-permute-start.27
  115.2 0.7 collective-permute-start.25
  115.9 0.9 shard_map.108
  116.8 0.7 collective-permute-start.28
  117.5 0.4 shard_map.109
  117.9 0.7 collective-permute-start.29
  118.6 1.3 collective-permute-start.30
  119.9 0.4 shard_map.110
  120.3 11.1 %collective-permute-done.30.refs_1_ = f32[48,128]{1,0:T(8,128)S(1)} collective-permute-done((f32[48,128]{1,0:T(8,128)S(1)}, f32[48,128]{1,0:T(8,128)S(1)}, u32[]{:S(2)}, u32[]{:S(2)}) %collective-permute-start.30) | collective-permute-done | bytes 24608 | tf_op jit(solution)/shard_map/ppermute | solution.py:456
  131.8 0.8 collective-permute-start.31
  132.6 0.7 collective-permute-start.33
  133.2 1.9 %collective-permute-start.32 = (f32[48,128]{1,0:T(8,128)S(1)}, f32[48,128]{1,0:T(8,128)S(1)}, u32[]{:S(2)}, u32[]{:S(2)}) collective-permute-start(f32[48,128]{1,0:T(8,128)S(1)} %get-tuple-element.188), channel_id=1, source_target_pairs={{0,8},{8,16},{16,24},{1,9},{9,17},{17,25},{2,10},{10,18},{18,26},{... | collective-permute-start | bytes 73736 | tf_op jit(solution)/shard_map/ppermute | solution.py:575
  135.2 0.4 shard_map.112
  135.6 1.0 collective-permute-done.32.refs_1_
  137.2 18.0 %all_to_all.11 = f32[32,1,128]{2,1,0:T(1,128)S(1)} all-to-all(f32[32,1,128]{2,1,0:T(1,128)S(1)} %bitcast.23), channel_id=1, replica_groups=mesh['line'=4,'patch'=8] {'line','patch'}, dimensions={0} | all-to-all | bytes 32768 | tf_op jit(solution)/shard_map/all_to_all | solution.py:594
  155.2 0.8 shard_map.116
  (61 shorter events, 7.4 us)
Async XLA Ops:
  2.3 6.6 %collective-permute-start = (f32[1,48,128]{2,1,0:T(8,128)}, f32[1,48,128]{2,1,0:T(8,128)S(1)}, u32[]{:S(2)}, u32[]{:S(2)}) collective-permute-start(f32[1,48,128]{2,1,0:T(8,128)} %get-tuple-element.103.refs_1_), channel_id=1, source_target_pairs={{0,8},{1,9},{2,10},{3,11},{4,12},{5,13},{6,14},{7,15}} | collective-permute-start | bytes 73736 | tf_op jit(solution)/shard_map/ppermute | solution.py:505
  7.1 1.7 %copy-start = (f32[2,48,1,128]{3,2,1,0:T(1,128)S(1)}, f32[2,48,1,128]{3,2,1,0:T(1,128)}, u32[]{:S(2)}) copy-start(f32[2,48,1,128]{3,2,1,0:T(1,128)} %param.7) | copy-start | bytes 147460
  9.3 0.7 collective-permute-start.1
  9.9 1.3 copy-start.1
  10.0 1.3 copy-start.5
  10.4 1.6 %collective-permute-start.2 = (f32[1,48,128]{2,1,0:T(8,128)S(1)}, f32[1,48,128]{2,1,0:T(8,128)S(1)}, u32[]{:S(2)}, u32[]{:S(2)}) collective-permute-start(f32[1,48,128]{2,1,0:T(8,128)S(1)} %get-tuple-element.107.after), channel_id=1, source_target_pairs={{16,24},{17,25},{18,26},{19,27},{20,28},{21,29},{22,30},{23,31}} | collective-permute-start | bytes 73736 | tf_op jit(solution)/shard_map/ppermute | solution.py:505
  12.6 0.7 collective-permute-start.3
  13.6 0.7 collective-permute-start.4
  14.7 19.3 %collective-permute-start.5 = (f32[48,128]{1,0:T(8,128)S(1)}, f32[48,128]{1,0:T(8,128)S(1)}, u32[]{:S(2)}, u32[]{:S(2)}) collective-permute-start(f32[48,128]{1,0:T(8,128)S(1)} %get-tuple-element.117), channel_id=1, source_target_pairs={{8,0},{9,1},{10,2},{11,3},{12,4},{13,5},{14,6},{15,7}} | collective-permute-start | bytes 73736 | tf_op jit(solution)/shard_map/ppermute | solution.py:535
  34.1 1.3 copy-start.2
  34.1 1.6 %copy-start.3 = (bf16[2,48,48,1,128]{4,2,3,1,0:T(8,128)(2,1)S(1)}, bf16[2,48,48,1,128]{4,2,3,1,0:T(8,128)(2,1)}, u32[]{:S(2)}) copy-start(bf16[2,48,48,1,128]{4,2,3,1,0:T(8,128)(2,1)} %param.12) | copy-start | bytes 3538948
  34.1 2.0 %copy-start.4 = (bf16[2,48,48,1,128]{4,2,3,1,0:T(8,128)(2,1)S(1)}, bf16[2,48,48,1,128]{4,2,3,1,0:T(8,128)(2,1)}, u32[]{:S(2)}) copy-start(bf16[2,48,48,1,128]{4,2,3,1,0:T(8,128)(2,1)} %param.11) | copy-start | bytes 3538948
  34.5 4.1 %collective-permute-start.6 = (f32[2,48,128]{2,1,0:T(8,128)S(1)}, f32[2,48,128]{2,1,0:T(8,128)S(1)}, u32[]{:S(2)}, u32[]{:S(2)}) collective-permute-start(f32[2,48,128]{2,1,0:T(8,128)S(1)} %get-tuple-element.118.direction.refs_0_), channel_id=1, source_target_pairs={{0,1},{2,3},{4,5},{6,7},{1,0},{3,2},{5,4},{7,6},{8,9},{10,11},{12,... | collective-permute-start | bytes 147464 | tf_op jit(solution)/shard_map/ppermute | solution.py:418
  34.6 4.3 %collective-permute-start.7 = (f32[2,48,128]{2,1,0:T(8,128)S(1)}, f32[2,48,128]{2,1,0:T(8,128)S(1)}, u32[]{:S(2)}, u32[]{:S(2)}) collective-permute-start(f32[2,48,128]{2,1,0:T(8,128)S(1)} %get-tuple-element.118.direction.refs_0_), channel_id=1, source_target_pairs={{1,2},{3,4},{5,6},{2,1},{4,3},{6,5},{9,10},{11,12},{13,14},{10,9},... | collective-permute-start | bytes 147464 | tf_op jit(solution)/shard_map/ppermute | solution.py:417
  40.0 3.4 %collective-permute-start.8 = (f32[2,48,128]{2,1,0:T(8,128)S(1)}, f32[2,48,128]{2,1,0:T(8,128)S(1)}, u32[]{:S(2)}, u32[]{:S(2)}) collective-permute-start(f32[2,48,128]{2,1,0:T(8,128)S(1)} %get-tuple-element.128), channel_id=1, source_target_pairs={{0,8},{1,9},{2,10},{3,11},{4,12},{5,13},{6,14},{7,15}} | collective-permute-start | bytes 147464 | tf_op jit(solution)/shard_map/ppermute | solution.py:505
  43.7 0.7 collective-permute-start.9
  44.8 0.7 collective-permute-start.10
  46.1 0.7 collective-permute-start.11
  47.2 25.0 %collective-permute-start.15 = (f32[48,48,128]{2,1,0:T(8,128)S(1)}, f32[48,48,128]{2,1,0:T(8,128)S(1)}, u32[]{:S(2)}, u32[]{:S(2)}) collective-permute-start(f32[48,48,128]{2,1,0:T(8,128)S(1)} %shard_map.87), channel_id=1, source_target_pairs={{24,16},{25,17},{26,18},{27,19},{28,20},{29,21},{30,22},{31,23}} | collective-permute-start | bytes 3538952 | tf_op jit(solution)/shard_map/ppermute | solution.py:534
  48.0 0.7 collective-permute-start.12
  49.0 21.5 %collective-permute-start.13 = (f32[48,128]{1,0:T(8,128)S(1)}, f32[48,128]{1,0:T(8,128)S(1)}, u32[]{:S(2)}, u32[]{:S(2)}) collective-permute-start(f32[48,128]{1,0:T(8,128)S(1)} %get-tuple-element.141), channel_id=1, source_target_pairs={{8,0},{9,1},{10,2},{11,3},{12,4},{13,5},{14,6},{15,7}} | collective-permute-start | bytes 73736 | tf_op jit(solution)/shard_map/ppermute | solution.py:535
  70.9 1.3 collective-permute-start.14
  71.0 1.4 collective-permute-start.16
  72.9 3.4 %collective-permute-start.18 = (f32[2,48,128]{2,1,0:T(8,128)S(1)}, f32[2,48,128]{2,1,0:T(8,128)S(1)}, u32[]{:S(2)}, u32[]{:S(2)}) collective-permute-start(f32[2,48,128]{2,1,0:T(8,128)S(1)} %get-tuple-element.151), channel_id=1, source_target_pairs={{0,8},{1,9},{2,10},{3,11},{4,12},{5,13},{6,14},{7,15}} | collective-permute-start | bytes 147464 | tf_op jit(solution)/shard_map/ppermute | solution.py:432
  76.7 1.6 %collective-permute-start.19 = (f32[2,48,128]{2,1,0:T(8,128)S(1)}, f32[2,48,128]{2,1,0:T(8,128)S(1)}, u32[]{:S(2)}, u32[]{:S(2)}) collective-permute-start(f32[2,48,128]{2,1,0:T(8,128)S(1)} %get-tuple-element.153), channel_id=1, source_target_pairs={{8,16},{9,17},{10,18},{11,19},{12,20},{13,21},{14,22},{15,23}} | collective-permute-start | bytes 147464 | tf_op jit(solution)/shard_map/ppermute | solution.py:432
  77.6 0.7 collective-permute-start.17
  79.1 0.7 collective-permute-start.20
  80.2 2.0 %collective-permute-start.21 = (f32[2,48,128]{2,1,0:T(8,128)S(1)}, f32[2,48,128]{2,1,0:T(8,128)S(1)}, u32[]{:S(2)}, u32[]{:S(2)}) collective-permute-start(f32[2,48,128]{2,1,0:T(8,128)S(1)} %get-tuple-element.160), channel_id=1, source_target_pairs={{16,24},{17,25},{18,26},{19,27},{20,28},{21,29},{22,30},{23,31}} | collective-permute-start | bytes 147464 | tf_op jit(solution)/shard_map/ppermute | solution.py:458
  80.9 27.3 %collective-permute-start.22 = (f32[48,128]{1,0:T(8,128)S(1)}, f32[48,128]{1,0:T(8,128)S(1)}, u32[]{:S(2)}, u32[]{:S(2)}) collective-permute-start(f32[48,128]{1,0:T(8,128)S(1)} %get-tuple-element.164), channel_id=1, source_target_pairs={{8,0},{9,1},{10,2},{11,3},{12,4},{13,5},{14,6},{15,7}} | collective-permute-start | bytes 73736 | tf_op jit(solution)/shard_map/ppermute | solution.py:456
  108.6 1.3 collective-permute-start.23
  108.7 1.4 collective-permute-start.24
  110.6 3.4 %collective-permute-start.26 = (f32[2,48,128]{2,1,0:T(8,128)S(1)}, f32[2,48,128]{2,1,0:T(8,128)S(1)}, u32[]{:S(2)}, u32[]{:S(2)}) collective-permute-start(f32[2,48,128]{2,1,0:T(8,128)S(1)} %get-tuple-element.171), channel_id=1, source_target_pairs={{0,8},{1,9},{2,10},{3,11},{4,12},{5,13},{6,14},{7,15}} | collective-permute-start | bytes 147464 | tf_op jit(solution)/shard_map/ppermute | solution.py:432
  114.4 1.6 %collective-permute-start.27 = (f32[2,48,128]{2,1,0:T(8,128)S(1)}, f32[2,48,128]{2,1,0:T(8,128)S(1)}, u32[]{:S(2)}, u32[]{:S(2)}) collective-permute-start(f32[2,48,128]{2,1,0:T(8,128)S(1)} %get-tuple-element.173), channel_id=1, source_target_pairs={{8,16},{9,17},{10,18},{11,19},{12,20},{13,21},{14,22},{15,23}} | collective-permute-start | bytes 147464 | tf_op jit(solution)/shard_map/ppermute | solution.py:432
  115.2 0.7 collective-permute-start.25
  116.8 0.7 collective-permute-start.28
  117.9 2.0 %collective-permute-start.29 = (f32[2,48,128]{2,1,0:T(8,128)S(1)}, f32[2,48,128]{2,1,0:T(8,128)S(1)}, u32[]{:S(2)}, u32[]{:S(2)}) collective-permute-start(f32[2,48,128]{2,1,0:T(8,128)S(1)} %get-tuple-element.180), channel_id=1, source_target_pairs={{16,24},{17,25},{18,26},{19,27},{20,28},{21,29},{22,30},{23,31}} | collective-permute-start | bytes 147464 | tf_op jit(solution)/shard_map/ppermute | solution.py:458
  118.6 12.8 %collective-permute-start.30 = (f32[48,128]{1,0:T(8,128)S(1)}, f32[48,128]{1,0:T(8,128)S(1)}, u32[]{:S(2)}, u32[]{:S(2)}) collective-permute-start(f32[48,128]{1,0:T(8,128)S(1)} %get-tuple-element.184), channel_id=1, source_target_pairs={{8,0},{9,1},{10,2},{11,3},{12,4},{13,5},{14,6},{15,7}} | collective-permute-start | bytes 73736 | tf_op jit(solution)/shard_map/ppermute | solution.py:456
  131.8 4.9 %collective-permute-start.31 = (f32[2,48,128]{2,1,0:T(8,128)S(1)}, f32[2,48,128]{2,1,0:T(8,128)S(1)}, u32[]{:S(2)}, u32[]{:S(2)}) collective-permute-start(f32[2,48,128]{2,1,0:T(8,128)S(1)} %get-tuple-element.185.direction.refs_3_), channel_id=1, source_target_pairs={{0,1},{2,3},{4,5},{6,7},{1,0},{3,2},{5,4},{7,6},{8,9},{10,11},{12,... | collective-permute-start | bytes 147464 | tf_op jit(solution)/shard_map/ppermute | solution.py:418
  132.6 4.4 %collective-permute-start.33 = (f32[2,48,128]{2,1,0:T(8,128)S(1)}, f32[2,48,128]{2,1,0:T(8,128)S(1)}, u32[]{:S(2)}, u32[]{:S(2)}) collective-permute-start(f32[2,48,128]{2,1,0:T(8,128)S(1)} %get-tuple-element.185.direction.refs_3_), channel_id=1, source_target_pairs={{1,2},{3,4},{5,6},{2,1},{4,3},{6,5},{9,10},{11,12},{13,14},{10,9},... | collective-permute-start | bytes 147464 | tf_op jit(solution)/shard_map/ppermute | solution.py:417
  133.2 3.4 %collective-permute-start.32 = (f32[48,128]{1,0:T(8,128)S(1)}, f32[48,128]{1,0:T(8,128)S(1)}, u32[]{:S(2)}, u32[]{:S(2)}) collective-permute-start(f32[48,128]{1,0:T(8,128)S(1)} %get-tuple-element.188), channel_id=1, source_target_pairs={{0,8},{8,16},{16,24},{1,9},{9,17},{17,25},{2,10},{10,18},{18,26},{... | collective-permute-start | bytes 73736 | tf_op jit(solution)/shard_map/ppermute | solution.py:575

commit v12 on v11

--- a/solution.py
+++ b/solution.py
@@ -561,8 +561,6 @@
         )
         directions.append(direction)
         near, far = rows_beside(direction, across)
-        if j == 1 and short:
-            near, response = lax.optimization_barrier((near, response))
         whole, image = stage(
             own_kernel,
             [field, field],

time: 157 us -> 148 us (0.943)
  waiting for transfers between devices: 81.8 us -> 73.5 us
    ppermute x4, waiting for transfers between devices: 36.6 us -> 28.3 us  [sweep_short(): parts.append(lax.ppermute(outgoing, 'line', [(turn + 1, turn)]))]
  transfers between devices with their start and end apart: 34 -> 34, of which waited for: 11 -> 11; matrix products, arithmetic and copies ran while one was open for 0% -> 0% of each run, Pallas kernels for 5% -> 6%
where the time goes in v12:
time: 148 us
  waiting for transfers between devices  73.5 us (50%)
  starting transfers between devices  32.1 us (22%)
  Pallas kernels  22.6 us (15%)
  blocking collectives  18 us (12%)
    ppermute x6, waiting for transfers between devices, per_device(): parts.append(lax.ppermute(outgoing, 'line', [(turn + 1, turn)]))  38 us
    ppermute x4, waiting for transfers between devices, sweep_short(): parts.append(lax.ppermute(outgoing, 'line', [(turn + 1, turn)]))  28.3 us
    all_to_all x1, blocking collectives, per_device(): sums = lax.all_to_all(sums, ('line', 'patch'), 0, 0, tiled=True)  18 us
    pallas_call x40, Pallas kernels, stage(): pl.pallas_call(kernel, out_shape=[jax.ShapeDtypeStruct(shape, jnp.float32...  16.6 us
    ppermute x6, starting transfers between devices, per_device(): parts.append(lax.ppermute(message, 'line', [(turn, turn + 1)]))  9.11 us
    ppermute x6, starting transfers between devices, per_device(): parts.append(lax.ppermute(outgoing, 'line', [(turn + 1, turn)]))  5.42 us
    ppermute x4, starting transfers between devices, sweep_short(): parts.append(lax.ppermute(message, 'line', [(turn, turn + 1)]))  4.58 us
    ppermute x4, starting transfers between devices, sweep_short(): parts.append(lax.ppermute(outgoing, 'line', [(turn + 1, turn)]))  3.91 us
  transfers between devices with their start and end apart: 34, of which 11 were waited for; matrix products, arithmetic and copies ran while one was open for 0% of the time, Pallas kernels for 6%

profile of v12, /device:TPU:0, one launch (start us, length us, event | category | flops | bytes accessed | tf_op | source)
XLA Modules:
  0.0 147.7 jit_solution(1140549824860071802)
XLA Ops:
  0.0 2.3 %shard_map.73 = (bf16[2,48,48,128]{3,2,1,0:T(8,128)(2,1)S(1)}, bf16[2,48,48,128]{3,2,1,0:T(8,128)(2,1)S(1)}, f32[1,48,128]{2,1,0:T(8,128)}) custom-call(f32[2,48,128]{2,1,0:T(8,128)} %bitcast.14, bf16[2,48,48,128]{3,2,1,0:T(8,128)(2,1)} %bitcast.25, bf16[2,48,48,128]{3,2,1,0:T(8,128)(2,1)} %bitcast.26), custom_call_target="tpu_custom_call" | custom-call | tf_op jit(solution)/shard_map/pallas_call | solution.py:73
  2.3 4.8 %collective-permute-start = (f32[1,48,128]{2,1,0:T(8,128)}, f32[1,48,128]{2,1,0:T(8,128)S(1)}, u32[]{:S(2)}, u32[]{:S(2)}) collective-permute-start(f32[1,48,128]{2,1,0:T(8,128)} %get-tuple-element.101.refs_1_), channel_id=1, source_target_pairs={{0,8},{1,9},{2,10},{3,11},{4,12},{5,13},{6,14},{7,15}} | collective-permute-start | bytes 73736 | tf_op jit(solution)/shard_map/ppermute | solution.py:505
  7.1 0.9 shard_map.74
  8.1 0.8 collective-permute-done.refs_0_
  9.3 0.7 collective-permute-start.1
  10.0 0.4 shard_map.77
  10.4 0.7 collective-permute-start.2
  11.2 0.7 shard_map.75.upper
  12.0 0.6 shard_map.78
  12.6 0.7 collective-permute-start.3
  13.6 0.7 collective-permute-start.4
  14.3 0.4 shard_map.82
  14.7 1.3 collective-permute-start.5
  16.0 18.0 %collective-permute-done.5.refs_1_ = f32[48,128]{1,0:T(8,128)S(1)} collective-permute-done((f32[48,128]{1,0:T(8,128)S(1)}, f32[48,128]{1,0:T(8,128)S(1)}, u32[]{:S(2)}, u32[]{:S(2)}) %collective-permute-start.5) | collective-permute-done | bytes 24608 | tf_op jit(solution)/shard_map/ppermute | solution.py:535
  34.6 0.8 collective-permute-start.7
  36.1 2.1 %shard_map.80 = (f32[2,48,48,128]{3,2,1,0:T(8,128)S(1)}, f32[2,48,48,128]{3,2,1,0:T(8,128)S(1)}, f32[2,48,48,128]{3,2,1,0:T(8,128)S(1)}) custom-call(bf16[2,48,48,128]{3,2,1,0:T(8,128)(2,1)S(1)} %bitcast.20, bf16[2,48,48,128]{3,2,1,0:T(8,128)(2,1)S(1)} %bitcast.21, bf16[2,48,48,128]{3,2,1,0:T(8,128)(2,1)S(1)} %bitcast.22, ...), custom_call_target="tpu_custom_call" | custom-call | tf_op jit(solution)/shard_map/pallas_call | solution.py:131
  38.9 1.1 shard_map.86
  40.0 1.6 %collective-permute-start.8 = (f32[2,48,128]{2,1,0:T(8,128)S(1)}, f32[2,48,128]{2,1,0:T(8,128)S(1)}, u32[]{:S(2)}, u32[]{:S(2)}) collective-permute-start(f32[2,48,128]{2,1,0:T(8,128)S(1)} %get-tuple-element.126), channel_id=1, source_target_pairs={{0,8},{1,9},{2,10},{3,11},{4,12},{5,13},{6,14},{7,15}} | collective-permute-start | bytes 147464 | tf_op jit(solution)/shard_map/ppermute | solution.py:505
  41.6 1.7 %collective-permute-done.8.refs_0_ = f32[2,48,128]{2,1,0:T(8,128)S(1)} collective-permute-done((f32[2,48,128]{2,1,0:T(8,128)S(1)}, f32[2,48,128]{2,1,0:T(8,128)S(1)}, u32[]{:S(2)}, u32[]{:S(2)}) %collective-permute-start.8) | collective-permute-done | bytes 49184 | tf_op jit(solution)/shard_map/ppermute | solution.py:505
  43.7 0.7 collective-permute-start.9
  44.4 0.4 shard_map.89
  44.8 0.7 collective-permute-start.10
  45.5 0.6 shard_map.90
  46.1 0.7 collective-permute-start.11
  47.2 0.7 collective-permute-start.16
  48.0 0.7 collective-permute-start.12
  49.0 1.5 collective-permute-start.13
  50.5 20.0 %collective-permute-done.13.refs_1_ = f32[48,128]{1,0:T(8,128)S(1)} collective-permute-done((f32[48,128]{1,0:T(8,128)S(1)}, f32[48,128]{1,0:T(8,128)S(1)}, u32[]{:S(2)}, u32[]{:S(2)}) %collective-permute-start.13) | collective-permute-done | bytes 24608 | tf_op jit(solution)/shard_map/ppermute | solution.py:535
  71.0 0.7 collective-permute-start.15
  71.7 0.5 shard_map.94
  72.4 0.5 shard_map.96
  72.9 1.6 %collective-permute-start.18 = (f32[2,48,128]{2,1,0:T(8,128)S(1)}, f32[2,48,128]{2,1,0:T(8,128)S(1)}, u32[]{:S(2)}, u32[]{:S(2)}) collective-permute-start(f32[2,48,128]{2,1,0:T(8,128)S(1)} %get-tuple-element.147), channel_id=1, source_target_pairs={{0,8},{1,9},{2,10},{3,11},{4,12},{5,13},{6,14},{7,15}} | collective-permute-start | bytes 147464 | tf_op jit(solution)/shard_map/ppermute | solution.py:432
  74.5 1.7 %collective-permute-done.18.refs_0_ = f32[2,48,128]{2,1,0:T(8,128)S(1)} collective-permute-done((f32[2,48,128]{2,1,0:T(8,128)S(1)}, f32[2,48,128]{2,1,0:T(8,128)S(1)}, u32[]{:S(2)}, u32[]{:S(2)}) %collective-permute-start.18) | collective-permute-done | bytes 49184 | tf_op jit(solution)/shard_map/ppermute | solution.py:432
  76.2 0.4 shard_map.98
  76.7 0.7 collective-permute-start.19
  77.5 0.7 collective-permute-start.17
  78.2 0.9 shard_map.99
  79.1 0.7 collective-permute-start.20
  79.8 0.4 shard_map.100
  80.2 0.7 collective-permute-start.21
  80.9 1.3 collective-permute-start.22
  82.2 0.4 shard_map.101
  82.6 17.2 %collective-permute-done.22.refs_1_ = f32[48,128]{1,0:T(8,128)S(1)} collective-permute-done((f32[48,128]{1,0:T(8,128)S(1)}, f32[48,128]{1,0:T(8,128)S(1)}, u32[]{:S(2)}, u32[]{:S(2)}) %collective-permute-start.22) | collective-permute-done | bytes 24608 | tf_op jit(solution)/shard_map/ppermute | solution.py:456
  100.3 0.7 collective-permute-start.24
  101.0 0.5 shard_map.103
  101.8 0.5 shard_map.105
  102.2 1.6 %collective-permute-start.26 = (f32[2,48,128]{2,1,0:T(8,128)S(1)}, f32[2,48,128]{2,1,0:T(8,128)S(1)}, u32[]{:S(2)}, u32[]{:S(2)}) collective-permute-start(f32[2,48,128]{2,1,0:T(8,128)S(1)} %get-tuple-element.167), channel_id=1, source_target_pairs={{0,8},{1,9},{2,10},{3,11},{4,12},{5,13},{6,14},{7,15}} | collective-permute-start | bytes 147464 | tf_op jit(solution)/shard_map/ppermute | solution.py:432
  103.9 1.7 %collective-permute-done.26.refs_0_ = f32[2,48,128]{2,1,0:T(8,128)S(1)} collective-permute-done((f32[2,48,128]{2,1,0:T(8,128)S(1)}, f32[2,48,128]{2,1,0:T(8,128)S(1)}, u32[]{:S(2)}, u32[]{:S(2)}) %collective-permute-start.26) | collective-permute-done | bytes 49184 | tf_op jit(solution)/shard_map/ppermute | solution.py:432
  106.0 0.7 collective-permute-start.27
  106.9 0.7 collective-permute-start.25
  107.6 0.9 shard_map.108
  108.5 0.7 collective-permute-start.28
  109.2 0.4 shard_map.109
  109.6 0.7 collective-permute-start.29
  110.3 1.3 collective-permute-start.30
  111.6 0.4 shard_map.110
  112.0 11.1 %collective-permute-done.30.refs_1_ = f32[48,128]{1,0:T(8,128)S(1)} collective-permute-done((f32[48,128]{1,0:T(8,128)S(1)}, f32[48,128]{1,0:T(8,128)S(1)}, u32[]{:S(2)}, u32[]{:S(2)}) %collective-permute-start.30) | collective-permute-done | bytes 24608 | tf_op jit(solution)/shard_map/ppermute | solution.py:456
  123.5 0.8 collective-permute-start.31
  124.3 0.7 collective-permute-start.33
  125.0 1.9 %collective-permute-start.32 = (f32[48,128]{1,0:T(8,128)S(1)}, f32[48,128]{1,0:T(8,128)S(1)}, u32[]{:S(2)}, u32[]{:S(2)}) collective-permute-start(f32[48,128]{1,0:T(8,128)S(1)} %get-tuple-element.184), channel_id=1, source_target_pairs={{0,8},{8,16},{16,24},{1,9},{9,17},{17,25},{2,10},{10,18},{18,26},{... | collective-permute-start | bytes 73736 | tf_op jit(solution)/shard_map/ppermute | solution.py:573
  126.9 0.4 shard_map.112
  127.4 1.0 collective-permute-done.32.refs_1_
  128.9 18.0 %all_to_all.11 = f32[32,1,128]{2,1,0:T(1,128)S(1)} all-to-all(f32[32,1,128]{2,1,0:T(1,128)S(1)} %bitcast.23), channel_id=1, replica_groups=mesh['line'=4,'patch'=8] {'line','patch'}, dimensions={0} | all-to-all | bytes 32768 | tf_op jit(solution)/shard_map/all_to_all | solution.py:592
  146.9 0.8 shard_map.116
  (61 shorter events, 7.4 us)
Async XLA Ops:
  2.3 6.6 %collective-permute-start = (f32[1,48,128]{2,1,0:T(8,128)}, f32[1,48,128]{2,1,0:T(8,128)S(1)}, u32[]{:S(2)}, u32[]{:S(2)}) collective-permute-start(f32[1,48,128]{2,1,0:T(8,128)} %get-tuple-element.101.refs_1_), channel_id=1, source_target_pairs={{0,8},{1,9},{2,10},{3,11},{4,12},{5,13},{6,14},{7,15}} | collective-permute-start | bytes 73736 | tf_op jit(solution)/shard_map/ppermute | solution.py:505
  7.1 1.7 %copy-start = (f32[2,48,1,128]{3,2,1,0:T(1,128)S(1)}, f32[2,48,1,128]{3,2,1,0:T(1,128)}, u32[]{:S(2)}) copy-start(f32[2,48,1,128]{3,2,1,0:T(1,128)} %param.7) | copy-start | bytes 147460
  9.3 0.7 collective-permute-start.1
  9.9 1.3 copy-start.1
  10.0 1.3 copy-start.5
  10.4 1.6 %collective-permute-start.2 = (f32[1,48,128]{2,1,0:T(8,128)S(1)}, f32[1,48,128]{2,1,0:T(8,128)S(1)}, u32[]{:S(2)}, u32[]{:S(2)}) collective-permute-start(f32[1,48,128]{2,1,0:T(8,128)S(1)} %get-tuple-element.105.after), channel_id=1, source_target_pairs={{16,24},{17,25},{18,26},{19,27},{20,28},{21,29},{22,30},{23,31}} | collective-permute-start | bytes 73736 | tf_op jit(solution)/shard_map/ppermute | solution.py:505
  12.6 0.7 collective-permute-start.3
  13.6 0.7 collective-permute-start.4
  14.7 19.3 %collective-permute-start.5 = (f32[48,128]{1,0:T(8,128)S(1)}, f32[48,128]{1,0:T(8,128)S(1)}, u32[]{:S(2)}, u32[]{:S(2)}) collective-permute-start(f32[48,128]{1,0:T(8,128)S(1)} %get-tuple-element.115), channel_id=1, source_target_pairs={{8,0},{9,1},{10,2},{11,3},{12,4},{13,5},{14,6},{15,7}} | collective-permute-start | bytes 73736 | tf_op jit(solution)/shard_map/ppermute | solution.py:535
  34.1 1.3 copy-start.2
  34.1 1.6 %copy-start.3 = (bf16[2,48,48,1,128]{4,2,3,1,0:T(8,128)(2,1)S(1)}, bf16[2,48,48,1,128]{4,2,3,1,0:T(8,128)(2,1)}, u32[]{:S(2)}) copy-start(bf16[2,48,48,1,128]{4,2,3,1,0:T(8,128)(2,1)} %param.12) | copy-start | bytes 3538948
  34.1 2.0 %copy-start.4 = (bf16[2,48,48,1,128]{4,2,3,1,0:T(8,128)(2,1)S(1)}, bf16[2,48,48,1,128]{4,2,3,1,0:T(8,128)(2,1)}, u32[]{:S(2)}) copy-start(bf16[2,48,48,1,128]{4,2,3,1,0:T(8,128)(2,1)} %param.11) | copy-start | bytes 3538948
  34.5 4.1 %collective-permute-start.6 = (f32[2,48,128]{2,1,0:T(8,128)S(1)}, f32[2,48,128]{2,1,0:T(8,128)S(1)}, u32[]{:S(2)}, u32[]{:S(2)}) collective-permute-start(f32[2,48,128]{2,1,0:T(8,128)S(1)} %get-tuple-element.116.direction.refs_0_), channel_id=1, source_target_pairs={{0,1},{2,3},{4,5},{6,7},{1,0},{3,2},{5,4},{7,6},{8,9},{10,11},{12,... | collective-permute-start | bytes 147464 | tf_op jit(solution)/shard_map/ppermute | solution.py:418
  34.6 4.3 %collective-permute-start.7 = (f32[2,48,128]{2,1,0:T(8,128)S(1)}, f32[2,48,128]{2,1,0:T(8,128)S(1)}, u32[]{:S(2)}, u32[]{:S(2)}) collective-permute-start(f32[2,48,128]{2,1,0:T(8,128)S(1)} %get-tuple-element.116.direction.refs_0_), channel_id=1, source_target_pairs={{1,2},{3,4},{5,6},{2,1},{4,3},{6,5},{9,10},{11,12},{13,14},{10,9},... | collective-permute-start | bytes 147464 | tf_op jit(solution)/shard_map/ppermute | solution.py:417
  40.0 3.4 %collective-permute-start.8 = (f32[2,48,128]{2,1,0:T(8,128)S(1)}, f32[2,48,128]{2,1,0:T(8,128)S(1)}, u32[]{:S(2)}, u32[]{:S(2)}) collective-permute-start(f32[2,48,128]{2,1,0:T(8,128)S(1)} %get-tuple-element.126), channel_id=1, source_target_pairs={{0,8},{1,9},{2,10},{3,11},{4,12},{5,13},{6,14},{7,15}} | collective-permute-start | bytes 147464 | tf_op jit(solution)/shard_map/ppermute | solution.py:505
  43.7 0.7 collective-permute-start.9
  44.8 0.7 collective-permute-start.10
  46.1 0.7 collective-permute-start.11
  47.2 31.0 %collective-permute-start.16 = (f32[48,48,128]{2,1,0:T(8,128)S(1)}, f32[48,48,128]{2,1,0:T(8,128)S(1)}, u32[]{:S(2)}, u32[]{:S(2)}) collective-permute-start(f32[48,48,128]{2,1,0:T(8,128)S(1)} %shard_map.87), channel_id=1, source_target_pairs={{24,16},{25,17},{26,18},{27,19},{28,20},{29,21},{30,22},{31,23}} | collective-permute-start | bytes 3538952 | tf_op jit(solution)/shard_map/ppermute | solution.py:534
  48.0 0.7 collective-permute-start.12
  49.0 21.5 %collective-permute-start.13 = (f32[48,128]{1,0:T(8,128)S(1)}, f32[48,128]{1,0:T(8,128)S(1)}, u32[]{:S(2)}, u32[]{:S(2)}) collective-permute-start(f32[48,128]{1,0:T(8,128)S(1)} %get-tuple-element.139), channel_id=1, source_target_pairs={{8,0},{9,1},{10,2},{11,3},{12,4},{13,5},{14,6},{15,7}} | collective-permute-start | bytes 73736 | tf_op jit(solution)/shard_map/ppermute | solution.py:535
  70.9 1.3 collective-permute-start.14
  71.0 1.4 collective-permute-start.15
  72.9 3.4 %collective-permute-start.18 = (f32[2,48,128]{2,1,0:T(8,128)S(1)}, f32[2,48,128]{2,1,0:T(8,128)S(1)}, u32[]{:S(2)}, u32[]{:S(2)}) collective-permute-start(f32[2,48,128]{2,1,0:T(8,128)S(1)} %get-tuple-element.147), channel_id=1, source_target_pairs={{0,8},{1,9},{2,10},{3,11},{4,12},{5,13},{6,14},{7,15}} | collective-permute-start | bytes 147464 | tf_op jit(solution)/shard_map/ppermute | solution.py:432
  76.7 1.6 %collective-permute-start.19 = (f32[2,48,128]{2,1,0:T(8,128)S(1)}, f32[2,48,128]{2,1,0:T(8,128)S(1)}, u32[]{:S(2)}, u32[]{:S(2)}) collective-permute-start(f32[2,48,128]{2,1,0:T(8,128)S(1)} %get-tuple-element.149), channel_id=1, source_target_pairs={{8,16},{9,17},{10,18},{11,19},{12,20},{13,21},{14,22},{15,23}} | collective-permute-start | bytes 147464 | tf_op jit(solution)/shard_map/ppermute | solution.py:432
  77.5 0.7 collective-permute-start.17
  79.1 0.7 collective-permute-start.20
  80.2 2.0 %collective-permute-start.21 = (f32[2,48,128]{2,1,0:T(8,128)S(1)}, f32[2,48,128]{2,1,0:T(8,128)S(1)}, u32[]{:S(2)}, u32[]{:S(2)}) collective-permute-start(f32[2,48,128]{2,1,0:T(8,128)S(1)} %get-tuple-element.156), channel_id=1, source_target_pairs={{16,24},{17,25},{18,26},{19,27},{20,28},{21,29},{22,30},{23,31}} | collective-permute-start | bytes 147464 | tf_op jit(solution)/shard_map/ppermute | solution.py:458
  80.9 18.9 %collective-permute-start.22 = (f32[48,128]{1,0:T(8,128)S(1)}, f32[48,128]{1,0:T(8,128)S(1)}, u32[]{:S(2)}, u32[]{:S(2)}) collective-permute-start(f32[48,128]{1,0:T(8,128)S(1)} %get-tuple-element.160), channel_id=1, source_target_pairs={{8,0},{9,1},{10,2},{11,3},{12,4},{13,5},{14,6},{15,7}} | collective-permute-start | bytes 73736 | tf_op jit(solution)/shard_map/ppermute | solution.py:456
  100.3 1.3 collective-permute-start.23
  100.3 1.4 collective-permute-start.24
  102.2 3.4 %collective-permute-start.26 = (f32[2,48,128]{2,1,0:T(8,128)S(1)}, f32[2,48,128]{2,1,0:T(8,128)S(1)}, u32[]{:S(2)}, u32[]{:S(2)}) collective-permute-start(f32[2,48,128]{2,1,0:T(8,128)S(1)} %get-tuple-element.167), channel_id=1, source_target_pairs={{0,8},{1,9},{2,10},{3,11},{4,12},{5,13},{6,14},{7,15}} | collective-permute-start | bytes 147464 | tf_op jit(solution)/shard_map/ppermute | solution.py:432
  106.0 1.6 %collective-permute-start.27 = (f32[2,48,128]{2,1,0:T(8,128)S(1)}, f32[2,48,128]{2,1,0:T(8,128)S(1)}, u32[]{:S(2)}, u32[]{:S(2)}) collective-permute-start(f32[2,48,128]{2,1,0:T(8,128)S(1)} %get-tuple-element.169), channel_id=1, source_target_pairs={{8,16},{9,17},{10,18},{11,19},{12,20},{13,21},{14,22},{15,23}} | collective-permute-start | bytes 147464 | tf_op jit(solution)/shard_map/ppermute | solution.py:432
  106.9 0.7 collective-permute-start.25
  108.5 0.7 collective-permute-start.28
  109.6 2.0 %collective-permute-start.29 = (f32[2,48,128]{2,1,0:T(8,128)S(1)}, f32[2,48,128]{2,1,0:T(8,128)S(1)}, u32[]{:S(2)}, u32[]{:S(2)}) collective-permute-start(f32[2,48,128]{2,1,0:T(8,128)S(1)} %get-tuple-element.176), channel_id=1, source_target_pairs={{16,24},{17,25},{18,26},{19,27},{20,28},{21,29},{22,30},{23,31}} | collective-permute-start | bytes 147464 | tf_op jit(solution)/shard_map/ppermute | solution.py:458
  110.3 12.8 %collective-permute-start.30 = (f32[48,128]{1,0:T(8,128)S(1)}, f32[48,128]{1,0:T(8,128)S(1)}, u32[]{:S(2)}, u32[]{:S(2)}) collective-permute-start(f32[48,128]{1,0:T(8,128)S(1)} %get-tuple-element.180), channel_id=1, source_target_pairs={{8,0},{9,1},{10,2},{11,3},{12,4},{13,5},{14,6},{15,7}} | collective-permute-start | bytes 73736 | tf_op jit(solution)/shard_map/ppermute | solution.py:456
  123.5 4.9 %collective-permute-start.31 = (f32[2,48,128]{2,1,0:T(8,128)S(1)}, f32[2,48,128]{2,1,0:T(8,128)S(1)}, u32[]{:S(2)}, u32[]{:S(2)}) collective-permute-start(f32[2,48,128]{2,1,0:T(8,128)S(1)} %get-tuple-element.181.direction.refs_3_), channel_id=1, source_target_pairs={{0,1},{2,3},{4,5},{6,7},{1,0},{3,2},{5,4},{7,6},{8,9},{10,11},{12,... | collective-permute-start | bytes 147464 | tf_op jit(solution)/shard_map/ppermute | solution.py:418
  124.3 4.4 %collective-permute-start.33 = (f32[2,48,128]{2,1,0:T(8,128)S(1)}, f32[2,48,128]{2,1,0:T(8,128)S(1)}, u32[]{:S(2)}, u32[]{:S(2)}) collective-permute-start(f32[2,48,128]{2,1,0:T(8,128)S(1)} %get-tuple-element.181.direction.refs_3_), channel_id=1, source_target_pairs={{1,2},{3,4},{5,6},{2,1},{4,3},{6,5},{9,10},{11,12},{13,14},{10,9},... | collective-permute-start | bytes 147464 | tf_op jit(solution)/shard_map/ppermute | solution.py:417
  125.0 3.4 %collective-permute-start.32 = (f32[48,128]{1,0:T(8,128)S(1)}, f32[48,128]{1,0:T(8,128)S(1)}, u32[]{:S(2)}, u32[]{:S(2)}) collective-permute-start(f32[48,128]{1,0:T(8,128)S(1)} %get-tuple-element.184), channel_id=1, source_target_pairs={{0,8},{8,16},{16,24},{1,9},{9,17},{17,25},{2,10},{10,18},{18,26},{... | collective-permute-start | bytes 73736 | tf_op jit(solution)/shard_map/ppermute | solution.py:573

commit v13 on v12

--- a/solution.py
+++ b/solution.py
@@ -75,7 +75,7 @@
         out_shape=[
             pltpu.VMEM(lower.shape, lower.dtype),
             pltpu.VMEM(pivot.shape, pivot.dtype),
-            jax.ShapeDtypeStruct((1, block, wide), jnp.float32),
+            pltpu.VMEM((1, block, wide), jnp.float32),
         ],
         in_specs=[pl.BlockSpec(memory_space=pl.ANY)] * 3,
         out_specs=[pl.BlockSpec(memory_space=pltpu.VMEM)] * 3,
@@ -145,7 +145,7 @@
     vmem = pl.BlockSpec(memory_space=pltpu.VMEM)
     return pl.pallas_call(
         kernel,
-        out_shape=[jax.ShapeDtypeStruct(shape, jnp.float32) for shape in out_shapes],
+        out_shape=[pltpu.VMEM(shape, jnp.float32) for shape in out_shapes],
         in_specs=[vmem] * len(operands),
         out_specs=[vmem] * len(out_shapes),
         scratch_shapes=[pltpu.VMEM(shape, jnp.float32) for shape in scratch],
@@ -191,7 +191,7 @@
     carried_in, refs = refs[:parts], refs[parts:]
     if has_last:
         last, *refs = refs
-    carried, message, entry, forward, work = refs
+    carried, message, forward, entry, work = refs
     add_up(carried_in, carried)
     set_entry(carried, entry)
     run_down(vector, lower, pivot, entry, forward, work)
@@ -253,6 +253,25 @@
     pl.when(lax.axis_index("line") == lax.axis_size("line") - 1)(body)
 
 
+def on_second(body):
+    pl.when(lax.axis_index("line") == 1)(body)
+
+
+def up_factor_kernel(upper, pivot, after, out):
+    on_second(lambda: multiply_lines(upper.at[1], pivot.at[1], out))
+
+
+def up_product_kernel(given, upper, pivot, after, first, second, work, made):
+    def body():
+        multiply_lines(given, upper.at[0], work)
+        multiply_lines(work, pivot.at[0], made)
+        size = first.shape[0]
+        first[...] = made[:size]
+        second[...] = made[size:]
+
+    on_second(body)
+
+
 def factor_kernel(lower, pivot, after, factor, out):
     def body():
         multiply_lines(lower.at[0], pivot.at[0], factor)
@@ -281,26 +300,37 @@
     outgoing[...] = result[0]
 
 
-def short_turn_kernel(parts, vector, lower, pivot, upper, response, alone, last, *refs):
-    carried_in = refs[:parts]
-    carried, message, upward, outgoing, forward, entry, work, result, coupled = refs[parts:]
-    add_up(carried_in, carried)
+def short_turn_kernel(
+    vector, lower, pivot, upper, response, alone, message, carried_in, received,
+    carried, passed, upward, to_second, to_first, forward, entry, work, result, coupled,
+):
+    carried[...] = carried_in[...] + received[...]
     set_entry(carried, entry)
     run_down(vector, lower, pivot, entry, forward, work)
-    message[0] = forward[forward.shape[0] - 1]
-    message[1] = last[...]
-    entry[...] = message[1] - message[0]
+    passed[...] = forward[forward.shape[0] - 1]
+    entry[...] = message[0] - passed[...]
     upward[...] = alone[...] + apply_turned(response, entry)
     run_up(forward, upper, pivot, upward, result, coupled)
-    outgoing[...] = result[0]
-
-
-def forward_kernel(parts, vector, lower, pivot, *refs):
-    carried_in = refs[:parts]
-    carried, forward, entry, work = refs[parts:]
-    add_up(carried_in, carried)
-    set_entry(carried, entry)
-    run_down(vector, lower, pivot, entry, forward, work)
+    to_second[...] = result[0]
+    to_first[...] = result[0]
+
+
+def short_end_kernel(
+    beside, beyond, onward, vector, lower, pivot, upper, forward_in, carried, first, second, upward,
+    result, coupled, last, forward, entry, work,
+):
+    forward[...] = forward_in[...]
+
+    def again():
+        entry[...] = carried[1] - onward[...]
+        run_down(vector, lower, pivot, entry, forward, work)
+
+    on_last(again)
+    size = first.shape[0]
+    through = apply_turned(first, beyond.at[:size]) + apply_turned(second, beyond.at[size:])
+    entry[...] = upward[...] + beside[...] + through
+    run_up(forward, upper, pivot, entry, result, coupled)
+    last[...] = result[result.shape[0] - 1]
 
 
 def own_kernel(vector, carried, lower, diag_block, direction, coupled, whole, image):
@@ -424,53 +454,34 @@
     return near, far
 
 
-def sweep_short(vector, message, alone_forward, last, lower, pivot, upper, response):
-    line = lax.axis_size("line")
+def sweep_short(vector, message, last, lower, pivot, upper, response, product):
     field, one = vector.shape, last.shape
-    parts = []
-    for turn in range(line - 2):
-        parts.append(lax.ppermute(message, "line", [(turn, turn + 1)]))
-        if turn == 0:
-            (alone,) = stage(
-                alone_kernel, [one], [alone_forward, upper, pivot], [field, field]
-            )
-            alone = lax.ppermute(alone, "line", [(line - 1, line - 2)])
-        if turn < line - 3:
-            carried, message = stage(
-                functools.partial(hop_down_kernel, len(parts), True),
-                [message.shape, message.shape],
-                [vector, lower, pivot, *parts, last],
-                [one, field, one],
-            )
-            parts = [carried]
-    carried_down, message, upward, outgoing, forward = stage(
-        functools.partial(short_turn_kernel, len(parts)),
-        [message.shape, message.shape, one, one, field],
-        [vector, lower, pivot, upper, response, alone, last, *parts],
+    received = lax.ppermute(message, "line", [(0, 1), (2, 3)])
+    carried, onto, forward = stage(
+        functools.partial(hop_down_kernel, 1, True),
+        [message.shape, message.shape, field],
+        [vector, lower, pivot, received, last],
+        [one, one],
+    )
+    received = lax.ppermute(onto, "line", [(1, 2)])
+    (alone,) = stage(alone_kernel, [one], [forward, upper, pivot], [field, field])
+    alone = lax.ppermute(alone, "line", [(3, 2), (1, 0)])
+    carried, passed, upward, to_second, to_first, forward = stage(
+        short_turn_kernel,
+        [message.shape, one, one, one, one, field],
+        [vector, lower, pivot, upper, response, alone, message, carried, received],
         [one, one, field, field],
     )
-    parts = [upward]
-    for turn in reversed(range(line - 2)):
-        if turn == 0:
-            outgoing, message = lax.optimization_barrier((outgoing, message))
-        parts.append(lax.ppermute(outgoing, "line", [(turn + 1, turn)]))
-        if turn == 0:
-            onward = lax.ppermute(message, "line", [(line - 2, line - 1)])
-            carried_down, whole_forward = stage(
-                functools.partial(forward_kernel, 2),
-                [message.shape, field],
-                [vector, lower, pivot, carried_down, onward],
-                [one, one],
-            )
-        if turn > 0:
-            carried, outgoing = stage(
-                functools.partial(hop_up_kernel, len(parts)),
-                [one, one],
-                [forward, upper, pivot, *parts],
-                [field, field],
-            )
-            parts = [carried]
-    return carried_down, whole_forward, parts
+    beside = lax.ppermute(to_second, "line", [(2, 1)])
+    beyond = lax.ppermute(to_first, "line", [(2, 0)])
+    onward = lax.ppermute(passed, "line", [(2, 3)])
+    direction, coupled, last = stage(
+        short_end_kernel,
+        [field, field, one],
+        [beside, beyond, onward, vector, lower, pivot, upper, forward, carried, *product, upward],
+        [field, one, one],
+    )
+    return direction, coupled, last, carried
 
 
 def per_device(newton_residual, diag_block, lower, upper, west, east, pivot_inverse):
@@ -493,15 +504,19 @@
     basis = []
     directions = []
     last = None
-    short = line > 2 and count == 2
+    short = line == 4 and count == 2
+    third = block // 3
     for j in range(ITERS):
         if j >= 2 and short:
-            carried_down, forward, parts = sweep_short(
-                vector, message, alone_forward, last, lower, pivot, upper, response
+            direction, coupled, last, carried_down = sweep_short(
+                vector, message, last, lower, pivot, upper, response, up_product
             )
         else:
             parts = []
             for turn in range(line - 1):
+                if j == 1 and turn == 2 and short:
+                    message, rest = lax.optimization_barrier((message, up_product[1]))
+                    up_product[1] = lax.ppermute(rest, "line", [(1, 0)])
                 parts.append(lax.ppermute(message, "line", [(turn, turn + 1)]))
                 if j == 0 and turn == 0:
                     (upper,) = load((upper,), message)
@@ -509,13 +524,16 @@
                     factor, response = stage(
                         factor_kernel, [(block,) + one] * 2, [lower, pivot, message]
                     )
+                    (up_factor,) = stage(
+                        up_factor_kernel, [(block,) + one], [upper, pivot, message]
+                    )
                 if turn < line - 2:
                     lasts = [] if last is None else [last]
-                    carried, message = stage(
+                    carried, message, _ = stage(
                         functools.partial(hop_down_kernel, len(parts), bool(lasts)),
-                        [message.shape, message.shape],
+                        [message.shape, message.shape, field],
                         [vector, lower, pivot, *parts, *lasts],
-                        [one, field, one],
+                        [one, one],
                     )
                     parts = [carried]
             parts = parts or [jnp.zeros_like(message)]
@@ -526,18 +544,30 @@
                 [one, one, field, field],
             )
             if j == 0 and short:
-                outgoing, response = lax.optimization_barrier((outgoing, response))
+                outgoing, response, up_factor = lax.optimization_barrier(
+                    (outgoing, response, up_factor)
+                )
             parts = []
             for turn in reversed(range(line - 1)):
                 if j == 1 and turn == line - 3 and short:
                     outgoing, ready = lax.optimization_barrier((outgoing, response))
                     response = lax.ppermute(ready, "line", [(line - 1, line - 2)])
+                if j == 1 and turn == 0 and short:
+                    outgoing, up_product[1] = lax.optimization_barrier(
+                        (outgoing, up_product[1])
+                    )
                 parts.append(lax.ppermute(outgoing, "line", [(turn + 1, turn)]))
                 if j == 0 and turn == line - 2:
                     diag_block, near_block, far_block = load(
                         (diag_block, east, west), outgoing, True
                     )
                 if j == 0 and turn == line - 3 and short:
+                    up_product = stage(
+                        up_product_kernel,
+                        [(third,) + one, (block - third,) + one],
+                        [up_factor, upper, pivot, outgoing],
+                        [(block,) + one] * 2,
+                    )
                     (response,) = stage(
                         response_kernel,
                         [(block,) + one],
@@ -552,14 +582,21 @@
                         [field, field],
                     )
                     parts = [carried]
+                    if j == 0 and turn == line - 3 and short:
+                        outgoing, *up_product = lax.optimization_barrier(
+                            (outgoing, *up_product)
+                        )
             parts = parts or [jnp.zeros_like(outgoing)]
-        direction, coupled, last = stage(
-            functools.partial(end_kernel, len(parts)),
-            [field, field, one],
-            [forward, upper, pivot, *parts],
-            [one],
-        )
+            direction, coupled, last = stage(
+                functools.partial(end_kernel, len(parts)),
+                [field, field, one],
+                [forward, upper, pivot, *parts],
+                [one],
+            )
         directions.append(direction)
+        if j == 1 and short:
+            direction, part = lax.optimization_barrier((direction, up_product[0]))
+            up_product[0] = lax.ppermute(part, "line", [(1, 0)])
         near, far = rows_beside(direction, across)
         whole, image = stage(
             own_kernel,
@@ -574,11 +611,11 @@
             beneath = [lower, below]
         (image,) = stage(near_kernel, [field], [image, near_block, near, *beneath])
         if j < ITERS - 1:
-            vector, message, alone_forward = stage(
+            vector, message = stage(
                 next_kernel,
-                [field, (2,) + one, field],
+                [field, (2,) + one],
                 [image, far_block, far, lower, pivot, last],
-                [one],
+                [field, one],
             )
             if j == 0 and short:
                 message, response = lax.optimization_barrier((message, response))

time: 148 us -> 161 us (1.088)
  starting transfers between devices: 32.1 us -> 44.3 us
  blocking collectives: 18 us -> 20.6 us
  waiting for transfers between devices: 73.5 us -> 71.8 us
    ppermute x6, waiting for transfers between devices: 38 us -> 24.3 us  [per_device(): parts.append(lax.ppermute(outgoing, 'line', [(turn + 1, turn)]))]
    ppermute x12 -> x14, waiting for transfers between devices: 31.8 us -> 44.2 us  [the longest x1 20.5 us: per_device(): up_product[1] = lax.ppermute(rest, 'line', [(1, 0)])]
    ppermute x12 -> x14, starting transfers between devices: 11.1 us -> 18.4 us  [the longest x2 6.65 us: sweep_short(): received = lax.ppermute(message, 'line', [(0, 1), (2, 3)])]
    ppermute x4, starting transfers between devices: 1.05 us -> 5.91 us  [rows_beside(): near = lax.ppermute(to_near, 'patch', even + [(b, a) for a, b in even])]
    all_to_all x1, blocking collectives: 18 us -> 20.6 us  [per_device(): sums = lax.all_to_all(sums, ('line', 'patch'), 0, 0, tiled=True)]
    pallas_call x40 -> x38, Pallas kernels: 16.6 us -> 16.5 us  [stage(): pl.pallas_call(kernel, out_shape=[pltpu.VMEM(shape, jnp.float32) for shap...]
  transfers between devices with their start and end apart: 34 -> 36, of which waited for: 11 -> 12; matrix products, arithmetic and copies ran while one was open for 0% -> 0% of each run, Pallas kernels for 6% -> 6%
where the time goes in v13:
time: 161 us
  waiting for transfers between devices  71.8 us (45%)
  starting transfers between devices  44.3 us (28%)
  Pallas kernels  21.9 us (14%)
  blocking collectives  20.6 us (13%)
    ppermute x6, waiting for transfers between devices, per_device(): parts.append(lax.ppermute(outgoing, 'line', [(turn + 1, turn)]))  24.3 us
    all_to_all x1, blocking collectives, per_device(): sums = lax.all_to_all(sums, ('line', 'patch'), 0, 0, tiled=True)  20.6 us
    ppermute x1, waiting for transfers between devices, per_device(): up_product[1] = lax.ppermute(rest, 'line', [(1, 0)])  20.5 us
    pallas_call x38, Pallas kernels, stage(): pl.pallas_call(kernel, out_shape=[pltpu.VMEM(shape, jnp.float32) for shap...  16.5 us
    ppermute x2, waiting for transfers between devices, sweep_short(): alone = lax.ppermute(alone, 'line', [(3, 2), (1, 0)])  12.8 us
    ppermute x6, starting transfers between devices, per_device(): parts.append(lax.ppermute(message, 'line', [(turn, turn + 1)]))  9.07 us
    ppermute x2, waiting for transfers between devices, sweep_short(): beyond = lax.ppermute(to_first, 'line', [(2, 0)])  7.47 us
    ppermute x2, starting transfers between devices, sweep_short(): received = lax.ppermute(message, 'line', [(0, 1), (2, 3)])  6.65 us
  transfers between devices with their start and end apart: 36, of which 12 were waited for; matrix products, arithmetic and copies ran while one was open for 0% of the time, Pallas kernels for 6%

profile of v13, /device:TPU:0, one launch (start us, length us, event | category | flops | bytes accessed | tf_op | source)
XLA Modules:
  0.0 160.6 jit_solution(14648336812807116991)
XLA Ops:
  0.0 1.7 %shard_map.73 = (bf16[2,48,48,128]{3,2,1,0:T(8,128)(2,1)S(1)}, bf16[2,48,48,128]{3,2,1,0:T(8,128)(2,1)S(1)}, f32[1,48,128]{2,1,0:T(8,128)S(1)}) custom-call(f32[2,48,128]{2,1,0:T(8,128)} %bitcast.15, bf16[2,48,48,128]{3,2,1,0:T(8,128)(2,1)} %bitcast.26, bf16[2,48,48,128]{3,2,1,0:T(8,128)(2,1)} %bitcast.27), custom_call_target="tpu_custom_call" | custom-call | tf_op jit(solution)/shard_map/pallas_call | solution.py:73
  1.7 4.8 %collective-permute-start = (f32[1,48,128]{2,1,0:T(8,128)S(1)}, f32[1,48,128]{2,1,0:T(8,128)S(1)}, u32[]{:S(2)}, u32[]{:S(2)}) collective-permute-start(f32[1,48,128]{2,1,0:T(8,128)S(1)} %get-tuple-element.103.refs_1_), channel_id=1, source_target_pairs={{0,8},{1,9},{2,10},{3,11},{4,12},{5,13},{6,14},{7,15}} | collective-permute-start | bytes 73736 | tf_op jit(solution)/shard_map/ppermute | solution.py:520
  6.5 0.9 shard_map.74
  7.5 0.6 collective-permute-done.refs_0_
  8.0 1.0 shard_map.76
  9.1 0.7 collective-permute-start.1
  9.7 1.0 shard_map.77
  10.8 0.7 collective-permute-start.2
  11.4 0.7 shard_map.75.upper
  12.2 0.6 shard_map.78
  12.8 0.7 collective-permute-start.3
  13.9 0.7 collective-permute-start.4
  15.0 1.3 collective-permute-start.5
  16.3 19.8 %collective-permute-done.5.refs_1_ = f32[48,128]{1,0:T(8,128)S(1)} collective-permute-done((f32[48,128]{1,0:T(8,128)S(1)}, f32[48,128]{1,0:T(8,128)S(1)}, u32[]{:S(2)}, u32[]{:S(2)}) %collective-permute-start.5) | collective-permute-done | bytes 24608 | tf_op jit(solution)/shard_map/ppermute | solution.py:559
  36.6 0.8 collective-permute-start.7
  38.2 2.1 %shard_map.81 = (f32[2,48,48,128]{3,2,1,0:T(8,128)S(1)}, f32[2,48,48,128]{3,2,1,0:T(8,128)S(1)}, f32[2,48,48,128]{3,2,1,0:T(8,128)S(1)}) custom-call(bf16[2,48,48,128]{3,2,1,0:T(8,128)(2,1)S(1)} %bitcast.21, bf16[2,48,48,128]{3,2,1,0:T(8,128)(2,1)S(1)} %bitcast.22, bf16[2,48,48,128]{3,2,1,0:T(8,128)(2,1)S(1)} %bitcast.23, ...), custom_call_target="tpu_custom_call" | custom-call | tf_op jit(solution)/shard_map/pallas_call | solution.py:131
  41.4 1.6 %collective-permute-start.8 = (f32[2,48,128]{2,1,0:T(8,128)S(1)}, f32[2,48,128]{2,1,0:T(8,128)S(1)}, u32[]{:S(2)}, u32[]{:S(2)}) collective-permute-start(f32[2,48,128]{2,1,0:T(8,128)S(1)} %get-tuple-element.132), channel_id=1, source_target_pairs={{0,8},{1,9},{2,10},{3,11},{4,12},{5,13},{6,14},{7,15}} | collective-permute-start | bytes 147464 | tf_op jit(solution)/shard_map/ppermute | solution.py:520
  43.0 1.7 %collective-permute-done.8.refs_0_ = f32[2,48,128]{2,1,0:T(8,128)S(1)} collective-permute-done((f32[2,48,128]{2,1,0:T(8,128)S(1)}, f32[2,48,128]{2,1,0:T(8,128)S(1)}, u32[]{:S(2)}, u32[]{:S(2)}) %collective-permute-start.8) | collective-permute-done | bytes 49184 | tf_op jit(solution)/shard_map/ppermute | solution.py:520
  44.8 1.0 shard_map.90
  45.8 0.7 collective-permute-start.9
  46.5 1.0 shard_map.91
  47.5 0.7 collective-permute-start.10
  48.2 0.6 shard_map.92
  48.8 0.7 collective-permute-start.11
  49.5 1.3 collective-permute-start.13
  51.2 0.7 collective-permute-start.17
  51.9 0.8 collective-permute-start.12
  53.2 20.5 %collective-permute-done.13.second = f32[32,48,128]{2,1,0:T(8,128)S(1)} collective-permute-done((f32[32,48,128]{2,1,0:T(8,128)S(1)}, f32[32,48,128]{2,1,0:T(8,128)S(1)}, u32[]{:S(2)}, u32[]{:S(2)}) %collective-permute-start.13) | collective-permute-done | bytes 786464 | tf_op jit(solution)/shard_map/ppermute | solution.py:519
  73.7 1.3 collective-permute-start.14
  75.0 4.4 %collective-permute-done.14.refs_1_ = f32[48,128]{1,0:T(8,128)S(1)} collective-permute-done((f32[48,128]{1,0:T(8,128)S(1)}, f32[48,128]{1,0:T(8,128)S(1)}, u32[]{:S(2)}, u32[]{:S(2)}) %collective-permute-start.14) | collective-permute-done | bytes 24608 | tf_op jit(solution)/shard_map/ppermute | solution.py:559
  79.8 1.3 collective-permute-start.24
  81.2 0.7 collective-permute-start.16
  81.8 0.5 shard_map.96
  83.1 4.6 %collective-permute-start.18 = (f32[2,48,128]{2,1,0:T(8,128)S(1)}, f32[2,48,128]{2,1,0:T(8,128)S(1)}, u32[]{:S(2)}, u32[]{:S(2)}) collective-permute-start(f32[2,48,128]{2,1,0:T(8,128)S(1)} %get-tuple-element.158.message), channel_id=1, source_target_pairs={{0,8},{16,24},{1,9},{17,25},{2,10},{18,26},{3,11},{19,27},{4,12},{... | collective-permute-start | bytes 147464 | tf_op jit(solution)/shard_map/ppermute | solution.py:459
  87.7 1.7 %collective-permute-done.18.refs_0_ = f32[2,48,128]{2,1,0:T(8,128)S(1)} collective-permute-done((f32[2,48,128]{2,1,0:T(8,128)S(1)}, f32[2,48,128]{2,1,0:T(8,128)S(1)}, u32[]{:S(2)}, u32[]{:S(2)}) %collective-permute-start.18) | collective-permute-done | bytes 49184 | tf_op jit(solution)/shard_map/ppermute | solution.py:459
  89.8 0.7 collective-permute-start.20
  90.7 1.3 collective-permute-start.19
  92.0 4.7 %collective-permute-done.19.alone = f32[48,128]{1,0:T(8,128)S(1)} collective-permute-done((f32[48,128]{1,0:T(8,128)S(1)}, f32[48,128]{1,0:T(8,128)S(1)}, u32[]{:S(2)}, u32[]{:S(2)}) %collective-permute-start.19) | collective-permute-done | bytes 24608 | tf_op jit(solution)/shard_map/ppermute | solution.py:468
  96.8 0.9 shard_map.101
  97.7 0.7 collective-permute-start.21
  98.3 1.3 collective-permute-start.22
  99.6 0.7 collective-permute-start.23
  100.3 3.7 %collective-permute-done.22.beyond = f32[48,128]{1,0:T(8,128)S(1)} collective-permute-done((f32[48,128]{1,0:T(8,128)S(1)}, f32[48,128]{1,0:T(8,128)S(1)}, u32[]{:S(2)}, u32[]{:S(2)}) %collective-permute-start.22) | collective-permute-done | bytes 24608 | tf_op jit(solution)/shard_map/ppermute | solution.py:476
  104.5 1.6 collective-permute-start.25
  106.1 0.7 collective-permute-start.26
  106.8 0.5 shard_map.103
  108.0 2.1 %collective-permute-start.27 = (f32[2,48,128]{2,1,0:T(8,128)S(1)}, f32[2,48,128]{2,1,0:T(8,128)S(1)}, u32[]{:S(2)}, u32[]{:S(2)}) collective-permute-start(f32[2,48,128]{2,1,0:T(8,128)S(1)} %get-tuple-element.175.message), channel_id=1, source_target_pairs={{0,8},{16,24},{1,9},{17,25},{2,10},{18,26},{3,11},{19,27},{4,12},{... | collective-permute-start | bytes 147464 | tf_op jit(solution)/shard_map/ppermute | solution.py:459
  110.0 1.7 %collective-permute-done.27.refs_0_ = f32[2,48,128]{2,1,0:T(8,128)S(1)} collective-permute-done((f32[2,48,128]{2,1,0:T(8,128)S(1)}, f32[2,48,128]{2,1,0:T(8,128)S(1)}, u32[]{:S(2)}, u32[]{:S(2)}) %collective-permute-start.27) | collective-permute-done | bytes 49184 | tf_op jit(solution)/shard_map/ppermute | solution.py:459
  112.2 0.7 collective-permute-start.29
  113.1 1.3 collective-permute-start.28
  114.4 8.0 %collective-permute-done.28.alone = f32[48,128]{1,0:T(8,128)S(1)} collective-permute-done((f32[48,128]{1,0:T(8,128)S(1)}, f32[48,128]{1,0:T(8,128)S(1)}, u32[]{:S(2)}, u32[]{:S(2)}) %collective-permute-start.28) | collective-permute-done | bytes 24608 | tf_op jit(solution)/shard_map/ppermute | solution.py:468
  122.4 0.9 shard_map.108
  123.3 0.7 collective-permute-start.30
  124.0 1.3 collective-permute-start.31
  125.3 0.7 collective-permute-start.32
  126.0 3.7 %collective-permute-done.31.beyond = f32[48,128]{1,0:T(8,128)S(1)} collective-permute-done((f32[48,128]{1,0:T(8,128)S(1)}, f32[48,128]{1,0:T(8,128)S(1)}, u32[]{:S(2)}, u32[]{:S(2)}) %collective-permute-start.31) | collective-permute-done | bytes 24608 | tf_op jit(solution)/shard_map/ppermute | solution.py:476
  129.7 0.5 shard_map.109
  130.2 4.2 %collective-permute-start.33 = (f32[2,48,128]{2,1,0:T(8,128)S(1)}, f32[2,48,128]{2,1,0:T(8,128)S(1)}, u32[]{:S(2)}, u32[]{:S(2)}) collective-permute-start(f32[2,48,128]{2,1,0:T(8,128)S(1)} %get-tuple-element.185.direction.refs_3_), channel_id=1, source_target_pairs={{0,1},{2,3},{4,5},{6,7},{1,0},{3,2},{5,4},{7,6},{8,9},{10,11},{12,... | collective-permute-start | bytes 147464 | tf_op jit(solution)/shard_map/ppermute | solution.py:448
  134.4 0.7 collective-permute-start.35
  135.0 2.1 %collective-permute-start.34 = (f32[48,128]{1,0:T(8,128)S(1)}, f32[48,128]{1,0:T(8,128)S(1)}, u32[]{:S(2)}, u32[]{:S(2)}) collective-permute-start(f32[48,128]{1,0:T(8,128)S(1)} %get-tuple-element.188), channel_id=1, source_target_pairs={{0,8},{8,16},{16,24},{1,9},{9,17},{17,25},{2,10},{10,18},{18,26},{... | collective-permute-start | bytes 73736 | tf_op jit(solution)/shard_map/ppermute | solution.py:610
  137.1 0.5 shard_map.110
  137.7 1.0 collective-permute-done.34.refs_1_
  139.2 20.6 %all_to_all.11 = f32[32,1,128]{2,1,0:T(1,128)S(1)} all-to-all(f32[32,1,128]{2,1,0:T(1,128)S(1)} %bitcast.24), channel_id=1, replica_groups=mesh['line'=4,'patch'=8] {'line','patch'}, dimensions={0} | all-to-all | bytes 32768 | tf_op jit(solution)/shard_map/all_to_all | solution.py:629
  159.9 0.6 copy.11
  (62 shorter events, 8.3 us)
Async XLA Ops:
  1.7 6.4 %collective-permute-start = (f32[1,48,128]{2,1,0:T(8,128)S(1)}, f32[1,48,128]{2,1,0:T(8,128)S(1)}, u32[]{:S(2)}, u32[]{:S(2)}) collective-permute-start(f32[1,48,128]{2,1,0:T(8,128)S(1)} %get-tuple-element.103.refs_1_), channel_id=1, source_target_pairs={{0,8},{1,9},{2,10},{3,11},{4,12},{5,13},{6,14},{7,15}} | collective-permute-start | bytes 73736 | tf_op jit(solution)/shard_map/ppermute | solution.py:520
  6.5 1.5 copy-start
  9.1 0.7 collective-permute-start.1
  9.7 1.7 %copy-start.1 = (bf16[2,48,48,1,128]{4,2,3,1,0:T(8,128)(2,1)S(1)}, bf16[2,48,48,1,128]{4,2,3,1,0:T(8,128)(2,1)}, u32[]{:S(2)}) copy-start(bf16[2,48,48,1,128]{4,2,3,1,0:T(8,128)(2,1)} %param.10) | copy-start | bytes 3538948
  10.8 1.4 collective-permute-start.2
  12.8 0.7 collective-permute-start.3
  13.9 0.7 collective-permute-start.4
  15.0 21.1 %collective-permute-start.5 = (f32[48,128]{1,0:T(8,128)S(1)}, f32[48,128]{1,0:T(8,128)S(1)}, u32[]{:S(2)}, u32[]{:S(2)}) collective-permute-start(f32[48,128]{1,0:T(8,128)S(1)} %get-tuple-element.121), channel_id=1, source_target_pairs={{8,0},{9,1},{10,2},{11,3},{12,4},{13,5},{14,6},{15,7}} | collective-permute-start | bytes 73736 | tf_op jit(solution)/shard_map/ppermute | solution.py:559
  36.2 1.3 copy-start.2
  36.2 1.6 %copy-start.3 = (bf16[2,48,48,1,128]{4,2,3,1,0:T(8,128)(2,1)S(1)}, bf16[2,48,48,1,128]{4,2,3,1,0:T(8,128)(2,1)}, u32[]{:S(2)}) copy-start(bf16[2,48,48,1,128]{4,2,3,1,0:T(8,128)(2,1)} %param.12) | copy-start | bytes 3538948
  36.2 2.0 %copy-start.4 = (bf16[2,48,48,1,128]{4,2,3,1,0:T(8,128)(2,1)S(1)}, bf16[2,48,48,1,128]{4,2,3,1,0:T(8,128)(2,1)}, u32[]{:S(2)}) copy-start(bf16[2,48,48,1,128]{4,2,3,1,0:T(8,128)(2,1)} %param.11) | copy-start | bytes 3538948
  36.6 4.2 %collective-permute-start.6 = (f32[2,48,128]{2,1,0:T(8,128)S(1)}, f32[2,48,128]{2,1,0:T(8,128)S(1)}, u32[]{:S(2)}, u32[]{:S(2)}) collective-permute-start(f32[2,48,128]{2,1,0:T(8,128)S(1)} %get-tuple-element.122.direction.refs_0_), channel_id=1, source_target_pairs={{0,1},{2,3},{4,5},{6,7},{1,0},{3,2},{5,4},{7,6},{8,9},{10,11},{12,... | collective-permute-start | bytes 147464 | tf_op jit(solution)/shard_map/ppermute | solution.py:448
  36.6 4.3 %collective-permute-start.7 = (f32[2,48,128]{2,1,0:T(8,128)S(1)}, f32[2,48,128]{2,1,0:T(8,128)S(1)}, u32[]{:S(2)}, u32[]{:S(2)}) collective-permute-start(f32[2,48,128]{2,1,0:T(8,128)S(1)} %get-tuple-element.122.direction.refs_0_), channel_id=1, source_target_pairs={{1,2},{3,4},{5,6},{2,1},{4,3},{6,5},{9,10},{11,12},{13,14},{10,9},... | collective-permute-start | bytes 147464 | tf_op jit(solution)/shard_map/ppermute | solution.py:447
  41.4 3.4 %collective-permute-start.8 = (f32[2,48,128]{2,1,0:T(8,128)S(1)}, f32[2,48,128]{2,1,0:T(8,128)S(1)}, u32[]{:S(2)}, u32[]{:S(2)}) collective-permute-start(f32[2,48,128]{2,1,0:T(8,128)S(1)} %get-tuple-element.132), channel_id=1, source_target_pairs={{0,8},{1,9},{2,10},{3,11},{4,12},{5,13},{6,14},{7,15}} | collective-permute-start | bytes 147464 | tf_op jit(solution)/shard_map/ppermute | solution.py:520
  45.8 0.7 collective-permute-start.9
  47.5 0.7 collective-permute-start.10
  48.8 2.0 %collective-permute-start.11 = (f32[48,128]{1,0:T(8,128)S(1)}, f32[48,128]{1,0:T(8,128)S(1)}, u32[]{:S(2)}, u32[]{:S(2)}) collective-permute-start(f32[48,128]{1,0:T(8,128)S(1)} %get-tuple-element.141), channel_id=1, source_target_pairs={{24,16},{25,17},{26,18},{27,19},{28,20},{29,21},{30,22},{31,23}} | collective-permute-start | bytes 73736 | tf_op jit(solution)/shard_map/ppermute | solution.py:559
  49.5 24.2 %collective-permute-start.13 = (f32[32,48,128]{2,1,0:T(8,128)S(1)}, f32[32,48,128]{2,1,0:T(8,128)S(1)}, u32[]{:S(2)}, u32[]{:S(2)}) collective-permute-start(f32[32,48,128]{2,1,0:T(8,128)S(1)} %get-tuple-element.148), channel_id=1, source_target_pairs={{8,0},{9,1},{10,2},{11,3},{12,4},{13,5},{14,6},{15,7}} | collective-permute-start | bytes 2359304 | tf_op jit(solution)/shard_map/ppermute | solution.py:519
  51.2 45.6 %collective-permute-start.17 = (f32[48,48,128]{2,1,0:T(8,128)S(1)}, f32[48,48,128]{2,1,0:T(8,128)S(1)}, u32[]{:S(2)}, u32[]{:S(2)}) collective-permute-start(f32[48,48,128]{2,1,0:T(8,128)S(1)} %shard_map.89), channel_id=1, source_target_pairs={{24,16},{25,17},{26,18},{27,19},{28,20},{29,21},{30,22},{31,23}} | collective-permute-start | bytes 3538952 | tf_op jit(solution)/shard_map/ppermute | solution.py:554
  51.9 0.9 collective-permute-start.12
  73.7 5.7 %collective-permute-start.14 = (f32[48,128]{1,0:T(8,128)S(1)}, f32[48,128]{1,0:T(8,128)S(1)}, u32[]{:S(2)}, u32[]{:S(2)}) collective-permute-start(f32[48,128]{1,0:T(8,128)S(1)} %get-tuple-element.149), channel_id=1, source_target_pairs={{8,0},{9,1},{10,2},{11,3},{12,4},{13,5},{14,6},{15,7}} | collective-permute-start | bytes 73736 | tf_op jit(solution)/shard_map/ppermute | solution.py:559
  79.8 20.5 %collective-permute-start.24 = (f32[16,48,128]{2,1,0:T(8,128)S(1)}, f32[16,48,128]{2,1,0:T(8,128)S(1)}, u32[]{:S(2)}, u32[]{:S(2)}) collective-permute-start(f32[16,48,128]{2,1,0:T(8,128)S(1)} %get-tuple-element.167), channel_id=1, source_target_pairs={{8,0},{9,1},{10,2},{11,3},{12,4},{13,5},{14,6},{15,7}} | collective-permute-start | bytes 1179656 | tf_op jit(solution)/shard_map/ppermute | solution.py:599
  81.1 1.3 collective-permute-start.15
  81.2 1.4 collective-permute-start.16
  83.1 6.3 %collective-permute-start.18 = (f32[2,48,128]{2,1,0:T(8,128)S(1)}, f32[2,48,128]{2,1,0:T(8,128)S(1)}, u32[]{:S(2)}, u32[]{:S(2)}) collective-permute-start(f32[2,48,128]{2,1,0:T(8,128)S(1)} %get-tuple-element.158.message), channel_id=1, source_target_pairs={{0,8},{16,24},{1,9},{17,25},{2,10},{18,26},{3,11},{19,27},{4,12},{... | collective-permute-start | bytes 147464 | tf_op jit(solution)/shard_map/ppermute | solution.py:459
  89.8 6.9 %collective-permute-start.20 = (f32[2,48,128]{2,1,0:T(8,128)S(1)}, f32[2,48,128]{2,1,0:T(8,128)S(1)}, u32[]{:S(2)}, u32[]{:S(2)}) collective-permute-start(f32[2,48,128]{2,1,0:T(8,128)S(1)} %get-tuple-element.161), channel_id=1, source_target_pairs={{8,16},{9,17},{10,18},{11,19},{12,20},{13,21},{14,22},{15,23}} | collective-permute-start | bytes 147464 | tf_op jit(solution)/shard_map/ppermute | solution.py:466
  90.7 6.0 %collective-permute-start.19 = (f32[48,128]{1,0:T(8,128)S(1)}, f32[48,128]{1,0:T(8,128)S(1)}, u32[]{:S(2)}, u32[]{:S(2)}) collective-permute-start(f32[48,128]{1,0:T(8,128)S(1)} %shard_map.100), channel_id=1, source_target_pairs={{24,16},{8,0},{25,17},{9,1},{26,18},{10,2},{27,19},{11,3},{28,20},... | collective-permute-start | bytes 73736 | tf_op jit(solution)/shard_map/ppermute | solution.py:468
  97.7 2.7 %collective-permute-start.21 = (f32[48,128]{1,0:T(8,128)S(1)}, f32[48,128]{1,0:T(8,128)S(1)}, u32[]{:S(2)}, u32[]{:S(2)}) collective-permute-start(f32[48,128]{1,0:T(8,128)S(1)} %get-tuple-element.163), channel_id=1, source_target_pairs={{16,8},{17,9},{18,10},{19,11},{20,12},{21,13},{22,14},{23,15}} | collective-permute-start | bytes 73736 | tf_op jit(solution)/shard_map/ppermute | solution.py:475
  98.3 5.7 %collective-permute-start.22 = (f32[48,128]{1,0:T(8,128)S(1)}, f32[48,128]{1,0:T(8,128)S(1)}, u32[]{:S(2)}, u32[]{:S(2)}) collective-permute-start(f32[48,128]{1,0:T(8,128)S(1)} %get-tuple-element.164), channel_id=1, source_target_pairs={{16,0},{17,1},{18,2},{19,3},{20,4},{21,5},{22,6},{23,7}} | collective-permute-start | bytes 73736 | tf_op jit(solution)/shard_map/ppermute | solution.py:476
  99.6 4.4 %collective-permute-start.23 = (f32[48,128]{1,0:T(8,128)S(1)}, f32[48,128]{1,0:T(8,128)S(1)}, u32[]{:S(2)}, u32[]{:S(2)}) collective-permute-start(f32[48,128]{1,0:T(8,128)S(1)} %get-tuple-element.165), channel_id=1, source_target_pairs={{16,24},{17,25},{18,26},{19,27},{20,28},{21,29},{22,30},{23,31}} | collective-permute-start | bytes 73736 | tf_op jit(solution)/shard_map/ppermute | solution.py:477
  104.5 2.7 %collective-permute-start.25 = (f32[2,48,128]{2,1,0:T(8,128)S(1)}, f32[2,48,128]{2,1,0:T(8,128)S(1)}, u32[]{:S(2)}, u32[]{:S(2)}) collective-permute-start(f32[2,48,128]{2,1,0:T(8,128)S(1)} %get-tuple-element.170.direction.refs_2_), channel_id=1, source_target_pairs={{0,1},{2,3},{4,5},{6,7},{1,0},{3,2},{5,4},{7,6},{8,9},{10,11},{12,... | collective-permute-start | bytes 147464 | tf_op jit(solution)/shard_map/ppermute | solution.py:448
  106.1 1.4 collective-permute-start.26
  108.0 3.8 %collective-permute-start.27 = (f32[2,48,128]{2,1,0:T(8,128)S(1)}, f32[2,48,128]{2,1,0:T(8,128)S(1)}, u32[]{:S(2)}, u32[]{:S(2)}) collective-permute-start(f32[2,48,128]{2,1,0:T(8,128)S(1)} %get-tuple-element.175.message), channel_id=1, source_target_pairs={{0,8},{16,24},{1,9},{17,25},{2,10},{18,26},{3,11},{19,27},{4,12},{... | collective-permute-start | bytes 147464 | tf_op jit(solution)/shard_map/ppermute | solution.py:459
  112.2 10.2 %collective-permute-start.29 = (f32[2,48,128]{2,1,0:T(8,128)S(1)}, f32[2,48,128]{2,1,0:T(8,128)S(1)}, u32[]{:S(2)}, u32[]{:S(2)}) collective-permute-start(f32[2,48,128]{2,1,0:T(8,128)S(1)} %get-tuple-element.178), channel_id=1, source_target_pairs={{8,16},{9,17},{10,18},{11,19},{12,20},{13,21},{14,22},{15,23}} | collective-permute-start | bytes 147464 | tf_op jit(solution)/shard_map/ppermute | solution.py:466
  113.1 9.3 %collective-permute-start.28 = (f32[48,128]{1,0:T(8,128)S(1)}, f32[48,128]{1,0:T(8,128)S(1)}, u32[]{:S(2)}, u32[]{:S(2)}) collective-permute-start(f32[48,128]{1,0:T(8,128)S(1)} %shard_map.107), channel_id=1, source_target_pairs={{24,16},{8,0},{25,17},{9,1},{26,18},{10,2},{27,19},{11,3},{28,20},... | collective-permute-start | bytes 73736 | tf_op jit(solution)/shard_map/ppermute | solution.py:468
  123.3 2.6 %collective-permute-start.30 = (f32[48,128]{1,0:T(8,128)S(1)}, f32[48,128]{1,0:T(8,128)S(1)}, u32[]{:S(2)}, u32[]{:S(2)}) collective-permute-start(f32[48,128]{1,0:T(8,128)S(1)} %get-tuple-element.180), channel_id=1, source_target_pairs={{16,8},{17,9},{18,10},{19,11},{20,12},{21,13},{22,14},{23,15}} | collective-permute-start | bytes 73736 | tf_op jit(solution)/shard_map/ppermute | solution.py:475
  124.0 5.7 %collective-permute-start.31 = (f32[48,128]{1,0:T(8,128)S(1)}, f32[48,128]{1,0:T(8,128)S(1)}, u32[]{:S(2)}, u32[]{:S(2)}) collective-permute-start(f32[48,128]{1,0:T(8,128)S(1)} %get-tuple-element.181), channel_id=1, source_target_pairs={{16,0},{17,1},{18,2},{19,3},{20,4},{21,5},{22,6},{23,7}} | collective-permute-start | bytes 73736 | tf_op jit(solution)/shard_map/ppermute | solution.py:476
  125.3 4.4 %collective-permute-start.32 = (f32[48,128]{1,0:T(8,128)S(1)}, f32[48,128]{1,0:T(8,128)S(1)}, u32[]{:S(2)}, u32[]{:S(2)}) collective-permute-start(f32[48,128]{1,0:T(8,128)S(1)} %get-tuple-element.182), channel_id=1, source_target_pairs={{16,24},{17,25},{18,26},{19,27},{20,28},{21,29},{22,30},{23,31}} | collective-permute-start | bytes 73736 | tf_op jit(solution)/shard_map/ppermute | solution.py:477
  130.2 8.4 %collective-permute-start.33 = (f32[2,48,128]{2,1,0:T(8,128)S(1)}, f32[2,48,128]{2,1,0:T(8,128)S(1)}, u32[]{:S(2)}, u32[]{:S(2)}) collective-permute-start(f32[2,48,128]{2,1,0:T(8,128)S(1)} %get-tuple-element.185.direction.refs_3_), channel_id=1, source_target_pairs={{0,1},{2,3},{4,5},{6,7},{1,0},{3,2},{5,4},{7,6},{8,9},{10,11},{12,... | collective-permute-start | bytes 147464 | tf_op jit(solution)/shard_map/ppermute | solution.py:448
  134.4 4.5 %collective-permute-start.35 = (f32[2,48,128]{2,1,0:T(8,128)S(1)}, f32[2,48,128]{2,1,0:T(8,128)S(1)}, u32[]{:S(2)}, u32[]{:S(2)}) collective-permute-start(f32[2,48,128]{2,1,0:T(8,128)S(1)} %get-tuple-element.185.direction.refs_3_), channel_id=1, source_target_pairs={{1,2},{3,4},{5,6},{2,1},{4,3},{6,5},{9,10},{11,12},{13,14},{10,9},... | collective-permute-start | bytes 147464 | tf_op jit(solution)/shard_map/ppermute | solution.py:447
  135.0 3.6 %collective-permute-start.34 = (f32[48,128]{1,0:T(8,128)S(1)}, f32[48,128]{1,0:T(8,128)S(1)}, u32[]{:S(2)}, u32[]{:S(2)}) collective-permute-start(f32[48,128]{1,0:T(8,128)S(1)} %get-tuple-element.188), channel_id=1, source_target_pairs={{0,8},{8,16},{16,24},{1,9},{9,17},{17,25},{2,10},{10,18},{18,26},{... | collective-permute-start | bytes 73736 | tf_op jit(solution)/shard_map/ppermute | solution.py:610

commit v14 on v13

--- a/solution.py
+++ b/solution.py
@@ -253,25 +253,6 @@
     pl.when(lax.axis_index("line") == lax.axis_size("line") - 1)(body)
 
 
-def on_second(body):
-    pl.when(lax.axis_index("line") == 1)(body)
-
-
-def up_factor_kernel(upper, pivot, after, out):
-    on_second(lambda: multiply_lines(upper.at[1], pivot.at[1], out))
-
-
-def up_product_kernel(given, upper, pivot, after, first, second, work, made):
-    def body():
-        multiply_lines(given, upper.at[0], work)
-        multiply_lines(work, pivot.at[0], made)
-        size = first.shape[0]
-        first[...] = made[:size]
-        second[...] = made[size:]
-
-    on_second(body)
-
-
 def factor_kernel(lower, pivot, after, factor, out):
     def body():
         multiply_lines(lower.at[0], pivot.at[0], factor)
@@ -302,7 +283,7 @@
 
 def short_turn_kernel(
     vector, lower, pivot, upper, response, alone, message, carried_in, received,
-    carried, passed, upward, to_second, to_first, forward, entry, work, result, coupled,
+    carried, upward, outgoing, passed, forward, entry, work, result, coupled,
 ):
     carried[...] = carried_in[...] + received[...]
     set_entry(carried, entry)
@@ -311,12 +292,11 @@
     entry[...] = message[0] - passed[...]
     upward[...] = alone[...] + apply_turned(response, entry)
     run_up(forward, upper, pivot, upward, result, coupled)
-    to_second[...] = result[0]
-    to_first[...] = result[0]
+    outgoing[...] = result[0]
 
 
 def short_end_kernel(
-    beside, beyond, onward, vector, lower, pivot, upper, forward_in, carried, first, second, upward,
+    vector, lower, pivot, upper, forward_in, carried, upward, received, onward,
     result, coupled, last, forward, entry, work,
 ):
     forward[...] = forward_in[...]
@@ -326,9 +306,7 @@
         run_down(vector, lower, pivot, entry, forward, work)
 
     on_last(again)
-    size = first.shape[0]
-    through = apply_turned(first, beyond.at[:size]) + apply_turned(second, beyond.at[size:])
-    entry[...] = upward[...] + beside[...] + through
+    entry[...] = upward[...] + received[...]
     run_up(forward, upper, pivot, entry, result, coupled)
     last[...] = result[result.shape[0] - 1]
 
@@ -454,7 +432,7 @@
     return near, far
 
 
-def sweep_short(vector, message, last, lower, pivot, upper, response, product):
+def sweep_short(vector, message, last, lower, pivot, upper, response):
     field, one = vector.shape, last.shape
     received = lax.ppermute(message, "line", [(0, 1), (2, 3)])
     carried, onto, forward = stage(
@@ -465,20 +443,27 @@
     )
     received = lax.ppermute(onto, "line", [(1, 2)])
     (alone,) = stage(alone_kernel, [one], [forward, upper, pivot], [field, field])
-    alone = lax.ppermute(alone, "line", [(3, 2), (1, 0)])
-    carried, passed, upward, to_second, to_first, forward = stage(
+    alone = lax.ppermute(alone, "line", [(3, 2)])
+    carried, upward, outgoing, passed, forward = stage(
         short_turn_kernel,
-        [message.shape, one, one, one, one, field],
+        [message.shape, one, one, one, field],
         [vector, lower, pivot, upper, response, alone, message, carried, received],
         [one, one, field, field],
     )
-    beside = lax.ppermute(to_second, "line", [(2, 1)])
-    beyond = lax.ppermute(to_first, "line", [(2, 0)])
+    received = lax.ppermute(outgoing, "line", [(2, 1)])
+    upward, outgoing = stage(
+        functools.partial(hop_up_kernel, 2),
+        [one, one],
+        [forward, upper, pivot, upward, received],
+        [field, field],
+    )
+    outgoing, passed = lax.optimization_barrier((outgoing, passed))
+    received = lax.ppermute(outgoing, "line", [(1, 0)])
     onward = lax.ppermute(passed, "line", [(2, 3)])
     direction, coupled, last = stage(
         short_end_kernel,
         [field, field, one],
-        [beside, beyond, onward, vector, lower, pivot, upper, forward, carried, *product, upward],
+        [vector, lower, pivot, upper, forward, carried, upward, received, onward],
         [field, one, one],
     )
     return direction, coupled, last, carried
@@ -505,18 +490,14 @@
     directions = []
     last = None
     short = line == 4 and count == 2
-    third = block // 3
     for j in range(ITERS):
         if j >= 2 and short:
             direction, coupled, last, carried_down = sweep_short(
-                vector, message, last, lower, pivot, upper, response, up_product
+                vector, message, last, lower, pivot, upper, response
             )
         else:
             parts = []
             for turn in range(line - 1):
-                if j == 1 and turn == 2 and short:
-                    message, rest = lax.optimization_barrier((message, up_product[1]))
-                    up_product[1] = lax.ppermute(rest, "line", [(1, 0)])
                 parts.append(lax.ppermute(message, "line", [(turn, turn + 1)]))
                 if j == 0 and turn == 0:
                     (upper,) = load((upper,), message)
@@ -524,16 +505,13 @@
                     factor, response = stage(
                         factor_kernel, [(block,) + one] * 2, [lower, pivot, message]
                     )
-                    (up_factor,) = stage(
-                        up_factor_kernel, [(block,) + one], [upper, pivot, message]
-                    )
                 if turn < line - 2:
                     lasts = [] if last is None else [last]
-                    carried, message, _ = stage(
+                    carried, message = stage(
                         functools.partial(hop_down_kernel, len(parts), bool(lasts)),
-                        [message.shape, message.shape, field],
+                        [message.shape, message.shape],
                         [vector, lower, pivot, *parts, *lasts],
-                        [one, one],
+                        [field, one, one],
                     )
                     parts = [carried]
             parts = parts or [jnp.zeros_like(message)]
@@ -544,30 +522,18 @@
                 [one, one, field, field],
             )
             if j == 0 and short:
-                outgoing, response, up_factor = lax.optimization_barrier(
-                    (outgoing, response, up_factor)
-                )
+                outgoing, response = lax.optimization_barrier((outgoing, response))
             parts = []
             for turn in reversed(range(line - 1)):
                 if j == 1 and turn == line - 3 and short:
                     outgoing, ready = lax.optimization_barrier((outgoing, response))
                     response = lax.ppermute(ready, "line", [(line - 1, line - 2)])
-                if j == 1 and turn == 0 and short:
-                    outgoing, up_product[1] = lax.optimization_barrier(
-                        (outgoing, up_product[1])
-                    )
                 parts.append(lax.ppermute(outgoing, "line", [(turn + 1, turn)]))
                 if j == 0 and turn == line - 2:
                     diag_block, near_block, far_block = load(
                         (diag_block, east, west), outgoing, True
                     )
                 if j == 0 and turn == line - 3 and short:
-                    up_product = stage(
-                        up_product_kernel,
-                        [(third,) + one, (block - third,) + one],
-                        [up_factor, upper, pivot, outgoing],
-                        [(block,) + one] * 2,
-                    )
                     (response,) = stage(
                         response_kernel,
                         [(block,) + one],
@@ -582,10 +548,6 @@
                         [field, field],
                     )
                     parts = [carried]
-                    if j == 0 and turn == line - 3 and short:
-                        outgoing, *up_product = lax.optimization_barrier(
-                            (outgoing, *up_product)
-                        )
             parts = parts or [jnp.zeros_like(outgoing)]
             direction, coupled, last = stage(
                 functools.partial(end_kernel, len(parts)),
@@ -594,9 +556,6 @@
                 [one],
             )
         directions.append(direction)
-        if j == 1 and short:
-            direction, part = lax.optimization_barrier((direction, up_product[0]))
-            up_product[0] = lax.ppermute(part, "line", [(1, 0)])
         near, far = rows_beside(direction, across)
         whole, image = stage(
             own_kernel,

time: 161 us -> 148 us (0.919)
  starting transfers between devices: 44.3 us -> 32.1 us
  waiting for transfers between devices: 71.8 us -> 74 us
  Pallas kernels: 21.9 us -> 19.9 us
    ppermute x6, waiting for transfers between devices: 24.3 us -> 38 us  [per_device(): parts.append(lax.ppermute(outgoing, 'line', [(turn + 1, turn)]))]
    ppermute x8 -> x6, waiting for transfers between devices: 40.7 us -> 29 us  [the longest x2 29 us: sweep_short(): received = lax.ppermute(outgoing, 'line', [(1, 0)])]
    ppermute x4, starting transfers between devices: 5.91 us -> 1.01 us  [rows_beside(): near = lax.ppermute(to_near, 'patch', even + [(b, a) for a, b in even])]
    ppermute x8 -> x6, starting transfers between devices: 9.08 us -> 5.23 us  [the longest x2 2.58 us: sweep_short(): received = lax.ppermute(outgoing, 'line', [(1, 0)])]
    ppermute x2, starting transfers between devices: 6.65 us -> 3.25 us  [sweep_short(): received = lax.ppermute(message, 'line', [(0, 1), (2, 3)])]
    pallas_call x38, Pallas kernels: 16.5 us -> 14.4 us  [stage(): pl.pallas_call(kernel, out_shape=[pltpu.VMEM(shape, jnp.float32) for shap...]
  transfers between devices with their start and end apart: 36 -> 34, of which waited for: 12 -> 10; matrix products, arithmetic and copies ran while one was open for 0% -> 0% of each run, Pallas kernels for 6% -> 6%
where the time goes in v14:
time: 148 us; the launch traced here: 147 us
  waiting for transfers between devices  74 us (50%)
  starting transfers between devices  32.1 us (22%)
  Pallas kernels  19.9 us (13%)
  blocking collectives  19 us (13%)
  local copies, waits for them, and re-layouts  1.48 us (1%)
    ppermute x6, waiting for transfers between devices, per_device(): parts.append(lax.ppermute(outgoing, 'line', [(turn + 1, turn)]))  38 us
    ppermute x2, waiting for transfers between devices, sweep_short(): received = lax.ppermute(outgoing, 'line', [(1, 0)])  29 us
    all_to_all x1, blocking collectives, per_device(): sums = lax.all_to_all(sums, ('line', 'patch'), 0, 0, tiled=True)  19 us
    pallas_call x38, Pallas kernels, stage(): pl.pallas_call(kernel, out_shape=[pltpu.VMEM(shape, jnp.float32) for shap...  14.4 us
    ppermute x6, starting transfers between devices, per_device(): parts.append(lax.ppermute(message, 'line', [(turn, turn + 1)]))  9.12 us
    ppermute x6, starting transfers between devices, per_device(): parts.append(lax.ppermute(outgoing, 'line', [(turn + 1, turn)]))  5.42 us
    ppermute x2, waiting for transfers between devices, sweep_short(): received = lax.ppermute(message, 'line', [(0, 1), (2, 3)])  3.46 us
    ppermute x2, starting transfers between devices, sweep_short(): received = lax.ppermute(message, 'line', [(0, 1), (2, 3)])  3.25 us
  transfers between devices with their start and end apart: 34, of which 10 were waited for; matrix products, arithmetic and copies ran while one was open for 0% of the time, Pallas kernels for 6%

profile of v14, /device:TPU:0, one launch (start us, length us, event | category | flops | bytes accessed | tf_op | source)
XLA Modules:
  0.0 147.0 jit_solution(5777169115748112689)
XLA Ops:
  0.0 1.7 %shard_map.73 = (bf16[2,48,48,128]{3,2,1,0:T(8,128)(2,1)S(1)}, bf16[2,48,48,128]{3,2,1,0:T(8,128)(2,1)S(1)}, f32[1,48,128]{2,1,0:T(8,128)S(1)}) custom-call(f32[2,48,128]{2,1,0:T(8,128)} %bitcast.15, bf16[2,48,48,128]{3,2,1,0:T(8,128)(2,1)} %bitcast.26, bf16[2,48,48,128]{3,2,1,0:T(8,128)(2,1)} %bitcast.27), custom_call_target="tpu_custom_call" | custom-call | tf_op jit(solution)/shard_map/pallas_call | solution.py:73
  1.7 4.8 %collective-permute-start = (f32[1,48,128]{2,1,0:T(8,128)S(1)}, f32[1,48,128]{2,1,0:T(8,128)S(1)}, u32[]{:S(2)}, u32[]{:S(2)}) collective-permute-start(f32[1,48,128]{2,1,0:T(8,128)S(1)} %get-tuple-element.97.refs_1_), channel_id=1, source_target_pairs={{0,8},{1,9},{2,10},{3,11},{4,12},{5,13},{6,14},{7,15}} | collective-permute-start | bytes 73736 | tf_op jit(solution)/shard_map/ppermute | solution.py:501
  6.5 0.9 shard_map.74
  7.5 0.6 collective-permute-done.refs_0_
  8.4 0.7 collective-permute-start.1
  9.1 0.4 shard_map.77
  9.6 0.7 collective-permute-start.2
  10.4 0.7 shard_map.75.upper
  11.1 0.6 shard_map.78
  11.7 0.7 collective-permute-start.3
  12.8 0.7 collective-permute-start.4
  13.5 0.4 shard_map.82
  13.9 1.3 collective-permute-start.5
  15.2 18.0 %collective-permute-done.5.refs_1_ = f32[48,128]{1,0:T(8,128)S(1)} collective-permute-done((f32[48,128]{1,0:T(8,128)S(1)}, f32[48,128]{1,0:T(8,128)S(1)}, u32[]{:S(2)}, u32[]{:S(2)}) %collective-permute-start.5) | collective-permute-done | bytes 24608 | tf_op jit(solution)/shard_map/ppermute | solution.py:531
  33.8 0.8 collective-permute-start.7
  35.2 2.1 %shard_map.80 = (f32[2,48,48,128]{3,2,1,0:T(8,128)S(1)}, f32[2,48,48,128]{3,2,1,0:T(8,128)S(1)}, f32[2,48,48,128]{3,2,1,0:T(8,128)S(1)}) custom-call(bf16[2,48,48,128]{3,2,1,0:T(8,128)(2,1)S(1)} %bitcast.21, bf16[2,48,48,128]{3,2,1,0:T(8,128)(2,1)S(1)} %bitcast.22, bf16[2,48,48,128]{3,2,1,0:T(8,128)(2,1)S(1)} %bitcast.23, ...), custom_call_target="tpu_custom_call" | custom-call | tf_op jit(solution)/shard_map/pallas_call | solution.py:131
  37.4 0.4 shard_map.84
  38.0 0.5 shard_map.86
  38.5 1.6 %collective-permute-start.8 = (f32[2,48,128]{2,1,0:T(8,128)S(1)}, f32[2,48,128]{2,1,0:T(8,128)S(1)}, u32[]{:S(2)}, u32[]{:S(2)}) collective-permute-start(f32[2,48,128]{2,1,0:T(8,128)S(1)} %get-tuple-element.122), channel_id=1, source_target_pairs={{0,8},{1,9},{2,10},{3,11},{4,12},{5,13},{6,14},{7,15}} | collective-permute-start | bytes 147464 | tf_op jit(solution)/shard_map/ppermute | solution.py:501
  40.1 1.7 %collective-permute-done.8.refs_0_ = f32[2,48,128]{2,1,0:T(8,128)S(1)} collective-permute-done((f32[2,48,128]{2,1,0:T(8,128)S(1)}, f32[2,48,128]{2,1,0:T(8,128)S(1)}, u32[]{:S(2)}, u32[]{:S(2)}) %collective-permute-start.8) | collective-permute-done | bytes 49184 | tf_op jit(solution)/shard_map/ppermute | solution.py:501
  42.3 0.7 collective-permute-start.9
  43.0 0.4 shard_map.89
  43.4 0.7 collective-permute-start.10
  44.1 0.6 shard_map.90
  44.7 0.7 collective-permute-start.11
  45.4 0.4 shard_map.91
  45.8 0.7 collective-permute-start.16
  46.5 0.7 collective-permute-start.12
  47.2 0.4 shard_map.92
  47.6 1.5 %collective-permute-start.13 = (f32[48,128]{1,0:T(8,128)S(1)}, f32[48,128]{1,0:T(8,128)S(1)}, u32[]{:S(2)}, u32[]{:S(2)}) collective-permute-start(f32[48,128]{1,0:T(8,128)S(1)} %get-tuple-element.135), channel_id=1, source_target_pairs={{8,0},{9,1},{10,2},{11,3},{12,4},{13,5},{14,6},{15,7}} | collective-permute-start | bytes 73736 | tf_op jit(solution)/shard_map/ppermute | solution.py:531
  49.1 20.0 %collective-permute-done.13.refs_1_ = f32[48,128]{1,0:T(8,128)S(1)} collective-permute-done((f32[48,128]{1,0:T(8,128)S(1)}, f32[48,128]{1,0:T(8,128)S(1)}, u32[]{:S(2)}, u32[]{:S(2)}) %collective-permute-start.13) | collective-permute-done | bytes 24608 | tf_op jit(solution)/shard_map/ppermute | solution.py:531
  69.6 0.7 collective-permute-start.15
  70.3 0.5 shard_map.94
  71.0 0.5 shard_map.96
  71.5 1.6 %collective-permute-start.17 = (f32[2,48,128]{2,1,0:T(8,128)S(1)}, f32[2,48,128]{2,1,0:T(8,128)S(1)}, u32[]{:S(2)}, u32[]{:S(2)}) collective-permute-start(f32[2,48,128]{2,1,0:T(8,128)S(1)} %get-tuple-element.142.message), channel_id=1, source_target_pairs={{0,8},{16,24},{1,9},{17,25},{2,10},{18,26},{3,11},{19,27},{4,12},{... | collective-permute-start | bytes 147464 | tf_op jit(solution)/shard_map/ppermute | solution.py:437
  73.1 1.7 %collective-permute-done.17.refs_0_ = f32[2,48,128]{2,1,0:T(8,128)S(1)} collective-permute-done((f32[2,48,128]{2,1,0:T(8,128)S(1)}, f32[2,48,128]{2,1,0:T(8,128)S(1)}, u32[]{:S(2)}, u32[]{:S(2)}) %collective-permute-start.17) | collective-permute-done | bytes 49184 | tf_op jit(solution)/shard_map/ppermute | solution.py:437
  75.3 0.7 collective-permute-start.19
  76.2 0.7 collective-permute-start.18
  76.9 0.9 shard_map.99
  77.8 0.7 collective-permute-start.20
  78.4 0.4 shard_map.100
  78.8 1.3 collective-permute-start.21
  80.1 0.7 collective-permute-start.22
  80.8 16.8 %collective-permute-done.21.received = f32[48,128]{1,0:T(8,128)S(1)} collective-permute-done((f32[48,128]{1,0:T(8,128)S(1)}, f32[48,128]{1,0:T(8,128)S(1)}, u32[]{:S(2)}, u32[]{:S(2)}) %collective-permute-start.21) | collective-permute-done | bytes 24608 | tf_op jit(solution)/shard_map/ppermute | solution.py:461
  98.1 0.7 collective-permute-start.24
  98.7 0.5 shard_map.102
  99.5 0.5 shard_map.104
  99.9 1.6 %collective-permute-start.25 = (f32[2,48,128]{2,1,0:T(8,128)S(1)}, f32[2,48,128]{2,1,0:T(8,128)S(1)}, u32[]{:S(2)}, u32[]{:S(2)}) collective-permute-start(f32[2,48,128]{2,1,0:T(8,128)S(1)} %get-tuple-element.160.message), channel_id=1, source_target_pairs={{0,8},{16,24},{1,9},{17,25},{2,10},{18,26},{3,11},{19,27},{4,12},{... | collective-permute-start | bytes 147464 | tf_op jit(solution)/shard_map/ppermute | solution.py:437
  101.6 1.7 %collective-permute-done.25.refs_0_ = f32[2,48,128]{2,1,0:T(8,128)S(1)} collective-permute-done((f32[2,48,128]{2,1,0:T(8,128)S(1)}, f32[2,48,128]{2,1,0:T(8,128)S(1)}, u32[]{:S(2)}, u32[]{:S(2)}) %collective-permute-start.25) | collective-permute-done | bytes 49184 | tf_op jit(solution)/shard_map/ppermute | solution.py:437
  103.3 0.4 shard_map.105
  103.7 0.7 collective-permute-start.27
  104.6 0.7 collective-permute-start.26
  105.3 0.9 shard_map.107
  106.2 0.7 collective-permute-start.28
  107.2 1.3 collective-permute-start.29
  108.5 0.7 collective-permute-start.30
  109.2 12.3 %collective-permute-done.29.received = f32[48,128]{1,0:T(8,128)S(1)} collective-permute-done((f32[48,128]{1,0:T(8,128)S(1)}, f32[48,128]{1,0:T(8,128)S(1)}, u32[]{:S(2)}, u32[]{:S(2)}) %collective-permute-start.29) | collective-permute-done | bytes 24608 | tf_op jit(solution)/shard_map/ppermute | solution.py:461
  121.8 0.8 collective-permute-start.31
  122.6 0.7 collective-permute-start.33
  123.3 1.9 %collective-permute-start.32 = (f32[48,128]{1,0:T(8,128)S(1)}, f32[48,128]{1,0:T(8,128)S(1)}, u32[]{:S(2)}, u32[]{:S(2)}) collective-permute-start(f32[48,128]{1,0:T(8,128)S(1)} %get-tuple-element.176), channel_id=1, source_target_pairs={{0,8},{8,16},{16,24},{1,9},{9,17},{17,25},{2,10},{10,18},{18,26},{... | collective-permute-start | bytes 73736 | tf_op jit(solution)/shard_map/ppermute | solution.py:569
  125.2 0.4 shard_map.110
  125.7 1.0 collective-permute-done.32.refs_1_
  127.3 19.0 %all_to_all.11 = f32[32,1,128]{2,1,0:T(1,128)S(1)} all-to-all(f32[32,1,128]{2,1,0:T(1,128)S(1)} %bitcast.24), channel_id=1, replica_groups=mesh['line'=4,'patch'=8] {'line','patch'}, dimensions={0} | all-to-all | bytes 32768 | tf_op jit(solution)/shard_map/all_to_all | solution.py:588
  146.4 0.6 copy.11
  (58 shorter events, 6.6 us)
Async XLA Ops:
  1.7 6.4 %collective-permute-start = (f32[1,48,128]{2,1,0:T(8,128)S(1)}, f32[1,48,128]{2,1,0:T(8,128)S(1)}, u32[]{:S(2)}, u32[]{:S(2)}) collective-permute-start(f32[1,48,128]{2,1,0:T(8,128)S(1)} %get-tuple-element.97.refs_1_), channel_id=1, source_target_pairs={{0,8},{1,9},{2,10},{3,11},{4,12},{5,13},{6,14},{7,15}} | collective-permute-start | bytes 73736 | tf_op jit(solution)/shard_map/ppermute | solution.py:501
  6.5 1.5 %copy-start = (f32[2,48,1,128]{3,2,1,0:T(1,128)S(1)}, f32[2,48,1,128]{3,2,1,0:T(1,128)}, u32[]{:S(2)}) copy-start(f32[2,48,1,128]{3,2,1,0:T(1,128)} %param.7) | copy-start | bytes 147460
  8.4 0.7 collective-permute-start.1
  9.1 1.3 copy-start.1
  9.6 1.6 %collective-permute-start.2 = (f32[1,48,128]{2,1,0:T(8,128)S(1)}, f32[1,48,128]{2,1,0:T(8,128)S(1)}, u32[]{:S(2)}, u32[]{:S(2)}) collective-permute-start(f32[1,48,128]{2,1,0:T(8,128)S(1)} %get-tuple-element.101.after), channel_id=1, source_target_pairs={{16,24},{17,25},{18,26},{19,27},{20,28},{21,29},{22,30},{23,31}} | collective-permute-start | bytes 73736 | tf_op jit(solution)/shard_map/ppermute | solution.py:501
  11.7 0.7 collective-permute-start.3
  12.8 0.7 collective-permute-start.4
  13.9 19.3 %collective-permute-start.5 = (f32[48,128]{1,0:T(8,128)S(1)}, f32[48,128]{1,0:T(8,128)S(1)}, u32[]{:S(2)}, u32[]{:S(2)}) collective-permute-start(f32[48,128]{1,0:T(8,128)S(1)} %get-tuple-element.111), channel_id=1, source_target_pairs={{8,0},{9,1},{10,2},{11,3},{12,4},{13,5},{14,6},{15,7}} | collective-permute-start | bytes 73736 | tf_op jit(solution)/shard_map/ppermute | solution.py:531
  33.3 1.3 copy-start.2
  33.3 1.6 %copy-start.3 = (bf16[2,48,48,1,128]{4,2,3,1,0:T(8,128)(2,1)S(1)}, bf16[2,48,48,1,128]{4,2,3,1,0:T(8,128)(2,1)}, u32[]{:S(2)}) copy-start(bf16[2,48,48,1,128]{4,2,3,1,0:T(8,128)(2,1)} %param.12) | copy-start | bytes 3538948
  33.3 2.0 %copy-start.4 = (bf16[2,48,48,1,128]{4,2,3,1,0:T(8,128)(2,1)S(1)}, bf16[2,48,48,1,128]{4,2,3,1,0:T(8,128)(2,1)}, u32[]{:S(2)}) copy-start(bf16[2,48,48,1,128]{4,2,3,1,0:T(8,128)(2,1)} %param.11) | copy-start | bytes 3538948
  33.7 4.1 %collective-permute-start.6 = (f32[2,48,128]{2,1,0:T(8,128)S(1)}, f32[2,48,128]{2,1,0:T(8,128)S(1)}, u32[]{:S(2)}, u32[]{:S(2)}) collective-permute-start(f32[2,48,128]{2,1,0:T(8,128)S(1)} %get-tuple-element.112.direction.refs_0_), channel_id=1, source_target_pairs={{0,1},{2,3},{4,5},{6,7},{1,0},{3,2},{5,4},{7,6},{8,9},{10,11},{12,... | collective-permute-start | bytes 147464 | tf_op jit(solution)/shard_map/ppermute | solution.py:426
  33.8 4.3 %collective-permute-start.7 = (f32[2,48,128]{2,1,0:T(8,128)S(1)}, f32[2,48,128]{2,1,0:T(8,128)S(1)}, u32[]{:S(2)}, u32[]{:S(2)}) collective-permute-start(f32[2,48,128]{2,1,0:T(8,128)S(1)} %get-tuple-element.112.direction.refs_0_), channel_id=1, source_target_pairs={{1,2},{3,4},{5,6},{2,1},{4,3},{6,5},{9,10},{11,12},{13,14},{10,9},... | collective-permute-start | bytes 147464 | tf_op jit(solution)/shard_map/ppermute | solution.py:425
  38.5 3.4 %collective-permute-start.8 = (f32[2,48,128]{2,1,0:T(8,128)S(1)}, f32[2,48,128]{2,1,0:T(8,128)S(1)}, u32[]{:S(2)}, u32[]{:S(2)}) collective-permute-start(f32[2,48,128]{2,1,0:T(8,128)S(1)} %get-tuple-element.122), channel_id=1, source_target_pairs={{0,8},{1,9},{2,10},{3,11},{4,12},{5,13},{6,14},{7,15}} | collective-permute-start | bytes 147464 | tf_op jit(solution)/shard_map/ppermute | solution.py:501
  42.3 0.7 collective-permute-start.9
  43.4 0.7 collective-permute-start.10
  44.7 0.7 collective-permute-start.11
  45.8 31.1 %collective-permute-start.16 = (f32[48,48,128]{2,1,0:T(8,128)S(1)}, f32[48,48,128]{2,1,0:T(8,128)S(1)}, u32[]{:S(2)}, u32[]{:S(2)}) collective-permute-start(f32[48,48,128]{2,1,0:T(8,128)S(1)} %shard_map.87), channel_id=1, source_target_pairs={{24,16},{25,17},{26,18},{27,19},{28,20},{29,21},{30,22},{31,23}} | collective-permute-start | bytes 3538952 | tf_op jit(solution)/shard_map/ppermute | solution.py:530
  46.5 0.7 collective-permute-start.12
  47.6 21.5 %collective-permute-start.13 = (f32[48,128]{1,0:T(8,128)S(1)}, f32[48,128]{1,0:T(8,128)S(1)}, u32[]{:S(2)}, u32[]{:S(2)}) collective-permute-start(f32[48,128]{1,0:T(8,128)S(1)} %get-tuple-element.135), channel_id=1, source_target_pairs={{8,0},{9,1},{10,2},{11,3},{12,4},{13,5},{14,6},{15,7}} | collective-permute-start | bytes 73736 | tf_op jit(solution)/shard_map/ppermute | solution.py:531
  69.5 1.3 collective-permute-start.14
  69.6 1.4 collective-permute-start.15
  71.5 3.4 %collective-permute-start.17 = (f32[2,48,128]{2,1,0:T(8,128)S(1)}, f32[2,48,128]{2,1,0:T(8,128)S(1)}, u32[]{:S(2)}, u32[]{:S(2)}) collective-permute-start(f32[2,48,128]{2,1,0:T(8,128)S(1)} %get-tuple-element.142.message), channel_id=1, source_target_pairs={{0,8},{16,24},{1,9},{17,25},{2,10},{18,26},{3,11},{19,27},{4,12},{... | collective-permute-start | bytes 147464 | tf_op jit(solution)/shard_map/ppermute | solution.py:437
  75.3 1.6 %collective-permute-start.19 = (f32[2,48,128]{2,1,0:T(8,128)S(1)}, f32[2,48,128]{2,1,0:T(8,128)S(1)}, u32[]{:S(2)}, u32[]{:S(2)}) collective-permute-start(f32[2,48,128]{2,1,0:T(8,128)S(1)} %get-tuple-element.145), channel_id=1, source_target_pairs={{8,16},{9,17},{10,18},{11,19},{12,20},{13,21},{14,22},{15,23}} | collective-permute-start | bytes 147464 | tf_op jit(solution)/shard_map/ppermute | solution.py:444
  76.2 0.7 collective-permute-start.18
  77.8 0.7 collective-permute-start.20
  78.8 18.7 %collective-permute-start.21 = (f32[48,128]{1,0:T(8,128)S(1)}, f32[48,128]{1,0:T(8,128)S(1)}, u32[]{:S(2)}, u32[]{:S(2)}) collective-permute-start(f32[48,128]{1,0:T(8,128)S(1)} %get-tuple-element.153), channel_id=1, source_target_pairs={{8,0},{9,1},{10,2},{11,3},{12,4},{13,5},{14,6},{15,7}} | collective-permute-start | bytes 73736 | tf_op jit(solution)/shard_map/ppermute | solution.py:461
  80.1 17.4 %collective-permute-start.22 = (f32[48,128]{1,0:T(8,128)S(1)}, f32[48,128]{1,0:T(8,128)S(1)}, u32[]{:S(2)}, u32[]{:S(2)}) collective-permute-start(f32[48,128]{1,0:T(8,128)S(1)} %get-tuple-element.154), channel_id=1, source_target_pairs={{16,24},{17,25},{18,26},{19,27},{20,28},{21,29},{22,30},{23,31}} | collective-permute-start | bytes 73736 | tf_op jit(solution)/shard_map/ppermute | solution.py:462
  98.0 1.3 collective-permute-start.23
  98.1 1.4 collective-permute-start.24
  99.9 3.4 %collective-permute-start.25 = (f32[2,48,128]{2,1,0:T(8,128)S(1)}, f32[2,48,128]{2,1,0:T(8,128)S(1)}, u32[]{:S(2)}, u32[]{:S(2)}) collective-permute-start(f32[2,48,128]{2,1,0:T(8,128)S(1)} %get-tuple-element.160.message), channel_id=1, source_target_pairs={{0,8},{16,24},{1,9},{17,25},{2,10},{18,26},{3,11},{19,27},{4,12},{... | collective-permute-start | bytes 147464 | tf_op jit(solution)/shard_map/ppermute | solution.py:437
  103.7 1.6 %collective-permute-start.27 = (f32[2,48,128]{2,1,0:T(8,128)S(1)}, f32[2,48,128]{2,1,0:T(8,128)S(1)}, u32[]{:S(2)}, u32[]{:S(2)}) collective-permute-start(f32[2,48,128]{2,1,0:T(8,128)S(1)} %get-tuple-element.163), channel_id=1, source_target_pairs={{8,16},{9,17},{10,18},{11,19},{12,20},{13,21},{14,22},{15,23}} | collective-permute-start | bytes 147464 | tf_op jit(solution)/shard_map/ppermute | solution.py:444
  104.6 0.7 collective-permute-start.26
  106.2 0.7 collective-permute-start.28
  107.2 14.2 %collective-permute-start.29 = (f32[48,128]{1,0:T(8,128)S(1)}, f32[48,128]{1,0:T(8,128)S(1)}, u32[]{:S(2)}, u32[]{:S(2)}) collective-permute-start(f32[48,128]{1,0:T(8,128)S(1)} %get-tuple-element.171), channel_id=1, source_target_pairs={{8,0},{9,1},{10,2},{11,3},{12,4},{13,5},{14,6},{15,7}} | collective-permute-start | bytes 73736 | tf_op jit(solution)/shard_map/ppermute | solution.py:461
  108.5 12.9 %collective-permute-start.30 = (f32[48,128]{1,0:T(8,128)S(1)}, f32[48,128]{1,0:T(8,128)S(1)}, u32[]{:S(2)}, u32[]{:S(2)}) collective-permute-start(f32[48,128]{1,0:T(8,128)S(1)} %get-tuple-element.172), channel_id=1, source_target_pairs={{16,24},{17,25},{18,26},{19,27},{20,28},{21,29},{22,30},{23,31}} | collective-permute-start | bytes 73736 | tf_op jit(solution)/shard_map/ppermute | solution.py:462
  121.8 4.9 %collective-permute-start.31 = (f32[2,48,128]{2,1,0:T(8,128)S(1)}, f32[2,48,128]{2,1,0:T(8,128)S(1)}, u32[]{:S(2)}, u32[]{:S(2)}) collective-permute-start(f32[2,48,128]{2,1,0:T(8,128)S(1)} %get-tuple-element.173.direction.refs_3_), channel_id=1, source_target_pairs={{0,1},{2,3},{4,5},{6,7},{1,0},{3,2},{5,4},{7,6},{8,9},{10,11},{12,... | collective-permute-start | bytes 147464 | tf_op jit(solution)/shard_map/ppermute | solution.py:426
  122.6 4.4 %collective-permute-start.33 = (f32[2,48,128]{2,1,0:T(8,128)S(1)}, f32[2,48,128]{2,1,0:T(8,128)S(1)}, u32[]{:S(2)}, u32[]{:S(2)}) collective-permute-start(f32[2,48,128]{2,1,0:T(8,128)S(1)} %get-tuple-element.173.direction.refs_3_), channel_id=1, source_target_pairs={{1,2},{3,4},{5,6},{2,1},{4,3},{6,5},{9,10},{11,12},{13,14},{10,9},... | collective-permute-start | bytes 147464 | tf_op jit(solution)/shard_map/ppermute | solution.py:425
  123.3 3.4 %collective-permute-start.32 = (f32[48,128]{1,0:T(8,128)S(1)}, f32[48,128]{1,0:T(8,128)S(1)}, u32[]{:S(2)}, u32[]{:S(2)}) collective-permute-start(f32[48,128]{1,0:T(8,128)S(1)} %get-tuple-element.176), channel_id=1, source_target_pairs={{0,8},{8,16},{16,24},{1,9},{9,17},{17,25},{2,10},{10,18},{18,26},{... | collective-permute-start | bytes 73736 | tf_op jit(solution)/shard_map/ppermute | solution.py:569

commit v15 on v14

--- a/solution.py
+++ b/solution.py
@@ -491,7 +491,7 @@
     last = None
     short = line == 4 and count == 2
     for j in range(ITERS):
-        if j >= 2 and short:
+        if j >= 1 and short:
             direction, coupled, last, carried_down = sweep_short(
                 vector, message, last, lower, pivot, upper, response
             )
@@ -525,9 +525,6 @@
                 outgoing, response = lax.optimization_barrier((outgoing, response))
             parts = []
             for turn in reversed(range(line - 1)):
-                if j == 1 and turn == line - 3 and short:
-                    outgoing, ready = lax.optimization_barrier((outgoing, response))
-                    response = lax.ppermute(ready, "line", [(line - 1, line - 2)])
                 parts.append(lax.ppermute(outgoing, "line", [(turn + 1, turn)]))
                 if j == 0 and turn == line - 2:
                     diag_block, near_block, far_block = load(
@@ -540,6 +537,7 @@
                         [factor, response, upper, pivot, outgoing],
                         [(block,) + one],
                     )
+                    response = lax.ppermute(response, "line", [(line - 1, line - 2)])
                 if turn > 0:
                     carried, outgoing = stage(
                         functools.partial(hop_up_kernel, len(parts)),
@@ -576,8 +574,6 @@
                 [image, far_block, far, lower, pivot, last],
                 [field, one],
             )
-            if j == 0 and short:
-                message, response = lax.optimization_barrier((message, response))
         else:
             (sums,) = stage(
                 last_kernel,

time: 148 us -> 151 us (1.020)
  starting transfers between devices: 32.1 us -> 35.4 us
    ppermute x2 -> x3, waiting for transfers between devices: 29 us -> 48.6 us  [sweep_short(): received = lax.ppermute(outgoing, 'line', [(1, 0)])]
    ppermute x6 -> x3, waiting for transfers between devices: 38 us -> 18.6 us  [per_device(): parts.append(lax.ppermute(outgoing, 'line', [(turn + 1, turn)]))]
    ppermute x4, starting transfers between devices: 1.01 us -> 4.24 us  [rows_beside(): near = lax.ppermute(to_near, 'patch', even + [(b, a) for a, b in even])]
    ppermute x6 -> x3, starting transfers between devices: 9.12 us -> 6.17 us  [per_device(): parts.append(lax.ppermute(message, 'line', [(turn, turn + 1)]))]
    ppermute x6 -> x3, starting transfers between devices: 5.42 us -> 2.62 us  [per_device(): parts.append(lax.ppermute(outgoing, 'line', [(turn + 1, turn)]))]
    ppermute x2 -> x3, starting transfers between devices: 3.25 us -> 5.17 us  [sweep_short(): received = lax.ppermute(message, 'line', [(0, 1), (2, 3)])]
    ppermute x6 -> x3, waiting for transfers between devices: 2.31 us -> 0.57 us  [per_device(): parts.append(lax.ppermute(message, 'line', [(turn, turn + 1)]))]
    ppermute x2 -> x3, waiting for transfers between devices: 3.46 us -> 5.19 us  [sweep_short(): received = lax.ppermute(message, 'line', [(0, 1), (2, 3)])]
where the time goes in v15:
time: 151 us; the launch traced here: 150 us
  waiting for transfers between devices  74.1 us (49%)
  starting transfers between devices  35.4 us (23%)
  Pallas kernels  19.4 us (13%)
  blocking collectives  19 us (13%)
  local copies, waits for them, and re-layouts  1.51 us (1%)
    ppermute x3, waiting for transfers between devices, sweep_short(): received = lax.ppermute(outgoing, 'line', [(1, 0)])  48.6 us
    all_to_all x1, blocking collectives, per_device(): sums = lax.all_to_all(sums, ('line', 'patch'), 0, 0, tiled=True)  19 us
    ppermute x3, waiting for transfers between devices, per_device(): parts.append(lax.ppermute(outgoing, 'line', [(turn + 1, turn)]))  18.6 us
    pallas_call x37, Pallas kernels, stage(): pl.pallas_call(kernel, out_shape=[pltpu.VMEM(shape, jnp.float32) for shap...  14 us
    ppermute x3, starting transfers between devices, per_device(): parts.append(lax.ppermute(message, 'line', [(turn, turn + 1)]))  6.17 us
    ppermute x3, waiting for transfers between devices, sweep_short(): received = lax.ppermute(message, 'line', [(0, 1), (2, 3)])  5.19 us
    ppermute x3, starting transfers between devices, sweep_short(): received = lax.ppermute(message, 'line', [(0, 1), (2, 3)])  5.17 us
    ppermute x4, starting transfers between devices, rows_beside(): near = lax.ppermute(to_near, 'patch', even + [(b, a) for a, b in even])  4.24 us
  transfers between devices with their start and end apart: 34, of which 10 were waited for; matrix products, arithmetic and copies ran while one was open for 0% of the time, Pallas kernels for 6%

profile of v15, /device:TPU:0, one launch (start us, length us, event | category | flops | bytes accessed | tf_op | source)
XLA Modules:
  0.0 150.1 jit_solution(3475088728938915588)
XLA Ops:
  0.0 1.7 %shard_map.73 = (bf16[2,48,48,128]{3,2,1,0:T(8,128)(2,1)S(1)}, bf16[2,48,48,128]{3,2,1,0:T(8,128)(2,1)S(1)}, f32[1,48,128]{2,1,0:T(8,128)S(1)}) custom-call(f32[2,48,128]{2,1,0:T(8,128)} %bitcast.15, bf16[2,48,48,128]{3,2,1,0:T(8,128)(2,1)} %bitcast.26, bf16[2,48,48,128]{3,2,1,0:T(8,128)(2,1)} %bitcast.27), custom_call_target="tpu_custom_call" | custom-call | tf_op jit(solution)/shard_map/pallas_call | solution.py:73
  1.7 4.8 %collective-permute-start = (f32[1,48,128]{2,1,0:T(8,128)S(1)}, f32[1,48,128]{2,1,0:T(8,128)S(1)}, u32[]{:S(2)}, u32[]{:S(2)}) collective-permute-start(f32[1,48,128]{2,1,0:T(8,128)S(1)} %get-tuple-element.94.refs_1_), channel_id=1, source_target_pairs={{0,8},{1,9},{2,10},{3,11},{4,12},{5,13},{6,14},{7,15}} | collective-permute-start | bytes 73736 | tf_op jit(solution)/shard_map/ppermute | solution.py:501
  6.5 0.9 shard_map.74
  7.5 0.6 collective-permute-done.refs_0_
  8.0 0.4 shard_map.76
  8.4 0.7 collective-permute-start.1
  9.1 0.4 shard_map.77
  9.6 0.7 collective-permute-start.2
  10.4 0.7 shard_map.75.upper
  11.1 0.6 shard_map.78
  11.7 0.7 collective-permute-start.3
  12.8 0.7 collective-permute-start.8
  13.6 0.7 collective-permute-start.4
  14.3 0.4 shard_map.82
  14.7 1.3 collective-permute-start.5
  16.0 18.6 %collective-permute-done.5.refs_1_ = f32[48,128]{1,0:T(8,128)S(1)} collective-permute-done((f32[48,128]{1,0:T(8,128)S(1)}, f32[48,128]{1,0:T(8,128)S(1)}, u32[]{:S(2)}, u32[]{:S(2)}) %collective-permute-start.5) | collective-permute-done | bytes 24608 | tf_op jit(solution)/shard_map/ppermute | solution.py:528
  35.1 0.8 collective-permute-start.7
  36.6 2.1 %shard_map.80 = (f32[2,48,48,128]{3,2,1,0:T(8,128)S(1)}, f32[2,48,48,128]{3,2,1,0:T(8,128)S(1)}, f32[2,48,48,128]{3,2,1,0:T(8,128)S(1)}) custom-call(bf16[2,48,48,128]{3,2,1,0:T(8,128)(2,1)S(1)} %bitcast.21, bf16[2,48,48,128]{3,2,1,0:T(8,128)(2,1)S(1)} %bitcast.22, bf16[2,48,48,128]{3,2,1,0:T(8,128)(2,1)S(1)} %bitcast.23, ...), custom_call_target="tpu_custom_call" | custom-call | tf_op jit(solution)/shard_map/pallas_call | solution.py:131
  39.3 0.5 shard_map.86
  39.8 1.6 %collective-permute-start.9 = (f32[2,48,128]{2,1,0:T(8,128)S(1)}, f32[2,48,128]{2,1,0:T(8,128)S(1)}, u32[]{:S(2)}, u32[]{:S(2)}) collective-permute-start(f32[2,48,128]{2,1,0:T(8,128)S(1)} %get-tuple-element.118.message), channel_id=1, source_target_pairs={{0,8},{16,24},{1,9},{17,25},{2,10},{18,26},{3,11},{19,27},{4,12},{... | collective-permute-start | bytes 147464 | tf_op jit(solution)/shard_map/ppermute | solution.py:437
  41.4 1.7 %collective-permute-done.9.refs_0_ = f32[2,48,128]{2,1,0:T(8,128)S(1)} collective-permute-done((f32[2,48,128]{2,1,0:T(8,128)S(1)}, f32[2,48,128]{2,1,0:T(8,128)S(1)}, u32[]{:S(2)}, u32[]{:S(2)}) %collective-permute-start.9) | collective-permute-done | bytes 49184 | tf_op jit(solution)/shard_map/ppermute | solution.py:437
  43.5 0.7 collective-permute-start.11
  44.4 0.7 collective-permute-start.10
  45.1 0.9 shard_map.90
  46.0 0.7 collective-permute-start.12
  46.7 0.4 shard_map.91
  47.1 1.3 collective-permute-start.13
  48.4 0.7 collective-permute-start.14
  49.1 24.1 %collective-permute-done.13.received = f32[48,128]{1,0:T(8,128)S(1)} collective-permute-done((f32[48,128]{1,0:T(8,128)S(1)}, f32[48,128]{1,0:T(8,128)S(1)}, u32[]{:S(2)}, u32[]{:S(2)}) %collective-permute-start.13) | collective-permute-done | bytes 24608 | tf_op jit(solution)/shard_map/ppermute | solution.py:461
  73.7 0.7 collective-permute-start.16
  74.3 0.5 shard_map.93
  75.1 0.4 shard_map.95
  75.5 1.6 %collective-permute-start.17 = (f32[2,48,128]{2,1,0:T(8,128)S(1)}, f32[2,48,128]{2,1,0:T(8,128)S(1)}, u32[]{:S(2)}, u32[]{:S(2)}) collective-permute-start(f32[2,48,128]{2,1,0:T(8,128)S(1)} %get-tuple-element.136.message), channel_id=1, source_target_pairs={{0,8},{16,24},{1,9},{17,25},{2,10},{18,26},{3,11},{19,27},{4,12},{... | collective-permute-start | bytes 147464 | tf_op jit(solution)/shard_map/ppermute | solution.py:437
  77.2 1.7 %collective-permute-done.17.refs_0_ = f32[2,48,128]{2,1,0:T(8,128)S(1)} collective-permute-done((f32[2,48,128]{2,1,0:T(8,128)S(1)}, f32[2,48,128]{2,1,0:T(8,128)S(1)}, u32[]{:S(2)}, u32[]{:S(2)}) %collective-permute-start.17) | collective-permute-done | bytes 49184 | tf_op jit(solution)/shard_map/ppermute | solution.py:437
  78.9 0.4 shard_map.96
  79.3 0.7 collective-permute-start.19
  80.2 0.7 collective-permute-start.18
  80.9 0.9 shard_map.98
  81.8 0.7 collective-permute-start.20
  82.5 0.4 shard_map.99
  82.9 1.3 collective-permute-start.21
  84.2 0.7 collective-permute-start.22
  84.9 12.3 %collective-permute-done.21.received = f32[48,128]{1,0:T(8,128)S(1)} collective-permute-done((f32[48,128]{1,0:T(8,128)S(1)}, f32[48,128]{1,0:T(8,128)S(1)}, u32[]{:S(2)}, u32[]{:S(2)}) %collective-permute-start.21) | collective-permute-done | bytes 24608 | tf_op jit(solution)/shard_map/ppermute | solution.py:461
  97.5 0.8 collective-permute-start.23
  98.3 0.7 collective-permute-start.24
  99.0 0.5 shard_map.101
  99.7 0.4 shard_map.103
  100.1 1.9 %collective-permute-start.25 = (f32[2,48,128]{2,1,0:T(8,128)S(1)}, f32[2,48,128]{2,1,0:T(8,128)S(1)}, u32[]{:S(2)}, u32[]{:S(2)}) collective-permute-start(f32[2,48,128]{2,1,0:T(8,128)S(1)} %get-tuple-element.154.message), channel_id=1, source_target_pairs={{0,8},{16,24},{1,9},{17,25},{2,10},{18,26},{3,11},{19,27},{4,12},{... | collective-permute-start | bytes 147464 | tf_op jit(solution)/shard_map/ppermute | solution.py:437
  102.0 1.7 %collective-permute-done.25.refs_0_ = f32[2,48,128]{2,1,0:T(8,128)S(1)} collective-permute-done((f32[2,48,128]{2,1,0:T(8,128)S(1)}, f32[2,48,128]{2,1,0:T(8,128)S(1)}, u32[]{:S(2)}, u32[]{:S(2)}) %collective-permute-start.25) | collective-permute-done | bytes 49184 | tf_op jit(solution)/shard_map/ppermute | solution.py:437
  103.8 0.4 shard_map.104
  104.2 0.7 collective-permute-start.27
  105.1 0.7 collective-permute-start.26
  105.8 0.9 shard_map.106
  106.6 0.7 collective-permute-start.28
  107.7 1.3 collective-permute-start.29
  109.0 0.7 collective-permute-start.30
  109.7 12.3 %collective-permute-done.29.received = f32[48,128]{1,0:T(8,128)S(1)} collective-permute-done((f32[48,128]{1,0:T(8,128)S(1)}, f32[48,128]{1,0:T(8,128)S(1)}, u32[]{:S(2)}, u32[]{:S(2)}) %collective-permute-start.29) | collective-permute-done | bytes 24608 | tf_op jit(solution)/shard_map/ppermute | solution.py:461
  122.3 3.3 %collective-permute-start.31 = (f32[2,48,128]{2,1,0:T(8,128)S(1)}, f32[2,48,128]{2,1,0:T(8,128)S(1)}, u32[]{:S(2)}, u32[]{:S(2)}) collective-permute-start(f32[2,48,128]{2,1,0:T(8,128)S(1)} %get-tuple-element.167.direction.refs_3_), channel_id=1, source_target_pairs={{0,1},{2,3},{4,5},{6,7},{1,0},{3,2},{5,4},{7,6},{8,9},{10,11},{12,... | collective-permute-start | bytes 147464 | tf_op jit(solution)/shard_map/ppermute | solution.py:426
  125.6 0.7 collective-permute-start.33
  126.3 1.9 %collective-permute-start.32 = (f32[48,128]{1,0:T(8,128)S(1)}, f32[48,128]{1,0:T(8,128)S(1)}, u32[]{:S(2)}, u32[]{:S(2)}) collective-permute-start(f32[48,128]{1,0:T(8,128)S(1)} %get-tuple-element.170), channel_id=1, source_target_pairs={{0,8},{8,16},{16,24},{1,9},{9,17},{17,25},{2,10},{10,18},{18,26},{... | collective-permute-start | bytes 73736 | tf_op jit(solution)/shard_map/ppermute | solution.py:567
  128.2 0.4 shard_map.109
  128.7 1.0 collective-permute-done.32.refs_1_
  130.3 19.0 %all_to_all.11 = f32[32,1,128]{2,1,0:T(1,128)S(1)} all-to-all(f32[32,1,128]{2,1,0:T(1,128)S(1)} %bitcast.24), channel_id=1, replica_groups=mesh['line'=4,'patch'=8] {'line','patch'}, dimensions={0} | all-to-all | bytes 32768 | tf_op jit(solution)/shard_map/all_to_all | solution.py:584
  149.5 0.6 copy.11
  (57 shorter events, 6.2 us)
Async XLA Ops:
  1.7 6.4 %collective-permute-start = (f32[1,48,128]{2,1,0:T(8,128)S(1)}, f32[1,48,128]{2,1,0:T(8,128)S(1)}, u32[]{:S(2)}, u32[]{:S(2)}) collective-permute-start(f32[1,48,128]{2,1,0:T(8,128)S(1)} %get-tuple-element.94.refs_1_), channel_id=1, source_target_pairs={{0,8},{1,9},{2,10},{3,11},{4,12},{5,13},{6,14},{7,15}} | collective-permute-start | bytes 73736 | tf_op jit(solution)/shard_map/ppermute | solution.py:501
  6.5 1.5 %copy-start = (f32[2,48,1,128]{3,2,1,0:T(1,128)S(1)}, f32[2,48,1,128]{3,2,1,0:T(1,128)}, u32[]{:S(2)}) copy-start(f32[2,48,1,128]{3,2,1,0:T(1,128)} %param.7) | copy-start | bytes 147460
  8.4 0.7 collective-permute-start.1
  9.1 1.3 copy-start.1
  9.6 1.6 %collective-permute-start.2 = (f32[1,48,128]{2,1,0:T(8,128)S(1)}, f32[1,48,128]{2,1,0:T(8,128)S(1)}, u32[]{:S(2)}, u32[]{:S(2)}) collective-permute-start(f32[1,48,128]{2,1,0:T(8,128)S(1)} %get-tuple-element.98.after), channel_id=1, source_target_pairs={{16,24},{17,25},{18,26},{19,27},{20,28},{21,29},{22,30},{23,31}} | collective-permute-start | bytes 73736 | tf_op jit(solution)/shard_map/ppermute | solution.py:501
  11.7 0.7 collective-permute-start.3
  12.8 32.3 %collective-permute-start.8 = (f32[48,48,128]{2,1,0:T(8,128)S(1)}, f32[48,48,128]{2,1,0:T(8,128)S(1)}, u32[]{:S(2)}, u32[]{:S(2)}) collective-permute-start(f32[48,48,128]{2,1,0:T(8,128)S(1)} %shard_map.87), channel_id=1, source_target_pairs={{24,16},{25,17},{26,18},{27,19},{28,20},{29,21},{30,22},{31,23}} | collective-permute-start | bytes 3538952 | tf_op jit(solution)/shard_map/ppermute | solution.py:540
  13.6 0.7 collective-permute-start.4
  14.7 19.9 %collective-permute-start.5 = (f32[48,128]{1,0:T(8,128)S(1)}, f32[48,128]{1,0:T(8,128)S(1)}, u32[]{:S(2)}, u32[]{:S(2)}) collective-permute-start(f32[48,128]{1,0:T(8,128)S(1)} %get-tuple-element.108), channel_id=1, source_target_pairs={{8,0},{9,1},{10,2},{11,3},{12,4},{13,5},{14,6},{15,7}} | collective-permute-start | bytes 73736 | tf_op jit(solution)/shard_map/ppermute | solution.py:528
  34.6 1.3 copy-start.2
  34.6 1.6 %copy-start.3 = (bf16[2,48,48,1,128]{4,2,3,1,0:T(8,128)(2,1)S(1)}, bf16[2,48,48,1,128]{4,2,3,1,0:T(8,128)(2,1)}, u32[]{:S(2)}) copy-start(bf16[2,48,48,1,128]{4,2,3,1,0:T(8,128)(2,1)} %param.12) | copy-start | bytes 3538948
  34.6 2.0 %copy-start.4 = (bf16[2,48,48,1,128]{4,2,3,1,0:T(8,128)(2,1)S(1)}, bf16[2,48,48,1,128]{4,2,3,1,0:T(8,128)(2,1)}, u32[]{:S(2)}) copy-start(bf16[2,48,48,1,128]{4,2,3,1,0:T(8,128)(2,1)} %param.11) | copy-start | bytes 3538948
  35.0 4.1 %collective-permute-start.6 = (f32[2,48,128]{2,1,0:T(8,128)S(1)}, f32[2,48,128]{2,1,0:T(8,128)S(1)}, u32[]{:S(2)}, u32[]{:S(2)}) collective-permute-start(f32[2,48,128]{2,1,0:T(8,128)S(1)} %get-tuple-element.109.direction.refs_0_), channel_id=1, source_target_pairs={{0,1},{2,3},{4,5},{6,7},{1,0},{3,2},{5,4},{7,6},{8,9},{10,11},{12,... | collective-permute-start | bytes 147464 | tf_op jit(solution)/shard_map/ppermute | solution.py:426
  35.1 4.2 %collective-permute-start.7 = (f32[2,48,128]{2,1,0:T(8,128)S(1)}, f32[2,48,128]{2,1,0:T(8,128)S(1)}, u32[]{:S(2)}, u32[]{:S(2)}) collective-permute-start(f32[2,48,128]{2,1,0:T(8,128)S(1)} %get-tuple-element.109.direction.refs_0_), channel_id=1, source_target_pairs={{1,2},{3,4},{5,6},{2,1},{4,3},{6,5},{9,10},{11,12},{13,14},{10,9},... | collective-permute-start | bytes 147464 | tf_op jit(solution)/shard_map/ppermute | solution.py:425
  39.8 3.4 %collective-permute-start.9 = (f32[2,48,128]{2,1,0:T(8,128)S(1)}, f32[2,48,128]{2,1,0:T(8,128)S(1)}, u32[]{:S(2)}, u32[]{:S(2)}) collective-permute-start(f32[2,48,128]{2,1,0:T(8,128)S(1)} %get-tuple-element.118.message), channel_id=1, source_target_pairs={{0,8},{16,24},{1,9},{17,25},{2,10},{18,26},{3,11},{19,27},{4,12},{... | collective-permute-start | bytes 147464 | tf_op jit(solution)/shard_map/ppermute | solution.py:437
  43.5 1.6 %collective-permute-start.11 = (f32[2,48,128]{2,1,0:T(8,128)S(1)}, f32[2,48,128]{2,1,0:T(8,128)S(1)}, u32[]{:S(2)}, u32[]{:S(2)}) collective-permute-start(f32[2,48,128]{2,1,0:T(8,128)S(1)} %get-tuple-element.121), channel_id=1, source_target_pairs={{8,16},{9,17},{10,18},{11,19},{12,20},{13,21},{14,22},{15,23}} | collective-permute-start | bytes 147464 | tf_op jit(solution)/shard_map/ppermute | solution.py:444
  44.4 0.7 collective-permute-start.10
  46.0 0.7 collective-permute-start.12
  47.1 26.1 %collective-permute-start.13 = (f32[48,128]{1,0:T(8,128)S(1)}, f32[48,128]{1,0:T(8,128)S(1)}, u32[]{:S(2)}, u32[]{:S(2)}) collective-permute-start(f32[48,128]{1,0:T(8,128)S(1)} %get-tuple-element.129), channel_id=1, source_target_pairs={{8,0},{9,1},{10,2},{11,3},{12,4},{13,5},{14,6},{15,7}} | collective-permute-start | bytes 73736 | tf_op jit(solution)/shard_map/ppermute | solution.py:461
  48.4 24.8 %collective-permute-start.14 = (f32[48,128]{1,0:T(8,128)S(1)}, f32[48,128]{1,0:T(8,128)S(1)}, u32[]{:S(2)}, u32[]{:S(2)}) collective-permute-start(f32[48,128]{1,0:T(8,128)S(1)} %get-tuple-element.130), channel_id=1, source_target_pairs={{16,24},{17,25},{18,26},{19,27},{20,28},{21,29},{22,30},{23,31}} | collective-permute-start | bytes 73736 | tf_op jit(solution)/shard_map/ppermute | solution.py:462
  73.6 1.3 collective-permute-start.15
  73.7 1.4 collective-permute-start.16
  75.5 3.4 %collective-permute-start.17 = (f32[2,48,128]{2,1,0:T(8,128)S(1)}, f32[2,48,128]{2,1,0:T(8,128)S(1)}, u32[]{:S(2)}, u32[]{:S(2)}) collective-permute-start(f32[2,48,128]{2,1,0:T(8,128)S(1)} %get-tuple-element.136.message), channel_id=1, source_target_pairs={{0,8},{16,24},{1,9},{17,25},{2,10},{18,26},{3,11},{19,27},{4,12},{... | collective-permute-start | bytes 147464 | tf_op jit(solution)/shard_map/ppermute | solution.py:437
  79.3 1.6 %collective-permute-start.19 = (f32[2,48,128]{2,1,0:T(8,128)S(1)}, f32[2,48,128]{2,1,0:T(8,128)S(1)}, u32[]{:S(2)}, u32[]{:S(2)}) collective-permute-start(f32[2,48,128]{2,1,0:T(8,128)S(1)} %get-tuple-element.139), channel_id=1, source_target_pairs={{8,16},{9,17},{10,18},{11,19},{12,20},{13,21},{14,22},{15,23}} | collective-permute-start | bytes 147464 | tf_op jit(solution)/shard_map/ppermute | solution.py:444
  80.2 0.7 collective-permute-start.18
  81.8 0.7 collective-permute-start.20
  82.9 14.2 %collective-permute-start.21 = (f32[48,128]{1,0:T(8,128)S(1)}, f32[48,128]{1,0:T(8,128)S(1)}, u32[]{:S(2)}, u32[]{:S(2)}) collective-permute-start(f32[48,128]{1,0:T(8,128)S(1)} %get-tuple-element.147), channel_id=1, source_target_pairs={{8,0},{9,1},{10,2},{11,3},{12,4},{13,5},{14,6},{15,7}} | collective-permute-start | bytes 73736 | tf_op jit(solution)/shard_map/ppermute | solution.py:461
  84.2 12.9 %collective-permute-start.22 = (f32[48,128]{1,0:T(8,128)S(1)}, f32[48,128]{1,0:T(8,128)S(1)}, u32[]{:S(2)}, u32[]{:S(2)}) collective-permute-start(f32[48,128]{1,0:T(8,128)S(1)} %get-tuple-element.148), channel_id=1, source_target_pairs={{16,24},{17,25},{18,26},{19,27},{20,28},{21,29},{22,30},{23,31}} | collective-permute-start | bytes 73736 | tf_op jit(solution)/shard_map/ppermute | solution.py:462
  97.5 1.9 %collective-permute-start.23 = (f32[2,48,128]{2,1,0:T(8,128)S(1)}, f32[2,48,128]{2,1,0:T(8,128)S(1)}, u32[]{:S(2)}, u32[]{:S(2)}) collective-permute-start(f32[2,48,128]{2,1,0:T(8,128)S(1)} %get-tuple-element.149.direction.refs_2_), channel_id=1, source_target_pairs={{0,1},{2,3},{4,5},{6,7},{1,0},{3,2},{5,4},{7,6},{8,9},{10,11},{12,... | collective-permute-start | bytes 147464 | tf_op jit(solution)/shard_map/ppermute | solution.py:426
  98.3 1.4 collective-permute-start.24
  100.1 3.7 %collective-permute-start.25 = (f32[2,48,128]{2,1,0:T(8,128)S(1)}, f32[2,48,128]{2,1,0:T(8,128)S(1)}, u32[]{:S(2)}, u32[]{:S(2)}) collective-permute-start(f32[2,48,128]{2,1,0:T(8,128)S(1)} %get-tuple-element.154.message), channel_id=1, source_target_pairs={{0,8},{16,24},{1,9},{17,25},{2,10},{18,26},{3,11},{19,27},{4,12},{... | collective-permute-start | bytes 147464 | tf_op jit(solution)/shard_map/ppermute | solution.py:437
  104.2 1.6 %collective-permute-start.27 = (f32[2,48,128]{2,1,0:T(8,128)S(1)}, f32[2,48,128]{2,1,0:T(8,128)S(1)}, u32[]{:S(2)}, u32[]{:S(2)}) collective-permute-start(f32[2,48,128]{2,1,0:T(8,128)S(1)} %get-tuple-element.157), channel_id=1, source_target_pairs={{8,16},{9,17},{10,18},{11,19},{12,20},{13,21},{14,22},{15,23}} | collective-permute-start | bytes 147464 | tf_op jit(solution)/shard_map/ppermute | solution.py:444
  105.1 0.7 collective-permute-start.26
  106.6 0.7 collective-permute-start.28
  107.7 14.2 %collective-permute-start.29 = (f32[48,128]{1,0:T(8,128)S(1)}, f32[48,128]{1,0:T(8,128)S(1)}, u32[]{:S(2)}, u32[]{:S(2)}) collective-permute-start(f32[48,128]{1,0:T(8,128)S(1)} %get-tuple-element.165), channel_id=1, source_target_pairs={{8,0},{9,1},{10,2},{11,3},{12,4},{13,5},{14,6},{15,7}} | collective-permute-start | bytes 73736 | tf_op jit(solution)/shard_map/ppermute | solution.py:461
  109.0 12.9 %collective-permute-start.30 = (f32[48,128]{1,0:T(8,128)S(1)}, f32[48,128]{1,0:T(8,128)S(1)}, u32[]{:S(2)}, u32[]{:S(2)}) collective-permute-start(f32[48,128]{1,0:T(8,128)S(1)} %get-tuple-element.166), channel_id=1, source_target_pairs={{16,24},{17,25},{18,26},{19,27},{20,28},{21,29},{22,30},{23,31}} | collective-permute-start | bytes 73736 | tf_op jit(solution)/shard_map/ppermute | solution.py:462
  122.3 7.4 %collective-permute-start.31 = (f32[2,48,128]{2,1,0:T(8,128)S(1)}, f32[2,48,128]{2,1,0:T(8,128)S(1)}, u32[]{:S(2)}, u32[]{:S(2)}) collective-permute-start(f32[2,48,128]{2,1,0:T(8,128)S(1)} %get-tuple-element.167.direction.refs_3_), channel_id=1, source_target_pairs={{0,1},{2,3},{4,5},{6,7},{1,0},{3,2},{5,4},{7,6},{8,9},{10,11},{12,... | collective-permute-start | bytes 147464 | tf_op jit(solution)/shard_map/ppermute | solution.py:426
  125.6 4.4 %collective-permute-start.33 = (f32[2,48,128]{2,1,0:T(8,128)S(1)}, f32[2,48,128]{2,1,0:T(8,128)S(1)}, u32[]{:S(2)}, u32[]{:S(2)}) collective-permute-start(f32[2,48,128]{2,1,0:T(8,128)S(1)} %get-tuple-element.167.direction.refs_3_), channel_id=1, source_target_pairs={{1,2},{3,4},{5,6},{2,1},{4,3},{6,5},{9,10},{11,12},{13,14},{10,9},... | collective-permute-start | bytes 147464 | tf_op jit(solution)/shard_map/ppermute | solution.py:425
  126.3 3.4 %collective-permute-start.32 = (f32[48,128]{1,0:T(8,128)S(1)}, f32[48,128]{1,0:T(8,128)S(1)}, u32[]{:S(2)}, u32[]{:S(2)}) collective-permute-start(f32[48,128]{1,0:T(8,128)S(1)} %get-tuple-element.170), channel_id=1, source_target_pairs={{0,8},{8,16},{16,24},{1,9},{9,17},{17,25},{2,10},{10,18},{18,26},{... | collective-permute-start | bytes 73736 | tf_op jit(solution)/shard_map/ppermute | solution.py:567

commit v16 on v14

--- a/solution.py
+++ b/solution.py
@@ -377,7 +377,7 @@
 
 
 def finish_kernel(parts_ref, *refs):
-    directions, out = refs[:-1], refs[-1]
+    *directions, final, out, sem = refs
     width = len(directions)
     total = jnp.sum(parts_ref[...], axis=0, keepdims=True)
     shape = (SUMS, total.shape[1])
@@ -411,6 +411,9 @@
         for j in range(1, width):
             step = step + coeffs[j] * directions[j][k]
         out[k] = step
+    copy = pltpu.make_async_copy(out, final, sem)
+    copy.start()
+    copy.wait()
 
 
 def rows_beside(field, across):
@@ -457,7 +460,6 @@
         [forward, upper, pivot, upward, received],
         [field, field],
     )
-    outgoing, passed = lax.optimization_barrier((outgoing, passed))
     received = lax.ppermute(outgoing, "line", [(1, 0)])
     onward = lax.ppermute(passed, "line", [(2, 3)])
     direction, coupled, last = stage(
@@ -586,7 +588,14 @@
                 [field],
             )
     sums = lax.all_to_all(sums, ("line", "patch"), 0, 0, tiled=True)
-    (step,) = stage(finish_kernel, [field], [sums, *directions])
+    step = pl.pallas_call(
+        finish_kernel,
+        out_shape=jax.ShapeDtypeStruct(field, jnp.float32),
+        in_specs=[pl.BlockSpec(memory_space=pltpu.VMEM)] * (1 + len(directions)),
+        out_specs=pl.BlockSpec(memory_space=pl.ANY),
+        scratch_shapes=[pltpu.VMEM(field, jnp.float32), pltpu.SemaphoreType.DMA],
+        compiler_params=pltpu.CompilerParams(vmem_limit_bytes=STAGE_ROOM),
+    )(sums, *directions)
     return step.reshape(shape)
 
 

time: 148 us -> 145 us (0.980)
    pallas_call x38 -> x37, Pallas kernels: 14.4 us -> 14.3 us  [stage(): pl.pallas_call(kernel, out_shape=[pltpu.VMEM(shape, jnp.float32) for shap...]
  transfers between devices with their start and end apart: 34 -> 34, of which waited for: 10 -> 10; matrix products, arithmetic and copies ran while one was open for 0% -> 0% of each run, Pallas kernels for 6% -> 7%
where the time goes in v16:
time: 145 us
  waiting for transfers between devices  72.6 us (50%)
  starting transfers between devices  32.1 us (22%)
  Pallas kernels  20.5 us (14%)
  blocking collectives  17.9 us (12%)
    ppermute x6, waiting for transfers between devices, per_device(): parts.append(lax.ppermute(outgoing, 'line', [(turn + 1, turn)]))  38 us
    ppermute x2, waiting for transfers between devices, sweep_short(): received = lax.ppermute(outgoing, 'line', [(1, 0)])  27.6 us
    all_to_all x1, blocking collectives, per_device(): sums = lax.all_to_all(sums, ('line', 'patch'), 0, 0, tiled=True)  17.9 us
    pallas_call x37, Pallas kernels, stage(): pl.pallas_call(kernel, out_shape=[pltpu.VMEM(shape, jnp.float32) for shap...  14.3 us
    ppermute x6, starting transfers between devices, per_device(): parts.append(lax.ppermute(message, 'line', [(turn, turn + 1)]))  9.12 us
    ppermute x6, starting transfers between devices, per_device(): parts.append(lax.ppermute(outgoing, 'line', [(turn + 1, turn)]))  5.42 us
    ppermute x2, waiting for transfers between devices, sweep_short(): received = lax.ppermute(message, 'line', [(0, 1), (2, 3)])  3.46 us
    ppermute x2, starting transfers between devices, sweep_short(): received = lax.ppermute(message, 'line', [(0, 1), (2, 3)])  3.25 us
  transfers between devices with their start and end apart: 34, of which 10 were waited for; matrix products, arithmetic and copies ran while one was open for 0% of the time, Pallas kernels for 7%

profile of v16, /device:TPU:0, one launch (start us, length us, event | category | flops | bytes accessed | tf_op | source)
XLA Modules:
  0.0 144.7 jit_solution(2416999154289329760)
XLA Ops:
  0.0 1.7 %shard_map.73 = (bf16[2,48,48,128]{3,2,1,0:T(8,128)(2,1)S(1)}, bf16[2,48,48,128]{3,2,1,0:T(8,128)(2,1)S(1)}, f32[1,48,128]{2,1,0:T(8,128)S(1)}) custom-call(f32[2,48,128]{2,1,0:T(8,128)} %bitcast.14, bf16[2,48,48,128]{3,2,1,0:T(8,128)(2,1)} %bitcast.25, bf16[2,48,48,128]{3,2,1,0:T(8,128)(2,1)} %bitcast.26), custom_call_target="tpu_custom_call" | custom-call | tf_op jit(solution)/shard_map/pallas_call | solution.py:73
  1.7 4.8 %collective-permute-start = (f32[1,48,128]{2,1,0:T(8,128)S(1)}, f32[1,48,128]{2,1,0:T(8,128)S(1)}, u32[]{:S(2)}, u32[]{:S(2)}) collective-permute-start(f32[1,48,128]{2,1,0:T(8,128)S(1)} %get-tuple-element.93.refs_1_), channel_id=1, source_target_pairs={{0,8},{1,9},{2,10},{3,11},{4,12},{5,13},{6,14},{7,15}} | collective-permute-start | bytes 73736 | tf_op jit(solution)/shard_map/ppermute | solution.py:503
  6.5 0.9 shard_map.74
  7.5 0.6 collective-permute-done.refs_0_
  8.4 0.7 collective-permute-start.1
  9.1 0.4 shard_map.77
  9.6 0.7 collective-permute-start.2
  10.4 0.7 shard_map.75.upper
  11.1 0.6 shard_map.78
  11.7 0.7 collective-permute-start.3
  12.8 0.7 collective-permute-start.4
  13.5 0.4 shard_map.82
  13.9 1.3 collective-permute-start.5
  15.2 18.0 %collective-permute-done.5.refs_1_ = f32[48,128]{1,0:T(8,128)S(1)} collective-permute-done((f32[48,128]{1,0:T(8,128)S(1)}, f32[48,128]{1,0:T(8,128)S(1)}, u32[]{:S(2)}, u32[]{:S(2)}) %collective-permute-start.5) | collective-permute-done | bytes 24608 | tf_op jit(solution)/shard_map/ppermute | solution.py:533
  33.8 0.8 collective-permute-start.7
  35.2 2.1 %shard_map.80 = (f32[2,48,48,128]{3,2,1,0:T(8,128)S(1)}, f32[2,48,48,128]{3,2,1,0:T(8,128)S(1)}, f32[2,48,48,128]{3,2,1,0:T(8,128)S(1)}) custom-call(bf16[2,48,48,128]{3,2,1,0:T(8,128)(2,1)S(1)} %bitcast.20, bf16[2,48,48,128]{3,2,1,0:T(8,128)(2,1)S(1)} %bitcast.21, bf16[2,48,48,128]{3,2,1,0:T(8,128)(2,1)S(1)} %bitcast.22, ...), custom_call_target="tpu_custom_call" | custom-call | tf_op jit(solution)/shard_map/pallas_call | solution.py:131
  37.4 0.4 shard_map.84
  38.0 0.5 shard_map.86
  38.5 1.6 %collective-permute-start.8 = (f32[2,48,128]{2,1,0:T(8,128)S(1)}, f32[2,48,128]{2,1,0:T(8,128)S(1)}, u32[]{:S(2)}, u32[]{:S(2)}) collective-permute-start(f32[2,48,128]{2,1,0:T(8,128)S(1)} %get-tuple-element.118), channel_id=1, source_target_pairs={{0,8},{1,9},{2,10},{3,11},{4,12},{5,13},{6,14},{7,15}} | collective-permute-start | bytes 147464 | tf_op jit(solution)/shard_map/ppermute | solution.py:503
  40.1 1.7 %collective-permute-done.8.refs_0_ = f32[2,48,128]{2,1,0:T(8,128)S(1)} collective-permute-done((f32[2,48,128]{2,1,0:T(8,128)S(1)}, f32[2,48,128]{2,1,0:T(8,128)S(1)}, u32[]{:S(2)}, u32[]{:S(2)}) %collective-permute-start.8) | collective-permute-done | bytes 49184 | tf_op jit(solution)/shard_map/ppermute | solution.py:503
  42.3 0.7 collective-permute-start.9
  43.0 0.4 shard_map.89
  43.4 0.7 collective-permute-start.10
  44.1 0.6 shard_map.90
  44.7 0.7 collective-permute-start.11
  45.8 0.7 collective-permute-start.16
  46.5 0.7 collective-permute-start.12
  47.2 0.4 shard_map.92
  47.6 1.5 %collective-permute-start.13 = (f32[48,128]{1,0:T(8,128)S(1)}, f32[48,128]{1,0:T(8,128)S(1)}, u32[]{:S(2)}, u32[]{:S(2)}) collective-permute-start(f32[48,128]{1,0:T(8,128)S(1)} %get-tuple-element.131), channel_id=1, source_target_pairs={{8,0},{9,1},{10,2},{11,3},{12,4},{13,5},{14,6},{15,7}} | collective-permute-start | bytes 73736 | tf_op jit(solution)/shard_map/ppermute | solution.py:533
  49.1 20.0 %collective-permute-done.13.refs_1_ = f32[48,128]{1,0:T(8,128)S(1)} collective-permute-done((f32[48,128]{1,0:T(8,128)S(1)}, f32[48,128]{1,0:T(8,128)S(1)}, u32[]{:S(2)}, u32[]{:S(2)}) %collective-permute-start.13) | collective-permute-done | bytes 24608 | tf_op jit(solution)/shard_map/ppermute | solution.py:533
  69.6 0.7 collective-permute-start.15
  70.3 0.5 shard_map.94
  71.0 0.5 shard_map.96
  71.5 1.6 %collective-permute-start.17 = (f32[2,48,128]{2,1,0:T(8,128)S(1)}, f32[2,48,128]{2,1,0:T(8,128)S(1)}, u32[]{:S(2)}, u32[]{:S(2)}) collective-permute-start(f32[2,48,128]{2,1,0:T(8,128)S(1)} %get-tuple-element.138.message), channel_id=1, source_target_pairs={{0,8},{16,24},{1,9},{17,25},{2,10},{18,26},{3,11},{19,27},{4,12},{... | collective-permute-start | bytes 147464 | tf_op jit(solution)/shard_map/ppermute | solution.py:440
  73.1 1.7 %collective-permute-done.17.refs_0_ = f32[2,48,128]{2,1,0:T(8,128)S(1)} collective-permute-done((f32[2,48,128]{2,1,0:T(8,128)S(1)}, f32[2,48,128]{2,1,0:T(8,128)S(1)}, u32[]{:S(2)}, u32[]{:S(2)}) %collective-permute-start.17) | collective-permute-done | bytes 49184 | tf_op jit(solution)/shard_map/ppermute | solution.py:440
  75.3 0.7 collective-permute-start.19
  76.2 0.7 collective-permute-start.18
  76.9 0.9 shard_map.99
  77.7 0.7 collective-permute-start.20
  78.4 0.7 collective-permute-start.22
  79.1 0.4 shard_map.100
  79.5 1.3 collective-permute-start.21
  80.8 16.8 %collective-permute-done.21.received = f32[48,128]{1,0:T(8,128)S(1)} collective-permute-done((f32[48,128]{1,0:T(8,128)S(1)}, f32[48,128]{1,0:T(8,128)S(1)}, u32[]{:S(2)}, u32[]{:S(2)}) %collective-permute-start.21) | collective-permute-done | bytes 24608 | tf_op jit(solution)/shard_map/ppermute | solution.py:463
  98.0 0.7 collective-permute-start.24
  98.7 0.5 shard_map.102
  99.5 0.5 shard_map.104
  99.9 1.6 %collective-permute-start.25 = (f32[2,48,128]{2,1,0:T(8,128)S(1)}, f32[2,48,128]{2,1,0:T(8,128)S(1)}, u32[]{:S(2)}, u32[]{:S(2)}) collective-permute-start(f32[2,48,128]{2,1,0:T(8,128)S(1)} %get-tuple-element.154.message), channel_id=1, source_target_pairs={{0,8},{16,24},{1,9},{17,25},{2,10},{18,26},{3,11},{19,27},{4,12},{... | collective-permute-start | bytes 147464 | tf_op jit(solution)/shard_map/ppermute | solution.py:440
  101.5 1.7 %collective-permute-done.25.refs_0_ = f32[2,48,128]{2,1,0:T(8,128)S(1)} collective-permute-done((f32[2,48,128]{2,1,0:T(8,128)S(1)}, f32[2,48,128]{2,1,0:T(8,128)S(1)}, u32[]{:S(2)}, u32[]{:S(2)}) %collective-permute-start.25) | collective-permute-done | bytes 49184 | tf_op jit(solution)/shard_map/ppermute | solution.py:440
  103.3 0.4 shard_map.105
  103.7 0.7 collective-permute-start.27
  104.6 0.7 collective-permute-start.26
  105.3 0.9 shard_map.107
  106.1 0.7 collective-permute-start.28
  106.8 0.7 collective-permute-start.30
  107.5 0.4 shard_map.108
  107.9 1.3 collective-permute-start.29
  109.2 10.8 %collective-permute-done.29.received = f32[48,128]{1,0:T(8,128)S(1)} collective-permute-done((f32[48,128]{1,0:T(8,128)S(1)}, f32[48,128]{1,0:T(8,128)S(1)}, u32[]{:S(2)}, u32[]{:S(2)}) %collective-permute-start.29) | collective-permute-done | bytes 24608 | tf_op jit(solution)/shard_map/ppermute | solution.py:463
  120.4 0.8 collective-permute-start.31
  121.2 0.7 collective-permute-start.33
  121.8 1.9 %collective-permute-start.32 = (f32[48,128]{1,0:T(8,128)S(1)}, f32[48,128]{1,0:T(8,128)S(1)}, u32[]{:S(2)}, u32[]{:S(2)}) collective-permute-start(f32[48,128]{1,0:T(8,128)S(1)} %get-tuple-element.168), channel_id=1, source_target_pairs={{0,8},{8,16},{16,24},{1,9},{9,17},{17,25},{2,10},{10,18},{18,26},{... | collective-permute-start | bytes 73736 | tf_op jit(solution)/shard_map/ppermute | solution.py:571
  123.8 0.4 shard_map.110
  124.3 1.0 collective-permute-done.32.refs_1_
  125.8 17.9 %all_to_all.11 = f32[32,1,128]{2,1,0:T(1,128)S(1)} all-to-all(f32[32,1,128]{2,1,0:T(1,128)S(1)} %bitcast.23), channel_id=1, replica_groups=mesh['line'=4,'patch'=8] {'line','patch'}, dimensions={0} | all-to-all | bytes 32768 | tf_op jit(solution)/shard_map/all_to_all | solution.py:590
  143.8 0.8 shard_map.114
  (57 shorter events, 6.5 us)
Async XLA Ops:
  1.7 6.4 %collective-permute-start = (f32[1,48,128]{2,1,0:T(8,128)S(1)}, f32[1,48,128]{2,1,0:T(8,128)S(1)}, u32[]{:S(2)}, u32[]{:S(2)}) collective-permute-start(f32[1,48,128]{2,1,0:T(8,128)S(1)} %get-tuple-element.93.refs_1_), channel_id=1, source_target_pairs={{0,8},{1,9},{2,10},{3,11},{4,12},{5,13},{6,14},{7,15}} | collective-permute-start | bytes 73736 | tf_op jit(solution)/shard_map/ppermute | solution.py:503
  6.5 1.5 %copy-start = (f32[2,48,1,128]{3,2,1,0:T(1,128)S(1)}, f32[2,48,1,128]{3,2,1,0:T(1,128)}, u32[]{:S(2)}) copy-start(f32[2,48,1,128]{3,2,1,0:T(1,128)} %param.7) | copy-start | bytes 147460
  8.4 0.7 collective-permute-start.1
  9.1 1.3 copy-start.1
  9.6 1.6 %collective-permute-start.2 = (f32[1,48,128]{2,1,0:T(8,128)S(1)}, f32[1,48,128]{2,1,0:T(8,128)S(1)}, u32[]{:S(2)}, u32[]{:S(2)}) collective-permute-start(f32[1,48,128]{2,1,0:T(8,128)S(1)} %get-tuple-element.97.after), channel_id=1, source_target_pairs={{16,24},{17,25},{18,26},{19,27},{20,28},{21,29},{22,30},{23,31}} | collective-permute-start | bytes 73736 | tf_op jit(solution)/shard_map/ppermute | solution.py:503
  11.7 0.7 collective-permute-start.3
  12.8 0.7 collective-permute-start.4
  13.9 19.3 %collective-permute-start.5 = (f32[48,128]{1,0:T(8,128)S(1)}, f32[48,128]{1,0:T(8,128)S(1)}, u32[]{:S(2)}, u32[]{:S(2)}) collective-permute-start(f32[48,128]{1,0:T(8,128)S(1)} %get-tuple-element.107), channel_id=1, source_target_pairs={{8,0},{9,1},{10,2},{11,3},{12,4},{13,5},{14,6},{15,7}} | collective-permute-start | bytes 73736 | tf_op jit(solution)/shard_map/ppermute | solution.py:533
  33.3 1.3 copy-start.2
  33.3 1.6 %copy-start.3 = (bf16[2,48,48,1,128]{4,2,3,1,0:T(8,128)(2,1)S(1)}, bf16[2,48,48,1,128]{4,2,3,1,0:T(8,128)(2,1)}, u32[]{:S(2)}) copy-start(bf16[2,48,48,1,128]{4,2,3,1,0:T(8,128)(2,1)} %param.12) | copy-start | bytes 3538948
  33.3 2.0 %copy-start.4 = (bf16[2,48,48,1,128]{4,2,3,1,0:T(8,128)(2,1)S(1)}, bf16[2,48,48,1,128]{4,2,3,1,0:T(8,128)(2,1)}, u32[]{:S(2)}) copy-start(bf16[2,48,48,1,128]{4,2,3,1,0:T(8,128)(2,1)} %param.11) | copy-start | bytes 3538948
  33.7 4.1 %collective-permute-start.6 = (f32[2,48,128]{2,1,0:T(8,128)S(1)}, f32[2,48,128]{2,1,0:T(8,128)S(1)}, u32[]{:S(2)}, u32[]{:S(2)}) collective-permute-start(f32[2,48,128]{2,1,0:T(8,128)S(1)} %get-tuple-element.108.direction.refs_0_), channel_id=1, source_target_pairs={{0,1},{2,3},{4,5},{6,7},{1,0},{3,2},{5,4},{7,6},{8,9},{10,11},{12,... | collective-permute-start | bytes 147464 | tf_op jit(solution)/shard_map/ppermute | solution.py:429
  33.8 4.3 %collective-permute-start.7 = (f32[2,48,128]{2,1,0:T(8,128)S(1)}, f32[2,48,128]{2,1,0:T(8,128)S(1)}, u32[]{:S(2)}, u32[]{:S(2)}) collective-permute-start(f32[2,48,128]{2,1,0:T(8,128)S(1)} %get-tuple-element.108.direction.refs_0_), channel_id=1, source_target_pairs={{1,2},{3,4},{5,6},{2,1},{4,3},{6,5},{9,10},{11,12},{13,14},{10,9},... | collective-permute-start | bytes 147464 | tf_op jit(solution)/shard_map/ppermute | solution.py:428
  38.5 3.4 %collective-permute-start.8 = (f32[2,48,128]{2,1,0:T(8,128)S(1)}, f32[2,48,128]{2,1,0:T(8,128)S(1)}, u32[]{:S(2)}, u32[]{:S(2)}) collective-permute-start(f32[2,48,128]{2,1,0:T(8,128)S(1)} %get-tuple-element.118), channel_id=1, source_target_pairs={{0,8},{1,9},{2,10},{3,11},{4,12},{5,13},{6,14},{7,15}} | collective-permute-start | bytes 147464 | tf_op jit(solution)/shard_map/ppermute | solution.py:503
  42.3 0.7 collective-permute-start.9
  43.4 0.7 collective-permute-start.10
  44.7 0.7 collective-permute-start.11
  45.8 31.1 %collective-permute-start.16 = (f32[48,48,128]{2,1,0:T(8,128)S(1)}, f32[48,48,128]{2,1,0:T(8,128)S(1)}, u32[]{:S(2)}, u32[]{:S(2)}) collective-permute-start(f32[48,48,128]{2,1,0:T(8,128)S(1)} %shard_map.87), channel_id=1, source_target_pairs={{24,16},{25,17},{26,18},{27,19},{28,20},{29,21},{30,22},{31,23}} | collective-permute-start | bytes 3538952 | tf_op jit(solution)/shard_map/ppermute | solution.py:532
  46.5 0.7 collective-permute-start.12
  47.6 21.5 %collective-permute-start.13 = (f32[48,128]{1,0:T(8,128)S(1)}, f32[48,128]{1,0:T(8,128)S(1)}, u32[]{:S(2)}, u32[]{:S(2)}) collective-permute-start(f32[48,128]{1,0:T(8,128)S(1)} %get-tuple-element.131), channel_id=1, source_target_pairs={{8,0},{9,1},{10,2},{11,3},{12,4},{13,5},{14,6},{15,7}} | collective-permute-start | bytes 73736 | tf_op jit(solution)/shard_map/ppermute | solution.py:533
  69.5 1.3 collective-permute-start.14
  69.6 1.4 collective-permute-start.15
  71.5 3.4 %collective-permute-start.17 = (f32[2,48,128]{2,1,0:T(8,128)S(1)}, f32[2,48,128]{2,1,0:T(8,128)S(1)}, u32[]{:S(2)}, u32[]{:S(2)}) collective-permute-start(f32[2,48,128]{2,1,0:T(8,128)S(1)} %get-tuple-element.138.message), channel_id=1, source_target_pairs={{0,8},{16,24},{1,9},{17,25},{2,10},{18,26},{3,11},{19,27},{4,12},{... | collective-permute-start | bytes 147464 | tf_op jit(solution)/shard_map/ppermute | solution.py:440
  75.3 1.6 %collective-permute-start.19 = (f32[2,48,128]{2,1,0:T(8,128)S(1)}, f32[2,48,128]{2,1,0:T(8,128)S(1)}, u32[]{:S(2)}, u32[]{:S(2)}) collective-permute-start(f32[2,48,128]{2,1,0:T(8,128)S(1)} %get-tuple-element.141), channel_id=1, source_target_pairs={{8,16},{9,17},{10,18},{11,19},{12,20},{13,21},{14,22},{15,23}} | collective-permute-start | bytes 147464 | tf_op jit(solution)/shard_map/ppermute | solution.py:447
  76.2 0.7 collective-permute-start.18
  77.7 1.3 collective-permute-start.20
  78.4 2.4 %collective-permute-start.22 = (f32[48,128]{1,0:T(8,128)S(1)}, f32[48,128]{1,0:T(8,128)S(1)}, u32[]{:S(2)}, u32[]{:S(2)}) collective-permute-start(f32[48,128]{1,0:T(8,128)S(1)} %get-tuple-element.148), channel_id=1, source_target_pairs={{16,24},{17,25},{18,26},{19,27},{20,28},{21,29},{22,30},{23,31}} | collective-permute-start | bytes 73736 | tf_op jit(solution)/shard_map/ppermute | solution.py:464
  79.5 18.1 %collective-permute-start.21 = (f32[48,128]{1,0:T(8,128)S(1)}, f32[48,128]{1,0:T(8,128)S(1)}, u32[]{:S(2)}, u32[]{:S(2)}) collective-permute-start(f32[48,128]{1,0:T(8,128)S(1)} %get-tuple-element.147), channel_id=1, source_target_pairs={{8,0},{9,1},{10,2},{11,3},{12,4},{13,5},{14,6},{15,7}} | collective-permute-start | bytes 73736 | tf_op jit(solution)/shard_map/ppermute | solution.py:463
  98.0 1.3 collective-permute-start.23
  98.0 1.4 collective-permute-start.24
  99.9 3.4 %collective-permute-start.25 = (f32[2,48,128]{2,1,0:T(8,128)S(1)}, f32[2,48,128]{2,1,0:T(8,128)S(1)}, u32[]{:S(2)}, u32[]{:S(2)}) collective-permute-start(f32[2,48,128]{2,1,0:T(8,128)S(1)} %get-tuple-element.154.message), channel_id=1, source_target_pairs={{0,8},{16,24},{1,9},{17,25},{2,10},{18,26},{3,11},{19,27},{4,12},{... | collective-permute-start | bytes 147464 | tf_op jit(solution)/shard_map/ppermute | solution.py:440
  103.7 1.6 %collective-permute-start.27 = (f32[2,48,128]{2,1,0:T(8,128)S(1)}, f32[2,48,128]{2,1,0:T(8,128)S(1)}, u32[]{:S(2)}, u32[]{:S(2)}) collective-permute-start(f32[2,48,128]{2,1,0:T(8,128)S(1)} %get-tuple-element.157), channel_id=1, source_target_pairs={{8,16},{9,17},{10,18},{11,19},{12,20},{13,21},{14,22},{15,23}} | collective-permute-start | bytes 147464 | tf_op jit(solution)/shard_map/ppermute | solution.py:447
  104.6 0.7 collective-permute-start.26
  106.1 1.3 collective-permute-start.28
  106.8 2.4 %collective-permute-start.30 = (f32[48,128]{1,0:T(8,128)S(1)}, f32[48,128]{1,0:T(8,128)S(1)}, u32[]{:S(2)}, u32[]{:S(2)}) collective-permute-start(f32[48,128]{1,0:T(8,128)S(1)} %get-tuple-element.164), channel_id=1, source_target_pairs={{16,24},{17,25},{18,26},{19,27},{20,28},{21,29},{22,30},{23,31}} | collective-permute-start | bytes 73736 | tf_op jit(solution)/shard_map/ppermute | solution.py:464
  107.9 12.1 %collective-permute-start.29 = (f32[48,128]{1,0:T(8,128)S(1)}, f32[48,128]{1,0:T(8,128)S(1)}, u32[]{:S(2)}, u32[]{:S(2)}) collective-permute-start(f32[48,128]{1,0:T(8,128)S(1)} %get-tuple-element.163), channel_id=1, source_target_pairs={{8,0},{9,1},{10,2},{11,3},{12,4},{13,5},{14,6},{15,7}} | collective-permute-start | bytes 73736 | tf_op jit(solution)/shard_map/ppermute | solution.py:463
  120.4 4.9 %collective-permute-start.31 = (f32[2,48,128]{2,1,0:T(8,128)S(1)}, f32[2,48,128]{2,1,0:T(8,128)S(1)}, u32[]{:S(2)}, u32[]{:S(2)}) collective-permute-start(f32[2,48,128]{2,1,0:T(8,128)S(1)} %get-tuple-element.165.direction.refs_3_), channel_id=1, source_target_pairs={{0,1},{2,3},{4,5},{6,7},{1,0},{3,2},{5,4},{7,6},{8,9},{10,11},{12,... | collective-permute-start | bytes 147464 | tf_op jit(solution)/shard_map/ppermute | solution.py:429
  121.2 4.4 %collective-permute-start.33 = (f32[2,48,128]{2,1,0:T(8,128)S(1)}, f32[2,48,128]{2,1,0:T(8,128)S(1)}, u32[]{:S(2)}, u32[]{:S(2)}) collective-permute-start(f32[2,48,128]{2,1,0:T(8,128)S(1)} %get-tuple-element.165.direction.refs_3_), channel_id=1, source_target_pairs={{1,2},{3,4},{5,6},{2,1},{4,3},{6,5},{9,10},{11,12},{13,14},{10,9},... | collective-permute-start | bytes 147464 | tf_op jit(solution)/shard_map/ppermute | solution.py:428
  121.8 3.4 %collective-permute-start.32 = (f32[48,128]{1,0:T(8,128)S(1)}, f32[48,128]{1,0:T(8,128)S(1)}, u32[]{:S(2)}, u32[]{:S(2)}) collective-permute-start(f32[48,128]{1,0:T(8,128)S(1)} %get-tuple-element.168), channel_id=1, source_target_pairs={{0,8},{8,16},{16,24},{1,9},{9,17},{17,25},{2,10},{10,18},{18,26},{... | collective-permute-start | bytes 73736 | tf_op jit(solution)/shard_map/ppermute | solution.py:571

commit v17 on v16

--- a/solution.py
+++ b/solution.py
@@ -377,7 +377,7 @@
 
 
 def finish_kernel(parts_ref, *refs):
-    *directions, final, out, sem = refs
+    *directions, final, sound, out, sem = refs
     width = len(directions)
     total = jnp.sum(parts_ref[...], axis=0, keepdims=True)
     shape = (SUMS, total.shape[1])
@@ -390,6 +390,17 @@
         for j in range(width + 1):
             place = place_of((i, j))
             gram[i, j] = sums[place : place + 1]
+    rest = {pair: value for pair, value in gram.items()}
+    good = jnp.ones_like(gram[0, 0])
+    for i in range(width + 1):
+        good = jnp.where(rest[i, i] > gram[i, i] * (1.0 / 256.0), good, 0.0)
+        good = jnp.where(gram[i, i] < 1e37, good, 0.0)
+        inverse = 1.0 / rest[i, i]
+        for j in range(i + 1, width + 1):
+            factor = rest[i, j] * inverse
+            for k in range(j, width + 1):
+                rest[j, k] = rest[j, k] - factor * rest[i, k]
+    sound[...] = good
     half = [[gram[j + 1, i] + gram[j, i] for i in range(width + 1)] for j in range(width)]
     normal = [[half[j][i + 1] + half[j][i] for i in range(width)] for j in range(width)]
     right = [half[j][0] for j in range(width)]
@@ -471,7 +482,134 @@
     return direction, coupled, last, carried
 
 
-def per_device(newton_residual, diag_block, lower, upper, west, east, pivot_inverse):
+def plain_halo(block, sides, width):
+    for axis, dim in sides:
+        count = lax.axis_size(axis)
+        forward = [(i, i + 1) for i in range(count - 1)]
+        backward = [(target, source) for source, target in forward]
+        low = lax.ppermute(
+            lax.slice_in_dim(block, block.shape[dim] - width, None, axis=dim), axis, forward
+        )
+        high = lax.ppermute(lax.slice_in_dim(block, 0, width, axis=dim), axis, backward)
+        block = jnp.concatenate([low, block, high], axis=dim)
+    return block
+
+
+def plain_passed(block, axis, distance):
+    devices = range(lax.axis_size(axis))
+    route = [(i - distance, i) for i in devices if i - distance in devices]
+    return lax.ppermute(block, axis, route)
+
+
+def plain_block_apply(block_mat, vector):
+    return jnp.sum(block_mat.astype(jnp.float32) * vector[:, None], axis=2)
+
+
+def plain_apply(block_mat, vector):
+    return jnp.sum(block_mat.astype(jnp.float32) * vector[None], axis=1)
+
+
+def plain_operator(field, diag_block, lower, upper, west, east):
+    padded = plain_halo(field, (("line", 0), ("patch", 2)), 1)
+    total = plain_block_apply(diag_block, field) + plain_block_apply(lower, padded[:-2, :, 1:-1])
+    total = total + plain_block_apply(upper, padded[2:, :, 1:-1])
+    return total + plain_block_apply(west, padded[1:-1, :, :-2]) + plain_block_apply(east, padded[1:-1, :, 2:])
+
+
+def plain_sweep_down(vector, lower, pivot, incoming):
+    previous = incoming
+    forward = []
+    for k in range(vector.shape[0]):
+        previous = plain_apply(pivot[k], vector[k] - plain_apply(lower[k], previous))
+        forward.append(previous)
+    return jnp.stack(forward)
+
+
+def plain_sweep_up(forward, upper, pivot, incoming):
+    count = forward.shape[0]
+    following = incoming
+    result = [None] * count
+    for k in reversed(range(count)):
+        following = forward[k] - plain_apply(pivot[k], plain_apply(upper[k], following))
+        result[k] = following
+    return jnp.stack(result)
+
+
+def plain_precondition(vector, lower, upper, pivot):
+    zero_carry = jnp.zeros_like(vector[0])
+    count = lax.axis_size("line")
+    incoming = zero_carry
+    for turn in range(count - 1):
+        outgoing_down = plain_sweep_down(vector, lower, pivot, incoming)[-1]
+        incoming = plain_passed(outgoing_down, "line", 1)
+    forward = plain_sweep_down(vector, lower, pivot, incoming)
+    outgoing = zero_carry
+    for turn in range(count - 1):
+        first_up = plain_sweep_up(forward, upper, pivot, outgoing)[0]
+        outgoing = plain_passed(first_up, "line", -1)
+    return plain_sweep_up(forward, upper, pivot, outgoing)
+
+
+def plain_norm_squared(vector):
+    return lax.psum(jnp.sum(vector * vector), ("line", "patch"))
+
+
+def least_squares(hess, beta):
+    width = hess.shape[1]
+    hess_rows = [hess[i] for i in range(width + 1)]
+    target = [beta] + [jnp.zeros((), jnp.float32) for i in range(width)]
+    for j in range(width):
+        first = hess_rows[j][j]
+        second = hess_rows[j + 1][j]
+        radius = jnp.sqrt(first * first + second * second)
+        cosine = first / radius
+        sine_part = second / radius
+        upper_row = cosine * hess_rows[j] + sine_part * hess_rows[j + 1]
+        lower_row = cosine * hess_rows[j + 1] - sine_part * hess_rows[j]
+        hess_rows[j] = upper_row
+        hess_rows[j + 1] = lower_row
+        top_value = cosine * target[j] + sine_part * target[j + 1]
+        low_value = cosine * target[j + 1] - sine_part * target[j]
+        target[j] = top_value
+        target[j + 1] = low_value
+    solution = [None] * width
+    for i in reversed(range(width)):
+        accum_value = target[i]
+        for k in range(i + 1, width):
+            accum_value = accum_value - hess_rows[i][k] * solution[k]
+        solution[i] = accum_value / hess_rows[i][i]
+    return solution
+
+
+def normalised(newton_residual, diag_block, lower, upper, west, east, pivot_inverse):
+    beta = jnp.sqrt(plain_norm_squared(newton_residual))
+    basis = [newton_residual / beta]
+    directions = []
+    columns = []
+    for j in range(ITERS):
+        direction = plain_precondition(basis[j], lower, upper, pivot_inverse)
+        directions.append(direction)
+        image = plain_operator(direction, diag_block, lower, upper, west, east)
+        projections = lax.psum(
+            jnp.stack([jnp.sum(member * image) for member in basis]), ("line", "patch")
+        )
+        for i in range(j + 1):
+            image = image - projections[i] * basis[i]
+        new_norm = jnp.sqrt(plain_norm_squared(image))
+        basis.append(image / new_norm)
+        columns.append(
+            jnp.concatenate([projections, new_norm[None], jnp.zeros((ITERS - 1 - j,), jnp.float32)])
+        )
+    hess = jnp.stack(columns, axis=1)
+    coeffs = least_squares(hess, beta)
+    newton_step = coeffs[0] * directions[0]
+    for j in range(1, ITERS):
+        newton_step = newton_step + coeffs[j] * directions[j]
+    return newton_step
+
+
+def per_device(*given):
+    newton_residual, diag_block, lower, upper, west, east, pivot_inverse = given
     shape = newton_residual.shape
     count, block, rows, across = shape
     wide = rows * across
@@ -588,15 +726,24 @@
                 [field],
             )
     sums = lax.all_to_all(sums, ("line", "patch"), 0, 0, tiled=True)
-    step = pl.pallas_call(
+    step, sound = pl.pallas_call(
         finish_kernel,
-        out_shape=jax.ShapeDtypeStruct(field, jnp.float32),
+        out_shape=[
+            jax.ShapeDtypeStruct(field, jnp.float32),
+            jax.ShapeDtypeStruct((1, wide), jnp.float32),
+        ],
         in_specs=[pl.BlockSpec(memory_space=pltpu.VMEM)] * (1 + len(directions)),
-        out_specs=pl.BlockSpec(memory_space=pl.ANY),
+        out_specs=[pl.BlockSpec(memory_space=pl.ANY), pl.BlockSpec(memory_space=pltpu.VMEM)],
         scratch_shapes=[pltpu.VMEM(field, jnp.float32), pltpu.SemaphoreType.DMA],
         compiler_params=pltpu.CompilerParams(vmem_limit_bytes=STAGE_ROOM),
     )(sums, *directions)
-    return step.reshape(shape)
+    return lax.cond(
+        sound[0, 0] > 0.5,
+        lambda step, *given: step,
+        lambda step, *given: normalised(*given),
+        step.reshape(shape),
+        *given,
+    )
 
 
 def solution(mesh):

time: 145 us -> 147 us (1.014)
  blocking collectives: 17.9 us -> 0 us
  starting transfers between devices: 32.1 us -> 43.1 us
  waiting for transfers between devices: 72.6 us -> 79.6 us
    all_to_all x1 -> x0, blocking collectives: 17.9 us -> none  [per_device(): sums = lax.all_to_all(sums, ('line', 'patch'), 0, 0, tiled=True)]
    all_to_all x0 -> x1, starting transfers between devices: none -> 11 us  [per_device(): sums = lax.all_to_all(sums, ('line', 'patch'), 0, 0, tiled=True)]
    all_to_all x0 -> x1, waiting for transfers between devices: none -> 7.07 us  [per_device(): sums = lax.all_to_all(sums, ('line', 'patch'), 0, 0, tiled=True)]
  transfers between devices with their start and end apart: 34 -> 35, of which waited for: 10 -> 11; matrix products, arithmetic and copies ran while one was open for 0% -> 0% of each run, Pallas kernels for 7% -> 7%
where the time goes in v17:
time: 147 us; the launch traced here: 146 us
  waiting for transfers between devices  79.6 us (54%)
  starting transfers between devices  43.1 us (29%)
  Pallas kernels  21.1 us (14%)
    ppermute x6, waiting for transfers between devices, per_device(): parts.append(lax.ppermute(outgoing, 'line', [(turn + 1, turn)]))  38 us
    ppermute x2, waiting for transfers between devices, sweep_short(): received = lax.ppermute(outgoing, 'line', [(1, 0)])  27.6 us
    pallas_call x37, Pallas kernels, stage(): pl.pallas_call(kernel, out_shape=[pltpu.VMEM(shape, jnp.float32) for shap...  14.9 us
    all_to_all x1, starting transfers between devices, per_device(): sums = lax.all_to_all(sums, ('line', 'patch'), 0, 0, tiled=True)  11 us
    ppermute x6, starting transfers between devices, per_device(): parts.append(lax.ppermute(message, 'line', [(turn, turn + 1)]))  9.12 us
    all_to_all x1, waiting for transfers between devices, per_device(): sums = lax.all_to_all(sums, ('line', 'patch'), 0, 0, tiled=True)  7.07 us
    ppermute x6, starting transfers between devices, per_device(): parts.append(lax.ppermute(outgoing, 'line', [(turn + 1, turn)]))  5.42 us
    ppermute x2, waiting for transfers between devices, sweep_short(): received = lax.ppermute(message, 'line', [(0, 1), (2, 3)])  3.46 us
  transfers between devices with their start and end apart: 35, of which 11 were waited for; matrix products, arithmetic and copies ran while one was open for 0% of the time, Pallas kernels for 7%

profile of v17, /device:TPU:0, one launch (start us, length us, event | category | flops | bytes accessed | tf_op | source)
XLA Modules:
  0.0 145.9 jit_solution(6811099523025196180)
XLA Ops:
  0.0 1.7 %shard_map.75 = (bf16[2,48,48,128]{3,2,1,0:T(8,128)(2,1)S(1)}, bf16[2,48,48,128]{3,2,1,0:T(8,128)(2,1)S(1)}, f32[1,48,128]{2,1,0:T(8,128)S(1)}) custom-call(f32[2,48,128]{2,1,0:T(8,128)} %bitcast.477, bf16[2,48,48,128]{3,2,1,0:T(8,128)(2,1)} %bitcast.460, bf16[2,48,48,128]{3,2,1,0:T(8,128)(2,1)} %bitcast.498), custom_call_target="tpu_custom_call" | custom-call | tf_op jit(solution)/shard_map/pallas_call | solution.py:73
  1.7 4.8 %collective-permute-start.40 = (f32[1,48,128]{2,1,0:T(8,128)S(1)}, f32[1,48,128]{2,1,0:T(8,128)S(1)}, u32[]{:S(2)}, u32[]{:S(2)}) collective-permute-start(f32[1,48,128]{2,1,0:T(8,128)S(1)} %get-tuple-element.122.refs_1_), channel_id=1, source_target_pairs={{0,8},{1,9},{2,10},{3,11},{4,12},{5,13},{6,14},{7,15}} | collective-permute-start | bytes 73736 | tf_op jit(solution)/shard_map/ppermute | solution.py:641
  6.5 0.9 shard_map.76
  7.5 0.6 collective-permute-done.40.refs_0_
  8.4 0.7 collective-permute-start.41
  9.1 0.4 shard_map.79
  9.6 0.7 collective-permute-start.42
  10.4 0.7 shard_map.77.upper
  11.1 0.6 shard_map.80
  11.8 0.7 collective-permute-start.43
  12.8 0.7 collective-permute-start.44
  13.5 0.4 shard_map.84
  13.9 1.3 collective-permute-start.45
  15.2 18.0 %collective-permute-done.45.refs_1_ = f32[48,128]{1,0:T(8,128)S(1)} collective-permute-done((f32[48,128]{1,0:T(8,128)S(1)}, f32[48,128]{1,0:T(8,128)S(1)}, u32[]{:S(2)}, u32[]{:S(2)}) %collective-permute-start.45) | collective-permute-done | bytes 24608 | tf_op jit(solution)/shard_map/ppermute | solution.py:671
  33.8 0.8 collective-permute-start.47
  35.2 2.1 %shard_map.82 = (f32[2,48,48,128]{3,2,1,0:T(8,128)S(1)}, f32[2,48,48,128]{3,2,1,0:T(8,128)S(1)}, f32[2,48,48,128]{3,2,1,0:T(8,128)S(1)}) custom-call(bf16[2,48,48,128]{3,2,1,0:T(8,128)(2,1)S(1)} %bitcast.474, bf16[2,48,48,128]{3,2,1,0:T(8,128)(2,1)S(1)} %bitcast.475, bf16[2,48,48,128]{3,2,1,0:T(8,128)(2,1)S(1)} %bitcast.476, ...), custom_call_target="tpu_custom_call" | custom-call | tf_op jit(solution)/shard_map/pallas_call | solution.py:131
  38.0 0.5 shard_map.88
  38.5 1.6 %collective-permute-start.48 = (f32[2,48,128]{2,1,0:T(8,128)S(1)}, f32[2,48,128]{2,1,0:T(8,128)S(1)}, u32[]{:S(2)}, u32[]{:S(2)}) collective-permute-start(f32[2,48,128]{2,1,0:T(8,128)S(1)} %get-tuple-element.147), channel_id=1, source_target_pairs={{0,8},{1,9},{2,10},{3,11},{4,12},{5,13},{6,14},{7,15}} | collective-permute-start | bytes 147464 | tf_op jit(solution)/shard_map/ppermute | solution.py:641
  40.2 1.7 %collective-permute-done.48.refs_0_ = f32[2,48,128]{2,1,0:T(8,128)S(1)} collective-permute-done((f32[2,48,128]{2,1,0:T(8,128)S(1)}, f32[2,48,128]{2,1,0:T(8,128)S(1)}, u32[]{:S(2)}, u32[]{:S(2)}) %collective-permute-start.48) | collective-permute-done | bytes 49184 | tf_op jit(solution)/shard_map/ppermute | solution.py:641
  42.3 0.7 collective-permute-start.49
  43.0 0.4 shard_map.91
  43.4 0.7 collective-permute-start.50
  44.1 0.6 shard_map.92
  44.7 0.7 collective-permute-start.51
  45.8 0.7 collective-permute-start.56
  46.5 0.7 collective-permute-start.52
  47.2 0.4 shard_map.94
  47.6 1.5 %collective-permute-start.53 = (f32[48,128]{1,0:T(8,128)S(1)}, f32[48,128]{1,0:T(8,128)S(1)}, u32[]{:S(2)}, u32[]{:S(2)}) collective-permute-start(f32[48,128]{1,0:T(8,128)S(1)} %get-tuple-element.160), channel_id=1, source_target_pairs={{8,0},{9,1},{10,2},{11,3},{12,4},{13,5},{14,6},{15,7}} | collective-permute-start | bytes 73736 | tf_op jit(solution)/shard_map/ppermute | solution.py:671
  49.1 20.0 %collective-permute-done.53.refs_1_ = f32[48,128]{1,0:T(8,128)S(1)} collective-permute-done((f32[48,128]{1,0:T(8,128)S(1)}, f32[48,128]{1,0:T(8,128)S(1)}, u32[]{:S(2)}, u32[]{:S(2)}) %collective-permute-start.53) | collective-permute-done | bytes 24608 | tf_op jit(solution)/shard_map/ppermute | solution.py:671
  69.6 0.7 collective-permute-start.55
  70.3 0.5 shard_map.96
  71.0 0.5 shard_map.98
  71.5 1.6 %collective-permute-start.57 = (f32[2,48,128]{2,1,0:T(8,128)S(1)}, f32[2,48,128]{2,1,0:T(8,128)S(1)}, u32[]{:S(2)}, u32[]{:S(2)}) collective-permute-start(f32[2,48,128]{2,1,0:T(8,128)S(1)} %get-tuple-element.167.message), channel_id=1, source_target_pairs={{0,8},{16,24},{1,9},{17,25},{2,10},{18,26},{3,11},{19,27},{4,12},{... | collective-permute-start | bytes 147464 | tf_op jit(solution)/shard_map/ppermute | solution.py:451
  73.2 1.7 %collective-permute-done.57.refs_0_ = f32[2,48,128]{2,1,0:T(8,128)S(1)} collective-permute-done((f32[2,48,128]{2,1,0:T(8,128)S(1)}, f32[2,48,128]{2,1,0:T(8,128)S(1)}, u32[]{:S(2)}, u32[]{:S(2)}) %collective-permute-start.57) | collective-permute-done | bytes 49184 | tf_op jit(solution)/shard_map/ppermute | solution.py:451
  75.3 0.7 collective-permute-start.59
  76.2 0.7 collective-permute-start.58
  76.9 0.9 shard_map.101
  77.7 0.7 collective-permute-start.60
  78.4 0.7 collective-permute-start.62
  79.1 0.4 shard_map.102
  79.5 1.3 collective-permute-start.61
  80.8 16.8 %collective-permute-done.61.received = f32[48,128]{1,0:T(8,128)S(1)} collective-permute-done((f32[48,128]{1,0:T(8,128)S(1)}, f32[48,128]{1,0:T(8,128)S(1)}, u32[]{:S(2)}, u32[]{:S(2)}) %collective-permute-start.61) | collective-permute-done | bytes 24608 | tf_op jit(solution)/shard_map/ppermute | solution.py:474
  98.0 0.7 collective-permute-start.64
  98.7 0.5 shard_map.104
  99.5 0.4 shard_map.106
  99.9 1.6 %collective-permute-start.65 = (f32[2,48,128]{2,1,0:T(8,128)S(1)}, f32[2,48,128]{2,1,0:T(8,128)S(1)}, u32[]{:S(2)}, u32[]{:S(2)}) collective-permute-start(f32[2,48,128]{2,1,0:T(8,128)S(1)} %get-tuple-element.183.message), channel_id=1, source_target_pairs={{0,8},{16,24},{1,9},{17,25},{2,10},{18,26},{3,11},{19,27},{4,12},{... | collective-permute-start | bytes 147464 | tf_op jit(solution)/shard_map/ppermute | solution.py:451
  101.5 1.7 %collective-permute-done.65.refs_0_ = f32[2,48,128]{2,1,0:T(8,128)S(1)} collective-permute-done((f32[2,48,128]{2,1,0:T(8,128)S(1)}, f32[2,48,128]{2,1,0:T(8,128)S(1)}, u32[]{:S(2)}, u32[]{:S(2)}) %collective-permute-start.65) | collective-permute-done | bytes 49184 | tf_op jit(solution)/shard_map/ppermute | solution.py:451
  103.7 0.7 collective-permute-start.67
  104.5 0.7 collective-permute-start.66
  105.2 0.9 shard_map.109
  106.1 0.7 collective-permute-start.68
  106.8 0.7 collective-permute-start.70
  107.5 0.4 shard_map.110
  107.9 1.3 collective-permute-start.69
  109.2 10.8 %collective-permute-done.69.received = f32[48,128]{1,0:T(8,128)S(1)} collective-permute-done((f32[48,128]{1,0:T(8,128)S(1)}, f32[48,128]{1,0:T(8,128)S(1)}, u32[]{:S(2)}, u32[]{:S(2)}) %collective-permute-start.69) | collective-permute-done | bytes 24608 | tf_op jit(solution)/shard_map/ppermute | solution.py:474
  120.4 0.8 collective-permute-start.71
  121.2 0.7 collective-permute-start.73
  121.8 1.9 %collective-permute-start.72 = (f32[48,128]{1,0:T(8,128)S(1)}, f32[48,128]{1,0:T(8,128)S(1)}, u32[]{:S(2)}, u32[]{:S(2)}) collective-permute-start(f32[48,128]{1,0:T(8,128)S(1)} %get-tuple-element.197), channel_id=1, source_target_pairs={{0,8},{8,16},{16,24},{1,9},{9,17},{17,25},{2,10},{10,18},{18,26},{... | collective-permute-start | bytes 73736 | tf_op jit(solution)/shard_map/ppermute | solution.py:709
  123.8 0.5 shard_map.112
  124.3 1.0 collective-permute-done.72.refs_1_
  125.6 0.9 shard_map.115
  126.4 11.0 %all-to-all-start = ((f32[32,1,128]{2,1,0:T(1,128)}), f32[32,1,128]{2,1,0:T(1,128)S(1)}, u32[]{:S(2)}, u32[]{:S(2)}) async-start(f32[32,1,128]{2,1,0:T(1,128)} %bitcast.206), calls=%async_computation | async-start | bytes 32768 | tf_op jit(solution)/shard_map/all_to_all | solution.py:728
  137.5 7.1 %all-to-all-done = f32[32,1,128]{2,1,0:T(1,128)S(1)} async-done(((f32[32,1,128]{2,1,0:T(1,128)}), f32[32,1,128]{2,1,0:T(1,128)S(1)}, u32[]{:S(2)}, u32[]{:S(2)}) %all-to-all-start) | async-done | bytes 16416 | tf_op jit(solution)/shard_map/all_to_all | solution.py:728
  144.5 0.8 shard_map.116
  (61 shorter events, 7.3 us)
Async XLA Ops:
  1.7 6.4 %collective-permute-start.40 = (f32[1,48,128]{2,1,0:T(8,128)S(1)}, f32[1,48,128]{2,1,0:T(8,128)S(1)}, u32[]{:S(2)}, u32[]{:S(2)}) collective-permute-start(f32[1,48,128]{2,1,0:T(8,128)S(1)} %get-tuple-element.122.refs_1_), channel_id=1, source_target_pairs={{0,8},{1,9},{2,10},{3,11},{4,12},{5,13},{6,14},{7,15}} | collective-permute-start | bytes 73736 | tf_op jit(solution)/shard_map/ppermute | solution.py:641
  6.5 1.5 %copy-start.26 = (f32[2,48,1,128]{3,2,1,0:T(1,128)S(1)}, f32[2,48,1,128]{3,2,1,0:T(1,128)}, u32[]{:S(2)}) copy-start(f32[2,48,1,128]{3,2,1,0:T(1,128)} %param.9) | copy-start | bytes 147460
  8.4 0.7 collective-permute-start.41
  9.1 1.3 copy-start
  9.6 1.6 %collective-permute-start.42 = (f32[1,48,128]{2,1,0:T(8,128)S(1)}, f32[1,48,128]{2,1,0:T(8,128)S(1)}, u32[]{:S(2)}, u32[]{:S(2)}) collective-permute-start(f32[1,48,128]{2,1,0:T(8,128)S(1)} %get-tuple-element.126.after), channel_id=1, source_target_pairs={{16,24},{17,25},{18,26},{19,27},{20,28},{21,29},{22,30},{23,31}} | collective-permute-start | bytes 73736 | tf_op jit(solution)/shard_map/ppermute | solution.py:641
  11.8 0.7 collective-permute-start.43
  12.8 0.7 collective-permute-start.44
  13.9 19.3 %collective-permute-start.45 = (f32[48,128]{1,0:T(8,128)S(1)}, f32[48,128]{1,0:T(8,128)S(1)}, u32[]{:S(2)}, u32[]{:S(2)}) collective-permute-start(f32[48,128]{1,0:T(8,128)S(1)} %get-tuple-element.136), channel_id=1, source_target_pairs={{8,0},{9,1},{10,2},{11,3},{12,4},{13,5},{14,6},{15,7}} | collective-permute-start | bytes 73736 | tf_op jit(solution)/shard_map/ppermute | solution.py:671
  33.3 1.3 copy-start.12
  33.3 1.6 %copy-start.16 = (bf16[2,48,48,1,128]{4,2,3,1,0:T(8,128)(2,1)S(1)}, bf16[2,48,48,1,128]{4,2,3,1,0:T(8,128)(2,1)}, u32[]{:S(2)}) copy-start(bf16[2,48,48,1,128]{4,2,3,1,0:T(8,128)(2,1)} %param.14) | copy-start | bytes 3538948
  33.3 2.0 %copy-start.21 = (bf16[2,48,48,1,128]{4,2,3,1,0:T(8,128)(2,1)S(1)}, bf16[2,48,48,1,128]{4,2,3,1,0:T(8,128)(2,1)}, u32[]{:S(2)}) copy-start(bf16[2,48,48,1,128]{4,2,3,1,0:T(8,128)(2,1)} %param.13) | copy-start | bytes 3538948
  33.7 4.1 %collective-permute-start.46 = (f32[2,48,128]{2,1,0:T(8,128)S(1)}, f32[2,48,128]{2,1,0:T(8,128)S(1)}, u32[]{:S(2)}, u32[]{:S(2)}) collective-permute-start(f32[2,48,128]{2,1,0:T(8,128)S(1)} %get-tuple-element.137.direction.refs_0_), channel_id=1, source_target_pairs={{0,1},{2,3},{4,5},{6,7},{1,0},{3,2},{5,4},{7,6},{8,9},{10,11},{12,... | collective-permute-start | bytes 147464 | tf_op jit(solution)/shard_map/ppermute | solution.py:440
  33.8 4.3 %collective-permute-start.47 = (f32[2,48,128]{2,1,0:T(8,128)S(1)}, f32[2,48,128]{2,1,0:T(8,128)S(1)}, u32[]{:S(2)}, u32[]{:S(2)}) collective-permute-start(f32[2,48,128]{2,1,0:T(8,128)S(1)} %get-tuple-element.137.direction.refs_0_), channel_id=1, source_target_pairs={{1,2},{3,4},{5,6},{2,1},{4,3},{6,5},{9,10},{11,12},{13,14},{10,9},... | collective-permute-start | bytes 147464 | tf_op jit(solution)/shard_map/ppermute | solution.py:439
  38.5 3.4 %collective-permute-start.48 = (f32[2,48,128]{2,1,0:T(8,128)S(1)}, f32[2,48,128]{2,1,0:T(8,128)S(1)}, u32[]{:S(2)}, u32[]{:S(2)}) collective-permute-start(f32[2,48,128]{2,1,0:T(8,128)S(1)} %get-tuple-element.147), channel_id=1, source_target_pairs={{0,8},{1,9},{2,10},{3,11},{4,12},{5,13},{6,14},{7,15}} | collective-permute-start | bytes 147464 | tf_op jit(solution)/shard_map/ppermute | solution.py:641
  42.3 0.7 collective-permute-start.49
  43.4 0.7 collective-permute-start.50
  44.7 0.7 collective-permute-start.51
  45.8 31.1 %collective-permute-start.56 = (f32[48,48,128]{2,1,0:T(8,128)S(1)}, f32[48,48,128]{2,1,0:T(8,128)S(1)}, u32[]{:S(2)}, u32[]{:S(2)}) collective-permute-start(f32[48,48,128]{2,1,0:T(8,128)S(1)} %shard_map.89), channel_id=1, source_target_pairs={{24,16},{25,17},{26,18},{27,19},{28,20},{29,21},{30,22},{31,23}} | collective-permute-start | bytes 3538952 | tf_op jit(solution)/shard_map/ppermute | solution.py:670
  46.5 0.7 collective-permute-start.52
  47.6 21.5 %collective-permute-start.53 = (f32[48,128]{1,0:T(8,128)S(1)}, f32[48,128]{1,0:T(8,128)S(1)}, u32[]{:S(2)}, u32[]{:S(2)}) collective-permute-start(f32[48,128]{1,0:T(8,128)S(1)} %get-tuple-element.160), channel_id=1, source_target_pairs={{8,0},{9,1},{10,2},{11,3},{12,4},{13,5},{14,6},{15,7}} | collective-permute-start | bytes 73736 | tf_op jit(solution)/shard_map/ppermute | solution.py:671
  69.5 1.3 collective-permute-start.54
  69.6 1.4 collective-permute-start.55
  71.5 3.4 %collective-permute-start.57 = (f32[2,48,128]{2,1,0:T(8,128)S(1)}, f32[2,48,128]{2,1,0:T(8,128)S(1)}, u32[]{:S(2)}, u32[]{:S(2)}) collective-permute-start(f32[2,48,128]{2,1,0:T(8,128)S(1)} %get-tuple-element.167.message), channel_id=1, source_target_pairs={{0,8},{16,24},{1,9},{17,25},{2,10},{18,26},{3,11},{19,27},{4,12},{... | collective-permute-start | bytes 147464 | tf_op jit(solution)/shard_map/ppermute | solution.py:451
  75.3 1.6 %collective-permute-start.59 = (f32[2,48,128]{2,1,0:T(8,128)S(1)}, f32[2,48,128]{2,1,0:T(8,128)S(1)}, u32[]{:S(2)}, u32[]{:S(2)}) collective-permute-start(f32[2,48,128]{2,1,0:T(8,128)S(1)} %get-tuple-element.170), channel_id=1, source_target_pairs={{8,16},{9,17},{10,18},{11,19},{12,20},{13,21},{14,22},{15,23}} | collective-permute-start | bytes 147464 | tf_op jit(solution)/shard_map/ppermute | solution.py:458
  76.2 0.7 collective-permute-start.58
  77.7 1.3 collective-permute-start.60
  78.4 2.4 %collective-permute-start.62 = (f32[48,128]{1,0:T(8,128)S(1)}, f32[48,128]{1,0:T(8,128)S(1)}, u32[]{:S(2)}, u32[]{:S(2)}) collective-permute-start(f32[48,128]{1,0:T(8,128)S(1)} %get-tuple-element.177), channel_id=1, source_target_pairs={{16,24},{17,25},{18,26},{19,27},{20,28},{21,29},{22,30},{23,31}} | collective-permute-start | bytes 73736 | tf_op jit(solution)/shard_map/ppermute | solution.py:475
  79.5 18.1 %collective-permute-start.61 = (f32[48,128]{1,0:T(8,128)S(1)}, f32[48,128]{1,0:T(8,128)S(1)}, u32[]{:S(2)}, u32[]{:S(2)}) collective-permute-start(f32[48,128]{1,0:T(8,128)S(1)} %get-tuple-element.176), channel_id=1, source_target_pairs={{8,0},{9,1},{10,2},{11,3},{12,4},{13,5},{14,6},{15,7}} | collective-permute-start | bytes 73736 | tf_op jit(solution)/shard_map/ppermute | solution.py:474
  98.0 1.3 collective-permute-start.63
  98.0 1.4 collective-permute-start.64
  99.9 3.4 %collective-permute-start.65 = (f32[2,48,128]{2,1,0:T(8,128)S(1)}, f32[2,48,128]{2,1,0:T(8,128)S(1)}, u32[]{:S(2)}, u32[]{:S(2)}) collective-permute-start(f32[2,48,128]{2,1,0:T(8,128)S(1)} %get-tuple-element.183.message), channel_id=1, source_target_pairs={{0,8},{16,24},{1,9},{17,25},{2,10},{18,26},{3,11},{19,27},{4,12},{... | collective-permute-start | bytes 147464 | tf_op jit(solution)/shard_map/ppermute | solution.py:451
  103.7 1.6 %collective-permute-start.67 = (f32[2,48,128]{2,1,0:T(8,128)S(1)}, f32[2,48,128]{2,1,0:T(8,128)S(1)}, u32[]{:S(2)}, u32[]{:S(2)}) collective-permute-start(f32[2,48,128]{2,1,0:T(8,128)S(1)} %get-tuple-element.186), channel_id=1, source_target_pairs={{8,16},{9,17},{10,18},{11,19},{12,20},{13,21},{14,22},{15,23}} | collective-permute-start | bytes 147464 | tf_op jit(solution)/shard_map/ppermute | solution.py:458
  104.5 0.7 collective-permute-start.66
  106.1 1.3 collective-permute-start.68
  106.8 2.4 %collective-permute-start.70 = (f32[48,128]{1,0:T(8,128)S(1)}, f32[48,128]{1,0:T(8,128)S(1)}, u32[]{:S(2)}, u32[]{:S(2)}) collective-permute-start(f32[48,128]{1,0:T(8,128)S(1)} %get-tuple-element.193), channel_id=1, source_target_pairs={{16,24},{17,25},{18,26},{19,27},{20,28},{21,29},{22,30},{23,31}} | collective-permute-start | bytes 73736 | tf_op jit(solution)/shard_map/ppermute | solution.py:475
  107.9 12.1 %collective-permute-start.69 = (f32[48,128]{1,0:T(8,128)S(1)}, f32[48,128]{1,0:T(8,128)S(1)}, u32[]{:S(2)}, u32[]{:S(2)}) collective-permute-start(f32[48,128]{1,0:T(8,128)S(1)} %get-tuple-element.192), channel_id=1, source_target_pairs={{8,0},{9,1},{10,2},{11,3},{12,4},{13,5},{14,6},{15,7}} | collective-permute-start | bytes 73736 | tf_op jit(solution)/shard_map/ppermute | solution.py:474
  120.4 4.9 %collective-permute-start.71 = (f32[2,48,128]{2,1,0:T(8,128)S(1)}, f32[2,48,128]{2,1,0:T(8,128)S(1)}, u32[]{:S(2)}, u32[]{:S(2)}) collective-permute-start(f32[2,48,128]{2,1,0:T(8,128)S(1)} %get-tuple-element.194.direction.refs_3_), channel_id=1, source_target_pairs={{0,1},{2,3},{4,5},{6,7},{1,0},{3,2},{5,4},{7,6},{8,9},{10,11},{12,... | collective-permute-start | bytes 147464 | tf_op jit(solution)/shard_map/ppermute | solution.py:440
  121.2 4.4 %collective-permute-start.73 = (f32[2,48,128]{2,1,0:T(8,128)S(1)}, f32[2,48,128]{2,1,0:T(8,128)S(1)}, u32[]{:S(2)}, u32[]{:S(2)}) collective-permute-start(f32[2,48,128]{2,1,0:T(8,128)S(1)} %get-tuple-element.194.direction.refs_3_), channel_id=1, source_target_pairs={{1,2},{3,4},{5,6},{2,1},{4,3},{6,5},{9,10},{11,12},{13,14},{10,9},... | collective-permute-start | bytes 147464 | tf_op jit(solution)/shard_map/ppermute | solution.py:439
  121.8 3.4 %collective-permute-start.72 = (f32[48,128]{1,0:T(8,128)S(1)}, f32[48,128]{1,0:T(8,128)S(1)}, u32[]{:S(2)}, u32[]{:S(2)}) collective-permute-start(f32[48,128]{1,0:T(8,128)S(1)} %get-tuple-element.197), channel_id=1, source_target_pairs={{0,8},{8,16},{16,24},{1,9},{9,17},{17,25},{2,10},{10,18},{18,26},{... | collective-permute-start | bytes 73736 | tf_op jit(solution)/shard_map/ppermute | solution.py:709
  125.5 19.8 %copy-start.5 = (bf16[2,48,48,1,128]{4,2,3,1,0:T(8,128)(2,1)S(1)}, bf16[2,48,48,1,128]{4,2,3,1,0:T(8,128)(2,1)}, u32[]{:S(2)}) copy-start(bf16[2,48,48,1,128]{4,2,3,1,0:T(8,128)(2,1)} %param.11) | copy-start | bytes 3538948
  126.4 18.1 %all-to-all-start = ((f32[32,1,128]{2,1,0:T(1,128)}), f32[32,1,128]{2,1,0:T(1,128)S(1)}, u32[]{:S(2)}, u32[]{:S(2)}) async-start(f32[32,1,128]{2,1,0:T(1,128)} %bitcast.206), calls=%async_computation | async-start | bytes 32768 | tf_op jit(solution)/shard_map/all_to_all | solution.py:728

commit v18 on v17

--- a/solution.py
+++ b/solution.py
@@ -323,12 +323,9 @@
         image[k] = value
 
 
-def near_kernel(image, near_block, near, *refs):
-    *below, out = refs
+def near_kernel(image, near_block, near, out):
     for k in range(image.shape[0]):
         out[k] = image[k] + apply_turned(near_block.at[k], near.at[k])
-    if below:
-        out[0] = out[0] + apply_turned(below[0].at[0], below[1])
 
 
 def next_kernel(image, far_block, far, lower, pivot, last, out, message, forward, work):
@@ -361,10 +358,11 @@
     out[...] = sums
 
 
-def last_kernel(image, far_block, far, sums_in, *refs):
+def last_kernel(lower, below, image, far_block, far, sums_in, *refs):
     *basis, out, newest = refs
     for k in range(image.shape[0]):
         newest[k] = image[k] + apply_turned(far_block.at[k], far.at[k])
+    newest[0] = newest[0] + apply_turned(lower.at[0], below)
     sums = sums_in[...]
     row = lax.broadcasted_iota(jnp.int32, sums.shape, 0)
     lane = lax.broadcasted_iota(jnp.int32, sums.shape, 1)
@@ -703,12 +701,10 @@
             [vector, carried_down, lower, diag_block, direction, coupled],
         )
         basis.append(whole)
-        beneath = []
         if j == ITERS - 1:
             (sums,) = stage(sums_kernel, [(SUMS, wide)], basis)
             below = lax.ppermute(last, "line", [(i, i + 1) for i in range(line - 1)])
-            beneath = [lower, below]
-        (image,) = stage(near_kernel, [field], [image, near_block, near, *beneath])
+        (image,) = stage(near_kernel, [field], [image, near_block, near])
         if j < ITERS - 1:
             vector, message = stage(
                 next_kernel,
@@ -722,7 +718,7 @@
             (sums,) = stage(
                 last_kernel,
                 [(devices, wide)],
-                [image, far_block, far, sums, *basis],
+                [lower, below, image, far_block, far, sums, *basis],
                 [field],
             )
     sums = lax.all_to_all(sums, ("line", "patch"), 0, 0, tiled=True)

time: 147 us -> 146 us (level)
  transfers between devices with their start and end apart: 35 -> 35, of which waited for: 11 -> 11; matrix products, arithmetic and copies ran while one was open for 0% -> 0% of each run, Pallas kernels for 7% -> 6%
where the time goes in v18:
time: 146 us
  waiting for transfers between devices  79.4 us (54%)
  starting transfers between devices  43.1 us (30%)
  Pallas kernels  21.2 us (15%)
    ppermute x6, waiting for transfers between devices, per_device(): parts.append(lax.ppermute(outgoing, 'line', [(turn + 1, turn)]))  38 us
    ppermute x2, waiting for transfers between devices, sweep_short(): received = lax.ppermute(outgoing, 'line', [(1, 0)])  27.6 us
    pallas_call x37, Pallas kernels, stage(): pl.pallas_call(kernel, out_shape=[pltpu.VMEM(shape, jnp.float32) for shap...  15 us
    all_to_all x1, starting transfers between devices, per_device(): sums = lax.all_to_all(sums, ('line', 'patch'), 0, 0, tiled=True)  11 us
    ppermute x6, starting transfers between devices, per_device(): parts.append(lax.ppermute(message, 'line', [(turn, turn + 1)]))  9.12 us
    all_to_all x1, waiting for transfers between devices, per_device(): sums = lax.all_to_all(sums, ('line', 'patch'), 0, 0, tiled=True)  7.07 us
    ppermute x6, starting transfers between devices, per_device(): parts.append(lax.ppermute(outgoing, 'line', [(turn + 1, turn)]))  5.42 us
    ppermute x2, waiting for transfers between devices, sweep_short(): received = lax.ppermute(message, 'line', [(0, 1), (2, 3)])  3.46 us
  transfers between devices with their start and end apart: 35, of which 11 were waited for; matrix products, arithmetic and copies ran while one was open for 0% of the time, Pallas kernels for 6%

profile of v18, /device:TPU:0, one launch (start us, length us, event | category | flops | bytes accessed | tf_op | source)
XLA Modules:
  0.0 145.7 jit_solution(12223513152364288521)
XLA Ops:
  0.0 1.7 %shard_map.75 = (bf16[2,48,48,128]{3,2,1,0:T(8,128)(2,1)S(1)}, bf16[2,48,48,128]{3,2,1,0:T(8,128)(2,1)S(1)}, f32[1,48,128]{2,1,0:T(8,128)S(1)}) custom-call(f32[2,48,128]{2,1,0:T(8,128)} %bitcast.477, bf16[2,48,48,128]{3,2,1,0:T(8,128)(2,1)} %bitcast.460, bf16[2,48,48,128]{3,2,1,0:T(8,128)(2,1)} %bitcast.498), custom_call_target="tpu_custom_call" | custom-call | tf_op jit(solution)/shard_map/pallas_call | solution.py:73
  1.7 4.8 %collective-permute-start.40 = (f32[1,48,128]{2,1,0:T(8,128)S(1)}, f32[1,48,128]{2,1,0:T(8,128)S(1)}, u32[]{:S(2)}, u32[]{:S(2)}) collective-permute-start(f32[1,48,128]{2,1,0:T(8,128)S(1)} %get-tuple-element.122.refs_1_), channel_id=1, source_target_pairs={{0,8},{1,9},{2,10},{3,11},{4,12},{5,13},{6,14},{7,15}} | collective-permute-start | bytes 73736 | tf_op jit(solution)/shard_map/ppermute | solution.py:639
  6.5 0.9 shard_map.76
  7.5 0.6 collective-permute-done.40.refs_0_
  8.4 0.7 collective-permute-start.41
  9.1 0.4 shard_map.79
  9.6 0.7 collective-permute-start.42
  10.4 0.7 shard_map.77.upper
  11.1 0.6 shard_map.80
  11.8 0.7 collective-permute-start.43
  12.8 0.7 collective-permute-start.44
  13.5 0.4 shard_map.84
  13.9 1.3 collective-permute-start.45
  15.2 18.0 %collective-permute-done.45.refs_1_ = f32[48,128]{1,0:T(8,128)S(1)} collective-permute-done((f32[48,128]{1,0:T(8,128)S(1)}, f32[48,128]{1,0:T(8,128)S(1)}, u32[]{:S(2)}, u32[]{:S(2)}) %collective-permute-start.45) | collective-permute-done | bytes 24608 | tf_op jit(solution)/shard_map/ppermute | solution.py:669
  33.8 0.8 collective-permute-start.47
  35.2 2.1 %shard_map.82 = (f32[2,48,48,128]{3,2,1,0:T(8,128)S(1)}, f32[2,48,48,128]{3,2,1,0:T(8,128)S(1)}, f32[2,48,48,128]{3,2,1,0:T(8,128)S(1)}) custom-call(bf16[2,48,48,128]{3,2,1,0:T(8,128)(2,1)S(1)} %bitcast.474, bf16[2,48,48,128]{3,2,1,0:T(8,128)(2,1)S(1)} %bitcast.475, bf16[2,48,48,128]{3,2,1,0:T(8,128)(2,1)S(1)} %bitcast.476, ...), custom_call_target="tpu_custom_call" | custom-call | tf_op jit(solution)/shard_map/pallas_call | solution.py:131
  38.0 0.5 shard_map.88
  38.5 1.6 %collective-permute-start.48 = (f32[2,48,128]{2,1,0:T(8,128)S(1)}, f32[2,48,128]{2,1,0:T(8,128)S(1)}, u32[]{:S(2)}, u32[]{:S(2)}) collective-permute-start(f32[2,48,128]{2,1,0:T(8,128)S(1)} %get-tuple-element.147), channel_id=1, source_target_pairs={{0,8},{1,9},{2,10},{3,11},{4,12},{5,13},{6,14},{7,15}} | collective-permute-start | bytes 147464 | tf_op jit(solution)/shard_map/ppermute | solution.py:639
  40.2 1.7 %collective-permute-done.48.refs_0_ = f32[2,48,128]{2,1,0:T(8,128)S(1)} collective-permute-done((f32[2,48,128]{2,1,0:T(8,128)S(1)}, f32[2,48,128]{2,1,0:T(8,128)S(1)}, u32[]{:S(2)}, u32[]{:S(2)}) %collective-permute-start.48) | collective-permute-done | bytes 49184 | tf_op jit(solution)/shard_map/ppermute | solution.py:639
  42.3 0.7 collective-permute-start.49
  43.0 0.4 shard_map.91
  43.4 0.7 collective-permute-start.50
  44.1 0.6 shard_map.92
  44.7 0.7 collective-permute-start.51
  45.8 0.7 collective-permute-start.56
  46.5 0.7 collective-permute-start.52
  47.2 0.4 shard_map.94
  47.6 1.5 %collective-permute-start.53 = (f32[48,128]{1,0:T(8,128)S(1)}, f32[48,128]{1,0:T(8,128)S(1)}, u32[]{:S(2)}, u32[]{:S(2)}) collective-permute-start(f32[48,128]{1,0:T(8,128)S(1)} %get-tuple-element.160), channel_id=1, source_target_pairs={{8,0},{9,1},{10,2},{11,3},{12,4},{13,5},{14,6},{15,7}} | collective-permute-start | bytes 73736 | tf_op jit(solution)/shard_map/ppermute | solution.py:669
  49.1 20.0 %collective-permute-done.53.refs_1_ = f32[48,128]{1,0:T(8,128)S(1)} collective-permute-done((f32[48,128]{1,0:T(8,128)S(1)}, f32[48,128]{1,0:T(8,128)S(1)}, u32[]{:S(2)}, u32[]{:S(2)}) %collective-permute-start.53) | collective-permute-done | bytes 24608 | tf_op jit(solution)/shard_map/ppermute | solution.py:669
  69.6 0.7 collective-permute-start.55
  70.3 0.5 shard_map.96
  71.0 0.5 shard_map.98
  71.5 1.6 %collective-permute-start.57 = (f32[2,48,128]{2,1,0:T(8,128)S(1)}, f32[2,48,128]{2,1,0:T(8,128)S(1)}, u32[]{:S(2)}, u32[]{:S(2)}) collective-permute-start(f32[2,48,128]{2,1,0:T(8,128)S(1)} %get-tuple-element.167.message), channel_id=1, source_target_pairs={{0,8},{16,24},{1,9},{17,25},{2,10},{18,26},{3,11},{19,27},{4,12},{... | collective-permute-start | bytes 147464 | tf_op jit(solution)/shard_map/ppermute | solution.py:449
  73.2 1.7 %collective-permute-done.57.refs_0_ = f32[2,48,128]{2,1,0:T(8,128)S(1)} collective-permute-done((f32[2,48,128]{2,1,0:T(8,128)S(1)}, f32[2,48,128]{2,1,0:T(8,128)S(1)}, u32[]{:S(2)}, u32[]{:S(2)}) %collective-permute-start.57) | collective-permute-done | bytes 49184 | tf_op jit(solution)/shard_map/ppermute | solution.py:449
  75.3 0.7 collective-permute-start.59
  76.2 0.7 collective-permute-start.58
  76.9 0.9 shard_map.101
  77.7 0.7 collective-permute-start.60
  78.4 0.7 collective-permute-start.62
  79.1 0.4 shard_map.102
  79.5 1.3 collective-permute-start.61
  80.8 16.8 %collective-permute-done.61.received = f32[48,128]{1,0:T(8,128)S(1)} collective-permute-done((f32[48,128]{1,0:T(8,128)S(1)}, f32[48,128]{1,0:T(8,128)S(1)}, u32[]{:S(2)}, u32[]{:S(2)}) %collective-permute-start.61) | collective-permute-done | bytes 24608 | tf_op jit(solution)/shard_map/ppermute | solution.py:472
  98.0 0.7 collective-permute-start.64
  98.7 0.5 shard_map.104
  99.5 0.4 shard_map.106
  99.9 1.6 %collective-permute-start.65 = (f32[2,48,128]{2,1,0:T(8,128)S(1)}, f32[2,48,128]{2,1,0:T(8,128)S(1)}, u32[]{:S(2)}, u32[]{:S(2)}) collective-permute-start(f32[2,48,128]{2,1,0:T(8,128)S(1)} %get-tuple-element.183.message), channel_id=1, source_target_pairs={{0,8},{16,24},{1,9},{17,25},{2,10},{18,26},{3,11},{19,27},{4,12},{... | collective-permute-start | bytes 147464 | tf_op jit(solution)/shard_map/ppermute | solution.py:449
  101.5 1.7 %collective-permute-done.65.refs_0_ = f32[2,48,128]{2,1,0:T(8,128)S(1)} collective-permute-done((f32[2,48,128]{2,1,0:T(8,128)S(1)}, f32[2,48,128]{2,1,0:T(8,128)S(1)}, u32[]{:S(2)}, u32[]{:S(2)}) %collective-permute-start.65) | collective-permute-done | bytes 49184 | tf_op jit(solution)/shard_map/ppermute | solution.py:449
  103.7 0.7 collective-permute-start.67
  104.5 0.7 collective-permute-start.66
  105.2 0.9 shard_map.109
  106.1 0.7 collective-permute-start.68
  106.8 0.7 collective-permute-start.70
  107.5 0.4 shard_map.110
  107.9 1.3 collective-permute-start.69
  109.2 10.8 %collective-permute-done.69.received = f32[48,128]{1,0:T(8,128)S(1)} collective-permute-done((f32[48,128]{1,0:T(8,128)S(1)}, f32[48,128]{1,0:T(8,128)S(1)}, u32[]{:S(2)}, u32[]{:S(2)}) %collective-permute-start.69) | collective-permute-done | bytes 24608 | tf_op jit(solution)/shard_map/ppermute | solution.py:472
  120.4 0.8 collective-permute-start.72
  121.2 0.7 collective-permute-start.73
  121.8 1.9 %collective-permute-start.71 = (f32[48,128]{1,0:T(8,128)S(1)}, f32[48,128]{1,0:T(8,128)S(1)}, u32[]{:S(2)}, u32[]{:S(2)}) collective-permute-start(f32[48,128]{1,0:T(8,128)S(1)} %get-tuple-element.194), channel_id=1, source_target_pairs={{0,8},{8,16},{16,24},{1,9},{9,17},{17,25},{2,10},{10,18},{18,26},{... | collective-permute-start | bytes 73736 | tf_op jit(solution)/shard_map/ppermute | solution.py:706
  123.8 0.5 shard_map.112
  124.5 0.7 collective-permute-done.71.below
  125.3 1.0 shard_map.115
  126.3 11.0 %all-to-all-start = ((f32[32,1,128]{2,1,0:T(1,128)}), f32[32,1,128]{2,1,0:T(1,128)S(1)}, u32[]{:S(2)}, u32[]{:S(2)}) async-start(f32[32,1,128]{2,1,0:T(1,128)} %bitcast.206), calls=%async_computation | async-start | bytes 32768 | tf_op jit(solution)/shard_map/all_to_all | solution.py:724
  137.3 7.1 %all-to-all-done = f32[32,1,128]{2,1,0:T(1,128)S(1)} async-done(((f32[32,1,128]{2,1,0:T(1,128)}), f32[32,1,128]{2,1,0:T(1,128)S(1)}, u32[]{:S(2)}, u32[]{:S(2)}) %all-to-all-start) | async-done | bytes 16416 | tf_op jit(solution)/shard_map/all_to_all | solution.py:724
  144.3 0.8 shard_map.116
  (61 shorter events, 7.2 us)
Async XLA Ops:
  1.7 6.4 %collective-permute-start.40 = (f32[1,48,128]{2,1,0:T(8,128)S(1)}, f32[1,48,128]{2,1,0:T(8,128)S(1)}, u32[]{:S(2)}, u32[]{:S(2)}) collective-permute-start(f32[1,48,128]{2,1,0:T(8,128)S(1)} %get-tuple-element.122.refs_1_), channel_id=1, source_target_pairs={{0,8},{1,9},{2,10},{3,11},{4,12},{5,13},{6,14},{7,15}} | collective-permute-start | bytes 73736 | tf_op jit(solution)/shard_map/ppermute | solution.py:639
  6.5 1.5 %copy-start.26 = (f32[2,48,1,128]{3,2,1,0:T(1,128)S(1)}, f32[2,48,1,128]{3,2,1,0:T(1,128)}, u32[]{:S(2)}) copy-start(f32[2,48,1,128]{3,2,1,0:T(1,128)} %param.9) | copy-start | bytes 147460
  8.4 0.7 collective-permute-start.41
  9.1 1.3 copy-start
  9.6 1.6 %collective-permute-start.42 = (f32[1,48,128]{2,1,0:T(8,128)S(1)}, f32[1,48,128]{2,1,0:T(8,128)S(1)}, u32[]{:S(2)}, u32[]{:S(2)}) collective-permute-start(f32[1,48,128]{2,1,0:T(8,128)S(1)} %get-tuple-element.126.after), channel_id=1, source_target_pairs={{16,24},{17,25},{18,26},{19,27},{20,28},{21,29},{22,30},{23,31}} | collective-permute-start | bytes 73736 | tf_op jit(solution)/shard_map/ppermute | solution.py:639
  11.8 0.7 collective-permute-start.43
  12.8 0.7 collective-permute-start.44
  13.9 19.3 %collective-permute-start.45 = (f32[48,128]{1,0:T(8,128)S(1)}, f32[48,128]{1,0:T(8,128)S(1)}, u32[]{:S(2)}, u32[]{:S(2)}) collective-permute-start(f32[48,128]{1,0:T(8,128)S(1)} %get-tuple-element.136), channel_id=1, source_target_pairs={{8,0},{9,1},{10,2},{11,3},{12,4},{13,5},{14,6},{15,7}} | collective-permute-start | bytes 73736 | tf_op jit(solution)/shard_map/ppermute | solution.py:669
  33.3 1.3 copy-start.12
  33.3 1.6 %copy-start.16 = (bf16[2,48,48,1,128]{4,2,3,1,0:T(8,128)(2,1)S(1)}, bf16[2,48,48,1,128]{4,2,3,1,0:T(8,128)(2,1)}, u32[]{:S(2)}) copy-start(bf16[2,48,48,1,128]{4,2,3,1,0:T(8,128)(2,1)} %param.14) | copy-start | bytes 3538948
  33.3 2.0 %copy-start.21 = (bf16[2,48,48,1,128]{4,2,3,1,0:T(8,128)(2,1)S(1)}, bf16[2,48,48,1,128]{4,2,3,1,0:T(8,128)(2,1)}, u32[]{:S(2)}) copy-start(bf16[2,48,48,1,128]{4,2,3,1,0:T(8,128)(2,1)} %param.13) | copy-start | bytes 3538948
  33.7 4.1 %collective-permute-start.46 = (f32[2,48,128]{2,1,0:T(8,128)S(1)}, f32[2,48,128]{2,1,0:T(8,128)S(1)}, u32[]{:S(2)}, u32[]{:S(2)}) collective-permute-start(f32[2,48,128]{2,1,0:T(8,128)S(1)} %get-tuple-element.137.direction.refs_0_), channel_id=1, source_target_pairs={{0,1},{2,3},{4,5},{6,7},{1,0},{3,2},{5,4},{7,6},{8,9},{10,11},{12,... | collective-permute-start | bytes 147464 | tf_op jit(solution)/shard_map/ppermute | solution.py:438
  33.8 4.3 %collective-permute-start.47 = (f32[2,48,128]{2,1,0:T(8,128)S(1)}, f32[2,48,128]{2,1,0:T(8,128)S(1)}, u32[]{:S(2)}, u32[]{:S(2)}) collective-permute-start(f32[2,48,128]{2,1,0:T(8,128)S(1)} %get-tuple-element.137.direction.refs_0_), channel_id=1, source_target_pairs={{1,2},{3,4},{5,6},{2,1},{4,3},{6,5},{9,10},{11,12},{13,14},{10,9},... | collective-permute-start | bytes 147464 | tf_op jit(solution)/shard_map/ppermute | solution.py:437
  38.5 3.4 %collective-permute-start.48 = (f32[2,48,128]{2,1,0:T(8,128)S(1)}, f32[2,48,128]{2,1,0:T(8,128)S(1)}, u32[]{:S(2)}, u32[]{:S(2)}) collective-permute-start(f32[2,48,128]{2,1,0:T(8,128)S(1)} %get-tuple-element.147), channel_id=1, source_target_pairs={{0,8},{1,9},{2,10},{3,11},{4,12},{5,13},{6,14},{7,15}} | collective-permute-start | bytes 147464 | tf_op jit(solution)/shard_map/ppermute | solution.py:639
  42.3 0.7 collective-permute-start.49
  43.4 0.7 collective-permute-start.50
  44.7 0.7 collective-permute-start.51
  45.8 31.1 %collective-permute-start.56 = (f32[48,48,128]{2,1,0:T(8,128)S(1)}, f32[48,48,128]{2,1,0:T(8,128)S(1)}, u32[]{:S(2)}, u32[]{:S(2)}) collective-permute-start(f32[48,48,128]{2,1,0:T(8,128)S(1)} %shard_map.89), channel_id=1, source_target_pairs={{24,16},{25,17},{26,18},{27,19},{28,20},{29,21},{30,22},{31,23}} | collective-permute-start | bytes 3538952 | tf_op jit(solution)/shard_map/ppermute | solution.py:668
  46.5 0.7 collective-permute-start.52
  47.6 21.5 %collective-permute-start.53 = (f32[48,128]{1,0:T(8,128)S(1)}, f32[48,128]{1,0:T(8,128)S(1)}, u32[]{:S(2)}, u32[]{:S(2)}) collective-permute-start(f32[48,128]{1,0:T(8,128)S(1)} %get-tuple-element.160), channel_id=1, source_target_pairs={{8,0},{9,1},{10,2},{11,3},{12,4},{13,5},{14,6},{15,7}} | collective-permute-start | bytes 73736 | tf_op jit(solution)/shard_map/ppermute | solution.py:669
  69.5 1.3 collective-permute-start.54
  69.6 1.4 collective-permute-start.55
  71.5 3.4 %collective-permute-start.57 = (f32[2,48,128]{2,1,0:T(8,128)S(1)}, f32[2,48,128]{2,1,0:T(8,128)S(1)}, u32[]{:S(2)}, u32[]{:S(2)}) collective-permute-start(f32[2,48,128]{2,1,0:T(8,128)S(1)} %get-tuple-element.167.message), channel_id=1, source_target_pairs={{0,8},{16,24},{1,9},{17,25},{2,10},{18,26},{3,11},{19,27},{4,12},{... | collective-permute-start | bytes 147464 | tf_op jit(solution)/shard_map/ppermute | solution.py:449
  75.3 1.6 %collective-permute-start.59 = (f32[2,48,128]{2,1,0:T(8,128)S(1)}, f32[2,48,128]{2,1,0:T(8,128)S(1)}, u32[]{:S(2)}, u32[]{:S(2)}) collective-permute-start(f32[2,48,128]{2,1,0:T(8,128)S(1)} %get-tuple-element.170), channel_id=1, source_target_pairs={{8,16},{9,17},{10,18},{11,19},{12,20},{13,21},{14,22},{15,23}} | collective-permute-start | bytes 147464 | tf_op jit(solution)/shard_map/ppermute | solution.py:456
  76.2 0.7 collective-permute-start.58
  77.7 1.3 collective-permute-start.60
  78.4 2.4 %collective-permute-start.62 = (f32[48,128]{1,0:T(8,128)S(1)}, f32[48,128]{1,0:T(8,128)S(1)}, u32[]{:S(2)}, u32[]{:S(2)}) collective-permute-start(f32[48,128]{1,0:T(8,128)S(1)} %get-tuple-element.177), channel_id=1, source_target_pairs={{16,24},{17,25},{18,26},{19,27},{20,28},{21,29},{22,30},{23,31}} | collective-permute-start | bytes 73736 | tf_op jit(solution)/shard_map/ppermute | solution.py:473
  79.5 18.1 %collective-permute-start.61 = (f32[48,128]{1,0:T(8,128)S(1)}, f32[48,128]{1,0:T(8,128)S(1)}, u32[]{:S(2)}, u32[]{:S(2)}) collective-permute-start(f32[48,128]{1,0:T(8,128)S(1)} %get-tuple-element.176), channel_id=1, source_target_pairs={{8,0},{9,1},{10,2},{11,3},{12,4},{13,5},{14,6},{15,7}} | collective-permute-start | bytes 73736 | tf_op jit(solution)/shard_map/ppermute | solution.py:472
  98.0 1.3 collective-permute-start.63
  98.0 1.4 collective-permute-start.64
  99.9 3.4 %collective-permute-start.65 = (f32[2,48,128]{2,1,0:T(8,128)S(1)}, f32[2,48,128]{2,1,0:T(8,128)S(1)}, u32[]{:S(2)}, u32[]{:S(2)}) collective-permute-start(f32[2,48,128]{2,1,0:T(8,128)S(1)} %get-tuple-element.183.message), channel_id=1, source_target_pairs={{0,8},{16,24},{1,9},{17,25},{2,10},{18,26},{3,11},{19,27},{4,12},{... | collective-permute-start | bytes 147464 | tf_op jit(solution)/shard_map/ppermute | solution.py:449
  103.7 1.6 %collective-permute-start.67 = (f32[2,48,128]{2,1,0:T(8,128)S(1)}, f32[2,48,128]{2,1,0:T(8,128)S(1)}, u32[]{:S(2)}, u32[]{:S(2)}) collective-permute-start(f32[2,48,128]{2,1,0:T(8,128)S(1)} %get-tuple-element.186), channel_id=1, source_target_pairs={{8,16},{9,17},{10,18},{11,19},{12,20},{13,21},{14,22},{15,23}} | collective-permute-start | bytes 147464 | tf_op jit(solution)/shard_map/ppermute | solution.py:456
  104.5 0.7 collective-permute-start.66
  106.1 1.3 collective-permute-start.68
  106.8 2.4 %collective-permute-start.70 = (f32[48,128]{1,0:T(8,128)S(1)}, f32[48,128]{1,0:T(8,128)S(1)}, u32[]{:S(2)}, u32[]{:S(2)}) collective-permute-start(f32[48,128]{1,0:T(8,128)S(1)} %get-tuple-element.193), channel_id=1, source_target_pairs={{16,24},{17,25},{18,26},{19,27},{20,28},{21,29},{22,30},{23,31}} | collective-permute-start | bytes 73736 | tf_op jit(solution)/shard_map/ppermute | solution.py:473
  107.9 12.1 %collective-permute-start.69 = (f32[48,128]{1,0:T(8,128)S(1)}, f32[48,128]{1,0:T(8,128)S(1)}, u32[]{:S(2)}, u32[]{:S(2)}) collective-permute-start(f32[48,128]{1,0:T(8,128)S(1)} %get-tuple-element.192), channel_id=1, source_target_pairs={{8,0},{9,1},{10,2},{11,3},{12,4},{13,5},{14,6},{15,7}} | collective-permute-start | bytes 73736 | tf_op jit(solution)/shard_map/ppermute | solution.py:472
  120.4 3.9 %collective-permute-start.72 = (f32[2,48,128]{2,1,0:T(8,128)S(1)}, f32[2,48,128]{2,1,0:T(8,128)S(1)}, u32[]{:S(2)}, u32[]{:S(2)}) collective-permute-start(f32[2,48,128]{2,1,0:T(8,128)S(1)} %get-tuple-element.195.direction.refs_3_), channel_id=1, source_target_pairs={{0,1},{2,3},{4,5},{6,7},{1,0},{3,2},{5,4},{7,6},{8,9},{10,11},{12,... | collective-permute-start | bytes 147464 | tf_op jit(solution)/shard_map/ppermute | solution.py:438
  121.2 4.1 %collective-permute-start.73 = (f32[2,48,128]{2,1,0:T(8,128)S(1)}, f32[2,48,128]{2,1,0:T(8,128)S(1)}, u32[]{:S(2)}, u32[]{:S(2)}) collective-permute-start(f32[2,48,128]{2,1,0:T(8,128)S(1)} %get-tuple-element.195.direction.refs_3_), channel_id=1, source_target_pairs={{1,2},{3,4},{5,6},{2,1},{4,3},{6,5},{9,10},{11,12},{13,14},{10,9},... | collective-permute-start | bytes 147464 | tf_op jit(solution)/shard_map/ppermute | solution.py:437
  121.8 3.4 %collective-permute-start.71 = (f32[48,128]{1,0:T(8,128)S(1)}, f32[48,128]{1,0:T(8,128)S(1)}, u32[]{:S(2)}, u32[]{:S(2)}) collective-permute-start(f32[48,128]{1,0:T(8,128)S(1)} %get-tuple-element.194), channel_id=1, source_target_pairs={{0,8},{8,16},{16,24},{1,9},{9,17},{17,25},{2,10},{10,18},{18,26},{... | collective-permute-start | bytes 73736 | tf_op jit(solution)/shard_map/ppermute | solution.py:706
  124.5 20.7 %copy-start.5 = (bf16[2,48,48,1,128]{4,2,3,1,0:T(8,128)(2,1)S(1)}, bf16[2,48,48,1,128]{4,2,3,1,0:T(8,128)(2,1)}, u32[]{:S(2)}) copy-start(bf16[2,48,48,1,128]{4,2,3,1,0:T(8,128)(2,1)} %param.11) | copy-start | bytes 3538948
  126.3 18.1 %all-to-all-start = ((f32[32,1,128]{2,1,0:T(1,128)}), f32[32,1,128]{2,1,0:T(1,128)S(1)}, u32[]{:S(2)}, u32[]{:S(2)}) async-start(f32[32,1,128]{2,1,0:T(1,128)} %bitcast.206), calls=%async_computation | async-start | bytes 32768 | tf_op jit(solution)/shard_map/all_to_all | solution.py:724

commit v19 on v17

--- a/solution.py
+++ b/solution.py
@@ -665,10 +665,10 @@
                 outgoing, response = lax.optimization_barrier((outgoing, response))
             parts = []
             for turn in reversed(range(line - 1)):
-                if j == 1 and turn == line - 3 and short:
-                    outgoing, ready = lax.optimization_barrier((outgoing, response))
+                parts.append(lax.ppermute(outgoing, "line", [(turn + 1, turn)]))
+                if j == 1 and turn == line - 2 and short:
+                    parts[-1], ready = lax.optimization_barrier((parts[-1], response))
                     response = lax.ppermute(ready, "line", [(line - 1, line - 2)])
-                parts.append(lax.ppermute(outgoing, "line", [(turn + 1, turn)]))
                 if j == 0 and turn == line - 2:
                     diag_block, near_block, far_block = load(
                         (diag_block, east, west), outgoing, True

time: 147 us -> 146 us (level)
  no operation moved by 1% of the time
where the time goes in v19:
time: 146 us; the launch traced here: 145 us
  waiting for transfers between devices  79.2 us (54%)
  starting transfers between devices  43.1 us (30%)
  Pallas kernels  21.1 us (14%)
    ppermute x6, waiting for transfers between devices, per_device(): parts.append(lax.ppermute(outgoing, 'line', [(turn + 1, turn)]))  38 us
    ppermute x2, waiting for transfers between devices, sweep_short(): received = lax.ppermute(outgoing, 'line', [(1, 0)])  27.2 us
    pallas_call x37, Pallas kernels, stage(): pl.pallas_call(kernel, out_shape=[pltpu.VMEM(shape, jnp.float32) for shap...  14.9 us
    all_to_all x1, starting transfers between devices, per_device(): sums = lax.all_to_all(sums, ('line', 'patch'), 0, 0, tiled=True)  11 us
    ppermute x6, starting transfers between devices, per_device(): parts.append(lax.ppermute(message, 'line', [(turn, turn + 1)]))  9.12 us
    all_to_all x1, waiting for transfers between devices, per_device(): sums = lax.all_to_all(sums, ('line', 'patch'), 0, 0, tiled=True)  7.07 us
    ppermute x6, starting transfers between devices, per_device(): parts.append(lax.ppermute(outgoing, 'line', [(turn + 1, turn)]))  5.42 us
    ppermute x2, waiting for transfers between devices, sweep_short(): received = lax.ppermute(message, 'line', [(0, 1), (2, 3)])  3.46 us
  transfers between devices with their start and end apart: 35, of which 11 were waited for; matrix products, arithmetic and copies ran while one was open for 0% of the time, Pallas kernels for 7%

profile of v19, /device:TPU:0, one launch (start us, length us, event | category | flops | bytes accessed | tf_op | source)
XLA Modules:
  0.0 145.4 jit_solution(13925801560311530516)
XLA Ops:
  0.0 1.7 %shard_map.75 = (bf16[2,48,48,128]{3,2,1,0:T(8,128)(2,1)S(1)}, bf16[2,48,48,128]{3,2,1,0:T(8,128)(2,1)S(1)}, f32[1,48,128]{2,1,0:T(8,128)S(1)}) custom-call(f32[2,48,128]{2,1,0:T(8,128)} %bitcast.477, bf16[2,48,48,128]{3,2,1,0:T(8,128)(2,1)} %bitcast.460, bf16[2,48,48,128]{3,2,1,0:T(8,128)(2,1)} %bitcast.498), custom_call_target="tpu_custom_call" | custom-call | tf_op jit(solution)/shard_map/pallas_call | solution.py:73
  1.7 4.8 %collective-permute-start.40 = (f32[1,48,128]{2,1,0:T(8,128)S(1)}, f32[1,48,128]{2,1,0:T(8,128)S(1)}, u32[]{:S(2)}, u32[]{:S(2)}) collective-permute-start(f32[1,48,128]{2,1,0:T(8,128)S(1)} %get-tuple-element.122.refs_1_), channel_id=1, source_target_pairs={{0,8},{1,9},{2,10},{3,11},{4,12},{5,13},{6,14},{7,15}} | collective-permute-start | bytes 73736 | tf_op jit(solution)/shard_map/ppermute | solution.py:641
  6.5 0.9 shard_map.76
  7.5 0.6 collective-permute-done.40.refs_0_
  8.4 0.7 collective-permute-start.41
  9.1 0.4 shard_map.79
  9.6 0.7 collective-permute-start.42
  10.4 0.7 shard_map.77.upper
  11.1 0.6 shard_map.80
  11.8 0.7 collective-permute-start.43
  12.8 0.7 collective-permute-start.44
  13.5 0.4 shard_map.84
  13.9 1.3 collective-permute-start.45
  15.2 18.0 %collective-permute-done.45.refs_1_ = f32[48,128]{1,0:T(8,128)S(1)} collective-permute-done((f32[48,128]{1,0:T(8,128)S(1)}, f32[48,128]{1,0:T(8,128)S(1)}, u32[]{:S(2)}, u32[]{:S(2)}) %collective-permute-start.45) | collective-permute-done | bytes 24608 | tf_op jit(solution)/shard_map/ppermute | solution.py:668
  33.8 0.8 collective-permute-start.47
  35.2 2.1 %shard_map.82 = (f32[2,48,48,128]{3,2,1,0:T(8,128)S(1)}, f32[2,48,48,128]{3,2,1,0:T(8,128)S(1)}, f32[2,48,48,128]{3,2,1,0:T(8,128)S(1)}) custom-call(bf16[2,48,48,128]{3,2,1,0:T(8,128)(2,1)S(1)} %bitcast.474, bf16[2,48,48,128]{3,2,1,0:T(8,128)(2,1)S(1)} %bitcast.475, bf16[2,48,48,128]{3,2,1,0:T(8,128)(2,1)S(1)} %bitcast.476, ...), custom_call_target="tpu_custom_call" | custom-call | tf_op jit(solution)/shard_map/pallas_call | solution.py:131
  38.0 0.5 shard_map.88
  38.5 1.6 %collective-permute-start.48 = (f32[2,48,128]{2,1,0:T(8,128)S(1)}, f32[2,48,128]{2,1,0:T(8,128)S(1)}, u32[]{:S(2)}, u32[]{:S(2)}) collective-permute-start(f32[2,48,128]{2,1,0:T(8,128)S(1)} %get-tuple-element.147), channel_id=1, source_target_pairs={{0,8},{1,9},{2,10},{3,11},{4,12},{5,13},{6,14},{7,15}} | collective-permute-start | bytes 147464 | tf_op jit(solution)/shard_map/ppermute | solution.py:641
  40.2 1.7 %collective-permute-done.48.refs_0_ = f32[2,48,128]{2,1,0:T(8,128)S(1)} collective-permute-done((f32[2,48,128]{2,1,0:T(8,128)S(1)}, f32[2,48,128]{2,1,0:T(8,128)S(1)}, u32[]{:S(2)}, u32[]{:S(2)}) %collective-permute-start.48) | collective-permute-done | bytes 49184 | tf_op jit(solution)/shard_map/ppermute | solution.py:641
  42.3 0.7 collective-permute-start.49
  43.0 0.4 shard_map.91
  43.4 0.7 collective-permute-start.50
  44.1 0.6 shard_map.92
  44.7 0.7 collective-permute-start.51
  45.4 0.7 collective-permute-start.56
  46.5 0.7 collective-permute-start.52
  47.2 0.4 shard_map.94
  47.6 1.5 %collective-permute-start.53 = (f32[48,128]{1,0:T(8,128)S(1)}, f32[48,128]{1,0:T(8,128)S(1)}, u32[]{:S(2)}, u32[]{:S(2)}) collective-permute-start(f32[48,128]{1,0:T(8,128)S(1)} %get-tuple-element.160), channel_id=1, source_target_pairs={{8,0},{9,1},{10,2},{11,3},{12,4},{13,5},{14,6},{15,7}} | collective-permute-start | bytes 73736 | tf_op jit(solution)/shard_map/ppermute | solution.py:668
  49.1 20.0 %collective-permute-done.53.refs_1_ = f32[48,128]{1,0:T(8,128)S(1)} collective-permute-done((f32[48,128]{1,0:T(8,128)S(1)}, f32[48,128]{1,0:T(8,128)S(1)}, u32[]{:S(2)}, u32[]{:S(2)}) %collective-permute-start.53) | collective-permute-done | bytes 24608 | tf_op jit(solution)/shard_map/ppermute | solution.py:668
  69.6 0.7 collective-permute-start.55
  70.2 0.5 shard_map.96
  71.0 0.5 shard_map.98
  71.5 1.6 %collective-permute-start.57 = (f32[2,48,128]{2,1,0:T(8,128)S(1)}, f32[2,48,128]{2,1,0:T(8,128)S(1)}, u32[]{:S(2)}, u32[]{:S(2)}) collective-permute-start(f32[2,48,128]{2,1,0:T(8,128)S(1)} %get-tuple-element.167.message), channel_id=1, source_target_pairs={{0,8},{16,24},{1,9},{17,25},{2,10},{18,26},{3,11},{19,27},{4,12},{... | collective-permute-start | bytes 147464 | tf_op jit(solution)/shard_map/ppermute | solution.py:451
  73.1 1.7 %collective-permute-done.57.refs_0_ = f32[2,48,128]{2,1,0:T(8,128)S(1)} collective-permute-done((f32[2,48,128]{2,1,0:T(8,128)S(1)}, f32[2,48,128]{2,1,0:T(8,128)S(1)}, u32[]{:S(2)}, u32[]{:S(2)}) %collective-permute-start.57) | collective-permute-done | bytes 49184 | tf_op jit(solution)/shard_map/ppermute | solution.py:451
  75.2 0.7 collective-permute-start.59
  76.1 0.7 collective-permute-start.58
  76.8 0.9 shard_map.101
  77.7 0.7 collective-permute-start.60
  78.4 0.7 collective-permute-start.62
  79.1 0.4 shard_map.102
  79.5 1.3 collective-permute-start.61
  80.8 16.4 %collective-permute-done.61.received = f32[48,128]{1,0:T(8,128)S(1)} collective-permute-done((f32[48,128]{1,0:T(8,128)S(1)}, f32[48,128]{1,0:T(8,128)S(1)}, u32[]{:S(2)}, u32[]{:S(2)}) %collective-permute-start.61) | collective-permute-done | bytes 24608 | tf_op jit(solution)/shard_map/ppermute | solution.py:474
  97.6 0.7 collective-permute-start.64
  98.3 0.5 shard_map.104
  99.0 0.4 shard_map.106
  99.5 1.6 %collective-permute-start.65 = (f32[2,48,128]{2,1,0:T(8,128)S(1)}, f32[2,48,128]{2,1,0:T(8,128)S(1)}, u32[]{:S(2)}, u32[]{:S(2)}) collective-permute-start(f32[2,48,128]{2,1,0:T(8,128)S(1)} %get-tuple-element.183.message), channel_id=1, source_target_pairs={{0,8},{16,24},{1,9},{17,25},{2,10},{18,26},{3,11},{19,27},{4,12},{... | collective-permute-start | bytes 147464 | tf_op jit(solution)/shard_map/ppermute | solution.py:451
  101.1 1.7 %collective-permute-done.65.refs_0_ = f32[2,48,128]{2,1,0:T(8,128)S(1)} collective-permute-done((f32[2,48,128]{2,1,0:T(8,128)S(1)}, f32[2,48,128]{2,1,0:T(8,128)S(1)}, u32[]{:S(2)}, u32[]{:S(2)}) %collective-permute-start.65) | collective-permute-done | bytes 49184 | tf_op jit(solution)/shard_map/ppermute | solution.py:451
  103.2 0.7 collective-permute-start.67
  104.1 0.7 collective-permute-start.66
  104.8 0.9 shard_map.109
  105.7 0.7 collective-permute-start.68
  106.4 0.7 collective-permute-start.70
  107.0 0.4 shard_map.110
  107.5 1.3 collective-permute-start.69
  108.8 10.8 %collective-permute-done.69.received = f32[48,128]{1,0:T(8,128)S(1)} collective-permute-done((f32[48,128]{1,0:T(8,128)S(1)}, f32[48,128]{1,0:T(8,128)S(1)}, u32[]{:S(2)}, u32[]{:S(2)}) %collective-permute-start.69) | collective-permute-done | bytes 24608 | tf_op jit(solution)/shard_map/ppermute | solution.py:474
  120.0 0.8 collective-permute-start.71
  120.8 0.7 collective-permute-start.73
  121.4 1.9 %collective-permute-start.72 = (f32[48,128]{1,0:T(8,128)S(1)}, f32[48,128]{1,0:T(8,128)S(1)}, u32[]{:S(2)}, u32[]{:S(2)}) collective-permute-start(f32[48,128]{1,0:T(8,128)S(1)} %get-tuple-element.197), channel_id=1, source_target_pairs={{0,8},{8,16},{16,24},{1,9},{9,17},{17,25},{2,10},{10,18},{18,26},{... | collective-permute-start | bytes 73736 | tf_op jit(solution)/shard_map/ppermute | solution.py:709
  123.4 0.5 shard_map.112
  123.9 1.0 collective-permute-done.72.refs_1_
  125.1 0.9 shard_map.115
  126.0 11.0 %all-to-all-start = ((f32[32,1,128]{2,1,0:T(1,128)}), f32[32,1,128]{2,1,0:T(1,128)S(1)}, u32[]{:S(2)}, u32[]{:S(2)}) async-start(f32[32,1,128]{2,1,0:T(1,128)} %bitcast.206), calls=%async_computation | async-start | bytes 32768 | tf_op jit(solution)/shard_map/all_to_all | solution.py:728
  137.0 7.1 %all-to-all-done = f32[32,1,128]{2,1,0:T(1,128)S(1)} async-done(((f32[32,1,128]{2,1,0:T(1,128)}), f32[32,1,128]{2,1,0:T(1,128)S(1)}, u32[]{:S(2)}, u32[]{:S(2)}) %all-to-all-start) | async-done | bytes 16416 | tf_op jit(solution)/shard_map/all_to_all | solution.py:728
  144.1 0.8 shard_map.116
  (61 shorter events, 7.3 us)
Async XLA Ops:
  1.7 6.4 %collective-permute-start.40 = (f32[1,48,128]{2,1,0:T(8,128)S(1)}, f32[1,48,128]{2,1,0:T(8,128)S(1)}, u32[]{:S(2)}, u32[]{:S(2)}) collective-permute-start(f32[1,48,128]{2,1,0:T(8,128)S(1)} %get-tuple-element.122.refs_1_), channel_id=1, source_target_pairs={{0,8},{1,9},{2,10},{3,11},{4,12},{5,13},{6,14},{7,15}} | collective-permute-start | bytes 73736 | tf_op jit(solution)/shard_map/ppermute | solution.py:641
  6.5 1.5 %copy-start.26 = (f32[2,48,1,128]{3,2,1,0:T(1,128)S(1)}, f32[2,48,1,128]{3,2,1,0:T(1,128)}, u32[]{:S(2)}) copy-start(f32[2,48,1,128]{3,2,1,0:T(1,128)} %param.9) | copy-start | bytes 147460
  8.4 0.7 collective-permute-start.41
  9.1 1.3 copy-start
  9.6 1.6 %collective-permute-start.42 = (f32[1,48,128]{2,1,0:T(8,128)S(1)}, f32[1,48,128]{2,1,0:T(8,128)S(1)}, u32[]{:S(2)}, u32[]{:S(2)}) collective-permute-start(f32[1,48,128]{2,1,0:T(8,128)S(1)} %get-tuple-element.126.after), channel_id=1, source_target_pairs={{16,24},{17,25},{18,26},{19,27},{20,28},{21,29},{22,30},{23,31}} | collective-permute-start | bytes 73736 | tf_op jit(solution)/shard_map/ppermute | solution.py:641
  11.8 0.7 collective-permute-start.43
  12.8 0.7 collective-permute-start.44
  13.9 19.3 %collective-permute-start.45 = (f32[48,128]{1,0:T(8,128)S(1)}, f32[48,128]{1,0:T(8,128)S(1)}, u32[]{:S(2)}, u32[]{:S(2)}) collective-permute-start(f32[48,128]{1,0:T(8,128)S(1)} %get-tuple-element.136), channel_id=1, source_target_pairs={{8,0},{9,1},{10,2},{11,3},{12,4},{13,5},{14,6},{15,7}} | collective-permute-start | bytes 73736 | tf_op jit(solution)/shard_map/ppermute | solution.py:668
  33.3 1.3 copy-start.12
  33.3 1.6 %copy-start.16 = (bf16[2,48,48,1,128]{4,2,3,1,0:T(8,128)(2,1)S(1)}, bf16[2,48,48,1,128]{4,2,3,1,0:T(8,128)(2,1)}, u32[]{:S(2)}) copy-start(bf16[2,48,48,1,128]{4,2,3,1,0:T(8,128)(2,1)} %param.14) | copy-start | bytes 3538948
  33.3 2.0 %copy-start.21 = (bf16[2,48,48,1,128]{4,2,3,1,0:T(8,128)(2,1)S(1)}, bf16[2,48,48,1,128]{4,2,3,1,0:T(8,128)(2,1)}, u32[]{:S(2)}) copy-start(bf16[2,48,48,1,128]{4,2,3,1,0:T(8,128)(2,1)} %param.13) | copy-start | bytes 3538948
  33.7 4.1 %collective-permute-start.46 = (f32[2,48,128]{2,1,0:T(8,128)S(1)}, f32[2,48,128]{2,1,0:T(8,128)S(1)}, u32[]{:S(2)}, u32[]{:S(2)}) collective-permute-start(f32[2,48,128]{2,1,0:T(8,128)S(1)} %get-tuple-element.137.direction.refs_0_), channel_id=1, source_target_pairs={{0,1},{2,3},{4,5},{6,7},{1,0},{3,2},{5,4},{7,6},{8,9},{10,11},{12,... | collective-permute-start | bytes 147464 | tf_op jit(solution)/shard_map/ppermute | solution.py:440
  33.8 4.3 %collective-permute-start.47 = (f32[2,48,128]{2,1,0:T(8,128)S(1)}, f32[2,48,128]{2,1,0:T(8,128)S(1)}, u32[]{:S(2)}, u32[]{:S(2)}) collective-permute-start(f32[2,48,128]{2,1,0:T(8,128)S(1)} %get-tuple-element.137.direction.refs_0_), channel_id=1, source_target_pairs={{1,2},{3,4},{5,6},{2,1},{4,3},{6,5},{9,10},{11,12},{13,14},{10,9},... | collective-permute-start | bytes 147464 | tf_op jit(solution)/shard_map/ppermute | solution.py:439
  38.5 3.4 %collective-permute-start.48 = (f32[2,48,128]{2,1,0:T(8,128)S(1)}, f32[2,48,128]{2,1,0:T(8,128)S(1)}, u32[]{:S(2)}, u32[]{:S(2)}) collective-permute-start(f32[2,48,128]{2,1,0:T(8,128)S(1)} %get-tuple-element.147), channel_id=1, source_target_pairs={{0,8},{1,9},{2,10},{3,11},{4,12},{5,13},{6,14},{7,15}} | collective-permute-start | bytes 147464 | tf_op jit(solution)/shard_map/ppermute | solution.py:641
  42.3 0.7 collective-permute-start.49
  43.4 0.7 collective-permute-start.50
  44.7 0.7 collective-permute-start.51
  45.4 31.4 %collective-permute-start.56 = (f32[48,48,128]{2,1,0:T(8,128)S(1)}, f32[48,48,128]{2,1,0:T(8,128)S(1)}, u32[]{:S(2)}, u32[]{:S(2)}) collective-permute-start(f32[48,48,128]{2,1,0:T(8,128)S(1)} %shard_map.89), channel_id=1, source_target_pairs={{24,16},{25,17},{26,18},{27,19},{28,20},{29,21},{30,22},{31,23}} | collective-permute-start | bytes 3538952 | tf_op jit(solution)/shard_map/ppermute | solution.py:671
  46.5 0.7 collective-permute-start.52
  47.6 21.5 %collective-permute-start.53 = (f32[48,128]{1,0:T(8,128)S(1)}, f32[48,128]{1,0:T(8,128)S(1)}, u32[]{:S(2)}, u32[]{:S(2)}) collective-permute-start(f32[48,128]{1,0:T(8,128)S(1)} %get-tuple-element.160), channel_id=1, source_target_pairs={{8,0},{9,1},{10,2},{11,3},{12,4},{13,5},{14,6},{15,7}} | collective-permute-start | bytes 73736 | tf_op jit(solution)/shard_map/ppermute | solution.py:668
  69.5 1.3 collective-permute-start.54
  69.6 1.4 collective-permute-start.55
  71.5 3.4 %collective-permute-start.57 = (f32[2,48,128]{2,1,0:T(8,128)S(1)}, f32[2,48,128]{2,1,0:T(8,128)S(1)}, u32[]{:S(2)}, u32[]{:S(2)}) collective-permute-start(f32[2,48,128]{2,1,0:T(8,128)S(1)} %get-tuple-element.167.message), channel_id=1, source_target_pairs={{0,8},{16,24},{1,9},{17,25},{2,10},{18,26},{3,11},{19,27},{4,12},{... | collective-permute-start | bytes 147464 | tf_op jit(solution)/shard_map/ppermute | solution.py:451
  75.2 1.6 %collective-permute-start.59 = (f32[2,48,128]{2,1,0:T(8,128)S(1)}, f32[2,48,128]{2,1,0:T(8,128)S(1)}, u32[]{:S(2)}, u32[]{:S(2)}) collective-permute-start(f32[2,48,128]{2,1,0:T(8,128)S(1)} %get-tuple-element.170), channel_id=1, source_target_pairs={{8,16},{9,17},{10,18},{11,19},{12,20},{13,21},{14,22},{15,23}} | collective-permute-start | bytes 147464 | tf_op jit(solution)/shard_map/ppermute | solution.py:458
  76.1 0.7 collective-permute-start.58
  77.7 1.3 collective-permute-start.60
  78.4 2.4 %collective-permute-start.62 = (f32[48,128]{1,0:T(8,128)S(1)}, f32[48,128]{1,0:T(8,128)S(1)}, u32[]{:S(2)}, u32[]{:S(2)}) collective-permute-start(f32[48,128]{1,0:T(8,128)S(1)} %get-tuple-element.177), channel_id=1, source_target_pairs={{16,24},{17,25},{18,26},{19,27},{20,28},{21,29},{22,30},{23,31}} | collective-permute-start | bytes 73736 | tf_op jit(solution)/shard_map/ppermute | solution.py:475
  79.5 17.7 %collective-permute-start.61 = (f32[48,128]{1,0:T(8,128)S(1)}, f32[48,128]{1,0:T(8,128)S(1)}, u32[]{:S(2)}, u32[]{:S(2)}) collective-permute-start(f32[48,128]{1,0:T(8,128)S(1)} %get-tuple-element.176), channel_id=1, source_target_pairs={{8,0},{9,1},{10,2},{11,3},{12,4},{13,5},{14,6},{15,7}} | collective-permute-start | bytes 73736 | tf_op jit(solution)/shard_map/ppermute | solution.py:474
  97.5 1.3 collective-permute-start.63
  97.6 1.4 collective-permute-start.64
  99.5 3.4 %collective-permute-start.65 = (f32[2,48,128]{2,1,0:T(8,128)S(1)}, f32[2,48,128]{2,1,0:T(8,128)S(1)}, u32[]{:S(2)}, u32[]{:S(2)}) collective-permute-start(f32[2,48,128]{2,1,0:T(8,128)S(1)} %get-tuple-element.183.message), channel_id=1, source_target_pairs={{0,8},{16,24},{1,9},{17,25},{2,10},{18,26},{3,11},{19,27},{4,12},{... | collective-permute-start | bytes 147464 | tf_op jit(solution)/shard_map/ppermute | solution.py:451
  103.2 1.6 %collective-permute-start.67 = (f32[2,48,128]{2,1,0:T(8,128)S(1)}, f32[2,48,128]{2,1,0:T(8,128)S(1)}, u32[]{:S(2)}, u32[]{:S(2)}) collective-permute-start(f32[2,48,128]{2,1,0:T(8,128)S(1)} %get-tuple-element.186), channel_id=1, source_target_pairs={{8,16},{9,17},{10,18},{11,19},{12,20},{13,21},{14,22},{15,23}} | collective-permute-start | bytes 147464 | tf_op jit(solution)/shard_map/ppermute | solution.py:458
  104.1 0.7 collective-permute-start.66
  105.7 1.3 collective-permute-start.68
  106.4 2.4 %collective-permute-start.70 = (f32[48,128]{1,0:T(8,128)S(1)}, f32[48,128]{1,0:T(8,128)S(1)}, u32[]{:S(2)}, u32[]{:S(2)}) collective-permute-start(f32[48,128]{1,0:T(8,128)S(1)} %get-tuple-element.193), channel_id=1, source_target_pairs={{16,24},{17,25},{18,26},{19,27},{20,28},{21,29},{22,30},{23,31}} | collective-permute-start | bytes 73736 | tf_op jit(solution)/shard_map/ppermute | solution.py:475
  107.5 12.1 %collective-permute-start.69 = (f32[48,128]{1,0:T(8,128)S(1)}, f32[48,128]{1,0:T(8,128)S(1)}, u32[]{:S(2)}, u32[]{:S(2)}) collective-permute-start(f32[48,128]{1,0:T(8,128)S(1)} %get-tuple-element.192), channel_id=1, source_target_pairs={{8,0},{9,1},{10,2},{11,3},{12,4},{13,5},{14,6},{15,7}} | collective-permute-start | bytes 73736 | tf_op jit(solution)/shard_map/ppermute | solution.py:474
  120.0 4.9 %collective-permute-start.71 = (f32[2,48,128]{2,1,0:T(8,128)S(1)}, f32[2,48,128]{2,1,0:T(8,128)S(1)}, u32[]{:S(2)}, u32[]{:S(2)}) collective-permute-start(f32[2,48,128]{2,1,0:T(8,128)S(1)} %get-tuple-element.194.direction.refs_3_), channel_id=1, source_target_pairs={{0,1},{2,3},{4,5},{6,7},{1,0},{3,2},{5,4},{7,6},{8,9},{10,11},{12,... | collective-permute-start | bytes 147464 | tf_op jit(solution)/shard_map/ppermute | solution.py:440
  120.8 4.4 %collective-permute-start.73 = (f32[2,48,128]{2,1,0:T(8,128)S(1)}, f32[2,48,128]{2,1,0:T(8,128)S(1)}, u32[]{:S(2)}, u32[]{:S(2)}) collective-permute-start(f32[2,48,128]{2,1,0:T(8,128)S(1)} %get-tuple-element.194.direction.refs_3_), channel_id=1, source_target_pairs={{1,2},{3,4},{5,6},{2,1},{4,3},{6,5},{9,10},{11,12},{13,14},{10,9},... | collective-permute-start | bytes 147464 | tf_op jit(solution)/shard_map/ppermute | solution.py:439
  121.4 3.4 %collective-permute-start.72 = (f32[48,128]{1,0:T(8,128)S(1)}, f32[48,128]{1,0:T(8,128)S(1)}, u32[]{:S(2)}, u32[]{:S(2)}) collective-permute-start(f32[48,128]{1,0:T(8,128)S(1)} %get-tuple-element.197), channel_id=1, source_target_pairs={{0,8},{8,16},{16,24},{1,9},{9,17},{17,25},{2,10},{10,18},{18,26},{... | collective-permute-start | bytes 73736 | tf_op jit(solution)/shard_map/ppermute | solution.py:709
  125.1 19.8 %copy-start.5 = (bf16[2,48,48,1,128]{4,2,3,1,0:T(8,128)(2,1)S(1)}, bf16[2,48,48,1,128]{4,2,3,1,0:T(8,128)(2,1)}, u32[]{:S(2)}) copy-start(bf16[2,48,48,1,128]{4,2,3,1,0:T(8,128)(2,1)} %param.11) | copy-start | bytes 3538948
  126.0 18.1 %all-to-all-start = ((f32[32,1,128]{2,1,0:T(1,128)}), f32[32,1,128]{2,1,0:T(1,128)S(1)}, u32[]{:S(2)}, u32[]{:S(2)}) async-start(f32[32,1,128]{2,1,0:T(1,128)} %bitcast.206), calls=%async_computation | async-start | bytes 32768 | tf_op jit(solution)/shard_map/all_to_all | solution.py:728
